TPU v7x, 32 devices: a whole 2x2x4 slice. The times are simulated.
32 devices in a mesh: dp: 16 (over z, x, core), mp: 2 (over y).
Axes of the slice: x: 2, y: 2, z: 4, core: 2. Of those that a mesh axis runs over, the one named last changes fastest.
Arguments:
- tokens: bfloat16 [24576, 1024], P('dp', 'mp'), may hold values from -6 to 6
- out_grad: bfloat16 [24576, 1024], P('dp', 'mp'), may hold values from -0.1875 to 0.1875
- master: float32 [2, 256, 128, 128], P('mp', 'dp'), may hold values from -0.1875 to 0.1875
- momentum: float32 [2, 256, 128, 128], P('mp', 'dp'), may hold values from -6 to 6
- residual: bfloat16 [16, 2, 256, 128, 128], P('dp', 'mp'), may hold values from -1.75 to 1.75
- kept_blocks: int32 [16, 2, 64], P('dp', 'mp'), may hold values from 0 to 255, as said below
Outputs:
- new_master: float32 [2, 256, 128, 128], P('mp', 'dp')
- new_momentum: float32 [2, 256, 128, 128], P('mp', 'dp')
- new_residual: bfloat16 [16, 2, 256, 128, 128], P('dp', 'mp')
Inputs may be any that keep to these rules, and one draw needn't show every extreme that they name: `kept_blocks`: each list names 64 distinct blocks of its shard.
All inputs are finite; a program needn't handle non-finite values.
Results may differ from a plain program's by a relative error of at most 0.0058.
Values may be sent and summed in bfloat16 or wider, within the bound.
No kernel may reach another device: no remote copies, remote signals or barrier semaphores. Data moves between devices by JAX's collectives and lax.ppermute only.
A program may use at most 128 MiB of HBM per device.

v0:
```python
import jax
import jax.numpy as jnp
from jax import lax
from jax.sharding import PartitionSpec as P

momentum_decay = 0.9
step_size = 0.01


def activation(values):
    return jax.nn.gelu(values, approximate=True)


def local(tokens, out_grad, master, momentum, residual, kept_blocks):
    whole_in, whole_grad = (
        lax.all_gather(tokens, "mp", axis=1, tiled=True),
        lax.all_gather(out_grad, "mp", axis=1, tiled=True),
    )
    tile_size = master.shape[-1]
    tok_rows, model_width = whole_in.shape
    block_count = residual.shape[2]
    first_count = block_count // 2
    row_blocks = model_width // tile_size
    col_blocks = first_count // row_blocks
    working = lax.all_gather(master.astype(jnp.bfloat16), "dp", axis=1, tiled=True)[0]
    first_layer_weight = working[:first_count].reshape(row_blocks, col_blocks, tile_size, tile_size)
    second_layer_weight = working[first_count:].reshape(
        col_blocks, row_blocks, tile_size, tile_size
    )
    input_block_tiles = whole_in.reshape(tok_rows, row_blocks, tile_size)
    gradient_block_tiles = whole_grad.reshape(tok_rows, row_blocks, tile_size)
    hidden_state = jnp.einsum(
        "lbm,bymi->lyi", input_block_tiles, first_layer_weight, preferred_element_type=jnp.float32
    )
    act_full, pullback = jax.vjp(activation, hidden_state)
    gelu_hidden_output = act_full.astype(jnp.bfloat16)
    act_grad = jnp.einsum(
        "dhr,vhzr->dvz",
        gradient_block_tiles,
        second_layer_weight,
        preferred_element_type=jnp.float32,
    )
    hidden_gradient = pullback(act_grad)[0].astype(jnp.bfloat16)
    first_layer_gradient = jnp.einsum(
        "hgl,hvo->gvlo", input_block_tiles, hidden_gradient, preferred_element_type=jnp.float32
    )
    second_g = jnp.einsum(
        "qvz,qxm->vxzm",
        gelu_hidden_output,
        gradient_block_tiles,
        preferred_element_type=jnp.float32,
    )
    grads = jnp.concatenate(
        [
            first_layer_gradient.reshape(first_count, tile_size, tile_size),
            second_g.reshape(first_count, tile_size, tile_size),
        ],
        axis=0,
    )
    grads = grads + residual[0, 0].astype(jnp.float32)
    chosen = kept_blocks[0, 0]
    flags = jnp.any(jnp.arange(block_count, dtype=jnp.int32)[None, :] == chosen[:, None], axis=0)[
        :, None, None
    ]
    new_residual = jnp.where(flags, 0.0, grads).astype(jnp.bfloat16)[None, None]
    masked = jnp.where(flags, grads, 0.0)
    owned = lax.psum_scatter(masked, "dp", scatter_dimension=0, tiled=True)
    new_momentum = momentum_decay * momentum + owned[None]
    new_master = master - step_size * new_momentum
    return (new_master, new_momentum, new_residual)


def solution(mesh):
    in_specs = (
        P("dp", "mp"),
        P("dp", "mp"),
        P("mp", "dp", None, None),
        P("mp", "dp", None, None),
        P("dp", "mp", None, None, None),
        P("dp", "mp", None),
    )
    out_specs = (
        P("mp", "dp", None, None),
        P("mp", "dp", None, None),
        P("dp", "mp", None, None, None),
    )
    return jax.shard_map(local, mesh=mesh, in_specs=in_specs, out_specs=out_specs, check_vma=False)
```

profile of v0, /device:TPU:0, one launch (start us, length us, event | category | flops | bytes accessed | tf_op | source)
XLA Modules:
  0.0 432.8 jit_solution(1606069800648749064)
XLA Ops:
  7.2 0.0 all-gather.6.cloned.1.call-start
  7.2 2.1 bitcast_convert_fusion
  9.3 0.0 all-gather.6.cloned.1.call-update
  9.3 0.0 all-gather.8.cloned.1.call-start
  9.4 2.6 copy.38
  12.0 0.0 all-gather.8.cloned.1.call-update
  12.0 0.0 all-gather.4.cloned.1.call-start
  12.1 2.6 copy.35
  14.7 0.0 reduce-scatter.2.cloned.1.call-start
  14.7 1.3 fusion.26
  16.0 72.4 %all-gather.6.cloned.1.call-done = bf16[1,256,128,128]{3,2,0,1:T(8,128)(2,1)} async-done(((bf16[1,16,128,128]{3,2,0,1:T(8,128)(2,1)}), bf16[1,256,128,128]{3,2,0,1:T(8,128)(2,1)}) %all-gather.6.cloned.1.call-update) | async-done | bytes 8388624 | tf_op jit(solution)/shard_map/all_gather | solution.py:25
  88.4 4.8 %slice.11 = bf16[1,128,128,128]{3,2,1,0:T(8,128)(2,1)} slice(bf16[1,256,128,128]{3,2,1,0:T(8,128)(2,1)} %bitcast.97), slice={[0:1], [0:128], [0:128], [0:128]} | slice | bytes 8388608 | tf_op jit(solution)/shard_map/slice | solution.py:26
  93.1 40.0 %all-gather.8.cloned.1.call-done = bf16[1536,1024]{0,1:T(8,128)(2,1)} async-done(((bf16[1536,512]{0,1:T(8,128)(2,1)}), bf16[1536,1024]{0,1:T(8,128)(2,1)}) %all-gather.8.cloned.1.call-update) | async-done | bytes 3145744 | tf_op jit(solution)/shard_map/all_gather | solution.py:16
  133.1 12.3 %fusion.31 = f32[1536,16,128,1]{2,0,1,3:T(8,128)} fusion(bf16[1536,8,128,1]{0,2,3,1:T(8,128)(2,1)} %bitcast.100, bf16[8,16,128,128]{3,2,1,0:T(8,128)(2,1)} %bitcast.98), kind=kOutput, calls=%fused_computation.39 | convolution fusion | flops 6442450944 | bytes 19922944 | tf_op jit(solution)/shard_map/lbm,bymi->lyi/dot_general | solution.py:32
  145.4 34.3 %all-gather.4.cloned.1.call-done = bf16[1536,1024]{0,1:T(8,128)(2,1)} async-done(((bf16[1536,512]{0,1:T(8,128)(2,1)}), bf16[1536,1024]{0,1:T(8,128)(2,1)}) %all-gather.4.cloned.1.call-update) | async-done | bytes 3145744 | tf_op jit(solution)/shard_map/all_gather | solution.py:17
  179.6 14.9 %fusion.15 = f32[16,128,8,128]{3,1,2,0:T(8,128)} fusion(bf16[1536,8,128,1]{0,2,1,3:T(8,128)(2,1)} %bitcast.102, f32[1536,16,128,1]{2,0,1,3:T(8,128)} %fusion.31), kind=kOutput, calls=%fused_computation.22 | convolution fusion | flops 6470762496 | bytes 24117248 | tf_op jit(solution)/shard_map/qvz,qxm->vxzm/dot_general | solution.py:47
  194.6 2.3 slice.10
  196.8 24.4 %fusion.23 = f32[8,16,128,128]{2,3,0,1:T(8,128)} fusion(bf16[1536,8,128,1]{0,2,1,3:T(8,128)(2,1)S(1)} %bitcast.101, f32[1536,16,128,1]{2,0,1,3:T(8,128)} %fusion.31, bf16[1536,8,128,1]{0,2,1,3:T(8,128)(2,1)} %bitcast.103, bf16[16,8,128,128]{3,2,1,0:T(8,128)(2,1)} %bitcast.99), kind=kOutput, calls=%fused_computation.29 | convolution fusion | flops 12947816448 | bytes 31457280 | tf_op jit(solution)/shard_map/hgl,hvo->gvlo/dot_general | solution.py:44
  221.2 9.2 %copy.44 = f32[8,16,128,128]{3,2,1,0:T(8,128)} copy(f32[8,16,128,128]{2,3,0,1:T(8,128)} %fusion.23) | data formatting | bytes 16777216 | tf_op jit(solution)/shard_map/hgl,hvo->gvlo/transpose | solution.py:44
  230.4 14.4 %fusion.1 = f32[256,128,128]{2,1,0:T(8,128)} fusion(bf16[1,1,256,128,128]{4,3,2,1,0:T(8,128)(2,1)} %param.10, f32[128,128,128]{2,1,0:T(8,128)} %bitcast.95, f32[128,128,128]{2,1,0:T(8,128)} %bitcast.93, pred[256]{0:T(512)(128)(4,1)S(1)} %copy-done.3), kind=kLoop, calls=%fused_computation.5 | loop fusion | flops 16777216 | bytes 41943296 | tf_op jit(solution)/shard_map/jit(_where)/select_n | solution.py:66
  244.8 0.0 reduce-scatter.2.cloned.1.call-update
  244.8 15.8 %fusion.3 = bf16[1,1,256,128,128]{4,3,2,1,0:T(8,128)(2,1)} fusion(bf16[1,1,256,128,128]{4,3,2,1,0:T(8,128)(2,1)} %param.10, f32[1,1,128,128,128]{4,3,2,1,0:T(8,128)} %bitcast.96, f32[1,1,128,128,128]{4,3,2,1,0:T(8,128)} %bitcast.94, pred[256]{0:T(512)(128)(4,1)S(1)} %copy-done.3), kind=kLoop, calls=%fused_computation.7 | loop fusion | flops 20971520 | bytes 33554688 | tf_op jit(solution)/shard_map/convert_element_type | solution.py:65
  260.6 162.8 %reduce-scatter.2.cloned.1.call-done = f32[16,128,128]{2,1,0:T(8,128)} async-done(((f32[256,128,128]{2,1,0:T(8,128)}), f32[16,128,128]{2,1,0:T(8,128)}) %reduce-scatter.2.cloned.1.call-update) | async-done | bytes 1048592 | tf_op jit(solution)/shard_map/reduce_scatter | solution.py:67
  423.5 2.8 multiply_subtract_fusion
  (11 shorter events, 0.0 us)
Async XLA Ops:
  7.2 81.2 %all-gather.6.cloned.1.call-start = ((), (), s32[]{:S(2)}) async-start(), calls=%async_computation.2 | async-start | bytes 8912896 | tf_op jit(solution)/shard_map/all_gather | solution.py:25
  9.3 123.8 %all-gather.8.cloned.1.call-start = ((), (), s32[]{:S(2)}) async-start(), calls=%async_computation.3 | async-start | bytes 4718592 | tf_op jit(solution)/shard_map/all_gather | solution.py:16
  12.0 167.6 %all-gather.4.cloned.1.call-start = ((), (), s32[]{:S(2)}) async-start(), calls=%async_computation.1 | async-start | bytes 4718592 | tf_op jit(solution)/shard_map/all_gather | solution.py:17
  14.7 408.8 %reduce-scatter.2.cloned.1.call-start = ((), (), s32[]{:S(2)}) async-start(), calls=%async_computation.4 | async-start | bytes 17825792 | tf_op jit(solution)/shard_map/reduce_scatter | solution.py:67
  179.6 14.9 %copy-start = (bf16[1,256,128,128]{3,2,0,1:T(8,128)(2,1)S(1)}, bf16[1,256,128,128]{3,2,0,1:T(8,128)(2,1)}, u32[]{:S(2)}) copy-start(bf16[1,256,128,128]{3,2,0,1:T(8,128)(2,1)} %all-gather.6.cloned.1.call-done) | copy-start | bytes 25165828
  179.6 17.2 %copy-start.4 = (bf16[1536,1024]{0,1:T(8,128)(2,1)S(1)}, bf16[1536,1024]{0,1:T(8,128)(2,1)}, u32[]{:S(2)}) copy-start(bf16[1536,1024]{0,1:T(8,128)(2,1)} %all-gather.8.cloned.1.call-done) | copy-start | bytes 9437188
  221.2 9.2 %copy-start.3 = (pred[256]{0:T(512)(128)(4,1)S(1)}, pred[256]{0:T(512)(128)(4,1)}, u32[]{:S(2)}) copy-start(pred[256]{0:T(512)(128)(4,1)} %fusion.26) | copy-start | bytes 772
  244.8 178.7 %copy-start.1 = (f32[1,16,128,128]{3,2,1,0:T(8,128)S(1)}, f32[1,16,128,128]{3,2,1,0:T(8,128)}, u32[]{:S(2)}) copy-start(f32[1,16,128,128]{3,2,1,0:T(8,128)} %param.8) | copy-start | bytes 3145732
  244.8 178.7 %copy-start.2 = (f32[1,16,128,128]{3,2,1,0:T(8,128)S(1)}, f32[1,16,128,128]{3,2,1,0:T(8,128)}, u32[]{:S(2)}) copy-start(f32[1,16,128,128]{3,2,1,0:T(8,128)} %param.9) | copy-start | bytes 3145732
Sparse Core Ops, SparseCore 0:
  10.7 77.5 all-gather.5
  89.9 43.1 all-gather.7
  134.7 44.9 all-gather.3
  244.9 178.4 reduce-scatter.1
where the time goes:
time: 433 us
  waiting for transfers between devices  309 us (71%)
  matrix products  51.5 us (12%)
  other arithmetic  36.4 us (8%)
  local copies, waits for them, and re-layouts  21.4 us (5%)
  between operations  13.8 us (3%)
    reduce_scatter x1, waiting for transfers between devices, local(): owned = lax.psum_scatter(masked, 'dp', scatter_dimension=0, tiled=True)  163 us
    all_gather x1, waiting for transfers between devices, local(): lax.all_gather(master.astype(jnp.bfloat16), 'dp', axis=1, tiled=True)[0]  72.4 us
    all_gather x1, waiting for transfers between devices, local(): lax.all_gather(tokens, 'mp', axis=1, tiled=True)  40 us
    all_gather x1, waiting for transfers between devices, local(): lax.all_gather(out_grad, 'mp', axis=1, tiled=True)  34.3 us
    dot_general x1, matrix products, local(): jnp.einsum('hgl,hvo->gvlo', input_block_tiles, hidden_gradient, preferred...  24.4 us
    convert_element_type x1, other arithmetic, local(): new_residual = jnp.where(flags, 0.0, grads).astype(jnp.bfloat16)[None, None]  15.8 us
    dot_general x1, matrix products, local(): jnp.einsum('qvz,qxm->vxzm', gelu_hidden_output, gradient_block_tiles, pre...  14.9 us
    select_n x1, other arithmetic, local(): masked = jnp.where(flags, grads, 0.0)  14.4 us
  transfers between devices with their start and end apart: 4, of which 4 were waited for; matrix products, arithmetic and copies ran while one was open for 9% of the time, Pallas kernels for 0%

commit v1 on v0

v1 whole, which is shorter than its diff:
```python
import functools

import jax
import jax.numpy as jnp
from jax import lax
from jax.experimental import pallas as pl
from jax.experimental.pallas import tpu as pltpu
from jax.sharding import PartitionSpec as P

momentum_decay = 0.9
step_size = 0.01
BF = jnp.bfloat16
F32 = jnp.float32
ANY = pl.BlockSpec(memory_space=pl.ANY)
GELU_S = 0.7978845608028654
GELU_C = 0.044715


def activation(values):
    return jax.nn.gelu(values, approximate=True)


def gelu_and_slope(v):
    sq = v * v
    t = jnp.tanh(v * (GELU_S + (GELU_S * GELU_C) * sq))
    half = 0.5 + 0.5 * t
    act = v * half
    slope = half + act * (1.0 - t) * (GELU_S + (3.0 * GELU_S * GELU_C) * sq)
    return act, slope


def unit_copies(owner, half, src, dst, sem, first, shift):
    if first:
        row = pl.multiple_of(((owner - shift) & 7) * 128, 128)
        lo, n = (0, 16) if half is None else (8 * half, 8)
        return [pltpu.make_async_copy(src, dst.at[pl.ds(lo, n), pl.ds(row, 128)], sem)]
    out = []
    for i in range(2):
        if half is None or half == i:
            row = pl.multiple_of((owner - 8) * 256 + 128 * i, 128)
            part = src.at[pl.ds(8 * i, 8)] if half is None else src
            out.append(pltpu.make_async_copy(part, dst.at[:, pl.ds(row, 128)], sem))
    return out


def load_weight(halves, first, owners, shift, srcs, dst, sem):
    for s, src in enumerate(srcs):
        owner = owners[s]

        @pl.when((owner < 8) if first else (owner >= 8))
        def _():
            for copy in unit_copies(owner, halves[s], src, dst, sem, first, shift):
                copy.start()


def pre_kernel(halves, owners, x_own, x_other, *refs):
    n = len(halves)
    srcs, (xa, slope_ref, w1, sem) = refs[:n], refs[n:]
    step = pl.program_id(0)
    shift = owners[n]

    @pl.when(step == 0)
    def _():
        load_weight(halves, True, owners, shift, srcs, w1, sem)

    for s in range(4):

        @pl.when(step == s)
        def _(s=s):
            src = x_own if s < 2 else x_other
            xa[...] = src[:, 256 * (s % 2) : 256 * (s % 2) + 256]

    @pl.when(step == 3)
    def _():
        pltpu.make_async_copy(w1, w1, sem).wait()

    @pl.when(step >= 4)
    def _():
        c = 2 * (step - 4)
        w = jnp.concatenate([w1[c], w1[c + 1]], axis=1)
        half = w.shape[0] // 2
        rows = x_own.shape[0]
        for r in range(0, rows, 512):
            pre = jnp.dot(x_own[r : r + 512, :], w[:half], preferred_element_type=F32)
            pre += jnp.dot(x_other[r : r + 512, :], w[half:], preferred_element_type=F32)
            act, slope = gelu_and_slope(pre)
            xa[r : r + 512, :] = act.astype(BF)
            slope_ref[r : r + 512, :] = slope


def hid_kernel(halves, owners, dy_own, dy_other, slope_ref, *refs):
    n = len(halves)
    srcs, rest = refs[:n], refs[n:]
    hd, w2, sem = rest[-3:]
    step = pl.program_id(0)
    shift = owners[n]

    @pl.when(step == 0)
    def _():
        load_weight(halves, False, owners, shift, srcs, w2, sem)

    for s in range(4):

        @pl.when(step == s)
        def _(s=s):
            src = dy_own if s < 2 else dy_other
            hd[...] = src[:, 256 * (s % 2) : 256 * (s % 2) + 256]

    @pl.when(step == 3)
    def _():
        pltpu.make_async_copy(w2, w2, sem).wait()

    @pl.when(step >= 4)
    def _():
        row = pl.multiple_of(256 * (step - 4), 256)
        w = jnp.concatenate([w2[(c + shift) & 7, pl.ds(row, 256), :] for c in range(8)], axis=1)
        half = w.shape[1] // 2
        dims = (((1,), (1,)), ((), ()))
        g = lax.dot_general(dy_own[...], w[:, :half], dims, preferred_element_type=F32)
        g += lax.dot_general(dy_other[...], w[:, half:], dims, preferred_element_type=F32)
        hd[...] = (g * slope_ref[...]).astype(BF)


def grad_kernel(info, flags, a_ref, b_ref, res_ref, *refs):
    new_res, mine, other = refs[-3:]
    group, h = pl.program_id(0), pl.program_id(1)
    g = info[3 * group]
    first = g < 4
    shift, core = info[info.shape[0] - 2], info[info.shape[0] - 1]
    grad = lax.dot_general(a_ref[...], b_ref[...], (((0,), (0,)), ((), ())), preferred_element_type=F32)
    for i in range(2):
        for j in range(8):
            slot = jnp.where(first, 8 * h + j, 8 * i + ((j + shift) & 7))
            target = jnp.where(first, i, h)
            flat = 16 * target + slot
            kept = flags[32 * g + flat] != 0
            v = grad[128 * i : 128 * i + 128, 128 * j : 128 * j + 128] + res_ref[0, flat].astype(F32)
            new_res[0, flat] = jnp.where(kept, 0.0, v).astype(BF)
            send = jnp.where(kept, v, 0.0).astype(BF)

            @pl.when(target == core)
            def _(send=send, slot=slot):
                mine[0, slot] = send

            @pl.when(target != core)
            def _(send=send, slot=slot):
                other[0, slot] = send


def run_pre(owners, halves, x_own, x_other, units):
    rows = x_own.shape[0]
    full = pl.BlockSpec(x_own.shape, lambda i, *_: (0, 0))
    return pl.pallas_call(
        functools.partial(pre_kernel, halves),
        grid_spec=pltpu.PrefetchScalarGridSpec(
            num_scalar_prefetch=1,
            grid=(12,),
            in_specs=[full, full] + [ANY] * len(units),
            out_specs=[
                pl.BlockSpec((rows, 256), lambda i, *_: (0, i)),
                pl.BlockSpec((rows, 256), lambda i, *_: (0, jnp.maximum(i - 4, 0))),
            ],
            scratch_shapes=[pltpu.VMEM((16, 1024, 128), BF), pltpu.SemaphoreType.DMA],
        ),
        out_shape=[jax.ShapeDtypeStruct((rows, 3072), BF), jax.ShapeDtypeStruct((rows, 2048), F32)],
        compiler_params=pltpu.CompilerParams(vmem_limit_bytes=40 * 2**20),
        cost_estimate=pl.CostEstimate(flops=2 * rows * 1024 * 2048, bytes_accessed=30_000_000, transcendentals=rows * 2048),
        name="pre_act",
    )(owners, x_own, x_other, *units)


def run_hid(owners, halves, dy_own, dy_other, slope, units, row_block, hd=None):
    rows = dy_own.shape[0]
    total = slope.shape[0]
    full = pl.BlockSpec(dy_own.shape, lambda i, *_: (0, 0))
    operands = [owners, dy_own, dy_other, slope, *units]
    specs = [full, full, pl.BlockSpec((rows, 256), lambda i, *_: (row_block, jnp.maximum(i - 4, 0)))] + [ANY] * len(units)
    alias = {}
    if hd is not None:
        alias = {len(operands): 0}
        operands.append(hd)
        specs.append(ANY)
    return pl.pallas_call(
        functools.partial(hid_kernel, halves),
        grid_spec=pltpu.PrefetchScalarGridSpec(
            num_scalar_prefetch=1,
            grid=(12,),
            in_specs=specs,
            out_specs=pl.BlockSpec((rows, 256), lambda i, *_: (row_block, jnp.where(i < 4, i + 8, i - 4))),
            scratch_shapes=[pltpu.VMEM((8, 2048, 128), BF), pltpu.SemaphoreType.DMA],
        ),
        out_shape=jax.ShapeDtypeStruct((total, 3072), BF),
        input_output_aliases=alias,
        compiler_params=pltpu.CompilerParams(vmem_limit_bytes=40 * 2**20),
        cost_estimate=pl.CostEstimate(flops=2 * rows * 1024 * 2048, bytes_accessed=30_000_000 * rows // total, transcendentals=0),
        name="hid_grad",
    )(*operands)


def run_grads(info, flags, xa, hd, residual, new_res, count):
    rows = xa.shape[0]
    operands = [info, flags, xa, hd, residual]
    block = lambda size: pl.BlockSpec((1, size, 128, 128), lambda i, h, info, *_: (info[3 * i], 0, 0, 0))
    local_block = pl.BlockSpec((1, 16, 128, 128), lambda i, h, *_: (i, 0, 0, 0))
    specs = [
        pl.BlockSpec((rows, 256), lambda i, h, info, *_: (0, jnp.where(info[3 * i] < 4, info[3 * i + 1], info[3 * i + 1] + h))),
        pl.BlockSpec((rows, 1024), lambda i, h, info, *_: (0, jnp.where(info[3 * i] < 4, h, 2))),
        block(32),
    ]
    alias = {}
    if new_res is not None:
        alias = {len(operands): 0}
        operands.append(new_res)
        specs.append(ANY)
    sent = jax.ShapeDtypeStruct((count, 16, 128, 128), BF)
    return pl.pallas_call(
        grad_kernel,
        grid_spec=pltpu.PrefetchScalarGridSpec(
            num_scalar_prefetch=2,
            grid=(count, 2),
            in_specs=specs,
            out_specs=[block(32), local_block, local_block],
        ),
        out_shape=[jax.ShapeDtypeStruct(residual.shape, BF), sent, sent],
        input_output_aliases=alias,
        compiler_params=pltpu.CompilerParams(vmem_limit_bytes=40 * 2**20),
        cost_estimate=pl.CostEstimate(flops=2 * rows * 1024 * 512 * count, bytes_accessed=12_000_000 * count, transcendentals=0),
        name="grad_blocks",
    )(*operands)


def chip_at(place):
    place = place % 8
    if isinstance(place, int):
        return 2 * place if place < 4 else 2 * (7 - place) + 1
    return jnp.where(place < 4, 2 * place, 2 * (7 - place) + 1)


def ring_pairs(step):
    return [(2 * chip_at(p) + c, 2 * chip_at(p + step) + c) for p in range(8) for c in range(2)]


UP, DOWN = ring_pairs(1), ring_pairs(-1)
CORES = [(i, i ^ 1) for i in range(16)]
PAIR = [(0, 1), (1, 0)]


def hop(array, pairs):
    return lax.ppermute(array, "dp", pairs)


def local_ring(tokens, out_grad, master, momentum, residual, kept_blocks):
    mine = lax.axis_index("dp").astype(jnp.int32)
    shard = lax.axis_index("mp").astype(jnp.int32)
    core = mine & 1
    chip = mine >> 1
    place = jnp.where((chip & 1) == 0, chip >> 1, 7 - (chip >> 1))
    rows = tokens.shape[0]

    x_other = lax.ppermute(tokens, "mp", PAIR)
    parts = 2
    size = rows // parts
    dy_own = [out_grad[i * size : (i + 1) * size] for i in range(parts)]
    dy_other = [lax.ppermute(t, "mp", PAIR) for t in dy_own]

    own = master[0].astype(BF)
    up1, down1 = hop(own, UP), hop(own, DOWN)
    up2, down2 = hop(up1, UP), hop(down1, DOWN)
    up3, down3 = hop(up2, UP), hop(down2, DOWN)
    up4, down4 = hop(up3[:8], UP), hop(down3[8:], DOWN)
    units = [own, up1, down1, up2, down2, up3, down3, up4, down4]
    offsets = [0, -1, 1, -2, 2, -3, 3, -4, 4]
    halves = [None] * 7 + [0, 1]
    units = units + [hop(u, CORES) for u in units]
    owners = [2 * chip_at(place + o) + core for o in offsets]
    owners = owners + [o ^ 1 for o in owners]
    halves = tuple(halves * 2)
    shift = 4 * shard
    owners = jnp.stack(owners + [shift])

    block_count = residual.shape[2]
    flags = jnp.any(jnp.arange(block_count, dtype=jnp.int32)[None, :] == kept_blocks[0, 0][:, None], axis=0)
    flags = flags.astype(jnp.int32)

    xa, slope = run_pre(owners, halves, tokens, x_other, units)
    hd = None
    for i in range(parts):
        hd = run_hid(owners, halves, dy_own[i], dy_other[i], slope, units, i, hd)

    stored = residual.reshape(8, 32, 128, 128)

    def info_of(distances):
        out = []
        for k in distances:
            g = chip_at(place + k)
            a = jnp.where(g < 4, (g - 2 * shard) & 3, 4 + 2 * (g - 4))
            out += [g, a, a]
        return jnp.stack(out + [shift, core])

    new_res = None
    sums = {}
    for distances in ([4], [3, 5], [2, 6, 1, 7, 0]):
        new_res, own_sum, other_sum = run_grads(info_of(distances), flags, xa, hd, stored, new_res, len(distances))
        for i, k in enumerate(distances):
            sums[k] = own_sum[i].astype(F32) + hop(other_sum[i], CORES).astype(F32)

    up, down = hop(sums[4][:8].astype(BF), UP), hop(sums[4][8:].astype(BF), DOWN)
    s3 = sums[3] + jnp.pad(up.astype(F32), ((0, 8), (0, 0), (0, 0)))
    s5 = sums[5] + jnp.pad(down.astype(F32), ((8, 0), (0, 0), (0, 0)))
    up, down = hop(s3.astype(BF), UP), hop(s5.astype(BF), DOWN)
    for k in (2, 1):
        up, down = hop((sums[k] + up.astype(F32)).astype(BF), UP), hop((sums[8 - k] + down.astype(F32)).astype(BF), DOWN)
    owned = sums[0] + up.astype(F32) + down.astype(F32)
    new_momentum = momentum_decay * momentum + owned[None]
    new_master = master - step_size * new_momentum
    return new_master, new_momentum, new_res.reshape(residual.shape)


def local_plain(tokens, out_grad, master, momentum, residual, kept_blocks):
    whole_in = lax.all_gather(tokens, "mp", axis=1, tiled=True)
    whole_grad = lax.all_gather(out_grad, "mp", axis=1, tiled=True)
    tile = master.shape[-1]
    width = whole_in.shape[1]
    block_count = residual.shape[2]
    half = block_count // 2
    rows = width // tile
    cols = half // rows
    working = lax.all_gather(master.astype(BF), "dp", axis=1, tiled=True)[0]
    first_w = working[:half].reshape(rows, cols, tile, tile).transpose(0, 2, 1, 3).reshape(width, cols * tile)
    second_w = working[half:].reshape(cols, rows, tile, tile).transpose(0, 2, 1, 3).reshape(cols * tile, width)
    pre = jnp.dot(whole_in, first_w, preferred_element_type=F32)
    act_full, pullback = jax.vjp(activation, pre)
    act = act_full.astype(BF)
    act_grad = jnp.dot(whole_grad, second_w.T, preferred_element_type=F32)
    hid = pullback(act_grad)[0].astype(BF)
    first_g = jnp.dot(whole_in.T, hid, preferred_element_type=F32)
    second_g = jnp.dot(act.T, whole_grad, preferred_element_type=F32)
    first_g = first_g.reshape(rows, tile, cols, tile).transpose(0, 2, 1, 3).reshape(half, tile, tile)
    second_g = second_g.reshape(cols, tile, rows, tile).transpose(0, 2, 1, 3).reshape(half, tile, tile)
    grads = jnp.concatenate([first_g, second_g], axis=0) + residual[0, 0].astype(F32)
    flags = jnp.any(jnp.arange(block_count, dtype=jnp.int32)[None, :] == kept_blocks[0, 0][:, None], axis=0)
    flags = flags[:, None, None]
    new_residual = jnp.where(flags, 0.0, grads).astype(BF)[None, None]
    owned = lax.psum_scatter(jnp.where(flags, grads, 0.0), "dp", scatter_dimension=0, tiled=True)
    new_momentum = momentum_decay * momentum + owned[None]
    return master - step_size * new_momentum, new_momentum, new_residual


def solution(mesh):
    ring = mesh.shape["dp"] == 16 and mesh.shape["mp"] == 2
    blocks = P("mp", "dp", None, None)
    left = P("dp", "mp", None, None, None)
    return jax.shard_map(
        local_ring if ring else local_plain,
        mesh=mesh,
        in_specs=(P("dp", "mp"), P("dp", "mp"), blocks, blocks, left, P("dp", "mp", None)),
        out_specs=(blocks, blocks, left),
        check_vma=False,
    )
```

time: 433 us -> 215 us (0.50)
  waiting for transfers between devices: 309 us -> 85.1 us
  Pallas kernels: 0 us -> 78.5 us
  matrix products: 51.5 us -> 0 us
  other arithmetic: 36.4 us -> 4.8 us
  starting transfers between devices: 0.16 us -> 23.8 us
  between operations: 13.8 us -> 1.11 us
    reduce_scatter x1 -> x0, waiting for transfers between devices: 163 us -> none  [local(): owned = lax.psum_scatter(masked, 'dp', scatter_dimension=0, tiled=True)]
    all_gather x3 -> x0, waiting for transfers between devices: 147 us -> none  [the longest x1 72.4 us: local(): lax.all_gather(master.astype(jnp.bfloat16), 'dp', axis=1, tiled=True)[0]]
    ppermute x0 -> x36, waiting for transfers between devices: none -> 85.1 us  [the longest x33 85.1 us: hop(): return lax.ppermute(array, 'dp', pairs)]
    pallas_call x0 -> x6, Pallas kernels: none -> 78.5 us  [the longest x3 36.9 us: run_grads(): pl.pallas_call(grad_kernel, grid_spec=pltpu.PrefetchScalarGridSpec(num_sc...]
    dot_general x3 -> x0, matrix products: 51.5 us -> none  [the longest x1 24.4 us: local(): jnp.einsum('hgl,hvo->gvlo', input_block_tiles, hidden_gradient, preferred...]
    ppermute x0 -> x36, starting transfers between devices: none -> 23.8 us  [the longest x33 20 us: hop(): return lax.ppermute(array, 'dp', pairs)]
    convert_element_type x2 -> x6, other arithmetic: 17.9 us -> 2.77 us  [the longest x1 1.43 us: local_ring(): own = master[0].astype(BF)]
    select_n x1 -> x0, other arithmetic: 14.4 us -> none  [local(): masked = jnp.where(flags, grads, 0.0)]
  transfers between devices with their start and end apart: 4 -> 36, of which waited for: 4 -> 14; matrix products, arithmetic and copies ran while one was open for 9% -> 2% of each run, Pallas kernels for 0% -> 28%
where the time goes in v1:
time: 215 us; the launch traced here: 213 us
  waiting for transfers between devices  85.1 us (40%)
  Pallas kernels  78.5 us (37%)
  starting transfers between devices  23.8 us (11%)
  local copies, waits for them, and re-layouts  20.1 us (9%)
  other arithmetic  4.8 us (2%)
    ppermute x33, waiting for transfers between devices, hop(): return lax.ppermute(array, 'dp', pairs)  85.1 us
    pallas_call x3, Pallas kernels, run_grads(): pl.pallas_call(grad_kernel, grid_spec=pltpu.PrefetchScalarGridSpec(num_sc...  36.9 us
    pallas_call x2, Pallas kernels, run_hid(): pl.pallas_call(functools.partial(hid_kernel, halves), grid_spec=pltpu.Pre...  25.3 us
    ppermute x33, starting transfers between devices, hop(): return lax.ppermute(array, 'dp', pairs)  20 us
    unnamed x70, local copies, waits for them, and re-layouts  18.3 us
    pallas_call x1, Pallas kernels, run_pre(): pl.pallas_call(functools.partial(pre_kernel, halves), grid_spec=pltpu.Pre...  16.3 us
  transfers between devices with their start and end apart: 36, of which 14 were waited for; matrix products, arithmetic and copies ran while one was open for 2% of the time, Pallas kernels for 28%

profile of v1, /device:TPU:0, one launch (start us, length us, event | category | flops | bytes accessed | tf_op | source)
XLA Modules:
  0.0 213.5 jit_solution(6288771930803764138)
XLA Ops:
  2.1 3.0 %collective-permute-start.2 = (bf16[16,128,128]{2,1,0:T(8,128)(2,1)S(1)}, bf16[16,128,128]{2,1,0:T(8,128)(2,1)S(1)}, u32[]{:S(2)}, u32[]{:S(2)}) collective-permute-start(bf16[16,128,128]{2,1,0:T(8,128)(2,1)S(1)} %convert_bitcast_fusion.refs_0_), channel_id=1, source_target_pairs={{0,4},{2,6},{8,0},{10,2},{16,8},{18,10},{24,16},{26,18},{28,24},{3... | collective-permute-start | bytes 1572872 | tf_op jit(solution)/shard_map/ppermute | solution.py:249
  5.2 11.9 %collective-permute-done.2.refs_2_ = bf16[16,128,128]{2,1,0:T(8,128)(2,1)S(1)} collective-permute-done((bf16[16,128,128]{2,1,0:T(8,128)(2,1)S(1)}, bf16[16,128,128]{2,1,0:T(8,128)(2,1)S(1)}, u32[]{:S(2)}, u32[]{:S(2)}) %collective-permute-start.2) | collective-permute-done | bytes 524320 | tf_op jit(solution)/shard_map/ppermute | solution.py:249
  17.1 1.7 collective-permute-start.4
  19.1 1.7 collective-permute-start
  20.8 9.4 %collective-permute-done.4.refs_4_ = bf16[16,128,128]{2,1,0:T(8,128)(2,1)S(1)} collective-permute-done((bf16[16,128,128]{2,1,0:T(8,128)(2,1)S(1)}, bf16[16,128,128]{2,1,0:T(8,128)(2,1)S(1)}, u32[]{:S(2)}, u32[]{:S(2)}) %collective-permute-start.4) | collective-permute-done | bytes 524320 | tf_op jit(solution)/shard_map/ppermute | solution.py:249
  33.5 8.8 %collective-permute-done.6.refs_6_ = bf16[16,128,128]{2,1,0:T(8,128)(2,1)S(1)} collective-permute-done((bf16[16,128,128]{2,1,0:T(8,128)(2,1)S(1)}, bf16[16,128,128]{2,1,0:T(8,128)(2,1)S(1)}, u32[]{:S(2)}, u32[]{:S(2)}) %collective-permute-start.6) | collective-permute-done | bytes 524320 | tf_op jit(solution)/shard_map/ppermute | solution.py:249
  44.9 1.6 collective-permute-start.8
  49.8 3.8 %collective-permute-done.8.refs_8_ = bf16[8,128,128]{2,1,0:T(8,128)(2,1)S(1)} collective-permute-done((bf16[8,128,128]{2,1,0:T(8,128)(2,1)S(1)}, bf16[8,128,128]{2,1,0:T(8,128)(2,1)S(1)}, u32[]{:S(2)}, u32[]{:S(2)}) %collective-permute-start.8) | collective-permute-done | bytes 262176 | tf_op jit(solution)/shard_map/ppermute | solution.py:249
  53.6 2.2 %collective-permute-done.7.refs_7_ = bf16[8,128,128]{2,1,0:T(8,128)(2,1)} collective-permute-done((bf16[8,128,128]{2,1,0:T(8,128)(2,1)S(1)}, bf16[8,128,128]{2,1,0:T(8,128)(2,1)}, u32[]{:S(2)}, u32[]{:S(2)}) %collective-permute-start.7) | collective-permute-done | bytes 262176 | tf_op jit(solution)/shard_map/ppermute | solution.py:249
  58.0 1.5 collective-permute-start.19
  71.8 16.3 %pre_act.1 = (bf16[1536,3072]{1,0:T(8,128)(2,1)}, f32[1536,2048]{1,0:T(8,128)}) custom-call(s32[19]{0:T(128)S(1)} %stack.164.owners, bf16[1536,512]{1,0:T(8,128)(2,1)S(1)} %copy-done.26, bf16[1536,512]{1,0:T(8,128)(2,1)S(1)} %copy-done.28, bf16[16,128,128]{2,1,0:T(8,128)(2,1)S(1)} %convert_bitcast_fusion.refs_0_, bf16[16,128,128]{2,1,0:T(8,128)(2,1)S(1)} %copy-done.1, ...), custom_call_target="tpu_custom_call" | custom-call | flops 6442450944 | bytes 30000000 | tf_op jit(solution)/shard_map/pre_act/pallas_call | solution.py:153
  88.2 12.9 %hid_grad.2.refs_18_ = bf16[1536,3072]{1,0:T(8,128)(2,1)} custom-call(s32[19]{0:T(128)S(1)} %stack.164.owners, bf16[768,512]{1,0:T(8,128)(2,1)} %get-tuple-element.34.dy_own, bf16[768,512]{1,0:T(8,128)(2,1)} %collective-permute-done.19.dy_other, f32[1536,2048]{1,0:T(8,128)} %get-tuple-element.15.slope_ref, ...), custom_call_target="tpu_custom_call" | custom-call | flops 3221225472 | bytes 15000000 | tf_op jit(solution)/shard_map/hid_grad/pallas_call | solution.py:183
  102.3 12.4 %hid_grad.3.b_ref = bf16[1536,3072]{1,0:T(8,128)(2,1)} custom-call(s32[19]{0:T(128)S(1)} %stack.164.owners, bf16[768,512]{1,0:T(8,128)(2,1)S(1)} %get-tuple-element.35.dy_own, bf16[768,512]{1,0:T(8,128)(2,1)} %collective-permute-done.18.dy_other, f32[1536,2048]{1,0:T(8,128)} %get-tuple-element.15.slope_ref, ...), custom_call_target="tpu_custom_call", output_to_operand_aliasing={{}: (22, {})} | custom-call | flops 3221225472 | bytes 15000000 | tf_op jit(solution)/shard_map/hid_grad/pallas_call | solution.py:183
  114.7 6.4 %grad_blocks.3 = (bf16[8,32,128,128]{3,2,1,0:T(8,128)(2,1)}, bf16[1,16,128,128]{3,2,1,0:T(8,128)(2,1)S(1)}, bf16[1,16,128,128]{3,2,1,0:T(8,128)(2,1)S(1)}) custom-call(s32[5]{0:T(128)S(1)} %stack.172.info, s32[256]{0:T(256)S(1)} %convert_element_type.124.flags, bf16[1536,3072]{1,0:T(8,128)(2,1)} %get-tuple-element.14.a_ref, ...), custom_call_target="tpu_custom_call" | custom-call | flops 1610612736 | bytes 12000000 | tf_op jit(solution)/shard_map/grad_blocks/pallas_call | solution.py:216
  121.1 9.2 %grad_blocks.4 = (bf16[8,32,128,128]{3,2,1,0:T(8,128)(2,1)}, bf16[2,16,128,128]{3,2,1,0:T(8,128)(2,1)S(1)}, bf16[2,16,128,128]{3,2,1,0:T(8,128)(2,1)S(1)}) custom-call(s32[8]{0:T(128)S(1)} %stack.169.info, s32[256]{0:T(256)S(1)} %convert_element_type.124.flags, bf16[1536,3072]{1,0:T(8,128)(2,1)} %get-tuple-element.14.a_ref, ...), custom_call_target="tpu_custom_call", output_to_operand_aliasing={{0}: (5, {})} | custom-call | flops 3221225472 | bytes 24000000 | tf_op jit(solution)/shard_map/grad_blocks/pallas_call | solution.py:216
  131.1 21.3 %grad_blocks.5 = (bf16[8,32,128,128]{3,2,1,0:T(8,128)(2,1)}, bf16[5,16,128,128]{3,2,1,0:T(8,128)(2,1)S(1)}, bf16[5,16,128,128]{3,2,1,0:T(8,128)(2,1)S(1)}) custom-call(s32[17]{0:T(128)S(1)} %stack.145.info, s32[256]{0:T(256)S(1)} %convert_element_type.124.flags, bf16[1536,3072]{1,0:T(8,128)(2,1)} %get-tuple-element.14.a_ref, ...), custom_call_target="tpu_custom_call", output_to_operand_aliasing={{0}: (5, {})} | custom-call | flops 8053063680 | bytes 60000000 | tf_op jit(solution)/shard_map/grad_blocks/pallas_call | solution.py:216
  152.6 1.8 collective-permute-start.25
  155.1 6.2 %collective-permute-done.25 = bf16[8,128,128]{2,1,0:T(8,128)(2,1)S(1)} collective-permute-done((bf16[8,128,128]{2,1,0:T(8,128)(2,1)S(1)}, bf16[8,128,128]{2,1,0:T(8,128)(2,1)S(1)}, u32[]{:S(2)}, u32[]{:S(2)}) %collective-permute-start.25) | collective-permute-done | bytes 262176 | tf_op jit(solution)/shard_map/ppermute | solution.py:249
  165.7 10.5 %collective-permute-done.26 = bf16[16,128,128]{2,1,0:T(8,128)(2,1)S(1)} collective-permute-done((bf16[16,128,128]{2,1,0:T(8,128)(2,1)S(1)}, bf16[16,128,128]{2,1,0:T(8,128)(2,1)S(1)}, u32[]{:S(2)}, u32[]{:S(2)}) %collective-permute-start.26) | collective-permute-done | bytes 524320 | tf_op jit(solution)/shard_map/ppermute | solution.py:249
  178.7 9.9 %collective-permute-done.27 = bf16[16,128,128]{2,1,0:T(8,128)(2,1)S(1)} collective-permute-done((bf16[16,128,128]{2,1,0:T(8,128)(2,1)S(1)}, bf16[16,128,128]{2,1,0:T(8,128)(2,1)S(1)}, u32[]{:S(2)}, u32[]{:S(2)}) %collective-permute-start.27) | collective-permute-done | bytes 524320 | tf_op jit(solution)/shard_map/ppermute | solution.py:249
  191.2 9.8 %collective-permute-done.34 = bf16[16,128,128]{2,1,0:T(8,128)(2,1)S(1)} collective-permute-done((bf16[16,128,128]{2,1,0:T(8,128)(2,1)S(1)}, bf16[16,128,128]{2,1,0:T(8,128)(2,1)S(1)}, u32[]{:S(2)}, u32[]{:S(2)}) %collective-permute-start.34) | collective-permute-done | bytes 524320 | tf_op jit(solution)/shard_map/ppermute | solution.py:249
  202.2 2.2 %collective-permute-done.28 = bf16[16,128,128]{2,1,0:T(8,128)(2,1)S(1)} collective-permute-done((bf16[16,128,128]{2,1,0:T(8,128)(2,1)S(1)}, bf16[16,128,128]{2,1,0:T(8,128)(2,1)S(1)}, u32[]{:S(2)}, u32[]{:S(2)}) %collective-permute-start.28) | collective-permute-done | bytes 524320 | tf_op jit(solution)/shard_map/ppermute | solution.py:249
  204.5 7.2 %collective-permute-done.35 = bf16[16,128,128]{2,1,0:T(8,128)(2,1)S(1)} collective-permute-done((bf16[16,128,128]{2,1,0:T(8,128)(2,1)S(1)}, bf16[16,128,128]{2,1,0:T(8,128)(2,1)S(1)}, u32[]{:S(2)}, u32[]{:S(2)}) %collective-permute-start.35) | collective-permute-done | bytes 524320 | tf_op jit(solution)/shard_map/ppermute | solution.py:249
  211.7 1.8 multiply_subtract_fusion
  (144 shorter events, 38.9 us)
Async XLA Ops:
  2.1 15.0 %collective-permute-start.2 = (bf16[16,128,128]{2,1,0:T(8,128)(2,1)S(1)}, bf16[16,128,128]{2,1,0:T(8,128)(2,1)S(1)}, u32[]{:S(2)}, u32[]{:S(2)}) collective-permute-start(bf16[16,128,128]{2,1,0:T(8,128)(2,1)S(1)} %convert_bitcast_fusion.refs_0_), channel_id=1, source_target_pairs={{0,4},{2,6},{8,0},{10,2},{16,8},{18,10},{24,16},{26,18},{28,24},{3... | collective-permute-start | bytes 1572872 | tf_op jit(solution)/shard_map/ppermute | solution.py:249
  5.1 13.7 %collective-permute-start.1 = (bf16[16,128,128]{2,1,0:T(8,128)(2,1)S(1)}, bf16[16,128,128]{2,1,0:T(8,128)(2,1)S(1)}, u32[]{:S(2)}, u32[]{:S(2)}) collective-permute-start(bf16[16,128,128]{2,1,0:T(8,128)(2,1)S(1)} %convert_bitcast_fusion.refs_0_), channel_id=1, source_target_pairs={{0,8},{2,10},{8,16},{10,18},{16,24},{18,26},{24,28},{26,30},{28,20... | collective-permute-start | bytes 1572872 | tf_op jit(solution)/shard_map/ppermute | solution.py:249
  17.1 13.1 %collective-permute-start.4 = (bf16[16,128,128]{2,1,0:T(8,128)(2,1)S(1)}, bf16[16,128,128]{2,1,0:T(8,128)(2,1)S(1)}, u32[]{:S(2)}, u32[]{:S(2)}) collective-permute-start(bf16[16,128,128]{2,1,0:T(8,128)(2,1)S(1)} %collective-permute-done.2.refs_2_), channel_id=1, source_target_pairs={{0,4},{2,6},{8,0},{10,2},{16,8},{18,10},{24,16},{26,18},{28,24},{3... | collective-permute-start | bytes 1572872 | tf_op jit(solution)/shard_map/ppermute | solution.py:249
  18.7 12.8 %collective-permute-start.3 = (bf16[16,128,128]{2,1,0:T(8,128)(2,1)S(1)}, bf16[16,128,128]{2,1,0:T(8,128)(2,1)S(1)}, u32[]{:S(2)}, u32[]{:S(2)}) collective-permute-start(bf16[16,128,128]{2,1,0:T(8,128)(2,1)S(1)} %collective-permute-done.1.refs_1_), channel_id=1, source_target_pairs={{0,8},{2,10},{8,16},{10,18},{16,24},{18,26},{24,28},{26,30},{28,20... | collective-permute-start | bytes 1572872 | tf_op jit(solution)/shard_map/ppermute | solution.py:249
  19.1 13.1 %collective-permute-start.9 = (bf16[16,128,128]{2,1,0:T(8,128)(2,1)S(1)}, bf16[16,128,128]{2,1,0:T(8,128)(2,1)S(1)}, u32[]{:S(2)}, u32[]{:S(2)}) collective-permute-start(bf16[16,128,128]{2,1,0:T(8,128)(2,1)S(1)} %convert_bitcast_fusion.refs_0_), channel_id=1, source_target_pairs={{0,2},{2,0},{4,6},{6,4},{8,10},{10,8},{12,14},{14,12},{16,18},{18,... | collective-permute-start | bytes 1572872 | tf_op jit(solution)/shard_map/ppermute | solution.py:249
  19.1 37.7 %collective-permute-start = (bf16[1536,512]{1,0:T(8,128)(2,1)}, bf16[1536,512]{1,0:T(8,128)(2,1)S(1)}, u32[]{:S(2)}, u32[]{:S(2)}) collective-permute-start(bf16[1536,512]{1,0:T(8,128)(2,1)} %x_own.1), channel_id=1, source_target_pairs={{0,1},{1,0},{2,3},{3,2},{4,5},{5,4},{6,7},{7,6},{8,9},{9,8},{10,11... | collective-permute-start | bytes 4718600 | tf_op jit(solution)/shard_map/ppermute | solution.py:260
  30.2 12.2 %collective-permute-start.6 = (bf16[16,128,128]{2,1,0:T(8,128)(2,1)S(1)}, bf16[16,128,128]{2,1,0:T(8,128)(2,1)S(1)}, u32[]{:S(2)}, u32[]{:S(2)}) collective-permute-start(bf16[16,128,128]{2,1,0:T(8,128)(2,1)S(1)} %collective-permute-done.4.refs_4_), channel_id=1, source_target_pairs={{0,4},{2,6},{8,0},{10,2},{16,8},{18,10},{24,16},{26,18},{28,24},{3... | collective-permute-start | bytes 1572872 | tf_op jit(solution)/shard_map/ppermute | solution.py:249
  32.2 11.8 %collective-permute-start.11 = (bf16[16,128,128]{2,1,0:T(8,128)(2,1)S(1)}, bf16[16,128,128]{2,1,0:T(8,128)(2,1)S(1)}, u32[]{:S(2)}, u32[]{:S(2)}) collective-permute-start(bf16[16,128,128]{2,1,0:T(8,128)(2,1)S(1)} %collective-permute-done.2.refs_2_), channel_id=1, source_target_pairs={{0,2},{2,0},{4,6},{6,4},{8,10},{10,8},{12,14},{14,12},{16,18},{18,... | collective-permute-start | bytes 1572872 | tf_op jit(solution)/shard_map/ppermute | solution.py:249
  33.0 13.4 %collective-permute-start.10 = (bf16[16,128,128]{2,1,0:T(8,128)(2,1)S(1)}, bf16[16,128,128]{2,1,0:T(8,128)(2,1)S(1)}, u32[]{:S(2)}, u32[]{:S(2)}) collective-permute-start(bf16[16,128,128]{2,1,0:T(8,128)(2,1)S(1)} %collective-permute-done.1.refs_1_), channel_id=1, source_target_pairs={{0,2},{2,0},{4,6},{6,4},{8,10},{10,8},{12,14},{14,12},{16,18},{18,... | collective-permute-start | bytes 1572872 | tf_op jit(solution)/shard_map/ppermute | solution.py:249
  48.5 12.1 %collective-permute-start.15 = (bf16[16,128,128]{2,1,0:T(8,128)(2,1)S(1)}, bf16[16,128,128]{2,1,0:T(8,128)(2,1)}, u32[]{:S(2)}, u32[]{:S(2)}) collective-permute-start(bf16[16,128,128]{2,1,0:T(8,128)(2,1)S(1)} %collective-permute-done.6.refs_6_), channel_id=1, source_target_pairs={{0,2},{2,0},{4,6},{6,4},{8,10},{10,8},{12,14},{14,12},{16,18},{18,... | collective-permute-start | bytes 1572872 | tf_op jit(solution)/shard_map/ppermute | solution.py:249
  58.0 30.1 %collective-permute-start.19 = (bf16[768,512]{1,0:T(8,128)(2,1)}, bf16[768,512]{1,0:T(8,128)(2,1)}, u32[]{:S(2)}, u32[]{:S(2)}) collective-permute-start(bf16[768,512]{1,0:T(8,128)(2,1)} %get-tuple-element.34.dy_own), channel_id=1, source_target_pairs={{0,1},{1,0},{2,3},{3,2},{4,5},{5,4},{6,7},{7,6},{8,9},{9,8},{10,11... | collective-permute-start | bytes 2359304 | tf_op jit(solution)/shard_map/ppermute | solution.py:264
  60.0 41.2 %collective-permute-start.18 = (bf16[768,512]{1,0:T(8,128)(2,1)S(1)}, bf16[768,512]{1,0:T(8,128)(2,1)}, u32[]{:S(2)}, u32[]{:S(2)}) collective-permute-start(bf16[768,512]{1,0:T(8,128)(2,1)S(1)} %get-tuple-element.35.dy_own), channel_id=1, source_target_pairs={{0,1},{1,0},{2,3},{3,2},{4,5},{5,4},{6,7},{7,6},{8,9},{9,8},{10,11... | collective-permute-start | bytes 2359304 | tf_op jit(solution)/shard_map/ppermute | solution.py:264
  121.1 31.4 %collective-permute-start.24 = (bf16[16,128,128]{2,1,0:T(8,128)(2,1)S(1)}, bf16[16,128,128]{2,1,0:T(8,128)(2,1)S(1)}, u32[]{:S(2)}, u32[]{:S(2)}) collective-permute-start(bf16[16,128,128]{2,1,0:T(8,128)(2,1)S(1)} %bitcast.91), channel_id=1, source_target_pairs={{0,2},{2,0},{4,6},{6,4},{8,10},{10,8},{12,14},{14,12},{16,18},{18,... | collective-permute-start | bytes 1572872 | tf_op jit(solution)/shard_map/ppermute | solution.py:249
  130.4 24.7 %collective-permute-start.23 = (bf16[16,128,128]{2,1,0:T(8,128)(2,1)S(1)}, bf16[16,128,128]{2,1,0:T(8,128)(2,1)S(1)}, u32[]{:S(2)}, u32[]{:S(2)}) collective-permute-start(bf16[16,128,128]{2,1,0:T(8,128)(2,1)S(1)} %get-tuple-element.38), channel_id=1, source_target_pairs={{0,2},{2,0},{4,6},{6,4},{8,10},{10,8},{12,14},{14,12},{16,18},{18,... | collective-permute-start | bytes 1572872 | tf_op jit(solution)/shard_map/ppermute | solution.py:249
  131.0 24.1 %collective-permute-start.31 = (bf16[16,128,128]{2,1,0:T(8,128)(2,1)S(1)}, bf16[16,128,128]{2,1,0:T(8,128)(2,1)S(1)}, u32[]{:S(2)}, u32[]{:S(2)}) collective-permute-start(bf16[16,128,128]{2,1,0:T(8,128)(2,1)S(1)} %get-tuple-element.39), channel_id=1, source_target_pairs={{0,2},{2,0},{4,6},{6,4},{8,10},{10,8},{12,14},{14,12},{16,18},{18,... | collective-permute-start | bytes 1572872 | tf_op jit(solution)/shard_map/ppermute | solution.py:249
  163.1 13.1 %collective-permute-start.26 = (bf16[16,128,128]{2,1,0:T(8,128)(2,1)S(1)}, bf16[16,128,128]{2,1,0:T(8,128)(2,1)S(1)}, u32[]{:S(2)}, u32[]{:S(2)}) collective-permute-start(bf16[16,128,128]{2,1,0:T(8,128)(2,1)S(1)} %get-tuple-element.36), channel_id=1, source_target_pairs={{0,8},{2,10},{8,16},{10,18},{16,24},{18,26},{24,28},{26,30},{28,20... | collective-permute-start | bytes 1572872 | tf_op jit(solution)/shard_map/ppermute | solution.py:249
  164.4 13.4 %collective-permute-start.30 = (bf16[16,128,128]{2,1,0:T(8,128)(2,1)S(1)}, bf16[16,128,128]{2,1,0:T(8,128)(2,1)S(1)}, u32[]{:S(2)}, u32[]{:S(2)}) collective-permute-start(bf16[16,128,128]{2,1,0:T(8,128)(2,1)S(1)} %get-tuple-element.28), channel_id=1, source_target_pairs={{0,2},{2,0},{4,6},{6,4},{8,10},{10,8},{12,14},{14,12},{16,18},{18,... | collective-permute-start | bytes 1572872 | tf_op jit(solution)/shard_map/ppermute | solution.py:249
  164.4 13.4 %collective-permute-start.21 = (bf16[16,128,128]{2,1,0:T(8,128)(2,1)S(1)}, bf16[16,128,128]{2,1,0:T(8,128)(2,1)S(1)}, u32[]{:S(2)}, u32[]{:S(2)}) collective-permute-start(bf16[16,128,128]{2,1,0:T(8,128)(2,1)S(1)} %get-tuple-element.31), channel_id=1, source_target_pairs={{0,2},{2,0},{4,6},{6,4},{8,10},{10,8},{12,14},{14,12},{16,18},{18,... | collective-permute-start | bytes 1572872 | tf_op jit(solution)/shard_map/ppermute | solution.py:249
  164.9 13.8 %collective-permute-start.33 = (bf16[16,128,128]{2,1,0:T(8,128)(2,1)S(1)}, bf16[16,128,128]{2,1,0:T(8,128)(2,1)S(1)}, u32[]{:S(2)}, u32[]{:S(2)}) collective-permute-start(bf16[16,128,128]{2,1,0:T(8,128)(2,1)S(1)} %get-tuple-element.37), channel_id=1, source_target_pairs={{0,4},{2,6},{8,0},{10,2},{16,8},{18,10},{24,16},{26,18},{28,24},{3... | collective-permute-start | bytes 1572872 | tf_op jit(solution)/shard_map/ppermute | solution.py:249
  176.5 12.2 %collective-permute-start.27 = (bf16[16,128,128]{2,1,0:T(8,128)(2,1)S(1)}, bf16[16,128,128]{2,1,0:T(8,128)(2,1)S(1)}, u32[]{:S(2)}, u32[]{:S(2)}) collective-permute-start(bf16[16,128,128]{2,1,0:T(8,128)(2,1)S(1)} %fusion.10), channel_id=1, source_target_pairs={{0,8},{2,10},{8,16},{10,18},{16,24},{18,26},{24,28},{26,30},{28,20... | collective-permute-start | bytes 1572872 | tf_op jit(solution)/shard_map/ppermute | solution.py:249
  177.7 13.5 %collective-permute-start.29 = (bf16[16,128,128]{2,1,0:T(8,128)(2,1)S(1)}, bf16[16,128,128]{2,1,0:T(8,128)(2,1)S(1)}, u32[]{:S(2)}, u32[]{:S(2)}) collective-permute-start(bf16[16,128,128]{2,1,0:T(8,128)(2,1)S(1)} %get-tuple-element.29), channel_id=1, source_target_pairs={{0,2},{2,0},{4,6},{6,4},{8,10},{10,8},{12,14},{14,12},{16,18},{18,... | collective-permute-start | bytes 1572872 | tf_op jit(solution)/shard_map/ppermute | solution.py:249
  189.1 11.9 %collective-permute-start.34 = (bf16[16,128,128]{2,1,0:T(8,128)(2,1)S(1)}, bf16[16,128,128]{2,1,0:T(8,128)(2,1)S(1)}, u32[]{:S(2)}, u32[]{:S(2)}) collective-permute-start(bf16[16,128,128]{2,1,0:T(8,128)(2,1)S(1)} %get-tuple-element.33), channel_id=1, source_target_pairs={{0,4},{2,6},{8,0},{10,2},{16,8},{18,10},{24,16},{26,18},{28,24},{3... | collective-permute-start | bytes 1572872 | tf_op jit(solution)/shard_map/ppermute | solution.py:249
  190.1 12.1 %collective-permute-start.20 = (bf16[16,128,128]{2,1,0:T(8,128)(2,1)S(1)}, bf16[16,128,128]{2,1,0:T(8,128)(2,1)S(1)}, u32[]{:S(2)}, u32[]{:S(2)}) collective-permute-start(bf16[16,128,128]{2,1,0:T(8,128)(2,1)S(1)} %get-tuple-element.27), channel_id=1, source_target_pairs={{0,2},{2,0},{4,6},{6,4},{8,10},{10,8},{12,14},{14,12},{16,18},{18,... | collective-permute-start | bytes 1572872 | tf_op jit(solution)/shard_map/ppermute | solution.py:249
  190.1 14.3 %collective-permute-start.28 = (bf16[16,128,128]{2,1,0:T(8,128)(2,1)S(1)}, bf16[16,128,128]{2,1,0:T(8,128)(2,1)S(1)}, u32[]{:S(2)}, u32[]{:S(2)}) collective-permute-start(bf16[16,128,128]{2,1,0:T(8,128)(2,1)S(1)} %get-tuple-element.32), channel_id=1, source_target_pairs={{0,8},{2,10},{8,16},{10,18},{16,24},{18,26},{24,28},{26,30},{28,20... | collective-permute-start | bytes 1572872 | tf_op jit(solution)/shard_map/ppermute | solution.py:249
  (47 other events, 563.7 us)

commit v2 on v1

v2 whole, which is shorter than its diff:
```python
import functools

import jax
import jax.numpy as jnp
from jax import lax
from jax.experimental import pallas as pl
from jax.experimental.pallas import tpu as pltpu
from jax.sharding import PartitionSpec as P

momentum_decay = 0.9
step_size = 0.01
BF = jnp.bfloat16
F32 = jnp.float32
ANY = pl.BlockSpec(memory_space=pl.ANY)
HBM = pltpu.HBM
GELU_S = 0.7978845608028654
GELU_C = 0.044715


def activation(values):
    return jax.nn.gelu(values, approximate=True)


def in_hbm(array):
    return pltpu.with_memory_space_constraint(array, HBM)


def gelu_and_slope(v):
    sq = v * v
    t = jnp.tanh(v * (GELU_S + (GELU_S * GELU_C) * sq))
    half = 0.5 + 0.5 * t
    act = v * half
    slope = half + act * (1.0 - t) * (GELU_S + (3.0 * GELU_S * GELU_C) * sq)
    return act, slope


def place_kernel(halves, owners, *refs):
    n = len(halves)
    srcs, (w1, w2, sem) = refs[:n], refs[-3:]
    shift = owners[n]

    def copies(s, first):
        owner, half = owners[s], halves[s]
        if first:
            row = pl.multiple_of(((owner - shift) & 7) * 128, 128)
            return pltpu.make_async_copy(srcs[s], w1.at[pl.ds(8 * half, 8), pl.ds(row, 128)], sem.at[s])
        row = pl.multiple_of((owner - 8) * 256 + 128 * half, 128)
        return pltpu.make_async_copy(srcs[s], w2.at[:, pl.ds(row, 128)], sem.at[s])

    for act in ("start", "wait"):
        for s in range(n):
            for first in (True, False):

                @pl.when((owners[s] < 8) if first else (owners[s] >= 8))
                def _(s=s, first=first):
                    getattr(copies(s, first), act)()


def pre_kernel(x_own, *refs):
    *x_other, w1, act_ref, slope_ref = refs
    w = jnp.concatenate([w1[0], w1[1]], axis=1)
    half = w.shape[0] // 2
    size = x_other[0].shape[0]
    for i, part in enumerate(x_other):
        r = i * size
        pre = jnp.dot(x_own[r : r + size, :], w[:half], preferred_element_type=F32)
        pre += jnp.dot(part[...], w[half:], preferred_element_type=F32)
        act, slope = gelu_and_slope(pre)
        act_ref[r : r + size, :] = act.astype(BF)
        slope_ref[r : r + size, :] = slope


def hid_kernel(shift_ref, dy_own, dy_other, w2, slope_ref, *refs):
    hid = refs[-1]
    shift = shift_ref[0]
    w = jnp.concatenate([w2[(c + shift) & 7] for c in range(8)], axis=1)
    half = w.shape[1] // 2
    dims = (((1,), (1,)), ((), ()))
    g = lax.dot_general(dy_own[...], w[:, :half], dims, preferred_element_type=F32)
    g += lax.dot_general(dy_other[...], w[:, half:], dims, preferred_element_type=F32)
    hid[...] = (g * slope_ref[...]).astype(BF)


def grad_kernel(info, flags, x_own, x_first, x_second, x_third, act_ref, hid_ref, dy_own, dy_first, dy_second, res_ref, *refs):
    new_res, mine, other, grad = refs[-4:]
    group, h = pl.program_id(0), pl.program_id(1)
    g, a = info[2 * group], info[2 * group + 1]
    first = g < 4
    shift, core = info[info.shape[0] - 2], info[info.shape[0] - 1]
    dims = (((0,), (0,)), ((), ()))
    dot = functools.partial(lax.dot_general, dimension_numbers=dims, preferred_element_type=F32)

    @pl.when(first & (a < 2))
    def _():
        grad[...] = dot(x_own[...], hid_ref[...])

    @pl.when(first & (a >= 2))
    def _():
        size = x_first.shape[0]
        parts = enumerate((x_first, x_second, x_third))
        grad[...] = sum(dot(part[...], hid_ref[i * size : (i + 1) * size, :]) for i, part in parts)

    @pl.when(jnp.logical_not(first))
    def _():
        size = dy_first.shape[0]
        grad[:, :512] = dot(act_ref[...], dy_own[...])
        grad[:, 512:] = dot(act_ref[:size, :], dy_first[...]) + dot(act_ref[size:, :], dy_second[...])

    for i in range(2):
        for j in range(8):
            slot = jnp.where(first, 8 * h + j, 8 * i + ((j + shift) & 7))
            target = jnp.where(first, i, h)
            flat = 16 * target + slot
            kept = flags[32 * g + flat] != 0
            v = grad[128 * i : 128 * i + 128, 128 * j : 128 * j + 128] + res_ref[0, flat].astype(F32)
            new_res[0, flat] = jnp.where(kept, 0.0, v).astype(BF)
            send = jnp.where(kept, v, 0.0).astype(BF)

            @pl.when(target == core)
            def _(send=send, slot=slot):
                mine[0, slot] = send

            @pl.when(target != core)
            def _(send=send, slot=slot):
                other[0, slot] = send


def run_place(owners, halves, units, weights):
    operands = [owners, *[in_hbm(u) for u in units]]
    alias = {}
    if weights is not None:
        alias = {len(operands): 0, len(operands) + 1: 1}
        operands += [in_hbm(w) for w in weights]
    return pl.pallas_call(
        functools.partial(place_kernel, halves),
        grid_spec=pltpu.PrefetchScalarGridSpec(
            num_scalar_prefetch=1,
            grid=(1,),
            in_specs=[ANY] * (len(operands) - 1),
            out_specs=[ANY, ANY],
            scratch_shapes=[pltpu.SemaphoreType.DMA((len(units),))],
        ),
        out_shape=[HBM((16, 1024, 128), BF), HBM((8, 2048, 128), BF)],
        input_output_aliases=alias,
        compiler_params=pltpu.CompilerParams(vmem_limit_bytes=2**20),
        cost_estimate=pl.CostEstimate(flops=0, bytes_accessed=len(units) * 2**19, transcendentals=0),
        name="place",
    )(*operands)


def run_pre(x_own, x_other, w1):
    rows = x_own.shape[0]
    full = [pl.BlockSpec(t.shape, lambda i: (0, 0)) for t in (x_own, *x_other)]
    column = pl.BlockSpec((rows, 256), lambda i: (0, i))
    return pl.pallas_call(
        pre_kernel,
        grid=(8,),
        in_specs=[*full, pl.BlockSpec((2, 1024, 128), lambda i: (i, 0, 0))],
        out_specs=[column, column],
        out_shape=[HBM((rows, 2048), BF), HBM((rows, 2048), F32)],
        compiler_params=pltpu.CompilerParams(vmem_limit_bytes=24 * 2**20),
        cost_estimate=pl.CostEstimate(flops=4 * rows * 1024 * 2048, bytes_accessed=26_000_000, transcendentals=rows * 2048),
        name="pre_act",
    )(in_hbm(x_own), *x_other, in_hbm(w1))


def run_hid(shift, dy_own, dy_other, w2, slope, row_block, hid=None):
    rows = dy_other.shape[0]
    column = pl.BlockSpec((rows, 256), lambda i, *_: (row_block, i))
    operands = [shift, in_hbm(dy_own), dy_other, in_hbm(w2), in_hbm(slope)]
    specs = [
        pl.BlockSpec((rows, 512), lambda i, *_: (row_block, 0)),
        pl.BlockSpec((rows, 512), lambda i, *_: (0, 0)),
        pl.BlockSpec((8, 256, 128), lambda i, *_: (0, i, 0)),
        column,
    ]
    alias = {}
    if hid is not None:
        alias = {len(operands): 0}
        operands.append(in_hbm(hid))
        specs.append(ANY)
    return pl.pallas_call(
        hid_kernel,
        grid_spec=pltpu.PrefetchScalarGridSpec(num_scalar_prefetch=1, grid=(8,), in_specs=specs, out_specs=column),
        out_shape=HBM(slope.shape, BF),
        input_output_aliases=alias,
        compiler_params=pltpu.CompilerParams(vmem_limit_bytes=18 * 2**20),
        cost_estimate=pl.CostEstimate(flops=3 * rows * 1024 * 2048, bytes_accessed=15_000_000, transcendentals=0),
        name="hid_grad",
    )(*operands)


def run_grads(info, flags, x_own, x_other, act, hid, dy_own, dy_other, residual, new_res, count):
    rows = act.shape[0]
    block = lambda size: pl.BlockSpec((1, size, 128, 128), lambda i, h, info, *_: (info[2 * i], 0, 0, 0))
    local_block = pl.BlockSpec((1, 16, 128, 128), lambda i, h, *_: (i, 0, 0, 0))
    whole = lambda t: pl.BlockSpec(t.shape, lambda i, h, *_: (0, 0))
    is_first = lambda i, info: info[2 * i] < 4
    held = [in_hbm(t) for t in (act, hid, dy_own)]
    operands = [info, flags, in_hbm(x_own), *x_other, *held, *dy_other, in_hbm(residual)]
    specs = [
        *[
            pl.BlockSpec((t.shape[0], 256), lambda i, h, info, *_: (0, jnp.where(is_first(i, info), info[2 * i + 1] & 1, 0)))
            for t in (x_own, *x_other)
        ],
        pl.BlockSpec((rows, 256), lambda i, h, info, *_: (0, jnp.where(is_first(i, info), 0, info[2 * i + 1] + h))),
        pl.BlockSpec((rows, 1024), lambda i, h, info, *_: (0, jnp.where(is_first(i, info), h, 0))),
        whole(dy_own),
        whole(dy_other[0]),
        whole(dy_other[1]),
        block(32),
    ]
    alias = {}
    if new_res is not None:
        alias = {len(operands): 0}
        operands.append(in_hbm(new_res))
        specs.append(ANY)
    sent = HBM((count, 16, 128, 128), BF)
    return pl.pallas_call(
        grad_kernel,
        grid_spec=pltpu.PrefetchScalarGridSpec(
            num_scalar_prefetch=2,
            grid=(count, 2),
            in_specs=specs,
            out_specs=[block(32), local_block, local_block],
            scratch_shapes=[pltpu.VMEM((256, 1024), F32)],
        ),
        out_shape=[HBM(residual.shape, BF), sent, sent],
        input_output_aliases=alias,
        compiler_params=pltpu.CompilerParams(vmem_limit_bytes=30 * 2**20),
        cost_estimate=pl.CostEstimate(flops=3 * rows * 1024 * 512 * count, bytes_accessed=10_000_000 * count, transcendentals=0),
        name="grad_blocks",
    )(*operands)


def chip_at(place):
    place = place % 8
    if isinstance(place, int):
        return 2 * place if place < 4 else 2 * (7 - place) + 1
    return jnp.where(place < 4, 2 * place, 2 * (7 - place) + 1)


def ring_pairs(step):
    return [(2 * chip_at(p) + c, 2 * chip_at(p + step) + c) for p in range(8) for c in range(2)]


UP, DOWN = ring_pairs(1), ring_pairs(-1)
CORES = [(i, i ^ 1) for i in range(16)]
PAIR = [(0, 1), (1, 0)]


def hop(array, pairs):
    return lax.ppermute(array, "dp", pairs)


def local_ring(tokens, out_grad, master, momentum, residual, kept_blocks):
    mine = lax.axis_index("dp").astype(jnp.int32)
    shard = lax.axis_index("mp").astype(jnp.int32)
    core = mine & 1
    chip = mine >> 1
    place = jnp.where((chip & 1) == 0, chip >> 1, 7 - (chip >> 1))
    rows = tokens.shape[0]

    parts = 2
    size = rows // parts
    dy_own = [out_grad[i * size : (i + 1) * size] for i in range(parts)]
    third = rows // 3
    x_other = [lax.ppermute(t, "mp", PAIR) for t in (tokens[:third], tokens[third : 2 * third], tokens[2 * third :])]
    dy_other = [lax.ppermute(t, "mp", PAIR) for t in dy_own]

    shift = 4 * shard
    own = [master[0, :8].astype(BF), master[0, 8:].astype(BF)]
    up, down = list(own), list(own)
    weights = None
    for k in range(1, 5):
        if k > 1:
            part = k - 2
            x_other[part], *both = lax.optimization_barrier((x_other[part], *up, *down))
            up, down = both[: len(up)], both[len(up) :]
        up = [hop(u, UP) for u in (up if k < 4 else up[:1])]
        down = [hop(u, DOWN) for u in (down if k < 4 else down[1:])]
        if weights is not None:
            *both, weights[0], weights[1] = lax.optimization_barrier((*up, *down, *weights))
            up, down = both[: len(up)], both[len(up) :]
        halves = [0, 1] if k == 4 else [0, 1, 0, 1]
        units = up + down
        owners = [2 * chip_at(place - k) + core] * len(up) + [2 * chip_at(place + k) + core] * len(down)
        if k == 1:
            units, halves, owners = own + units, [0, 1] + halves, [mine, mine] + owners
        units = units + [hop(u, CORES) for u in units]
        owners = jnp.stack(owners + [o ^ 1 for o in owners] + [shift])
        weights = list(run_place(owners, tuple(halves * 2), units, weights))

    block_count = residual.shape[2]
    flags = jnp.any(jnp.arange(block_count, dtype=jnp.int32)[None, :] == kept_blocks[0, 0][:, None], axis=0)
    flags = flags.astype(jnp.int32)

    x_other[2], dy_other[0] = lax.optimization_barrier((x_other[2], dy_other[0]))
    act, slope = run_pre(tokens, x_other, weights[0])
    hid = None
    for i in range(parts):
        hid = run_hid(shift[None], out_grad, dy_other[i], weights[1], slope, i, hid)

    stored = residual.reshape(8, 32, 128, 128)

    def info_of(distances):
        out = []
        for k in distances:
            g = chip_at(place + k)
            a = jnp.where(g < 4, (g - 2 * shard) & 3, 2 * (g - 4))
            out += [g, a]
        return jnp.stack(out + [shift, core])

    new_res, sums, up, down = None, {}, {}, {}

    def add_up(distances):
        nonlocal new_res
        new_res, own_sum, other_sum = run_grads(
            info_of(distances), flags, tokens, x_other, act, hid, out_grad, dy_other, stored, new_res, len(distances)
        )
        other_sum = hop(other_sum, CORES)
        for i, k in enumerate(distances):
            for h in range(2):
                part = slice(8 * h, 8 * h + 8)
                sums[k, h] = own_sum[i, part].astype(F32) + other_sum[i, part].astype(F32)

    def send(k):
        nonlocal flags
        ups = {(k, h): sums[k, h] + (up[k + 1, h].astype(F32) if (k + 1, h) in up else 0.0) for h in range(2) if k < 4 or h == 0}
        downs = {(k, h): sums[8 - k, h] + (down[k + 1, h].astype(F32) if (k + 1, h) in down else 0.0) for h in range(2) if k < 4 or h == 1}
        ups, downs = [{key: t.astype(BF) for key, t in part.items()} for part in (ups, downs)]
        flags, ups, downs = lax.optimization_barrier((flags, ups, downs))
        up.update({key: hop(t, UP) for key, t in ups.items()})
        down.update({key: hop(t, DOWN) for key, t in downs.items()})

    add_up([4])
    add_up([3, 5])
    send(4)
    add_up([2, 6])
    send(3)
    add_up([1, 7, 0])
    send(2)
    send(1)
    owned = jnp.concatenate([sums[0, h] + up[1, h].astype(F32) + down[1, h].astype(F32) for h in range(2)], axis=0)
    new_momentum = momentum_decay * momentum + owned[None]
    new_master = master - step_size * new_momentum
    return new_master, new_momentum, new_res.reshape(residual.shape)


def local_plain(tokens, out_grad, master, momentum, residual, kept_blocks):
    whole_in = lax.all_gather(tokens, "mp", axis=1, tiled=True)
    whole_grad = lax.all_gather(out_grad, "mp", axis=1, tiled=True)
    tile = master.shape[-1]
    width = whole_in.shape[1]
    block_count = residual.shape[2]
    half = block_count // 2
    rows = width // tile
    cols = half // rows
    working = lax.all_gather(master.astype(BF), "dp", axis=1, tiled=True)[0]
    first_w = working[:half].reshape(rows, cols, tile, tile).transpose(0, 2, 1, 3).reshape(width, cols * tile)
    second_w = working[half:].reshape(cols, rows, tile, tile).transpose(0, 2, 1, 3).reshape(cols * tile, width)
    pre = jnp.dot(whole_in, first_w, preferred_element_type=F32)
    act_full, pullback = jax.vjp(activation, pre)
    act = act_full.astype(BF)
    act_grad = jnp.dot(whole_grad, second_w.T, preferred_element_type=F32)
    hid = pullback(act_grad)[0].astype(BF)
    first_g = jnp.dot(whole_in.T, hid, preferred_element_type=F32)
    second_g = jnp.dot(act.T, whole_grad, preferred_element_type=F32)
    first_g = first_g.reshape(rows, tile, cols, tile).transpose(0, 2, 1, 3).reshape(half, tile, tile)
    second_g = second_g.reshape(cols, tile, rows, tile).transpose(0, 2, 1, 3).reshape(half, tile, tile)
    grads = jnp.concatenate([first_g, second_g], axis=0) + residual[0, 0].astype(F32)
    flags = jnp.any(jnp.arange(block_count, dtype=jnp.int32)[None, :] == kept_blocks[0, 0][:, None], axis=0)
    flags = flags[:, None, None]
    new_residual = jnp.where(flags, 0.0, grads).astype(BF)[None, None]
    owned = lax.psum_scatter(jnp.where(flags, grads, 0.0), "dp", scatter_dimension=0, tiled=True)
    new_momentum = momentum_decay * momentum + owned[None]
    return master - step_size * new_momentum, new_momentum, new_residual


def solution(mesh):
    ring = mesh.shape["dp"] == 16 and mesh.shape["mp"] == 2
    blocks = P("mp", "dp", None, None)
    left = P("dp", "mp", None, None, None)
    return jax.shard_map(
        local_ring if ring else local_plain,
        mesh=mesh,
        in_specs=(P("dp", "mp"), P("dp", "mp"), blocks, blocks, left, P("dp", "mp", None)),
        out_specs=(blocks, blocks, left),
        check_vma=False,
    )
```

time: 215 us -> 442 us (2.06)
  Pallas kernels: 78.5 us -> 343 us
  waiting for transfers between devices: 85.1 us -> 41.1 us
  starting transfers between devices: 23.8 us -> 41.4 us
  local copies, waits for them, and re-layouts: 20.1 us -> 5.56 us
    pallas_call x3 -> x7, Pallas kernels: 41.6 us -> 296 us  [the longest x4 261 us: run_place(): pl.pallas_call(functools.partial(place_kernel, halves), grid_spec=pltpu.P...]
    ppermute x33 -> x48, waiting for transfers between devices: 85.1 us -> 41.1 us  [hop(): return lax.ppermute(array, 'dp', pairs)]
    unnamed x70 -> x46, local copies, waits for them, and re-layouts: 18.3 us -> 2.22 us
    ppermute x33 -> x48, starting transfers between devices: 20 us -> 34.5 us  [hop(): return lax.ppermute(array, 'dp', pairs)]
    pallas_call x3 -> x4, Pallas kernels: 36.9 us -> 47.8 us  [run_grads(): pl.pallas_call(grad_kernel, grid_spec=pltpu.PrefetchScalarGridSpec(num_sc...]
  transfers between devices with their start and end apart: 36 -> 53, of which waited for: 14 -> 15; matrix products, arithmetic and copies ran while one was open for 2% -> 2% of each run, Pallas kernels for 28% -> 74%
where the time goes in v2:
time: 442 us; the launch traced here: 441 us
  Pallas kernels  343 us (78%)
  starting transfers between devices  41.4 us (9%)
  waiting for transfers between devices  41.1 us (9%)
  other arithmetic  8.08 us (2%)
  local copies, waits for them, and re-layouts  5.56 us (1%)
    pallas_call x4, Pallas kernels, run_place(): pl.pallas_call(functools.partial(place_kernel, halves), grid_spec=pltpu.P...  261 us
    pallas_call x4, Pallas kernels, run_grads(): pl.pallas_call(grad_kernel, grid_spec=pltpu.PrefetchScalarGridSpec(num_sc...  47.8 us
    ppermute x48, waiting for transfers between devices, hop(): return lax.ppermute(array, 'dp', pairs)  41.1 us
    ppermute x48, starting transfers between devices, hop(): return lax.ppermute(array, 'dp', pairs)  34.5 us
    pallas_call x2, Pallas kernels, run_hid(): pl.pallas_call(hid_kernel, grid_spec=pltpu.PrefetchScalarGridSpec(num_sca...  20.1 us
    pallas_call x1, Pallas kernels, run_pre(): pl.pallas_call(pre_kernel, grid=(8,), in_specs=[*full, pl.BlockSpec((2, 1...  14.6 us
  transfers between devices with their start and end apart: 53, of which 15 were waited for; matrix products, arithmetic and copies ran while one was open for 2% of the time, Pallas kernels for 74%

profile of v2, /device:TPU:0, one launch (start us, length us, event | category | flops | bytes accessed | tf_op | source)
XLA Modules:
  0.0 440.8 jit_solution(16200419897151661082)
XLA Ops:
  4.0 2.7 collective-permute-start
  10.8 5.1 %collective-permute-done.4.refs_5_ = bf16[8,128,128]{2,1,0:T(8,128)(2,1)S(1)} collective-permute-done((bf16[8,128,128]{2,1,0:T(8,128)(2,1)S(1)}, bf16[8,128,128]{2,1,0:T(8,128)(2,1)S(1)}, u32[]{:S(2)}, u32[]{:S(2)}) %collective-permute-start.4) | collective-permute-done | bytes 262176 | tf_op jit(solution)/shard_map/ppermute | solution.py:253
  17.5 3.2 collective-permute-done.3.refs_4_
  28.0 97.1 %place.4 = (bf16[16,1024,128]{2,1,0:T(8,128)(2,1)}, bf16[8,2048,128]{2,1,0:T(8,128)(2,1)}) custom-call(s32[13]{0:T(128)S(1)} %stack.174.owners, bf16[8,128,128]{2,1,0:T(8,128)(2,1)} %copy-done.7, bf16[8,128,128]{2,1,0:T(8,128)(2,1)} %copy-done.6, bf16[8,128,128]{2,1,0:T(8,128)(2,1)} %collective-permute-done.1.refs_2_, ...), custom_call_target="tpu_custom_call" | custom-call | bytes 6291456 | tf_op jit(solution)/shard_map/place/pallas_call | solution.py:134
  132.2 65.2 %place.5 = (bf16[16,1024,128]{2,1,0:T(8,128)(2,1)}, bf16[8,2048,128]{2,1,0:T(8,128)(2,1)}) custom-call(s32[9]{0:T(128)S(1)} %stack.179.owners, bf16[8,128,128]{2,1,0:T(8,128)(2,1)} %collective-permute-done.6.refs_0_, bf16[8,128,128]{2,1,0:T(8,128)(2,1)} %collective-permute-done.7.refs_1_, ...), custom_call_target="tpu_custom_call", output_to_operand_aliasing={{0}: (9, {}), {1}: (10, {})} | custom-call | bytes 4194304 | tf_op jit(solution)/shard_map/place/pallas_call | solution.py:134
  203.9 65.3 %place.6 = (bf16[16,1024,128]{2,1,0:T(8,128)(2,1)}, bf16[8,2048,128]{2,1,0:T(8,128)(2,1)}) custom-call(s32[9]{0:T(128)S(1)} %stack.189.owners, bf16[8,128,128]{2,1,0:T(8,128)(2,1)} %copy-done.16, bf16[8,128,128]{2,1,0:T(8,128)(2,1)} %collective-permute-done.18.refs_1_, ...), custom_call_target="tpu_custom_call", output_to_operand_aliasing={{0}: (9, {}), {1}: (10, {})} | custom-call | bytes 4194304 | tf_op jit(solution)/shard_map/place/pallas_call | solution.py:134
  271.7 33.5 %place.7 = (bf16[16,1024,128]{2,1,0:T(8,128)(2,1)}, bf16[8,2048,128]{2,1,0:T(8,128)(2,1)}) custom-call(s32[5]{0:T(128)S(1)} %stack.184.owners, bf16[8,128,128]{2,1,0:T(8,128)(2,1)} %copy-done.8, bf16[8,128,128]{2,1,0:T(8,128)(2,1)} %collective-permute-done.27.refs_1_, ...), custom_call_target="tpu_custom_call", output_to_operand_aliasing={{0}: (5, {}), {1}: (6, {})} | custom-call | bytes 2097152 | tf_op jit(solution)/shard_map/place/pallas_call | solution.py:134
  305.2 14.6 %pre_act.1 = (bf16[1536,2048]{1,0:T(8,128)(2,1)}, f32[1536,2048]{1,0:T(8,128)}) custom-call(bf16[1536,512]{1,0:T(8,128)(2,1)} %x_own.9, bf16[512,512]{1,0:T(8,128)(2,1)S(1)} %collective-permute-done.refs_0_.x_first, bf16[512,512]{1,0:T(8,128)(2,1)S(1)} %collective-permute-done.5.refs_1_.x_second, ...), custom_call_target="tpu_custom_call" | custom-call | flops 12884901888 | bytes 26000000 | tf_op jit(solution)/shard_map/pre_act/pallas_call | solution.py:155
  319.8 10.0 %hid_grad.2.refs_0_ = bf16[1536,2048]{1,0:T(8,128)(2,1)} custom-call(s32[1]{0:T(128)} %bitcast.6.shift_ref, bf16[1536,512]{1,0:T(8,128)(2,1)} %dy_own.11, bf16[768,512]{1,0:T(8,128)(2,1)S(1)} %collective-permute-done.25.dy_other.dy_first, bf16[8,2048,128]{2,1,0:T(8,128)(2,1)} %get-tuple-element.110.w2, f32[1536,2048]{1,0:T(8,128)} %get-tuple-element.111.slope_ref), custom_call_target="tpu_custom_call" | custom-call | flops 4831838208 | bytes 15000000 | tf_op jit(solution)/shard_map/hid_grad/pallas_call | solution.py:182
  329.9 10.0 %hid_grad.3.hid_ref = bf16[1536,2048]{1,0:T(8,128)(2,1)} custom-call(s32[1]{0:T(128)} %bitcast.6.shift_ref, bf16[1536,512]{1,0:T(8,128)(2,1)} %dy_own.11, bf16[768,512]{1,0:T(8,128)(2,1)S(1)} %collective-permute-done.34.dy_other.dy_second, bf16[8,2048,128]{2,1,0:T(8,128)(2,1)} %get-tuple-element.110.w2, ...), custom_call_target="tpu_custom_call", output_to_operand_aliasing={{}: (5, {})} | custom-call | flops 4831838208 | bytes 15000000 | tf_op jit(solution)/shard_map/hid_grad/pallas_call | solution.py:182
  339.9 7.8 %grad_blocks.4 = (bf16[8,32,128,128]{3,2,1,0:T(8,128)(2,1)}, bf16[1,16,128,128]{3,2,1,0:T(8,128)(2,1)}, bf16[1,16,128,128]{3,2,1,0:T(8,128)(2,1)}) custom-call(s32[4]{0:T(128)S(1)} %pad_add_fusion.info, s32[256]{0:T(256)S(1)} %convert_element_type.233.flags, bf16[1536,512]{1,0:T(8,128)(2,1)} %x_own.9, ...), custom_call_target="tpu_custom_call" | custom-call | flops 2415919104 | bytes 10000000 | tf_op jit(solution)/shard_map/grad_blocks/pallas_call | solution.py:219
  347.8 11.3 %grad_blocks.5 = (bf16[8,32,128,128]{3,2,1,0:T(8,128)(2,1)}, bf16[2,16,128,128]{3,2,1,0:T(8,128)(2,1)}, bf16[2,16,128,128]{3,2,1,0:T(8,128)(2,1)}) custom-call(s32[6]{0:T(128)S(1)} %stack.194.info, s32[256]{0:T(256)S(1)} %convert_element_type.233.flags, bf16[1536,512]{1,0:T(8,128)(2,1)} %x_own.9, ...), custom_call_target="tpu_custom_call", output_to_operand_aliasing={{0}: (12, {})} | custom-call | flops 4831838208 | bytes 20000000 | tf_op jit(solution)/shard_map/grad_blocks/pallas_call | solution.py:219
  363.2 12.1 %grad_blocks.6 = (bf16[8,32,128,128]{3,2,1,0:T(8,128)(2,1)}, bf16[2,16,128,128]{3,2,1,0:T(8,128)(2,1)}, bf16[2,16,128,128]{3,2,1,0:T(8,128)(2,1)}) custom-call(s32[6]{0:T(128)S(1)} %stack.199.info, s32[256]{0:T(256)S(1)} %convert_element_type.233.flags, bf16[1536,512]{1,0:T(8,128)(2,1)} %x_own.9, ...), custom_call_target="tpu_custom_call", output_to_operand_aliasing={{0}: (12, {})} | custom-call | flops 4831838208 | bytes 20000000 | tf_op jit(solution)/shard_map/grad_blocks/pallas_call | solution.py:219
  377.8 16.5 %grad_blocks.7 = (bf16[8,32,128,128]{3,2,1,0:T(8,128)(2,1)}, bf16[3,16,128,128]{3,2,1,0:T(8,128)(2,1)}, bf16[3,16,128,128]{3,2,1,0:T(8,128)(2,1)}) custom-call(s32[8]{0:T(128)S(1)} %stack.164.info, s32[256]{0:T(256)S(1)} %convert_element_type.233.flags, bf16[1536,512]{1,0:T(8,128)(2,1)} %x_own.9, ...), custom_call_target="tpu_custom_call", output_to_operand_aliasing={{0}: (12, {})} | custom-call | flops 7247757312 | bytes 30000000 | tf_op jit(solution)/shard_map/grad_blocks/pallas_call | solution.py:219
  397.8 6.5 %collective-permute-done.41 = bf16[8,128,128]{2,1,0:T(8,128)(2,1)S(1)} collective-permute-done((bf16[8,128,128]{2,1,0:T(8,128)(2,1)S(1)}, bf16[8,128,128]{2,1,0:T(8,128)(2,1)S(1)}, u32[]{:S(2)}, u32[]{:S(2)}) %collective-permute-start.41) | collective-permute-done | bytes 262176 | tf_op jit(solution)/shard_map/ppermute | solution.py:253
  404.3 2.2 collective-permute-start.44
  406.4 2.9 collective-permute-done.42
  409.3 2.1 collective-permute-done.44
  412.0 2.1 collective-permute-start.46
  416.3 5.1 %collective-permute-done.45 = bf16[8,128,128]{2,1,0:T(8,128)(2,1)S(1)} collective-permute-done((bf16[8,128,128]{2,1,0:T(8,128)(2,1)S(1)}, bf16[8,128,128]{2,1,0:T(8,128)(2,1)S(1)}, u32[]{:S(2)}, u32[]{:S(2)}) %collective-permute-start.45) | collective-permute-done | bytes 262176 | tf_op jit(solution)/shard_map/ppermute | solution.py:253
  421.4 2.9 collective-permute-done.46
  424.3 2.0 collective-permute-done.48
  430.9 4.4 collective-permute-done.49
  436.1 2.0 collective-permute-done.51
  (160 shorter events, 52.9 us)
Async XLA Ops:
  4.0 18.0 %collective-permute-start = (bf16[512,512]{1,0:T(8,128)(2,1)S(1)}, bf16[512,512]{1,0:T(8,128)(2,1)S(1)}, u32[]{:S(2)}, u32[]{:S(2)}) collective-permute-start(bf16[512,512]{1,0:T(8,128)(2,1)S(1)} %get-tuple-element.161), channel_id=1, source_target_pairs={{0,1},{1,0},{2,3},{3,2},{4,5},{5,4},{6,7},{7,6},{8,9},{9,8},{10,11... | collective-permute-start | bytes 1572872 | tf_op jit(solution)/shard_map/ppermute | solution.py:268
  22.5 102.6 %collective-permute-start.6 = (bf16[8,128,128]{2,1,0:T(8,128)(2,1)}, bf16[8,128,128]{2,1,0:T(8,128)(2,1)}, u32[]{:S(2)}, u32[]{:S(2)}) collective-permute-start(bf16[8,128,128]{2,1,0:T(8,128)(2,1)} %collective-permute-done.1.refs_2_), channel_id=1, source_target_pairs={{0,8},{2,10},{8,16},{10,18},{16,24},{18,26},{24,28},{26,30},{28,20... | collective-permute-start | bytes 786440 | tf_op jit(solution)/shard_map/ppermute | solution.py:253
  23.0 102.0 %collective-permute-start.7 = (bf16[8,128,128]{2,1,0:T(8,128)(2,1)}, bf16[8,128,128]{2,1,0:T(8,128)(2,1)}, u32[]{:S(2)}, u32[]{:S(2)}) collective-permute-start(bf16[8,128,128]{2,1,0:T(8,128)(2,1)} %collective-permute-done.2.refs_3_), channel_id=1, source_target_pairs={{0,8},{2,10},{8,16},{10,18},{16,24},{18,26},{24,28},{26,30},{28,20... | collective-permute-start | bytes 786440 | tf_op jit(solution)/shard_map/ppermute | solution.py:253
  24.6 100.5 %collective-permute-start.8 = (bf16[8,128,128]{2,1,0:T(8,128)(2,1)}, bf16[8,128,128]{2,1,0:T(8,128)(2,1)}, u32[]{:S(2)}, u32[]{:S(2)}) collective-permute-start(bf16[8,128,128]{2,1,0:T(8,128)(2,1)} %collective-permute-done.3.refs_4_), channel_id=1, source_target_pairs={{0,4},{2,6},{8,0},{10,2},{16,8},{18,10},{24,16},{26,18},{28,24},{3... | collective-permute-start | bytes 786440 | tf_op jit(solution)/shard_map/ppermute | solution.py:253
  25.1 100.0 %collective-permute-start.9 = (bf16[8,128,128]{2,1,0:T(8,128)(2,1)S(1)}, bf16[8,128,128]{2,1,0:T(8,128)(2,1)}, u32[]{:S(2)}, u32[]{:S(2)}) collective-permute-start(bf16[8,128,128]{2,1,0:T(8,128)(2,1)S(1)} %collective-permute-done.4.refs_5_), channel_id=1, source_target_pairs={{0,4},{2,6},{8,0},{10,2},{16,8},{18,10},{24,16},{26,18},{28,24},{3... | collective-permute-start | bytes 786440 | tf_op jit(solution)/shard_map/ppermute | solution.py:253
  27.3 98.9 %collective-permute-start.5 = (bf16[512,512]{1,0:T(8,128)(2,1)S(1)}, bf16[512,512]{1,0:T(8,128)(2,1)S(1)}, u32[]{:S(2)}, u32[]{:S(2)}) collective-permute-start(bf16[512,512]{1,0:T(8,128)(2,1)S(1)} %get-tuple-element.160), channel_id=1, source_target_pairs={{0,1},{1,0},{2,3},{3,2},{4,5},{5,4},{6,7},{7,6},{8,9},{9,8},{10,11... | collective-permute-start | bytes 1572872 | tf_op jit(solution)/shard_map/ppermute | solution.py:268
  126.2 71.3 %collective-permute-start.17 = (bf16[8,128,128]{2,1,0:T(8,128)(2,1)}, bf16[8,128,128]{2,1,0:T(8,128)(2,1)S(1)}, u32[]{:S(2)}, u32[]{:S(2)}) collective-permute-start(bf16[8,128,128]{2,1,0:T(8,128)(2,1)} %collective-permute-done.6.refs_0_), channel_id=1, source_target_pairs={{0,8},{2,10},{8,16},{10,18},{16,24},{18,26},{24,28},{26,30},{28,20... | collective-permute-start | bytes 786440 | tf_op jit(solution)/shard_map/ppermute | solution.py:253
  126.9 70.6 %collective-permute-start.18 = (bf16[8,128,128]{2,1,0:T(8,128)(2,1)}, bf16[8,128,128]{2,1,0:T(8,128)(2,1)}, u32[]{:S(2)}, u32[]{:S(2)}) collective-permute-start(bf16[8,128,128]{2,1,0:T(8,128)(2,1)} %collective-permute-done.7.refs_1_), channel_id=1, source_target_pairs={{0,8},{2,10},{8,16},{10,18},{16,24},{18,26},{24,28},{26,30},{28,20... | collective-permute-start | bytes 786440 | tf_op jit(solution)/shard_map/ppermute | solution.py:253
  128.3 69.2 %collective-permute-start.19 = (bf16[8,128,128]{2,1,0:T(8,128)(2,1)}, bf16[8,128,128]{2,1,0:T(8,128)(2,1)}, u32[]{:S(2)}, u32[]{:S(2)}) collective-permute-start(bf16[8,128,128]{2,1,0:T(8,128)(2,1)} %collective-permute-done.8.refs_2_), channel_id=1, source_target_pairs={{0,4},{2,6},{8,0},{10,2},{16,8},{18,10},{24,16},{26,18},{28,24},{3... | collective-permute-start | bytes 786440 | tf_op jit(solution)/shard_map/ppermute | solution.py:253
  128.9 68.6 %collective-permute-start.20 = (bf16[8,128,128]{2,1,0:T(8,128)(2,1)}, bf16[8,128,128]{2,1,0:T(8,128)(2,1)}, u32[]{:S(2)}, u32[]{:S(2)}) collective-permute-start(bf16[8,128,128]{2,1,0:T(8,128)(2,1)} %collective-permute-done.9.refs_3_), channel_id=1, source_target_pairs={{0,4},{2,6},{8,0},{10,2},{16,8},{18,10},{24,16},{26,18},{28,24},{3... | collective-permute-start | bytes 786440 | tf_op jit(solution)/shard_map/ppermute | solution.py:253
  130.6 69.2 %collective-permute-start.16 = (bf16[512,512]{1,0:T(8,128)(2,1)S(1)}, bf16[512,512]{1,0:T(8,128)(2,1)S(1)}, u32[]{:S(2)}, u32[]{:S(2)}) collective-permute-start(bf16[512,512]{1,0:T(8,128)(2,1)S(1)} %get-tuple-element.159), channel_id=1, source_target_pairs={{0,1},{1,0},{2,3},{3,2},{4,5},{5,4},{6,7},{7,6},{8,9},{9,8},{10,11... | collective-permute-start | bytes 1572872 | tf_op jit(solution)/shard_map/ppermute | solution.py:268
  199.4 72.4 %collective-permute-start.25 = (bf16[768,512]{1,0:T(8,128)(2,1)}, bf16[768,512]{1,0:T(8,128)(2,1)S(1)}, u32[]{:S(2)}, u32[]{:S(2)}) collective-permute-start(bf16[768,512]{1,0:T(8,128)(2,1)} %get-tuple-element.158), channel_id=1, source_target_pairs={{0,1},{1,0},{2,3},{3,2},{4,5},{5,4},{6,7},{7,6},{8,9},{9,8},{10,11... | collective-permute-start | bytes 2359304 | tf_op jit(solution)/shard_map/ppermute | solution.py:269
  201.1 68.1 %collective-permute-start.26 = (bf16[8,128,128]{2,1,0:T(8,128)(2,1)S(1)}, bf16[8,128,128]{2,1,0:T(8,128)(2,1)S(1)}, u32[]{:S(2)}, u32[]{:S(2)}) collective-permute-start(bf16[8,128,128]{2,1,0:T(8,128)(2,1)S(1)} %collective-permute-done.17.refs_0_), channel_id=1, source_target_pairs={{0,8},{2,10},{8,16},{10,18},{16,24},{18,26},{24,28},{26,30},{28,20... | collective-permute-start | bytes 786440 | tf_op jit(solution)/shard_map/ppermute | solution.py:253
  201.6 67.7 %collective-permute-start.27 = (bf16[8,128,128]{2,1,0:T(8,128)(2,1)}, bf16[8,128,128]{2,1,0:T(8,128)(2,1)}, u32[]{:S(2)}, u32[]{:S(2)}) collective-permute-start(bf16[8,128,128]{2,1,0:T(8,128)(2,1)} %collective-permute-done.20.refs_3_), channel_id=1, source_target_pairs={{0,4},{2,6},{8,0},{10,2},{16,8},{18,10},{24,16},{26,18},{28,24},{3... | collective-permute-start | bytes 786440 | tf_op jit(solution)/shard_map/ppermute | solution.py:253
  269.8 60.1 %collective-permute-start.34 = (bf16[768,512]{1,0:T(8,128)(2,1)}, bf16[768,512]{1,0:T(8,128)(2,1)S(1)}, u32[]{:S(2)}, u32[]{:S(2)}) collective-permute-start(bf16[768,512]{1,0:T(8,128)(2,1)} %get-tuple-element.157), channel_id=1, source_target_pairs={{0,1},{1,0},{2,3},{3,2},{4,5},{5,4},{6,7},{7,6},{8,9},{9,8},{10,11... | collective-permute-start | bytes 2359304 | tf_op jit(solution)/shard_map/ppermute | solution.py:269
  347.8 12.0 %collective-permute-start.35 = (bf16[1,16,128,128]{3,2,1,0:T(8,128)(2,1)}, bf16[1,16,128,128]{3,2,1,0:T(8,128)(2,1)}, u32[]{:S(2)}, u32[]{:S(2)}) collective-permute-start(bf16[1,16,128,128]{3,2,1,0:T(8,128)(2,1)} %get-tuple-element.114), channel_id=1, source_target_pairs={{0,2},{2,0},{4,6},{6,4},{8,10},{10,8},{12,14},{14,12},{16,18},{18,... | collective-permute-start | bytes 1572872 | tf_op jit(solution)/shard_map/ppermute | solution.py:253
  359.1 16.3 %collective-permute-start.36 = (bf16[2,16,128,128]{3,2,1,0:T(8,128)(2,1)}, bf16[2,16,128,128]{3,2,1,0:T(8,128)(2,1)}, u32[]{:S(2)}, u32[]{:S(2)}) collective-permute-start(bf16[2,16,128,128]{3,2,1,0:T(8,128)(2,1)} %get-tuple-element.118), channel_id=1, source_target_pairs={{0,2},{2,0},{4,6},{6,4},{8,10},{10,8},{12,14},{14,12},{16,18},{18,... | collective-permute-start | bytes 3145736 | tf_op jit(solution)/shard_map/ppermute | solution.py:253
  361.1 15.4 %collective-permute-start.37 = (bf16[8,128,128]{2,1,0:T(8,128)(2,1)S(1)}, bf16[8,128,128]{2,1,0:T(8,128)(2,1)S(1)}, u32[]{:S(2)}, u32[]{:S(2)}) collective-permute-start(bf16[8,128,128]{2,1,0:T(8,128)(2,1)S(1)} %get-tuple-element.119), channel_id=1, source_target_pairs={{0,8},{2,10},{8,16},{10,18},{16,24},{18,26},{24,28},{26,30},{28,20... | collective-permute-start | bytes 786440 | tf_op jit(solution)/shard_map/ppermute | solution.py:253
  362.4 14.1 %collective-permute-start.38 = (bf16[8,128,128]{2,1,0:T(8,128)(2,1)S(1)}, bf16[8,128,128]{2,1,0:T(8,128)(2,1)S(1)}, u32[]{:S(2)}, u32[]{:S(2)}) collective-permute-start(bf16[8,128,128]{2,1,0:T(8,128)(2,1)S(1)} %get-tuple-element.120), channel_id=1, source_target_pairs={{0,4},{2,6},{8,0},{10,2},{16,8},{18,10},{24,16},{26,18},{28,24},{3... | collective-permute-start | bytes 786440 | tf_op jit(solution)/shard_map/ppermute | solution.py:253
  375.3 36.1 %collective-permute-start.40 = (bf16[2,16,128,128]{3,2,1,0:T(8,128)(2,1)}, bf16[2,16,128,128]{3,2,1,0:T(8,128)(2,1)S(1)}, u32[]{:S(2)}, u32[]{:S(2)}) collective-permute-start(bf16[2,16,128,128]{3,2,1,0:T(8,128)(2,1)} %get-tuple-element.127), channel_id=1, source_target_pairs={{0,2},{2,0},{4,6},{6,4},{8,10},{10,8},{12,14},{14,12},{16,18},{18,... | collective-permute-start | bytes 3145736 | tf_op jit(solution)/shard_map/ppermute | solution.py:253
  394.3 32.0 %collective-permute-start.39 = (bf16[3,16,128,128]{3,2,1,0:T(8,128)(2,1)}, bf16[3,16,128,128]{3,2,1,0:T(8,128)(2,1)S(1)}, u32[]{:S(2)}, u32[]{:S(2)}) collective-permute-start(bf16[3,16,128,128]{3,2,1,0:T(8,128)(2,1)} %get-tuple-element.125), channel_id=1, source_target_pairs={{0,2},{2,0},{4,6},{6,4},{8,10},{10,8},{12,14},{14,12},{16,18},{18,... | collective-permute-start | bytes 4718600 | tf_op jit(solution)/shard_map/ppermute | solution.py:253
  395.7 13.6 %collective-permute-start.42 = (bf16[8,128,128]{2,1,0:T(8,128)(2,1)S(1)}, bf16[8,128,128]{2,1,0:T(8,128)(2,1)S(1)}, u32[]{:S(2)}, u32[]{:S(2)}) collective-permute-start(bf16[8,128,128]{2,1,0:T(8,128)(2,1)S(1)} %get-tuple-element.129), channel_id=1, source_target_pairs={{0,8},{2,10},{8,16},{10,18},{16,24},{18,26},{24,28},{26,30},{28,20... | collective-permute-start | bytes 786440 | tf_op jit(solution)/shard_map/ppermute | solution.py:253
  396.4 12.9 %collective-permute-start.43 = (bf16[8,128,128]{2,1,0:T(8,128)(2,1)S(1)}, bf16[8,128,128]{2,1,0:T(8,128)(2,1)S(1)}, u32[]{:S(2)}, u32[]{:S(2)}) collective-permute-start(bf16[8,128,128]{2,1,0:T(8,128)(2,1)S(1)} %get-tuple-element.130), channel_id=1, source_target_pairs={{0,4},{2,6},{8,0},{10,2},{16,8},{18,10},{24,16},{26,18},{28,24},{3... | collective-permute-start | bytes 786440 | tf_op jit(solution)/shard_map/ppermute | solution.py:253
  412.0 12.3 %collective-permute-start.46 = (bf16[8,128,128]{2,1,0:T(8,128)(2,1)S(1)}, bf16[8,128,128]{2,1,0:T(8,128)(2,1)S(1)}, u32[]{:S(2)}, u32[]{:S(2)}) collective-permute-start(bf16[8,128,128]{2,1,0:T(8,128)(2,1)S(1)} %get-tuple-element.133), channel_id=1, source_target_pairs={{0,8},{2,10},{8,16},{10,18},{16,24},{18,26},{24,28},{26,30},{28,20... | collective-permute-start | bytes 786440 | tf_op jit(solution)/shard_map/ppermute | solution.py:253
  (52 other events, 573.2 us)

commit v3 on v2

v3 whole, which is shorter than its diff:
```python
import functools

import jax
import jax.numpy as jnp
from jax import lax
from jax.experimental import pallas as pl
from jax.experimental.pallas import tpu as pltpu
from jax.sharding import PartitionSpec as P

momentum_decay = 0.9
step_size = 0.01
BF = jnp.bfloat16
F32 = jnp.float32
ANY = pl.BlockSpec(memory_space=pl.ANY)
HBM = pltpu.HBM
GELU_S = 0.7978845608028654
GELU_C = 0.044715


def activation(values):
    return jax.nn.gelu(values, approximate=True)


def in_hbm(array):
    return pltpu.with_memory_space_constraint(array, HBM)


def gelu_and_slope(v):
    sq = v * v
    t = jnp.tanh(v * (GELU_S + (GELU_S * GELU_C) * sq))
    half = 0.5 + 0.5 * t
    act = v * half
    slope = half + act * (1.0 - t) * (GELU_S + (3.0 * GELU_S * GELU_C) * sq)
    return act, slope


def load_weight(halves, first, owners, srcs, dst, sem):
    shift = owners[len(halves)]
    for s, half in enumerate(halves):
        owner = owners[s]

        @pl.when((owner < 8) if first else (owner >= 8))
        def _(s=s, half=half, owner=owner):
            if first:
                row = pl.multiple_of(((owner - shift) & 7) * 128, 128)
                place = dst.at[pl.ds(8 * half, 8), pl.ds(row, 128)]
            else:
                row = pl.multiple_of((owner - 8) * 256 + 128 * half, 128)
                place = dst.at[:, pl.ds(row, 128)]
            pltpu.make_async_copy(srcs[s], place, sem).start()


def pre_kernel(halves, owners, x_own, *refs):
    units, (*x_other, act_t, x_t, slope_ref, w1, sem) = refs[: len(halves)], refs[len(halves) :]
    step = pl.program_id(0)
    size = x_other[0].shape[0]

    @pl.when(step == 0)
    def _():
        load_weight(halves, True, owners, units, w1, sem)

    for s in range(4):

        @pl.when(step == s)
        def _(s=s):
            lanes = slice(256 * (s % 2), 256 * (s % 2) + 256)
            if s < 2:
                x_t[...] = x_own[:, lanes].T
            else:
                for i, part in enumerate(x_other):
                    x_t[:, i * size : (i + 1) * size] = part[:size, lanes].T

    @pl.when(step == 0)
    def _():
        pltpu.make_async_copy(w1, w1, sem).wait()

    w = jnp.concatenate([w1[2 * step], w1[2 * step + 1]], axis=1)
    half = w.shape[0] // 2
    for r in range(0, x_own.shape[0], 256):
        i, o = r // size, r % size
        pre = jnp.dot(x_own[r : r + 256, :], w[:half], preferred_element_type=F32)
        pre += jnp.dot(x_other[i][o : o + 256, :], w[half:], preferred_element_type=F32)
        act, slope = gelu_and_slope(pre)
        act_t[:, r : r + 256] = act.astype(BF).T
        slope_ref[r : r + 256, :] = slope


def hid_first_kernel(halves, owners, dy_own, dy_other, slope_ref, *refs):
    units, (hid, w2_t, w2, sem) = refs[: len(halves)], refs[len(halves) :]
    step = pl.program_id(0)
    shift = owners[len(halves)]

    @pl.when(step == 0)
    def _():
        load_weight(halves, False, owners, units, w2, sem)
        pltpu.make_async_copy(w2, w2, sem).wait()

    row = pl.multiple_of(256 * step, 256)
    for c in range(8):
        w2_t[128 * c : 128 * c + 128, :] = w2[(c + shift) & 7, pl.ds(row, 256), :].T
    hid_block(dy_own, dy_other, w2_t, slope_ref, hid)


def hid_block(dy_own, dy_other, w2_t, slope_ref, hid):
    half = w2_t.shape[0] // 2
    skip = dy_other.shape[0] - dy_own.shape[0]
    for r in range(0, dy_own.shape[0], 256):
        rows = slice(r, r + 256)
        g = jnp.dot(dy_own[rows, :], w2_t[:half, :], preferred_element_type=F32)
        g += jnp.dot(dy_other[r + skip : r + skip + 256, :], w2_t[half:, :], preferred_element_type=F32)
        hid[rows, :] = (g * slope_ref[rows, :]).astype(BF)


def hid_second_kernel(dy_own, dy_other, slope_ref, w2_t, _, hid):
    hid_block(dy_own, dy_other, w2_t, slope_ref, hid)


def grad_kernel(info, flags, x_t, act_t, hid_ref, dy_own, dy_first, dy_second, res_ref, *refs):
    new_res, mine, other = refs[-3:]
    group, h, n = pl.program_id(0), pl.program_id(1), pl.program_id(2)
    g = info[2 * group]
    shift, core = info[info.shape[0] - 2], info[info.shape[0] - 1]
    dot = functools.partial(jnp.dot, preferred_element_type=F32)

    def finish(value, flat):
        kept = flags[32 * g + flat] != 0
        value = value + res_ref[0, flat].astype(F32)
        new_res[0, flat] = jnp.where(kept, 0.0, value).astype(BF)
        return jnp.where(kept, value, 0.0).astype(BF)

    @pl.when(g < 4)
    def _():
        grad = dot(x_t[...], hid_ref[...])
        for out, row in ((mine, core), (other, 1 - core)):
            for j in range(2):
                lanes = slice(128 * j, 128 * j + 128)
                slot = 8 * h + 2 * n + j
                out[0, slot] = finish(jnp.where(row == 0, grad[:128, lanes], grad[128:, lanes]), 16 * row + slot)

    def second(grad, out):
        for i in range(2):
            for j in range(2):
                slot = 8 * i + ((2 * n + j + shift) & 7)
                out[0, slot] = finish(grad[128 * i : 128 * i + 128, 128 * j : 128 * j + 128], 16 * h + slot)

    for out, here in ((mine, h == core), (other, h != core)):

        @pl.when((g >= 4) & here & (n < 2))
        def _(out=out):
            second(dot(act_t[...], dy_own[...]), out)

        @pl.when((g >= 4) & here & (n >= 2))
        def _(out=out):
            size = dy_second.shape[0]
            second(dot(act_t[:, :size], dy_first[dy_first.shape[0] - size :, :]) + dot(act_t[:, size:], dy_second[...]), out)


def run_pre(owners, halves, x_own, x_other, units):
    rows = x_own.shape[0]
    whole = lambda t: pl.BlockSpec(t.shape, lambda i, *_: (0, 0))
    return pl.pallas_call(
        functools.partial(pre_kernel, halves),
        grid_spec=pltpu.PrefetchScalarGridSpec(
            num_scalar_prefetch=1,
            grid=(8,),
            in_specs=[whole(x_own)] + [ANY] * len(units) + [whole(t) for t in x_other],
            out_specs=[
                pl.BlockSpec((256, rows), lambda i, *_: (i, 0)),
                pl.BlockSpec((256, rows), lambda i, *_: (jnp.minimum(i, 3), 0)),
                pl.BlockSpec((rows, 256), lambda i, *_: (0, i)),
            ],
            scratch_shapes=[pltpu.VMEM((16, 1024, 128), BF), pltpu.SemaphoreType.DMA],
        ),
        out_shape=[HBM((2048, rows), BF), HBM((1024, rows), BF), HBM((rows, 2048), F32)],
        compiler_params=pltpu.CompilerParams(vmem_limit_bytes=30 * 2**20),
        cost_estimate=pl.CostEstimate(flops=5 * rows * 1024 * 2048, bytes_accessed=26_000_000, transcendentals=rows * 2048),
        name="pre_act",
    )(owners, in_hbm(x_own), *[in_hbm(u) for u in units], *x_other)


def run_hid_first(owners, halves, dy_own, dy_other, slope, units):
    rows = slope.shape[0] // 2
    column = pl.BlockSpec((rows, 256), lambda i, *_: (0, i))
    part = pl.BlockSpec((rows, 512), lambda i, *_: (0, 0))
    both = pl.BlockSpec(dy_other.shape, lambda i, *_: (0, 0))
    return pl.pallas_call(
        functools.partial(hid_first_kernel, halves),
        grid_spec=pltpu.PrefetchScalarGridSpec(
            num_scalar_prefetch=1,
            grid=(8,),
            in_specs=[part, both, column] + [ANY] * len(units),
            out_specs=[column, pl.BlockSpec((1024, 256), lambda i, *_: (0, i))],
            scratch_shapes=[pltpu.VMEM((8, 2048, 128), BF), pltpu.SemaphoreType.DMA],
        ),
        out_shape=[HBM(slope.shape, BF), HBM((1024, 2048), BF)],
        compiler_params=pltpu.CompilerParams(vmem_limit_bytes=24 * 2**20),
        cost_estimate=pl.CostEstimate(flops=4 * rows * 1024 * 2048, bytes_accessed=18_000_000, transcendentals=0),
        name="hid_first",
    )(owners, in_hbm(dy_own), dy_other, in_hbm(slope), *[in_hbm(u) for u in units])


def run_hid_second(dy_own, dy_other, slope, w2_t, hid):
    rows = dy_other.shape[0]
    column = pl.BlockSpec((rows, 256), lambda i: (1, i))
    return pl.pallas_call(
        hid_second_kernel,
        grid=(8,),
        in_specs=[
            pl.BlockSpec((rows, 512), lambda i: (1, 0)),
            pl.BlockSpec((rows, 512), lambda i: (0, 0)),
            column,
            pl.BlockSpec((1024, 256), lambda i: (0, i)),
            ANY,
        ],
        out_specs=column,
        out_shape=HBM(slope.shape, BF),
        input_output_aliases={4: 0},
        compiler_params=pltpu.CompilerParams(vmem_limit_bytes=20 * 2**20),
        cost_estimate=pl.CostEstimate(flops=3 * rows * 1024 * 2048, bytes_accessed=15_000_000, transcendentals=0),
        name="hid_second",
    )(in_hbm(dy_own), dy_other, in_hbm(slope), in_hbm(w2_t), in_hbm(hid))


def run_grads(info, flags, x_t, act_t, hid, dy_own, dy_other, residual, new_res, count):
    rows = hid.shape[0]
    block = pl.BlockSpec((1, 32, 128, 128), lambda i, h, n, info, *_: (info[2 * i], 0, 0, 0))
    local_block = pl.BlockSpec((1, 16, 128, 128), lambda i, h, n, *_: (i, 0, 0, 0))

    def spec(shape, first, index):
        def at(i, h, n, info, *_):
            return tuple(jnp.where((info[2 * i] < 4) == first, t, 0) for t in index(info[2 * i + 1], h, n))

        return pl.BlockSpec(shape, at)

    held = [in_hbm(t) for t in (x_t, act_t, hid, dy_own)]
    operands = [info, flags, *held, *dy_other, in_hbm(residual)]
    specs = [
        spec((256, rows), True, lambda a, h, n: (a, 0)),
        spec((256, rows), False, lambda a, h, n: (a + h, 0)),
        spec((rows, 256), True, lambda a, h, n: (0, 4 * h + n)),
        spec((rows, 256), False, lambda a, h, n: (0, jnp.minimum(n, 1))),
        *[spec((t.shape[0], 256), False, lambda a, h, n: (0, jnp.maximum(n - 2, 0))) for t in dy_other],
        block,
    ]
    alias = {}
    if new_res is not None:
        alias = {len(operands): 0}
        operands.append(in_hbm(new_res))
        specs.append(ANY)
    sent = HBM((count, 16, 128, 128), BF)
    return pl.pallas_call(
        grad_kernel,
        grid_spec=pltpu.PrefetchScalarGridSpec(
            num_scalar_prefetch=2,
            grid=(count, 2, 4),
            in_specs=specs,
            out_specs=[block, local_block, local_block],
        ),
        out_shape=[HBM(residual.shape, BF), sent, sent],
        input_output_aliases=alias,
        compiler_params=pltpu.CompilerParams(vmem_limit_bytes=24 * 2**20),
        cost_estimate=pl.CostEstimate(flops=3 * rows * 1024 * 512 * count, bytes_accessed=10_000_000 * count, transcendentals=0),
        name="grad_blocks",
    )(*operands)


def chip_at(place):
    place = place % 8
    if isinstance(place, int):
        return 2 * place if place < 4 else 2 * (7 - place) + 1
    return jnp.where(place < 4, 2 * place, 2 * (7 - place) + 1)


def ring_pairs(step):
    return [(2 * chip_at(p) + c, 2 * chip_at(p + step) + c) for p in range(8) for c in range(2)]


UP, DOWN = ring_pairs(1), ring_pairs(-1)
CORES = [(i, i ^ 1) for i in range(16)]
PAIR = [(0, 1), (1, 0)]


def hop(array, pairs):
    return lax.ppermute(array, "dp", pairs)


def local_ring(tokens, out_grad, master, momentum, residual, kept_blocks):
    mine = lax.axis_index("dp").astype(jnp.int32)
    shard = lax.axis_index("mp").astype(jnp.int32)
    core = mine & 1
    chip = mine >> 1
    place = jnp.where((chip & 1) == 0, chip >> 1, 7 - (chip >> 1))
    rows = tokens.shape[0]

    third, half = rows // 3, rows // 2
    swap = lambda t: lax.ppermute(t, "mp", PAIR)
    x_other = [swap(tokens[:third]), swap(tokens[third : 2 * third])]
    x_other.append(swap(jnp.concatenate([tokens[2 * third :], out_grad[:half]], axis=0)))
    dy_late = swap(out_grad[half:])

    shift = 4 * shard
    own = [master[0, :8].astype(BF), master[0, 8:].astype(BF)]
    up, down = list(own), list(own)
    units, halves, owners = list(own), [0, 1], [mine, mine]
    for k in range(1, 5):
        if 1 < k < 4:
            part = k - 2
            x_other[part], *both = lax.optimization_barrier((x_other[part], *up, *down))
            up, down = both[: len(up)], both[len(up) :]
        up = [hop(u, UP) for u in (up if k < 4 else up[:1])]
        down = [hop(u, DOWN) for u in (down if k < 4 else down[1:])]
        halves += [0, 1] if k == 4 else [0, 1, 0, 1]
        units += up + down
        owners += [2 * chip_at(place - k) + core] * len(up) + [2 * chip_at(place + k) + core] * len(down)
    units = units + [hop(u, CORES) for u in units]
    halves = tuple(halves * 2)
    owners = jnp.stack(owners + [o ^ 1 for o in owners] + [shift])

    block_count = residual.shape[2]
    flags = jnp.any(jnp.arange(block_count, dtype=jnp.int32)[None, :] == kept_blocks[0, 0][:, None], axis=0)
    flags = flags.astype(jnp.int32)

    act_t, x_t, slope = run_pre(owners, halves, tokens, x_other, units)
    hid, w2_t = run_hid_first(owners, halves, out_grad, x_other[2], slope, units)
    hid = run_hid_second(out_grad, dy_late, slope, w2_t, hid)
    dy_other = [x_other[2], dy_late]

    stored = residual.reshape(8, 32, 128, 128)

    def info_of(distances):
        out = []
        for k in distances:
            g = chip_at(place + k)
            a = jnp.where(g < 4, (g - 2 * shard) & 3, 2 * (g - 4))
            out += [g, a]
        return jnp.stack(out + [shift, core])

    new_res, sums, up, down = None, {}, {}, {}

    def add_up(distances):
        nonlocal new_res
        new_res, own_sum, other_sum = run_grads(
            info_of(distances), flags, x_t, act_t, hid, out_grad, dy_other, stored, new_res, len(distances)
        )
        other_sum = hop(other_sum, CORES)
        for i, k in enumerate(distances):
            for h in range(2):
                part = slice(8 * h, 8 * h + 8)
                sums[k, h] = own_sum[i, part].astype(F32) + other_sum[i, part].astype(F32)

    def send(k):
        nonlocal flags
        ups = {(k, h): sums[k, h] + (up[k + 1, h].astype(F32) if (k + 1, h) in up else 0.0) for h in range(2) if k < 4 or h == 0}
        downs = {(k, h): sums[8 - k, h] + (down[k + 1, h].astype(F32) if (k + 1, h) in down else 0.0) for h in range(2) if k < 4 or h == 1}
        ups, downs = [{key: t.astype(BF) for key, t in part.items()} for part in (ups, downs)]
        flags, ups, downs = lax.optimization_barrier((flags, ups, downs))
        up.update({key: hop(t, UP) for key, t in ups.items()})
        down.update({key: hop(t, DOWN) for key, t in downs.items()})

    add_up([4])
    add_up([3, 5])
    send(4)
    add_up([2, 6])
    send(3)
    add_up([1, 7, 0])
    send(2)
    send(1)
    owned = jnp.concatenate([sums[0, h] + up[1, h].astype(F32) + down[1, h].astype(F32) for h in range(2)], axis=0)
    new_momentum = momentum_decay * momentum + owned[None]
    new_master = master - step_size * new_momentum
    return new_master, new_momentum, new_res.reshape(residual.shape)


def local_plain(tokens, out_grad, master, momentum, residual, kept_blocks):
    whole_in = lax.all_gather(tokens, "mp", axis=1, tiled=True)
    whole_grad = lax.all_gather(out_grad, "mp", axis=1, tiled=True)
    tile = master.shape[-1]
    width = whole_in.shape[1]
    block_count = residual.shape[2]
    half = block_count // 2
    rows = width // tile
    cols = half // rows
    working = lax.all_gather(master.astype(BF), "dp", axis=1, tiled=True)[0]
    first_w = working[:half].reshape(rows, cols, tile, tile).transpose(0, 2, 1, 3).reshape(width, cols * tile)
    second_w = working[half:].reshape(cols, rows, tile, tile).transpose(0, 2, 1, 3).reshape(cols * tile, width)
    pre = jnp.dot(whole_in, first_w, preferred_element_type=F32)
    act_full, pullback = jax.vjp(activation, pre)
    act = act_full.astype(BF)
    act_grad = jnp.dot(whole_grad, second_w.T, preferred_element_type=F32)
    hid = pullback(act_grad)[0].astype(BF)
    first_g = jnp.dot(whole_in.T, hid, preferred_element_type=F32)
    second_g = jnp.dot(act.T, whole_grad, preferred_element_type=F32)
    first_g = first_g.reshape(rows, tile, cols, tile).transpose(0, 2, 1, 3).reshape(half, tile, tile)
    second_g = second_g.reshape(cols, tile, rows, tile).transpose(0, 2, 1, 3).reshape(half, tile, tile)
    grads = jnp.concatenate([first_g, second_g], axis=0) + residual[0, 0].astype(F32)
    flags = jnp.any(jnp.arange(block_count, dtype=jnp.int32)[None, :] == kept_blocks[0, 0][:, None], axis=0)
    flags = flags[:, None, None]
    new_residual = jnp.where(flags, 0.0, grads).astype(BF)[None, None]
    owned = lax.psum_scatter(jnp.where(flags, grads, 0.0), "dp", scatter_dimension=0, tiled=True)
    new_momentum = momentum_decay * momentum + owned[None]
    return master - step_size * new_momentum, new_momentum, new_residual


def solution(mesh):
    ring = mesh.shape["dp"] == 16 and mesh.shape["mp"] == 2
    blocks = P("mp", "dp", None, None)
    left = P("dp", "mp", None, None, None)
    return jax.shard_map(
        local_ring if ring else local_plain,
        mesh=mesh,
        in_specs=(P("dp", "mp"), P("dp", "mp"), blocks, blocks, left, P("dp", "mp", None)),
        out_specs=(blocks, blocks, left),
        check_vma=False,
    )
```

time: 442 us -> 234 us (0.53)
  Pallas kernels: 343 us -> 111 us
  waiting for transfers between devices: 41.1 us -> 71 us
    pallas_call x7 -> x3, Pallas kernels: 296 us -> 41.6 us  [the longest x1 18.9 us: run_pre(): pl.pallas_call(functools.partial(pre_kernel, halves), grid_spec=pltpu.Pre...]
    ppermute x48, waiting for transfers between devices: 41.1 us -> 66.1 us  [hop(): return lax.ppermute(array, 'dp', pairs)]
    pallas_call x4, Pallas kernels: 47.8 us -> 69.8 us  [run_grads(): pl.pallas_call(grad_kernel, grid_spec=pltpu.PrefetchScalarGridSpec(num_sc...]
    ppermute x5 -> x4, waiting for transfers between devices: 0.01 us -> 4.92 us  [local_ring(): swap = lambda t: lax.ppermute(t, 'mp', PAIR)]
  transfers between devices with their start and end apart: 53 -> 52, of which waited for: 15 -> 23; matrix products, arithmetic and copies ran while one was open for 2% -> 2% of each run, Pallas kernels for 74% -> 40%
where the time goes in v3:
time: 234 us; the launch traced here: 233 us
  Pallas kernels  111 us (47%)
  waiting for transfers between devices  71 us (30%)
  starting transfers between devices  40.1 us (17%)
  other arithmetic  5.95 us (3%)
  local copies, waits for them, and re-layouts  3.08 us (1%)
    pallas_call x4, Pallas kernels, run_grads(): pl.pallas_call(grad_kernel, grid_spec=pltpu.PrefetchScalarGridSpec(num_sc...  69.8 us
    ppermute x48, waiting for transfers between devices, hop(): return lax.ppermute(array, 'dp', pairs)  66.1 us
    ppermute x48, starting transfers between devices, hop(): return lax.ppermute(array, 'dp', pairs)  34.4 us
    pallas_call x1, Pallas kernels, run_pre(): pl.pallas_call(functools.partial(pre_kernel, halves), grid_spec=pltpu.Pre...  18.9 us
    pallas_call x1, Pallas kernels, run_hid_first(): pl.pallas_call(functools.partial(hid_first_kernel, halves), grid_spec=plt...  12.8 us
    pallas_call x1, Pallas kernels, run_hid_second(): pl.pallas_call(hid_second_kernel, grid=(8,), in_specs=[pl.BlockSpec((rows...  9.93 us
    ppermute x4, starting transfers between devices, local_ring(): swap = lambda t: lax.ppermute(t, 'mp', PAIR)  5.66 us
    ppermute x4, waiting for transfers between devices, local_ring(): swap = lambda t: lax.ppermute(t, 'mp', PAIR)  4.92 us
  transfers between devices with their start and end apart: 52, of which 23 were waited for; matrix products, arithmetic and copies ran while one was open for 2% of the time, Pallas kernels for 40%

profile of v3, /device:TPU:0, one launch (start us, length us, event | category | flops | bytes accessed | tf_op | source)
XLA Modules:
  0.0 232.7 jit_solution(13470162493863595264)
XLA Ops:
  2.2 3.0 %collective-permute-start.4 = (bf16[512,512]{1,0:T(8,128)(2,1)S(1)}, bf16[512,512]{1,0:T(8,128)(2,1)S(1)}, u32[]{:S(2)}, u32[]{:S(2)}) collective-permute-start(bf16[512,512]{1,0:T(8,128)(2,1)S(1)} %get-tuple-element.109), channel_id=1, source_target_pairs={{0,1},{1,0},{2,3},{3,2},{4,5},{5,4},{6,7},{7,6},{8,9},{9,8},{10,11... | collective-permute-start | bytes 1572872 | tf_op jit(solution)/shard_map/ppermute | solution.py:296
  9.5 5.2 %collective-permute-done.3.refs_5_ = bf16[8,128,128]{2,1,0:T(8,128)(2,1)S(1)} collective-permute-done((bf16[8,128,128]{2,1,0:T(8,128)(2,1)S(1)}, bf16[8,128,128]{2,1,0:T(8,128)(2,1)S(1)}, u32[]{:S(2)}, u32[]{:S(2)}) %collective-permute-start.3) | collective-permute-done | bytes 262176 | tf_op jit(solution)/shard_map/ppermute | solution.py:284
  24.1 4.9 %collective-permute-done.9.refs_33_ = bf16[512,512]{1,0:T(8,128)(2,1)S(1)} collective-permute-done((bf16[512,512]{1,0:T(8,128)(2,1)S(1)}, bf16[512,512]{1,0:T(8,128)(2,1)S(1)}, u32[]{:S(2)}, u32[]{:S(2)}) %collective-permute-start.9) | collective-permute-done | bytes 524320 | tf_op jit(solution)/shard_map/ppermute | solution.py:296
  30.8 3.6 %collective-permute-done.6.refs_7_ = bf16[8,128,128]{2,1,0:T(8,128)(2,1)S(1)} collective-permute-done((bf16[8,128,128]{2,1,0:T(8,128)(2,1)S(1)}, bf16[8,128,128]{2,1,0:T(8,128)(2,1)S(1)}, u32[]{:S(2)}, u32[]{:S(2)}) %collective-permute-start.6) | collective-permute-done | bytes 262176 | tf_op jit(solution)/shard_map/ppermute | solution.py:284
  39.3 4.1 %collective-permute-done.8.refs_9_ = bf16[8,128,128]{2,1,0:T(8,128)(2,1)S(1)} collective-permute-done((bf16[8,128,128]{2,1,0:T(8,128)(2,1)S(1)}, bf16[8,128,128]{2,1,0:T(8,128)(2,1)S(1)}, u32[]{:S(2)}, u32[]{:S(2)}) %collective-permute-start.8) | collective-permute-done | bytes 262176 | tf_op jit(solution)/shard_map/ppermute | solution.py:284
  48.5 4.7 %collective-permute-done.10.refs_10_ = bf16[8,128,128]{2,1,0:T(8,128)(2,1)S(1)} collective-permute-done((bf16[8,128,128]{2,1,0:T(8,128)(2,1)S(1)}, bf16[8,128,128]{2,1,0:T(8,128)(2,1)S(1)}, u32[]{:S(2)}, u32[]{:S(2)}) %collective-permute-start.10) | collective-permute-done | bytes 262176 | tf_op jit(solution)/shard_map/ppermute | solution.py:284
  53.2 5.1 %collective-permute-done.11.refs_11_ = bf16[8,128,128]{2,1,0:T(8,128)(2,1)S(1)} collective-permute-done((bf16[8,128,128]{2,1,0:T(8,128)(2,1)S(1)}, bf16[8,128,128]{2,1,0:T(8,128)(2,1)S(1)}, u32[]{:S(2)}, u32[]{:S(2)}) %collective-permute-start.11) | collective-permute-done | bytes 262176 | tf_op jit(solution)/shard_map/ppermute | solution.py:284
  61.9 5.3 %collective-permute-done.14.refs_14_ = bf16[8,128,128]{2,1,0:T(8,128)(2,1)} collective-permute-done((bf16[8,128,128]{2,1,0:T(8,128)(2,1)S(1)}, bf16[8,128,128]{2,1,0:T(8,128)(2,1)}, u32[]{:S(2)}, u32[]{:S(2)}) %collective-permute-start.14) | collective-permute-done | bytes 262176 | tf_op jit(solution)/shard_map/ppermute | solution.py:284
  67.8 2.4 %collective-permute-done.15.refs_15_ = bf16[8,128,128]{2,1,0:T(8,128)(2,1)} collective-permute-done((bf16[8,128,128]{2,1,0:T(8,128)(2,1)}, bf16[8,128,128]{2,1,0:T(8,128)(2,1)}, u32[]{:S(2)}, u32[]{:S(2)}) %collective-permute-start.15) | collective-permute-done | bytes 262176 | tf_op jit(solution)/shard_map/ppermute | solution.py:284
  72.1 18.9 %pre_act.1 = (bf16[2048,1536]{1,0:T(8,128)(2,1)}, bf16[1024,1536]{1,0:T(8,128)(2,1)}, f32[1536,2048]{1,0:T(8,128)}) custom-call(s32[33]{0:T(128)S(1)} %stack.174.owners, bf16[1536,512]{1,0:T(8,128)(2,1)} %x_own.1, bf16[8,128,128]{2,1,0:T(8,128)(2,1)} %copy-done.5, bf16[8,128,128]{2,1,0:T(8,128)(2,1)} %copy-done.4, bf16[8,128,128]{2,1,0:T(8,128)(2,1)} %copy-done.12, ...), custom_call_target="tpu_custom_call" | custom-call | flops 16106127360 | bytes 26000000 | tf_op jit(solution)/shard_map/pre_act/pallas_call | solution.py:161
  91.0 12.8 %hid_first.1 = (bf16[1536,2048]{1,0:T(8,128)(2,1)}, bf16[1024,2048]{1,0:T(8,128)(2,1)}) custom-call(s32[33]{0:T(128)S(1)} %stack.174.owners, bf16[1536,512]{1,0:T(8,128)(2,1)} %dy_own.11, bf16[1280,512]{1,0:T(8,128)(2,1)S(1)} %collective-permute-done.32.refs_34_.dy_other.dy_first, f32[1536,2048]{1,0:T(8,128)} %get-tuple-element.58.slope_ref, ...), custom_call_target="tpu_custom_call" | custom-call | flops 6442450944 | bytes 18000000 | tf_op jit(solution)/shard_map/hid_first/pallas_call | solution.py:186
  103.8 9.9 %hid_second.1.hid_ref = bf16[1536,2048]{1,0:T(8,128)(2,1)} custom-call(bf16[1536,512]{1,0:T(8,128)(2,1)} %dy_own.11, bf16[768,512]{1,0:T(8,128)(2,1)S(1)} %collective-permute-done.33.dy_other.dy_second, f32[1536,2048]{1,0:T(8,128)} %get-tuple-element.58.slope_ref, bf16[1024,2048]{1,0:T(8,128)(2,1)} %get-tuple-element.59.w2_t, ...), custom_call_target="tpu_custom_call", output_to_operand_aliasing={{}: (4, {})} | custom-call | flops 4831838208 | bytes 15000000 | tf_op jit(solution)/shard_map/hid_second/pallas_call | solution.py:205
  113.7 9.0 %grad_blocks.4 = (bf16[8,32,128,128]{3,2,1,0:T(8,128)(2,1)}, bf16[1,16,128,128]{3,2,1,0:T(8,128)(2,1)}, bf16[1,16,128,128]{3,2,1,0:T(8,128)(2,1)}) custom-call(s32[4]{0:T(128)S(1)} %pad_add_fusion.info, s32[256]{0:T(256)S(1)} %convert_element_type.233.flags, bf16[1024,1536]{1,0:T(8,128)(2,1)} %get-tuple-element.56.x_t, ...), custom_call_target="tpu_custom_call" | custom-call | flops 2415919104 | bytes 10000000 | tf_op jit(solution)/shard_map/grad_blocks/pallas_call | solution.py:251
  122.9 16.6 %grad_blocks.5 = (bf16[8,32,128,128]{3,2,1,0:T(8,128)(2,1)}, bf16[2,16,128,128]{3,2,1,0:T(8,128)(2,1)}, bf16[2,16,128,128]{3,2,1,0:T(8,128)(2,1)}) custom-call(s32[6]{0:T(128)S(1)} %stack.179.info, s32[256]{0:T(256)S(1)} %convert_element_type.233.flags, bf16[1024,1536]{1,0:T(8,128)(2,1)} %get-tuple-element.56.x_t, ...), custom_call_target="tpu_custom_call", output_to_operand_aliasing={{0}: (9, {})} | custom-call | flops 4831838208 | bytes 20000000 | tf_op jit(solution)/shard_map/grad_blocks/pallas_call | solution.py:251
  141.4 3.1 %collective-permute-start.36 = (bf16[8,128,128]{2,1,0:T(8,128)(2,1)S(1)}, bf16[8,128,128]{2,1,0:T(8,128)(2,1)S(1)}, u32[]{:S(2)}, u32[]{:S(2)}) collective-permute-start(bf16[8,128,128]{2,1,0:T(8,128)(2,1)S(1)} %get-tuple-element.67), channel_id=1, source_target_pairs={{0,8},{2,10},{8,16},{10,18},{16,24},{18,26},{24,28},{26,30},{28,20... | collective-permute-start | bytes 786440 | tf_op jit(solution)/shard_map/ppermute | solution.py:284
  144.5 18.0 %grad_blocks.6 = (bf16[8,32,128,128]{3,2,1,0:T(8,128)(2,1)}, bf16[2,16,128,128]{3,2,1,0:T(8,128)(2,1)}, bf16[2,16,128,128]{3,2,1,0:T(8,128)(2,1)}) custom-call(s32[6]{0:T(128)S(1)} %stack.184.info, s32[256]{0:T(256)S(1)} %convert_element_type.233.flags, bf16[1024,1536]{1,0:T(8,128)(2,1)} %get-tuple-element.56.x_t, ...), custom_call_target="tpu_custom_call", output_to_operand_aliasing={{0}: (9, {})} | custom-call | flops 4831838208 | bytes 20000000 | tf_op jit(solution)/shard_map/grad_blocks/pallas_call | solution.py:251
  163.0 26.2 %grad_blocks.7 = (bf16[8,32,128,128]{3,2,1,0:T(8,128)(2,1)}, bf16[3,16,128,128]{3,2,1,0:T(8,128)(2,1)}, bf16[3,16,128,128]{3,2,1,0:T(8,128)(2,1)}) custom-call(s32[8]{0:T(128)S(1)} %stack.152.info, s32[256]{0:T(256)S(1)} %convert_element_type.233.flags, bf16[1024,1536]{1,0:T(8,128)(2,1)} %get-tuple-element.56.x_t, ...), custom_call_target="tpu_custom_call", output_to_operand_aliasing={{0}: (9, {})} | custom-call | flops 7247757312 | bytes 30000000 | tf_op jit(solution)/shard_map/grad_blocks/pallas_call | solution.py:251
  193.5 5.2 %collective-permute-done.40 = bf16[8,128,128]{2,1,0:T(8,128)(2,1)S(1)} collective-permute-done((bf16[8,128,128]{2,1,0:T(8,128)(2,1)S(1)}, bf16[8,128,128]{2,1,0:T(8,128)(2,1)S(1)}, u32[]{:S(2)}, u32[]{:S(2)}) %collective-permute-start.40) | collective-permute-done | bytes 262176 | tf_op jit(solution)/shard_map/ppermute | solution.py:284
  198.8 4.7 %collective-permute-done.41 = bf16[8,128,128]{2,1,0:T(8,128)(2,1)S(1)} collective-permute-done((bf16[8,128,128]{2,1,0:T(8,128)(2,1)S(1)}, bf16[8,128,128]{2,1,0:T(8,128)(2,1)S(1)}, u32[]{:S(2)}, u32[]{:S(2)}) %collective-permute-start.41) | collective-permute-done | bytes 262176 | tf_op jit(solution)/shard_map/ppermute | solution.py:284
  203.5 2.4 %collective-permute-done.43 = bf16[8,128,128]{2,1,0:T(8,128)(2,1)S(1)} collective-permute-done((bf16[8,128,128]{2,1,0:T(8,128)(2,1)S(1)}, bf16[8,128,128]{2,1,0:T(8,128)(2,1)S(1)}, u32[]{:S(2)}, u32[]{:S(2)}) %collective-permute-start.43) | collective-permute-done | bytes 262176 | tf_op jit(solution)/shard_map/ppermute | solution.py:284
  210.5 5.1 %collective-permute-done.44 = bf16[8,128,128]{2,1,0:T(8,128)(2,1)S(1)} collective-permute-done((bf16[8,128,128]{2,1,0:T(8,128)(2,1)S(1)}, bf16[8,128,128]{2,1,0:T(8,128)(2,1)S(1)}, u32[]{:S(2)}, u32[]{:S(2)}) %collective-permute-start.44) | collective-permute-done | bytes 262176 | tf_op jit(solution)/shard_map/ppermute | solution.py:284
  215.6 2.8 %collective-permute-done.45 = bf16[8,128,128]{2,1,0:T(8,128)(2,1)S(1)} collective-permute-done((bf16[8,128,128]{2,1,0:T(8,128)(2,1)S(1)}, bf16[8,128,128]{2,1,0:T(8,128)(2,1)S(1)}, u32[]{:S(2)}, u32[]{:S(2)}) %collective-permute-start.45) | collective-permute-done | bytes 262176 | tf_op jit(solution)/shard_map/ppermute | solution.py:284
  224.8 3.2 %collective-permute-done.48 = bf16[8,128,128]{2,1,0:T(8,128)(2,1)S(1)} collective-permute-done((bf16[8,128,128]{2,1,0:T(8,128)(2,1)S(1)}, bf16[8,128,128]{2,1,0:T(8,128)(2,1)S(1)}, u32[]{:S(2)}, u32[]{:S(2)}) %collective-permute-start.48) | collective-permute-done | bytes 262176 | tf_op jit(solution)/shard_map/ppermute | solution.py:284
  228.0 2.8 %collective-permute-done.50 = bf16[8,128,128]{2,1,0:T(8,128)(2,1)S(1)} collective-permute-done((bf16[8,128,128]{2,1,0:T(8,128)(2,1)S(1)}, bf16[8,128,128]{2,1,0:T(8,128)(2,1)S(1)}, u32[]{:S(2)}, u32[]{:S(2)}) %collective-permute-start.50) | collective-permute-done | bytes 262176 | tf_op jit(solution)/shard_map/ppermute | solution.py:284
  (172 shorter events, 52.5 us)
Async XLA Ops:
  2.2 17.9 %collective-permute-start.4 = (bf16[512,512]{1,0:T(8,128)(2,1)S(1)}, bf16[512,512]{1,0:T(8,128)(2,1)S(1)}, u32[]{:S(2)}, u32[]{:S(2)}) collective-permute-start(bf16[512,512]{1,0:T(8,128)(2,1)S(1)} %get-tuple-element.109), channel_id=1, source_target_pairs={{0,1},{1,0},{2,3},{3,2},{4,5},{5,4},{6,7},{7,6},{8,9},{9,8},{10,11... | collective-permute-start | bytes 1572872 | tf_op jit(solution)/shard_map/ppermute | solution.py:296
  7.5 11.4 %collective-permute-start.2 = (bf16[8,128,128]{2,1,0:T(8,128)(2,1)S(1)}, bf16[8,128,128]{2,1,0:T(8,128)(2,1)S(1)}, u32[]{:S(2)}, u32[]{:S(2)}) collective-permute-start(bf16[8,128,128]{2,1,0:T(8,128)(2,1)S(1)} %get-tuple-element.113.refs_0_), channel_id=1, source_target_pairs={{0,4},{2,6},{8,0},{10,2},{16,8},{18,10},{24,16},{26,18},{28,24},{3... | collective-permute-start | bytes 786440 | tf_op jit(solution)/shard_map/ppermute | solution.py:284
  9.0 11.1 %collective-permute-start = (bf16[8,128,128]{2,1,0:T(8,128)(2,1)S(1)}, bf16[8,128,128]{2,1,0:T(8,128)(2,1)S(1)}, u32[]{:S(2)}, u32[]{:S(2)}) collective-permute-start(bf16[8,128,128]{2,1,0:T(8,128)(2,1)S(1)} %get-tuple-element.113.refs_0_), channel_id=1, source_target_pairs={{0,8},{2,10},{8,16},{10,18},{16,24},{18,26},{24,28},{26,30},{28,20... | collective-permute-start | bytes 786440 | tf_op jit(solution)/shard_map/ppermute | solution.py:284
  16.2 12.8 %collective-permute-start.9 = (bf16[512,512]{1,0:T(8,128)(2,1)S(1)}, bf16[512,512]{1,0:T(8,128)(2,1)S(1)}, u32[]{:S(2)}, u32[]{:S(2)}) collective-permute-start(bf16[512,512]{1,0:T(8,128)(2,1)S(1)} %get-tuple-element.108), channel_id=1, source_target_pairs={{0,1},{1,0},{2,3},{3,2},{4,5},{5,4},{6,7},{7,6},{8,9},{9,8},{10,11... | collective-permute-start | bytes 1572872 | tf_op jit(solution)/shard_map/ppermute | solution.py:296
  20.9 13.5 %collective-permute-start.6 = (bf16[8,128,128]{2,1,0:T(8,128)(2,1)S(1)}, bf16[8,128,128]{2,1,0:T(8,128)(2,1)S(1)}, u32[]{:S(2)}, u32[]{:S(2)}) collective-permute-start(bf16[8,128,128]{2,1,0:T(8,128)(2,1)S(1)} %collective-permute-done.1.refs_3_), channel_id=1, source_target_pairs={{0,8},{2,10},{8,16},{10,18},{16,24},{18,26},{24,28},{26,30},{28,20... | collective-permute-start | bytes 786440 | tf_op jit(solution)/shard_map/ppermute | solution.py:284
  23.5 19.8 %collective-permute-start.19 = (bf16[8,128,128]{2,1,0:T(8,128)(2,1)S(1)}, bf16[8,128,128]{2,1,0:T(8,128)(2,1)S(1)}, u32[]{:S(2)}, u32[]{:S(2)}) collective-permute-start(bf16[8,128,128]{2,1,0:T(8,128)(2,1)S(1)} %collective-permute-done.1.refs_3_), channel_id=1, source_target_pairs={{0,2},{2,0},{4,6},{6,4},{8,10},{10,8},{12,14},{14,12},{16,18},{18,... | collective-permute-start | bytes 786440 | tf_op jit(solution)/shard_map/ppermute | solution.py:284
  23.6 20.3 %collective-permute-start.20 = (bf16[8,128,128]{2,1,0:T(8,128)(2,1)S(1)}, bf16[8,128,128]{2,1,0:T(8,128)(2,1)S(1)}, u32[]{:S(2)}, u32[]{:S(2)}) collective-permute-start(bf16[8,128,128]{2,1,0:T(8,128)(2,1)S(1)} %collective-permute-done.2.refs_4_), channel_id=1, source_target_pairs={{0,2},{2,0},{4,6},{6,4},{8,10},{10,8},{12,14},{14,12},{16,18},{18,... | collective-permute-start | bytes 786440 | tf_op jit(solution)/shard_map/ppermute | solution.py:284
  29.0 15.0 %collective-permute-start.18 = (bf16[8,128,128]{2,1,0:T(8,128)(2,1)S(1)}, bf16[8,128,128]{2,1,0:T(8,128)(2,1)S(1)}, u32[]{:S(2)}, u32[]{:S(2)}) collective-permute-start(bf16[8,128,128]{2,1,0:T(8,128)(2,1)S(1)} %collective-permute-done.refs_2_), channel_id=1, source_target_pairs={{0,2},{2,0},{4,6},{6,4},{8,10},{10,8},{12,14},{14,12},{16,18},{18,... | collective-permute-start | bytes 786440 | tf_op jit(solution)/shard_map/ppermute | solution.py:284
  38.4 33.4 %collective-permute-start.32 = (bf16[1280,512]{1,0:T(8,128)(2,1)}, bf16[1280,512]{1,0:T(8,128)(2,1)S(1)}, u32[]{:S(2)}, u32[]{:S(2)}) collective-permute-start(bf16[1280,512]{1,0:T(8,128)(2,1)} %pad_maximum_fusion), channel_id=1, source_target_pairs={{0,1},{1,0},{2,3},{3,2},{4,5},{5,4},{6,7},{7,6},{8,9},{9,8},{10,11... | collective-permute-start | bytes 3932168 | tf_op jit(solution)/shard_map/ppermute | solution.py:296
  45.6 12.7 %collective-permute-start.11 = (bf16[8,128,128]{2,1,0:T(8,128)(2,1)S(1)}, bf16[8,128,128]{2,1,0:T(8,128)(2,1)S(1)}, u32[]{:S(2)}, u32[]{:S(2)}) collective-permute-start(bf16[8,128,128]{2,1,0:T(8,128)(2,1)S(1)} %collective-permute-done.6.refs_7_), channel_id=1, source_target_pairs={{0,8},{2,10},{8,16},{10,18},{16,24},{18,26},{24,28},{26,30},{28,20... | collective-permute-start | bytes 786440 | tf_op jit(solution)/shard_map/ppermute | solution.py:284
  47.3 11.1 %collective-permute-start.12 = (bf16[8,128,128]{2,1,0:T(8,128)(2,1)S(1)}, bf16[8,128,128]{2,1,0:T(8,128)(2,1)S(1)}, u32[]{:S(2)}, u32[]{:S(2)}) collective-permute-start(bf16[8,128,128]{2,1,0:T(8,128)(2,1)S(1)} %collective-permute-done.7.refs_8_), channel_id=1, source_target_pairs={{0,4},{2,6},{8,0},{10,2},{16,8},{18,10},{24,16},{26,18},{28,24},{3... | collective-permute-start | bytes 786440 | tf_op jit(solution)/shard_map/ppermute | solution.py:284
  47.7 13.4 %collective-permute-start.13 = (bf16[8,128,128]{2,1,0:T(8,128)(2,1)S(1)}, bf16[8,128,128]{2,1,0:T(8,128)(2,1)}, u32[]{:S(2)}, u32[]{:S(2)}) collective-permute-start(bf16[8,128,128]{2,1,0:T(8,128)(2,1)S(1)} %collective-permute-done.8.refs_9_), channel_id=1, source_target_pairs={{0,4},{2,6},{8,0},{10,2},{16,8},{18,10},{24,16},{26,18},{28,24},{3... | collective-permute-start | bytes 786440 | tf_op jit(solution)/shard_map/ppermute | solution.py:284
  70.6 33.2 %collective-permute-start.33 = (bf16[768,512]{1,0:T(8,128)(2,1)}, bf16[768,512]{1,0:T(8,128)(2,1)S(1)}, u32[]{:S(2)}, u32[]{:S(2)}) collective-permute-start(bf16[768,512]{1,0:T(8,128)(2,1)} %get-tuple-element.105), channel_id=1, source_target_pairs={{0,1},{1,0},{2,3},{3,2},{4,5},{5,4},{6,7},{7,6},{8,9},{9,8},{10,11... | collective-permute-start | bytes 2359304 | tf_op jit(solution)/shard_map/ppermute | solution.py:296
  122.7 17.3 %collective-permute-start.34 = (bf16[1,16,128,128]{3,2,1,0:T(8,128)(2,1)}, bf16[1,16,128,128]{3,2,1,0:T(8,128)(2,1)}, u32[]{:S(2)}, u32[]{:S(2)}) collective-permute-start(bf16[1,16,128,128]{3,2,1,0:T(8,128)(2,1)} %get-tuple-element.62), channel_id=1, source_target_pairs={{0,2},{2,0},{4,6},{6,4},{8,10},{10,8},{12,14},{14,12},{16,18},{18,... | collective-permute-start | bytes 1572872 | tf_op jit(solution)/shard_map/ppermute | solution.py:284
  139.5 23.0 %collective-permute-start.35 = (bf16[2,16,128,128]{3,2,1,0:T(8,128)(2,1)}, bf16[2,16,128,128]{3,2,1,0:T(8,128)(2,1)S(1)}, u32[]{:S(2)}, u32[]{:S(2)}) collective-permute-start(bf16[2,16,128,128]{3,2,1,0:T(8,128)(2,1)} %get-tuple-element.66), channel_id=1, source_target_pairs={{0,2},{2,0},{4,6},{6,4},{8,10},{10,8},{12,14},{14,12},{16,18},{18,... | collective-permute-start | bytes 3145736 | tf_op jit(solution)/shard_map/ppermute | solution.py:284
  141.4 21.3 %collective-permute-start.36 = (bf16[8,128,128]{2,1,0:T(8,128)(2,1)S(1)}, bf16[8,128,128]{2,1,0:T(8,128)(2,1)S(1)}, u32[]{:S(2)}, u32[]{:S(2)}) collective-permute-start(bf16[8,128,128]{2,1,0:T(8,128)(2,1)S(1)} %get-tuple-element.67), channel_id=1, source_target_pairs={{0,8},{2,10},{8,16},{10,18},{16,24},{18,26},{24,28},{26,30},{28,20... | collective-permute-start | bytes 786440 | tf_op jit(solution)/shard_map/ppermute | solution.py:284
  144.5 18.2 %collective-permute-start.37 = (bf16[8,128,128]{2,1,0:T(8,128)(2,1)S(1)}, bf16[8,128,128]{2,1,0:T(8,128)(2,1)S(1)}, u32[]{:S(2)}, u32[]{:S(2)}) collective-permute-start(bf16[8,128,128]{2,1,0:T(8,128)(2,1)S(1)} %get-tuple-element.68), channel_id=1, source_target_pairs={{0,4},{2,6},{8,0},{10,2},{16,8},{18,10},{24,16},{26,18},{28,24},{3... | collective-permute-start | bytes 786440 | tf_op jit(solution)/shard_map/ppermute | solution.py:284
  162.5 43.4 %collective-permute-start.39 = (bf16[2,16,128,128]{3,2,1,0:T(8,128)(2,1)}, bf16[2,16,128,128]{3,2,1,0:T(8,128)(2,1)S(1)}, u32[]{:S(2)}, u32[]{:S(2)}) collective-permute-start(bf16[2,16,128,128]{3,2,1,0:T(8,128)(2,1)} %get-tuple-element.75), channel_id=1, source_target_pairs={{0,2},{2,0},{4,6},{6,4},{8,10},{10,8},{12,14},{14,12},{16,18},{18,... | collective-permute-start | bytes 3145736 | tf_op jit(solution)/shard_map/ppermute | solution.py:284
  189.1 31.1 %collective-permute-start.38 = (bf16[3,16,128,128]{3,2,1,0:T(8,128)(2,1)}, bf16[3,16,128,128]{3,2,1,0:T(8,128)(2,1)S(1)}, u32[]{:S(2)}, u32[]{:S(2)}) collective-permute-start(bf16[3,16,128,128]{3,2,1,0:T(8,128)(2,1)} %get-tuple-element.73), channel_id=1, source_target_pairs={{0,2},{2,0},{4,6},{6,4},{8,10},{10,8},{12,14},{14,12},{16,18},{18,... | collective-permute-start | bytes 4718600 | tf_op jit(solution)/shard_map/ppermute | solution.py:284
  191.5 12.0 %collective-permute-start.41 = (bf16[8,128,128]{2,1,0:T(8,128)(2,1)S(1)}, bf16[8,128,128]{2,1,0:T(8,128)(2,1)S(1)}, u32[]{:S(2)}, u32[]{:S(2)}) collective-permute-start(bf16[8,128,128]{2,1,0:T(8,128)(2,1)S(1)} %get-tuple-element.77), channel_id=1, source_target_pairs={{0,8},{2,10},{8,16},{10,18},{16,24},{18,26},{24,28},{26,30},{28,20... | collective-permute-start | bytes 786440 | tf_op jit(solution)/shard_map/ppermute | solution.py:284
  192.6 10.9 %collective-permute-start.42 = (bf16[8,128,128]{2,1,0:T(8,128)(2,1)S(1)}, bf16[8,128,128]{2,1,0:T(8,128)(2,1)S(1)}, u32[]{:S(2)}, u32[]{:S(2)}) collective-permute-start(bf16[8,128,128]{2,1,0:T(8,128)(2,1)S(1)} %get-tuple-element.78), channel_id=1, source_target_pairs={{0,4},{2,6},{8,0},{10,2},{16,8},{18,10},{24,16},{26,18},{28,24},{3... | collective-permute-start | bytes 786440 | tf_op jit(solution)/shard_map/ppermute | solution.py:284
  207.8 10.7 %collective-permute-start.45 = (bf16[8,128,128]{2,1,0:T(8,128)(2,1)S(1)}, bf16[8,128,128]{2,1,0:T(8,128)(2,1)S(1)}, u32[]{:S(2)}, u32[]{:S(2)}) collective-permute-start(bf16[8,128,128]{2,1,0:T(8,128)(2,1)S(1)} %get-tuple-element.81), channel_id=1, source_target_pairs={{0,8},{2,10},{8,16},{10,18},{16,24},{18,26},{24,28},{26,30},{28,20... | collective-permute-start | bytes 786440 | tf_op jit(solution)/shard_map/ppermute | solution.py:284
  208.9 9.6 %collective-permute-start.46 = (bf16[8,128,128]{2,1,0:T(8,128)(2,1)S(1)}, bf16[8,128,128]{2,1,0:T(8,128)(2,1)S(1)}, u32[]{:S(2)}, u32[]{:S(2)}) collective-permute-start(bf16[8,128,128]{2,1,0:T(8,128)(2,1)S(1)} %get-tuple-element.82), channel_id=1, source_target_pairs={{0,4},{2,6},{8,0},{10,2},{16,8},{18,10},{24,16},{26,18},{28,24},{3... | collective-permute-start | bytes 786440 | tf_op jit(solution)/shard_map/ppermute | solution.py:284
  209.8 10.4 %collective-permute-start.47 = (bf16[8,128,128]{2,1,0:T(8,128)(2,1)S(1)}, bf16[8,128,128]{2,1,0:T(8,128)(2,1)S(1)}, u32[]{:S(2)}, u32[]{:S(2)}) collective-permute-start(bf16[8,128,128]{2,1,0:T(8,128)(2,1)S(1)} %get-tuple-element.83), channel_id=1, source_target_pairs={{0,4},{2,6},{8,0},{10,2},{16,8},{18,10},{24,16},{26,18},{28,24},{3... | collective-permute-start | bytes 786440 | tf_op jit(solution)/shard_map/ppermute | solution.py:284
  (61 other events, 733.0 us)

commit v4 on v3

--- a/solution.py
+++ b/solution.py
@@ -43,11 +43,13 @@
         def _(s=s, half=half, owner=owner):
             if first:
                 row = pl.multiple_of(((owner - shift) & 7) * 128, 128)
-                place = dst.at[pl.ds(8 * half, 8), pl.ds(row, 128)]
-            else:
-                row = pl.multiple_of((owner - 8) * 256 + 128 * half, 128)
-                place = dst.at[:, pl.ds(row, 128)]
-            pltpu.make_async_copy(srcs[s], place, sem).start()
+                slots = pl.ds(0, 16) if half is None else pl.ds(8 * half, 8)
+                pltpu.make_async_copy(srcs[s], dst.at[slots, pl.ds(row, 128)], sem).start()
+                return
+            for i in (0, 1) if half is None else (half,):
+                row = pl.multiple_of((owner - 8) * 256 + 128 * i, 128)
+                src = srcs[s].at[pl.ds(8 * i, 8)] if half is None else srcs[s]
+                pltpu.make_async_copy(src, dst.at[:, pl.ds(row, 128)], sem).start()
 
 
 def pre_kernel(halves, owners, x_own, *refs):
@@ -67,8 +69,8 @@
             if s < 2:
                 x_t[...] = x_own[:, lanes].T
             else:
-                for i, part in enumerate(x_other):
-                    x_t[:, i * size : (i + 1) * size] = part[:size, lanes].T
+                x_t[:, :size] = x_other[0][:, lanes].T
+                x_t[:, size:] = x_other[1][: x_own.shape[0] - size, lanes].T
 
     @pl.when(step == 0)
     def _():
@@ -77,16 +79,16 @@
     w = jnp.concatenate([w1[2 * step], w1[2 * step + 1]], axis=1)
     half = w.shape[0] // 2
     for r in range(0, x_own.shape[0], 256):
-        i, o = r // size, r % size
+        i, o = (0, r) if r < size else (1, r - size)
         pre = jnp.dot(x_own[r : r + 256, :], w[:half], preferred_element_type=F32)
         pre += jnp.dot(x_other[i][o : o + 256, :], w[half:], preferred_element_type=F32)
         act, slope = gelu_and_slope(pre)
         act_t[:, r : r + 256] = act.astype(BF).T
-        slope_ref[r : r + 256, :] = slope
+        slope_ref[0, r : r + 256, :] = slope
 
 
 def hid_first_kernel(halves, owners, dy_own, dy_other, slope_ref, *refs):
-    units, (hid, w2_t, w2, sem) = refs[: len(halves)], refs[len(halves) :]
+    units, (hid, dy, w2_t, w2, sem) = refs[: len(halves)], refs[len(halves) :]
     step = pl.program_id(0)
     shift = owners[len(halves)]
 
@@ -97,25 +99,29 @@
 
     row = pl.multiple_of(256 * step, 256)
     for c in range(8):
-        w2_t[128 * c : 128 * c + 128, :] = w2[(c + shift) & 7, pl.ds(row, 256), :].T
-    hid_block(dy_own, dy_other, w2_t, slope_ref, hid)
-
-
-def hid_block(dy_own, dy_other, w2_t, slope_ref, hid):
-    half = w2_t.shape[0] // 2
+        w2_t[0, 128 * c : 128 * c + 128, :] = w2[(c + shift) & 7, pl.ds(row, 256), :].T
+    hid_block(dy_own, dy_other, w2_t, slope_ref, hid, dy)
+
+
+def hid_block(dy_own, dy_other, w2_t, slope_ref, hid, dy):
+    half = w2_t.shape[1] // 2
     skip = dy_other.shape[0] - dy_own.shape[0]
-    for r in range(0, dy_own.shape[0], 256):
-        rows = slice(r, r + 256)
-        g = jnp.dot(dy_own[rows, :], w2_t[:half, :], preferred_element_type=F32)
-        g += jnp.dot(dy_other[r + skip : r + skip + 256, :], w2_t[half:, :], preferred_element_type=F32)
-        hid[rows, :] = (g * slope_ref[rows, :]).astype(BF)
-
-
-def hid_second_kernel(dy_own, dy_other, slope_ref, w2_t, _, hid):
-    hid_block(dy_own, dy_other, w2_t, slope_ref, hid)
-
-
-def grad_kernel(info, flags, x_t, act_t, hid_ref, dy_own, dy_first, dy_second, res_ref, *refs):
+    g = jnp.dot(dy_own[...], w2_t[0, :half, :], preferred_element_type=F32)
+    g += jnp.dot(dy_other[skip:, :], w2_t[0, half:, :], preferred_element_type=F32)
+    hid[0] = (g * slope_ref[0]).astype(BF)
+    for s in range(4):
+
+        @pl.when(pl.program_id(0) == s)
+        def _(s=s):
+            lanes = slice(256 * (s % 2), 256 * (s % 2) + 256)
+            dy[0] = dy_own[:, lanes] if s < 2 else dy_other[skip:, lanes]
+
+
+def hid_second_kernel(dy_own, dy_other, slope_ref, w2_t, _, __, hid, dy):
+    hid_block(dy_own, dy_other, w2_t, slope_ref, hid, dy)
+
+
+def grad_kernel(info, flags, x_t, act_t, hid_ref, dy_ref, res_ref, *refs):
     new_res, mine, other = refs[-3:]
     group, h, n = pl.program_id(0), pl.program_id(1), pl.program_id(2)
     g = info[2 * group]
@@ -130,29 +136,24 @@
 
     @pl.when(g < 4)
     def _():
-        grad = dot(x_t[...], hid_ref[...])
-        for out, row in ((mine, core), (other, 1 - core)):
-            for j in range(2):
-                lanes = slice(128 * j, 128 * j + 128)
-                slot = 8 * h + 2 * n + j
-                out[0, slot] = finish(jnp.where(row == 0, grad[:128, lanes], grad[128:, lanes]), 16 * row + slot)
-
-    def second(grad, out):
-        for i in range(2):
-            for j in range(2):
-                slot = 8 * i + ((2 * n + j + shift) & 7)
-                out[0, slot] = finish(grad[128 * i : 128 * i + 128, 128 * j : 128 * j + 128], 16 * h + slot)
+        for c in range(2):
+            grad = dot(x_t[...], hid_ref[c])
+            for out, row in ((mine, core), (other, 1 - core)):
+                for j in range(2):
+                    lanes = slice(128 * j, 128 * j + 128)
+                    slot = 8 * h + 4 * n + 2 * c + j
+                    out[0, slot] = finish(jnp.where(row == 0, grad[:128, lanes], grad[128:, lanes]), 16 * row + slot)
 
     for out, here in ((mine, h == core), (other, h != core)):
 
-        @pl.when((g >= 4) & here & (n < 2))
+        @pl.when((g >= 4) & here)
         def _(out=out):
-            second(dot(act_t[...], dy_own[...]), out)
-
-        @pl.when((g >= 4) & here & (n >= 2))
-        def _(out=out):
-            size = dy_second.shape[0]
-            second(dot(act_t[:, :size], dy_first[dy_first.shape[0] - size :, :]) + dot(act_t[:, size:], dy_second[...]), out)
+            for c in range(2):
+                grad = dot(act_t[...], dy_ref[c])
+                for i in range(2):
+                    for j in range(2):
+                        slot = 8 * i + ((4 * n + 2 * c + j + shift) & 7)
+                        out[0, slot] = finish(grad[128 * i : 128 * i + 128, 128 * j : 128 * j + 128], 16 * h + slot)
 
 
 def run_pre(owners, halves, x_own, x_other, units):
@@ -167,11 +168,11 @@
             out_specs=[
                 pl.BlockSpec((256, rows), lambda i, *_: (i, 0)),
                 pl.BlockSpec((256, rows), lambda i, *_: (jnp.minimum(i, 3), 0)),
-                pl.BlockSpec((rows, 256), lambda i, *_: (0, i)),
+                pl.BlockSpec((1, rows, 256), lambda i, *_: (i, 0, 0)),
             ],
             scratch_shapes=[pltpu.VMEM((16, 1024, 128), BF), pltpu.SemaphoreType.DMA],
         ),
-        out_shape=[HBM((2048, rows), BF), HBM((1024, rows), BF), HBM((rows, 2048), F32)],
+        out_shape=[HBM((2048, rows), BF), HBM((1024, rows), BF), HBM((8, rows, 256), F32)],
         compiler_params=pltpu.CompilerParams(vmem_limit_bytes=30 * 2**20),
         cost_estimate=pl.CostEstimate(flops=5 * rows * 1024 * 2048, bytes_accessed=26_000_000, transcendentals=rows * 2048),
         name="pre_act",
@@ -179,50 +180,55 @@
 
 
 def run_hid_first(owners, halves, dy_own, dy_other, slope, units):
-    rows = slope.shape[0] // 2
-    column = pl.BlockSpec((rows, 256), lambda i, *_: (0, i))
-    part = pl.BlockSpec((rows, 512), lambda i, *_: (0, 0))
-    both = pl.BlockSpec(dy_other.shape, lambda i, *_: (0, 0))
+    total = slope.shape[1]
+    rows = total // 2
+    part = lambda size: pl.BlockSpec((1, rows, 256), lambda i, *_: (jnp.minimum(i, size - 1), 0, 0))
     return pl.pallas_call(
         functools.partial(hid_first_kernel, halves),
         grid_spec=pltpu.PrefetchScalarGridSpec(
             num_scalar_prefetch=1,
             grid=(8,),
-            in_specs=[part, both, column] + [ANY] * len(units),
-            out_specs=[column, pl.BlockSpec((1024, 256), lambda i, *_: (0, i))],
+            in_specs=[
+                pl.BlockSpec((rows, 512), lambda i, *_: (0, 0)),
+                pl.BlockSpec(dy_other.shape, lambda i, *_: (0, 0)),
+                part(8),
+                *[ANY] * len(units),
+            ],
+            out_specs=[part(8), part(4), pl.BlockSpec((1, 1024, 256), lambda i, *_: (i, 0, 0))],
             scratch_shapes=[pltpu.VMEM((8, 2048, 128), BF), pltpu.SemaphoreType.DMA],
         ),
-        out_shape=[HBM(slope.shape, BF), HBM((1024, 2048), BF)],
+        out_shape=[HBM((8, total, 256), BF), HBM((4, total, 256), BF), HBM((8, 1024, 256), BF)],
         compiler_params=pltpu.CompilerParams(vmem_limit_bytes=24 * 2**20),
         cost_estimate=pl.CostEstimate(flops=4 * rows * 1024 * 2048, bytes_accessed=18_000_000, transcendentals=0),
         name="hid_first",
     )(owners, in_hbm(dy_own), dy_other, in_hbm(slope), *[in_hbm(u) for u in units])
 
 
-def run_hid_second(dy_own, dy_other, slope, w2_t, hid):
+def run_hid_second(dy_own, dy_other, slope, w2_t, hid, dy):
     rows = dy_other.shape[0]
-    column = pl.BlockSpec((rows, 256), lambda i: (1, i))
+    part = lambda size: pl.BlockSpec((1, rows, 256), lambda i: (jnp.minimum(i, size - 1), 1, 0))
     return pl.pallas_call(
         hid_second_kernel,
         grid=(8,),
         in_specs=[
             pl.BlockSpec((rows, 512), lambda i: (1, 0)),
             pl.BlockSpec((rows, 512), lambda i: (0, 0)),
-            column,
-            pl.BlockSpec((1024, 256), lambda i: (0, i)),
+            part(8),
+            pl.BlockSpec((1, 1024, 256), lambda i: (i, 0, 0)),
+            ANY,
             ANY,
         ],
-        out_specs=column,
-        out_shape=HBM(slope.shape, BF),
-        input_output_aliases={4: 0},
+        out_specs=[part(8), part(4)],
+        out_shape=[HBM(hid.shape, BF), HBM(dy.shape, BF)],
+        input_output_aliases={4: 0, 5: 1},
         compiler_params=pltpu.CompilerParams(vmem_limit_bytes=20 * 2**20),
         cost_estimate=pl.CostEstimate(flops=3 * rows * 1024 * 2048, bytes_accessed=15_000_000, transcendentals=0),
         name="hid_second",
-    )(in_hbm(dy_own), dy_other, in_hbm(slope), in_hbm(w2_t), in_hbm(hid))
-
-
-def run_grads(info, flags, x_t, act_t, hid, dy_own, dy_other, residual, new_res, count):
-    rows = hid.shape[0]
+    )(in_hbm(dy_own), dy_other, in_hbm(slope), in_hbm(w2_t), in_hbm(hid), in_hbm(dy))
+
+
+def run_grads(info, flags, x_t, act_t, hid, dy, residual, new_res, count):
+    rows = hid.shape[1]
     block = pl.BlockSpec((1, 32, 128, 128), lambda i, h, n, info, *_: (info[2 * i], 0, 0, 0))
     local_block = pl.BlockSpec((1, 16, 128, 128), lambda i, h, n, *_: (i, 0, 0, 0))
 
@@ -232,14 +238,12 @@
 
         return pl.BlockSpec(shape, at)
 
-    held = [in_hbm(t) for t in (x_t, act_t, hid, dy_own)]
-    operands = [info, flags, *held, *dy_other, in_hbm(residual)]
+    operands = [info, flags, *[in_hbm(t) for t in (x_t, act_t, hid, dy, residual)]]
     specs = [
         spec((256, rows), True, lambda a, h, n: (a, 0)),
         spec((256, rows), False, lambda a, h, n: (a + h, 0)),
-        spec((rows, 256), True, lambda a, h, n: (0, 4 * h + n)),
-        spec((rows, 256), False, lambda a, h, n: (0, jnp.minimum(n, 1))),
-        *[spec((t.shape[0], 256), False, lambda a, h, n: (0, jnp.maximum(n - 2, 0))) for t in dy_other],
+        spec((2, rows, 256), True, lambda a, h, n: (2 * h + n, 0, 0)),
+        spec((2, rows, 256), False, lambda a, h, n: (n, 0, 0)),
         block,
     ]
     alias = {}
@@ -252,7 +256,7 @@
         grad_kernel,
         grid_spec=pltpu.PrefetchScalarGridSpec(
             num_scalar_prefetch=2,
-            grid=(count, 2, 4),
+            grid=(count, 2, 2),
             in_specs=specs,
             out_specs=[block, local_block, local_block],
         ),
@@ -294,24 +298,22 @@
 
     third, half = rows // 3, rows // 2
     swap = lambda t: lax.ppermute(t, "mp", PAIR)
-    x_other = [swap(tokens[:third]), swap(tokens[third : 2 * third])]
-    x_other.append(swap(jnp.concatenate([tokens[2 * third :], out_grad[:half]], axis=0)))
+    x_other = [swap(tokens[:third]), swap(jnp.concatenate([tokens[third:], out_grad[:half]], axis=0))]
     dy_late = swap(out_grad[half:])
 
     shift = 4 * shard
-    own = [master[0, :8].astype(BF), master[0, 8:].astype(BF)]
-    up, down = list(own), list(own)
-    units, halves, owners = list(own), [0, 1], [mine, mine]
+    own = master[0].astype(BF)
+    up = down = own
+    units, halves, owners = [own], [None], [mine]
     for k in range(1, 5):
-        if 1 < k < 4:
-            part = k - 2
-            x_other[part], *both = lax.optimization_barrier((x_other[part], *up, *down))
-            up, down = both[: len(up)], both[len(up) :]
-        up = [hop(u, UP) for u in (up if k < 4 else up[:1])]
-        down = [hop(u, DOWN) for u in (down if k < 4 else down[1:])]
-        halves += [0, 1] if k == 4 else [0, 1, 0, 1]
-        units += up + down
-        owners += [2 * chip_at(place - k) + core] * len(up) + [2 * chip_at(place + k) + core] * len(down)
+        if k == 2:
+            x_other[0], up, down = lax.optimization_barrier((x_other[0], up, down))
+        if k == 4:
+            up, down = up[:8], down[8:]
+        up, down = hop(up, UP), hop(down, DOWN)
+        halves += [0, 1] if k == 4 else [None, None]
+        units += [up, down]
+        owners += [2 * chip_at(place - k) + core, 2 * chip_at(place + k) + core]
     units = units + [hop(u, CORES) for u in units]
     halves = tuple(halves * 2)
     owners = jnp.stack(owners + [o ^ 1 for o in owners] + [shift])
@@ -321,9 +323,8 @@
     flags = flags.astype(jnp.int32)
 
     act_t, x_t, slope = run_pre(owners, halves, tokens, x_other, units)
-    hid, w2_t = run_hid_first(owners, halves, out_grad, x_other[2], slope, units)
-    hid = run_hid_second(out_grad, dy_late, slope, w2_t, hid)
-    dy_other = [x_other[2], dy_late]
+    hid, dy, w2_t = run_hid_first(owners, halves, out_grad, x_other[1], slope, units)
+    hid, dy = run_hid_second(out_grad, dy_late, slope, w2_t, hid, dy)
 
     stored = residual.reshape(8, 32, 128, 128)
 
@@ -340,7 +341,7 @@
     def add_up(distances):
         nonlocal new_res
         new_res, own_sum, other_sum = run_grads(
-            info_of(distances), flags, x_t, act_t, hid, out_grad, dy_other, stored, new_res, len(distances)
+            info_of(distances), flags, x_t, act_t, hid, dy, stored, new_res, len(distances)
         )
         other_sum = hop(other_sum, CORES)
         for i, k in enumerate(distances):

time: 234 us -> 214 us (0.915)
  Pallas kernels: 111 us -> 98.8 us
  starting transfers between devices: 40.1 us -> 29.8 us
  waiting for transfers between devices: 71 us -> 73.9 us
    pallas_call x4, Pallas kernels: 69.8 us -> 55.7 us  [run_grads(): pl.pallas_call(grad_kernel, grid_spec=pltpu.PrefetchScalarGridSpec(num_sc...]
    ppermute x4 -> x3, waiting for transfers between devices: 4.92 us -> 16.1 us  [local_ring(): swap = lambda t: lax.ppermute(t, 'mp', PAIR)]
    ppermute x48 -> x35, starting transfers between devices: 34.4 us -> 25.7 us  [hop(): return lax.ppermute(array, 'dp', pairs)]
    ppermute x48 -> x35, waiting for transfers between devices: 66.1 us -> 57.8 us  [hop(): return lax.ppermute(array, 'dp', pairs)]
    ppermute x4 -> x3, starting transfers between devices: 5.66 us -> 4.1 us  [local_ring(): swap = lambda t: lax.ppermute(t, 'mp', PAIR)]
  transfers between devices with their start and end apart: 52 -> 38, of which waited for: 23 -> 19; matrix products, arithmetic and copies ran while one was open for 2% -> 2% of each run, Pallas kernels for 40% -> 38%
where the time goes in v4:
time: 214 us; the launch traced here: 213 us
  Pallas kernels  98.8 us (46%)
  waiting for transfers between devices  73.9 us (35%)
  starting transfers between devices  29.8 us (14%)
  other arithmetic  6.2 us (3%)
  local copies, waits for them, and re-layouts  2.66 us (1%)
    ppermute x35, waiting for transfers between devices, hop(): return lax.ppermute(array, 'dp', pairs)  57.8 us
    pallas_call x4, Pallas kernels, run_grads(): pl.pallas_call(grad_kernel, grid_spec=pltpu.PrefetchScalarGridSpec(num_sc...  55.7 us
    ppermute x35, starting transfers between devices, hop(): return lax.ppermute(array, 'dp', pairs)  25.7 us
    pallas_call x1, Pallas kernels, run_pre(): pl.pallas_call(functools.partial(pre_kernel, halves), grid_spec=pltpu.Pre...  19.1 us
    ppermute x3, waiting for transfers between devices, local_ring(): swap = lambda t: lax.ppermute(t, 'mp', PAIR)  16.1 us
    pallas_call x1, Pallas kernels, run_hid_first(): pl.pallas_call(functools.partial(hid_first_kernel, halves), grid_spec=plt...  13.6 us
    pallas_call x1, Pallas kernels, run_hid_second(): pl.pallas_call(hid_second_kernel, grid=(8,), in_specs=[pl.BlockSpec((rows...  10.3 us
  transfers between devices with their start and end apart: 38, of which 19 were waited for; matrix products, arithmetic and copies ran while one was open for 2% of the time, Pallas kernels for 38%

profile of v4, /device:TPU:0, one launch (start us, length us, event | category | flops | bytes accessed | tf_op | source)
XLA Modules:
  0.0 212.6 jit_solution(7022429219015035399)
XLA Ops:
  1.9 3.0 %collective-permute-start.2 = (bf16[512,512]{1,0:T(8,128)(2,1)S(1)}, bf16[512,512]{1,0:T(8,128)(2,1)S(1)}, u32[]{:S(2)}, u32[]{:S(2)}) collective-permute-start(bf16[512,512]{1,0:T(8,128)(2,1)S(1)} %slice.114), channel_id=1, source_target_pairs={{0,1},{1,0},{2,3},{3,2},{4,5},{5,4},{6,7},{7,6},{8,9},{9,8},{10,11... | collective-permute-start | bytes 1572872 | tf_op jit(solution)/shard_map/ppermute | solution.py:300
  9.3 7.5 %collective-permute-done.2.refs_18_ = bf16[512,512]{1,0:T(8,128)(2,1)S(1)} collective-permute-done((bf16[512,512]{1,0:T(8,128)(2,1)S(1)}, bf16[512,512]{1,0:T(8,128)(2,1)S(1)}, u32[]{:S(2)}, u32[]{:S(2)}) %collective-permute-start.2) | collective-permute-done | bytes 524320 | tf_op jit(solution)/shard_map/ppermute | solution.py:300
  16.8 2.8 %collective-permute-done.1.refs_2_ = bf16[16,128,128]{2,1,0:T(8,128)(2,1)S(1)} collective-permute-done((bf16[16,128,128]{2,1,0:T(8,128)(2,1)S(1)}, bf16[16,128,128]{2,1,0:T(8,128)(2,1)S(1)}, u32[]{:S(2)}, u32[]{:S(2)}) %collective-permute-start.1) | collective-permute-done | bytes 524320 | tf_op jit(solution)/shard_map/ppermute | solution.py:288
  24.8 8.3 %collective-permute-done.3.refs_3_ = bf16[16,128,128]{2,1,0:T(8,128)(2,1)S(1)} collective-permute-done((bf16[16,128,128]{2,1,0:T(8,128)(2,1)S(1)}, bf16[16,128,128]{2,1,0:T(8,128)(2,1)S(1)}, u32[]{:S(2)}, u32[]{:S(2)}) %collective-permute-start.3) | collective-permute-done | bytes 524320 | tf_op jit(solution)/shard_map/ppermute | solution.py:288
  35.6 8.7 %collective-permute-done.5.refs_5_ = bf16[16,128,128]{2,1,0:T(8,128)(2,1)S(1)} collective-permute-done((bf16[16,128,128]{2,1,0:T(8,128)(2,1)S(1)}, bf16[16,128,128]{2,1,0:T(8,128)(2,1)S(1)}, u32[]{:S(2)}, u32[]{:S(2)}) %collective-permute-start.5) | collective-permute-done | bytes 524320 | tf_op jit(solution)/shard_map/ppermute | solution.py:288
  47.7 6.2 %collective-permute-done.7.refs_7_ = bf16[8,128,128]{2,1,0:T(8,128)(2,1)} collective-permute-done((bf16[8,128,128]{2,1,0:T(8,128)(2,1)S(1)}, bf16[8,128,128]{2,1,0:T(8,128)(2,1)}, u32[]{:S(2)}, u32[]{:S(2)}) %collective-permute-start.7) | collective-permute-done | bytes 262176 | tf_op jit(solution)/shard_map/ppermute | solution.py:288
  55.8 8.6 %collective-permute-done.18.refs_19_.dy_other = bf16[1792,512]{1,0:T(8,128)(2,1)S(1)} collective-permute-done((bf16[1792,512]{1,0:T(8,128)(2,1)}, bf16[1792,512]{1,0:T(8,128)(2,1)S(1)}, u32[]{:S(2)}, u32[]{:S(2)}) %collective-permute-start.18) | collective-permute-done | bytes 1835040 | tf_op jit(solution)/shard_map/ppermute | solution.py:300
  65.0 19.1 %pre_act.1 = (bf16[2048,1536]{1,0:T(8,128)(2,1)}, bf16[1024,1536]{1,0:T(8,128)(2,1)}, f32[8,1536,256]{2,1,0:T(8,128)}) custom-call(s32[19]{0:T(128)S(1)} %stack.160.owners, bf16[1536,512]{1,0:T(8,128)(2,1)} %x_own.1, bf16[16,128,128]{2,1,0:T(8,128)(2,1)} %copy-done.2, bf16[16,128,128]{2,1,0:T(8,128)(2,1)} %copy-done.11, bf16[16,128,128]{2,1,0:T(8,128)(2,1)} %copy-done.10, ...), custom_call_target="tpu_custom_call" | custom-call | flops 16106127360 | bytes 26000000 | tf_op jit(solution)/shard_map/pre_act/pallas_call | solution.py:162
  84.2 13.6 %hid_first.1 = (bf16[8,1536,256]{2,1,0:T(8,128)(2,1)}, bf16[4,1536,256]{2,1,0:T(8,128)(2,1)}, bf16[8,1024,256]{2,1,0:T(8,128)(2,1)}) custom-call(s32[19]{0:T(128)S(1)} %stack.160.owners, bf16[1536,512]{1,0:T(8,128)(2,1)} %dy_own.3, bf16[1792,512]{1,0:T(8,128)(2,1)S(1)} %collective-permute-done.18.refs_19_.dy_other, ...), custom_call_target="tpu_custom_call" | custom-call | flops 6442450944 | bytes 18000000 | tf_op jit(solution)/shard_map/hid_first/pallas_call | solution.py:186
  97.7 10.3 %hid_second.1 = (bf16[8,1536,256]{2,1,0:T(8,128)(2,1)}, bf16[4,1536,256]{2,1,0:T(8,128)(2,1)}) custom-call(bf16[1536,512]{1,0:T(8,128)(2,1)} %dy_own.3, bf16[768,512]{1,0:T(8,128)(2,1)S(1)} %collective-permute-done.19.dy_other, f32[8,1536,256]{2,1,0:T(8,128)} %get-tuple-element.47.slope_ref, ...), custom_call_target="tpu_custom_call", output_to_operand_aliasing={{0}: (4, {}), {1}: (5, {})} | custom-call | flops 4831838208 | bytes 15000000 | tf_op jit(solution)/shard_map/hid_second/pallas_call | solution.py:210
  108.1 8.2 %grad_blocks.4 = (bf16[8,32,128,128]{3,2,1,0:T(8,128)(2,1)}, bf16[1,16,128,128]{3,2,1,0:T(8,128)(2,1)}, bf16[1,16,128,128]{3,2,1,0:T(8,128)(2,1)}) custom-call(s32[4]{0:T(128)S(1)} %pad_add_fusion.info, s32[256]{0:T(256)S(1)} %convert_element_type.232.flags, bf16[1024,1536]{1,0:T(8,128)(2,1)} %get-tuple-element.45.x_t, ...), custom_call_target="tpu_custom_call" | custom-call | flops 2415919104 | bytes 10000000 | tf_op jit(solution)/shard_map/grad_blocks/pallas_call | solution.py:255
  116.3 14.0 %grad_blocks.5 = (bf16[8,32,128,128]{3,2,1,0:T(8,128)(2,1)}, bf16[2,16,128,128]{3,2,1,0:T(8,128)(2,1)}, bf16[2,16,128,128]{3,2,1,0:T(8,128)(2,1)}) custom-call(s32[6]{0:T(128)S(1)} %stack.165.info, s32[256]{0:T(256)S(1)} %convert_element_type.232.flags, bf16[1024,1536]{1,0:T(8,128)(2,1)} %get-tuple-element.45.x_t, ...), custom_call_target="tpu_custom_call", output_to_operand_aliasing={{0}: (7, {})} | custom-call | flops 4831838208 | bytes 20000000 | tf_op jit(solution)/shard_map/grad_blocks/pallas_call | solution.py:255
  133.2 14.3 %grad_blocks.6 = (bf16[8,32,128,128]{3,2,1,0:T(8,128)(2,1)}, bf16[2,16,128,128]{3,2,1,0:T(8,128)(2,1)}, bf16[2,16,128,128]{3,2,1,0:T(8,128)(2,1)}) custom-call(s32[6]{0:T(128)S(1)} %stack.170.info, s32[256]{0:T(256)S(1)} %convert_element_type.232.flags, bf16[1024,1536]{1,0:T(8,128)(2,1)} %get-tuple-element.45.x_t, ...), custom_call_target="tpu_custom_call", output_to_operand_aliasing={{0}: (7, {})} | custom-call | flops 4831838208 | bytes 20000000 | tf_op jit(solution)/shard_map/grad_blocks/pallas_call | solution.py:255
  147.9 19.2 %grad_blocks.7 = (bf16[8,32,128,128]{3,2,1,0:T(8,128)(2,1)}, bf16[3,16,128,128]{3,2,1,0:T(8,128)(2,1)}, bf16[3,16,128,128]{3,2,1,0:T(8,128)(2,1)}) custom-call(s32[8]{0:T(128)S(1)} %stack.138.info, s32[256]{0:T(256)S(1)} %convert_element_type.232.flags, bf16[1024,1536]{1,0:T(8,128)(2,1)} %get-tuple-element.45.x_t, ...), custom_call_target="tpu_custom_call", output_to_operand_aliasing={{0}: (7, {})} | custom-call | flops 7247757312 | bytes 30000000 | tf_op jit(solution)/shard_map/grad_blocks/pallas_call | solution.py:255
  169.0 1.9 collective-permute-start.27
  171.0 5.9 %collective-permute-done.26 = bf16[8,128,128]{2,1,0:T(8,128)(2,1)S(1)} collective-permute-done((bf16[8,128,128]{2,1,0:T(8,128)(2,1)S(1)}, bf16[8,128,128]{2,1,0:T(8,128)(2,1)S(1)}, u32[]{:S(2)}, u32[]{:S(2)}) %collective-permute-start.26) | collective-permute-done | bytes 262176 | tf_op jit(solution)/shard_map/ppermute | solution.py:288
  176.9 1.7 collective-permute-start.29
  178.6 3.0 %collective-permute-done.27 = bf16[8,128,128]{2,1,0:T(8,128)(2,1)S(1)} collective-permute-done((bf16[8,128,128]{2,1,0:T(8,128)(2,1)S(1)}, bf16[8,128,128]{2,1,0:T(8,128)(2,1)S(1)}, u32[]{:S(2)}, u32[]{:S(2)}) %collective-permute-start.27) | collective-permute-done | bytes 262176 | tf_op jit(solution)/shard_map/ppermute | solution.py:288
  181.6 2.6 %collective-permute-done.29 = bf16[8,128,128]{2,1,0:T(8,128)(2,1)S(1)} collective-permute-done((bf16[8,128,128]{2,1,0:T(8,128)(2,1)S(1)}, bf16[8,128,128]{2,1,0:T(8,128)(2,1)S(1)}, u32[]{:S(2)}, u32[]{:S(2)}) %collective-permute-start.29) | collective-permute-done | bytes 262176 | tf_op jit(solution)/shard_map/ppermute | solution.py:288
  188.8 5.2 %collective-permute-done.30 = bf16[8,128,128]{2,1,0:T(8,128)(2,1)S(1)} collective-permute-done((bf16[8,128,128]{2,1,0:T(8,128)(2,1)S(1)}, bf16[8,128,128]{2,1,0:T(8,128)(2,1)S(1)}, u32[]{:S(2)}, u32[]{:S(2)}) %collective-permute-start.30) | collective-permute-done | bytes 262176 | tf_op jit(solution)/shard_map/ppermute | solution.py:288
  194.0 2.8 %collective-permute-done.31 = bf16[8,128,128]{2,1,0:T(8,128)(2,1)S(1)} collective-permute-done((bf16[8,128,128]{2,1,0:T(8,128)(2,1)S(1)}, bf16[8,128,128]{2,1,0:T(8,128)(2,1)S(1)}, u32[]{:S(2)}, u32[]{:S(2)}) %collective-permute-start.31) | collective-permute-done | bytes 262176 | tf_op jit(solution)/shard_map/ppermute | solution.py:288
  198.9 2.1 collective-permute-start.34
  201.0 2.0 collective-permute-start.36
  203.0 3.4 %collective-permute-done.34 = bf16[8,128,128]{2,1,0:T(8,128)(2,1)S(1)} collective-permute-done((bf16[8,128,128]{2,1,0:T(8,128)(2,1)S(1)}, bf16[8,128,128]{2,1,0:T(8,128)(2,1)S(1)}, u32[]{:S(2)}, u32[]{:S(2)}) %collective-permute-start.34) | collective-permute-done | bytes 262176 | tf_op jit(solution)/shard_map/ppermute | solution.py:288
  (121 shorter events, 36.9 us)
Async XLA Ops:
  1.9 15.0 %collective-permute-start.2 = (bf16[512,512]{1,0:T(8,128)(2,1)S(1)}, bf16[512,512]{1,0:T(8,128)(2,1)S(1)}, u32[]{:S(2)}, u32[]{:S(2)}) collective-permute-start(bf16[512,512]{1,0:T(8,128)(2,1)S(1)} %slice.114), channel_id=1, source_target_pairs={{0,1},{1,0},{2,3},{3,2},{4,5},{5,4},{6,7},{7,6},{8,9},{9,8},{10,11... | collective-permute-start | bytes 1572872 | tf_op jit(solution)/shard_map/ppermute | solution.py:300
  6.2 13.4 %collective-permute-start.1 = (bf16[16,128,128]{2,1,0:T(8,128)(2,1)S(1)}, bf16[16,128,128]{2,1,0:T(8,128)(2,1)S(1)}, u32[]{:S(2)}, u32[]{:S(2)}) collective-permute-start(bf16[16,128,128]{2,1,0:T(8,128)(2,1)S(1)} %convert_bitcast_fusion.refs_0_), channel_id=1, source_target_pairs={{0,4},{2,6},{8,0},{10,2},{16,8},{18,10},{24,16},{26,18},{28,24},{3... | collective-permute-start | bytes 1572872 | tf_op jit(solution)/shard_map/ppermute | solution.py:288
  7.8 13.1 %collective-permute-start = (bf16[16,128,128]{2,1,0:T(8,128)(2,1)S(1)}, bf16[16,128,128]{2,1,0:T(8,128)(2,1)S(1)}, u32[]{:S(2)}, u32[]{:S(2)}) collective-permute-start(bf16[16,128,128]{2,1,0:T(8,128)(2,1)S(1)} %convert_bitcast_fusion.refs_0_), channel_id=1, source_target_pairs={{0,8},{2,10},{8,16},{10,18},{16,24},{18,26},{24,28},{26,30},{28,20... | collective-permute-start | bytes 1572872 | tf_op jit(solution)/shard_map/ppermute | solution.py:288
  20.9 12.2 %collective-permute-start.3 = (bf16[16,128,128]{2,1,0:T(8,128)(2,1)S(1)}, bf16[16,128,128]{2,1,0:T(8,128)(2,1)S(1)}, u32[]{:S(2)}, u32[]{:S(2)}) collective-permute-start(bf16[16,128,128]{2,1,0:T(8,128)(2,1)S(1)} %collective-permute-done.refs_1_), channel_id=1, source_target_pairs={{0,8},{2,10},{8,16},{10,18},{16,24},{18,26},{24,28},{26,30},{28,20... | collective-permute-start | bytes 1572872 | tf_op jit(solution)/shard_map/ppermute | solution.py:288
  21.4 12.4 %collective-permute-start.4 = (bf16[16,128,128]{2,1,0:T(8,128)(2,1)S(1)}, bf16[16,128,128]{2,1,0:T(8,128)(2,1)S(1)}, u32[]{:S(2)}, u32[]{:S(2)}) collective-permute-start(bf16[16,128,128]{2,1,0:T(8,128)(2,1)S(1)} %collective-permute-done.1.refs_2_), channel_id=1, source_target_pairs={{0,4},{2,6},{8,0},{10,2},{16,8},{18,10},{24,16},{26,18},{28,24},{3... | collective-permute-start | bytes 1572872 | tf_op jit(solution)/shard_map/ppermute | solution.py:288
  24.2 40.2 %collective-permute-start.18 = (bf16[1792,512]{1,0:T(8,128)(2,1)}, bf16[1792,512]{1,0:T(8,128)(2,1)S(1)}, u32[]{:S(2)}, u32[]{:S(2)}) collective-permute-start(bf16[1792,512]{1,0:T(8,128)(2,1)} %pad_maximum_fusion), channel_id=1, source_target_pairs={{0,1},{1,0},{2,3},{3,2},{4,5},{5,4},{6,7},{7,6},{8,9},{9,8},{10,11... | collective-permute-start | bytes 5505032 | tf_op jit(solution)/shard_map/ppermute | solution.py:300
  24.8 10.3 %collective-permute-start.9 = (bf16[16,128,128]{2,1,0:T(8,128)(2,1)S(1)}, bf16[16,128,128]{2,1,0:T(8,128)(2,1)S(1)}, u32[]{:S(2)}, u32[]{:S(2)}) collective-permute-start(bf16[16,128,128]{2,1,0:T(8,128)(2,1)S(1)} %convert_bitcast_fusion.refs_0_), channel_id=1, source_target_pairs={{0,2},{2,0},{4,6},{6,4},{8,10},{10,8},{12,14},{14,12},{16,18},{18,... | collective-permute-start | bytes 1572872 | tf_op jit(solution)/shard_map/ppermute | solution.py:288
  33.0 11.3 %collective-permute-start.5 = (bf16[16,128,128]{2,1,0:T(8,128)(2,1)S(1)}, bf16[16,128,128]{2,1,0:T(8,128)(2,1)S(1)}, u32[]{:S(2)}, u32[]{:S(2)}) collective-permute-start(bf16[16,128,128]{2,1,0:T(8,128)(2,1)S(1)} %collective-permute-done.3.refs_3_), channel_id=1, source_target_pairs={{0,8},{2,10},{8,16},{10,18},{16,24},{18,26},{24,28},{26,30},{28,20... | collective-permute-start | bytes 1572872 | tf_op jit(solution)/shard_map/ppermute | solution.py:288
  33.8 11.2 %collective-permute-start.6 = (bf16[16,128,128]{2,1,0:T(8,128)(2,1)S(1)}, bf16[16,128,128]{2,1,0:T(8,128)(2,1)S(1)}, u32[]{:S(2)}, u32[]{:S(2)}) collective-permute-start(bf16[16,128,128]{2,1,0:T(8,128)(2,1)S(1)} %collective-permute-done.4.refs_4_), channel_id=1, source_target_pairs={{0,4},{2,6},{8,0},{10,2},{16,8},{18,10},{24,16},{26,18},{28,24},{3... | collective-permute-start | bytes 1572872 | tf_op jit(solution)/shard_map/ppermute | solution.py:288
  35.1 11.5 %collective-permute-start.10 = (bf16[16,128,128]{2,1,0:T(8,128)(2,1)S(1)}, bf16[16,128,128]{2,1,0:T(8,128)(2,1)S(1)}, u32[]{:S(2)}, u32[]{:S(2)}) collective-permute-start(bf16[16,128,128]{2,1,0:T(8,128)(2,1)S(1)} %collective-permute-done.refs_1_), channel_id=1, source_target_pairs={{0,2},{2,0},{4,6},{6,4},{8,10},{10,8},{12,14},{14,12},{16,18},{18,... | collective-permute-start | bytes 1572872 | tf_op jit(solution)/shard_map/ppermute | solution.py:288
  47.1 17.9 %collective-permute-start.14 = (bf16[16,128,128]{2,1,0:T(8,128)(2,1)S(1)}, bf16[16,128,128]{2,1,0:T(8,128)(2,1)}, u32[]{:S(2)}, u32[]{:S(2)}) collective-permute-start(bf16[16,128,128]{2,1,0:T(8,128)(2,1)S(1)} %collective-permute-done.5.refs_5_), channel_id=1, source_target_pairs={{0,2},{2,0},{4,6},{6,4},{8,10},{10,8},{12,14},{14,12},{16,18},{18,... | collective-permute-start | bytes 1572872 | tf_op jit(solution)/shard_map/ppermute | solution.py:288
  47.1 17.8 %collective-permute-start.15 = (bf16[16,128,128]{2,1,0:T(8,128)(2,1)S(1)}, bf16[16,128,128]{2,1,0:T(8,128)(2,1)}, u32[]{:S(2)}, u32[]{:S(2)}) collective-permute-start(bf16[16,128,128]{2,1,0:T(8,128)(2,1)S(1)} %collective-permute-done.6.refs_6_), channel_id=1, source_target_pairs={{0,2},{2,0},{4,6},{6,4},{8,10},{10,8},{12,14},{14,12},{16,18},{18,... | collective-permute-start | bytes 1572872 | tf_op jit(solution)/shard_map/ppermute | solution.py:288
  53.9 11.1 %collective-permute-start.16 = (bf16[8,128,128]{2,1,0:T(8,128)(2,1)}, bf16[8,128,128]{2,1,0:T(8,128)(2,1)}, u32[]{:S(2)}, u32[]{:S(2)}) collective-permute-start(bf16[8,128,128]{2,1,0:T(8,128)(2,1)} %collective-permute-done.7.refs_7_), channel_id=1, source_target_pairs={{0,2},{2,0},{4,6},{6,4},{8,10},{10,8},{12,14},{14,12},{16,18},{18,... | collective-permute-start | bytes 786440 | tf_op jit(solution)/shard_map/ppermute | solution.py:288
  64.4 33.3 %collective-permute-start.19 = (bf16[768,512]{1,0:T(8,128)(2,1)}, bf16[768,512]{1,0:T(8,128)(2,1)S(1)}, u32[]{:S(2)}, u32[]{:S(2)}) collective-permute-start(bf16[768,512]{1,0:T(8,128)(2,1)} %get-tuple-element.97), channel_id=1, source_target_pairs={{0,1},{1,0},{2,3},{3,2},{4,5},{5,4},{6,7},{7,6},{8,9},{9,8},{10,11... | collective-permute-start | bytes 2359304 | tf_op jit(solution)/shard_map/ppermute | solution.py:300
  116.2 14.7 %collective-permute-start.20 = (bf16[1,16,128,128]{3,2,1,0:T(8,128)(2,1)}, bf16[1,16,128,128]{3,2,1,0:T(8,128)(2,1)S(1)}, u32[]{:S(2)}, u32[]{:S(2)}) collective-permute-start(bf16[1,16,128,128]{3,2,1,0:T(8,128)(2,1)} %get-tuple-element.54), channel_id=1, source_target_pairs={{0,2},{2,0},{4,6},{6,4},{8,10},{10,8},{12,14},{14,12},{16,18},{18,... | collective-permute-start | bytes 1572872 | tf_op jit(solution)/shard_map/ppermute | solution.py:288
  130.2 17.3 %collective-permute-start.21 = (bf16[2,16,128,128]{3,2,1,0:T(8,128)(2,1)}, bf16[2,16,128,128]{3,2,1,0:T(8,128)(2,1)S(1)}, u32[]{:S(2)}, u32[]{:S(2)}) collective-permute-start(bf16[2,16,128,128]{3,2,1,0:T(8,128)(2,1)} %get-tuple-element.58), channel_id=1, source_target_pairs={{0,2},{2,0},{4,6},{6,4},{8,10},{10,8},{12,14},{14,12},{16,18},{18,... | collective-permute-start | bytes 3145736 | tf_op jit(solution)/shard_map/ppermute | solution.py:288
  131.1 16.6 %collective-permute-start.22 = (bf16[8,128,128]{2,1,0:T(8,128)(2,1)S(1)}, bf16[8,128,128]{2,1,0:T(8,128)(2,1)S(1)}, u32[]{:S(2)}, u32[]{:S(2)}) collective-permute-start(bf16[8,128,128]{2,1,0:T(8,128)(2,1)S(1)} %get-tuple-element.59), channel_id=1, source_target_pairs={{0,8},{2,10},{8,16},{10,18},{16,24},{18,26},{24,28},{26,30},{28,20... | collective-permute-start | bytes 786440 | tf_op jit(solution)/shard_map/ppermute | solution.py:288
  132.0 15.7 %collective-permute-start.23 = (bf16[8,128,128]{2,1,0:T(8,128)(2,1)S(1)}, bf16[8,128,128]{2,1,0:T(8,128)(2,1)S(1)}, u32[]{:S(2)}, u32[]{:S(2)}) collective-permute-start(bf16[8,128,128]{2,1,0:T(8,128)(2,1)S(1)} %get-tuple-element.60), channel_id=1, source_target_pairs={{0,4},{2,6},{8,0},{10,2},{16,8},{18,10},{24,16},{26,18},{28,24},{3... | collective-permute-start | bytes 786440 | tf_op jit(solution)/shard_map/ppermute | solution.py:288
  147.5 36.8 %collective-permute-start.25 = (bf16[2,16,128,128]{3,2,1,0:T(8,128)(2,1)}, bf16[2,16,128,128]{3,2,1,0:T(8,128)(2,1)S(1)}, u32[]{:S(2)}, u32[]{:S(2)}) collective-permute-start(bf16[2,16,128,128]{3,2,1,0:T(8,128)(2,1)} %get-tuple-element.67), channel_id=1, source_target_pairs={{0,2},{2,0},{4,6},{6,4},{8,10},{10,8},{12,14},{14,12},{16,18},{18,... | collective-permute-start | bytes 3145736 | tf_op jit(solution)/shard_map/ppermute | solution.py:288
  167.2 31.2 %collective-permute-start.24 = (bf16[3,16,128,128]{3,2,1,0:T(8,128)(2,1)}, bf16[3,16,128,128]{3,2,1,0:T(8,128)(2,1)S(1)}, u32[]{:S(2)}, u32[]{:S(2)}) collective-permute-start(bf16[3,16,128,128]{3,2,1,0:T(8,128)(2,1)} %get-tuple-element.65), channel_id=1, source_target_pairs={{0,2},{2,0},{4,6},{6,4},{8,10},{10,8},{12,14},{14,12},{16,18},{18,... | collective-permute-start | bytes 4718600 | tf_op jit(solution)/shard_map/ppermute | solution.py:288
  169.0 12.6 %collective-permute-start.27 = (bf16[8,128,128]{2,1,0:T(8,128)(2,1)S(1)}, bf16[8,128,128]{2,1,0:T(8,128)(2,1)S(1)}, u32[]{:S(2)}, u32[]{:S(2)}) collective-permute-start(bf16[8,128,128]{2,1,0:T(8,128)(2,1)S(1)} %get-tuple-element.69), channel_id=1, source_target_pairs={{0,8},{2,10},{8,16},{10,18},{16,24},{18,26},{24,28},{26,30},{28,20... | collective-permute-start | bytes 786440 | tf_op jit(solution)/shard_map/ppermute | solution.py:288
  170.9 10.7 %collective-permute-start.28 = (bf16[8,128,128]{2,1,0:T(8,128)(2,1)S(1)}, bf16[8,128,128]{2,1,0:T(8,128)(2,1)S(1)}, u32[]{:S(2)}, u32[]{:S(2)}) collective-permute-start(bf16[8,128,128]{2,1,0:T(8,128)(2,1)S(1)} %get-tuple-element.70), channel_id=1, source_target_pairs={{0,4},{2,6},{8,0},{10,2},{16,8},{18,10},{24,16},{26,18},{28,24},{3... | collective-permute-start | bytes 786440 | tf_op jit(solution)/shard_map/ppermute | solution.py:288
  186.1 10.7 %collective-permute-start.31 = (bf16[8,128,128]{2,1,0:T(8,128)(2,1)S(1)}, bf16[8,128,128]{2,1,0:T(8,128)(2,1)S(1)}, u32[]{:S(2)}, u32[]{:S(2)}) collective-permute-start(bf16[8,128,128]{2,1,0:T(8,128)(2,1)S(1)} %get-tuple-element.73), channel_id=1, source_target_pairs={{0,8},{2,10},{8,16},{10,18},{16,24},{18,26},{24,28},{26,30},{28,20... | collective-permute-start | bytes 786440 | tf_op jit(solution)/shard_map/ppermute | solution.py:288
  188.2 10.2 %collective-permute-start.33 = (bf16[8,128,128]{2,1,0:T(8,128)(2,1)S(1)}, bf16[8,128,128]{2,1,0:T(8,128)(2,1)S(1)}, u32[]{:S(2)}, u32[]{:S(2)}) collective-permute-start(bf16[8,128,128]{2,1,0:T(8,128)(2,1)S(1)} %get-tuple-element.75), channel_id=1, source_target_pairs={{0,4},{2,6},{8,0},{10,2},{16,8},{18,10},{24,16},{26,18},{28,24},{3... | collective-permute-start | bytes 786440 | tf_op jit(solution)/shard_map/ppermute | solution.py:288
  (35 other events, 495.6 us)

commit v5 on v4

--- a/solution.py
+++ b/solution.py
@@ -13,6 +13,7 @@
 F32 = jnp.float32
 ANY = pl.BlockSpec(memory_space=pl.ANY)
 HBM = pltpu.HBM
+VMEM = pltpu.VMEM
 GELU_S = 0.7978845608028654
 GELU_C = 0.044715
 
@@ -23,6 +24,10 @@
 
 def in_hbm(array):
     return pltpu.with_memory_space_constraint(array, HBM)
+
+
+def in_vmem(array):
+    return pltpu.with_memory_space_constraint(array, VMEM)
 
 
 def gelu_and_slope(v):
@@ -97,18 +102,20 @@
         load_weight(halves, False, owners, units, w2, sem)
         pltpu.make_async_copy(w2, w2, sem).wait()
 
-    row = pl.multiple_of(256 * step, 256)
-    for c in range(8):
-        w2_t[0, 128 * c : 128 * c + 128, :] = w2[(c + shift) & 7, pl.ds(row, 256), :].T
+    for j in range(2):
+        row = pl.multiple_of(512 * step + 256 * j, 256)
+        for c in range(8):
+            w2_t[j, 128 * c : 128 * c + 128, :] = w2[(c + shift) & 7, pl.ds(row, 256), :].T
     hid_block(dy_own, dy_other, w2_t, slope_ref, hid, dy)
 
 
 def hid_block(dy_own, dy_other, w2_t, slope_ref, hid, dy):
     half = w2_t.shape[1] // 2
     skip = dy_other.shape[0] - dy_own.shape[0]
-    g = jnp.dot(dy_own[...], w2_t[0, :half, :], preferred_element_type=F32)
-    g += jnp.dot(dy_other[skip:, :], w2_t[0, half:, :], preferred_element_type=F32)
-    hid[0] = (g * slope_ref[0]).astype(BF)
+    for j in range(2):
+        g = jnp.dot(dy_own[...], w2_t[j, :half, :], preferred_element_type=F32)
+        g += jnp.dot(dy_other[skip:, :], w2_t[j, half:, :], preferred_element_type=F32)
+        hid[j] = (g * slope_ref[j]).astype(BF)
     for s in range(4):
 
         @pl.when(pl.program_id(0) == s)
@@ -123,7 +130,7 @@
 
 def grad_kernel(info, flags, x_t, act_t, hid_ref, dy_ref, res_ref, *refs):
     new_res, mine, other = refs[-3:]
-    group, h, n = pl.program_id(0), pl.program_id(1), pl.program_id(2)
+    group, h = pl.program_id(0), pl.program_id(1)
     g = info[2 * group]
     shift, core = info[info.shape[0] - 2], info[info.shape[0] - 1]
     dot = functools.partial(jnp.dot, preferred_element_type=F32)
@@ -136,23 +143,23 @@
 
     @pl.when(g < 4)
     def _():
-        for c in range(2):
+        for c in range(4):
             grad = dot(x_t[...], hid_ref[c])
             for out, row in ((mine, core), (other, 1 - core)):
                 for j in range(2):
                     lanes = slice(128 * j, 128 * j + 128)
-                    slot = 8 * h + 4 * n + 2 * c + j
+                    slot = 8 * h + 2 * c + j
                     out[0, slot] = finish(jnp.where(row == 0, grad[:128, lanes], grad[128:, lanes]), 16 * row + slot)
 
     for out, here in ((mine, h == core), (other, h != core)):
 
         @pl.when((g >= 4) & here)
         def _(out=out):
-            for c in range(2):
+            for c in range(4):
                 grad = dot(act_t[...], dy_ref[c])
                 for i in range(2):
                     for j in range(2):
-                        slot = 8 * i + ((4 * n + 2 * c + j + shift) & 7)
+                        slot = 8 * i + ((2 * c + j + shift) & 7)
                         out[0, slot] = finish(grad[128 * i : 128 * i + 128, 128 * j : 128 * j + 128], 16 * h + slot)
 
 
@@ -172,8 +179,8 @@
             ],
             scratch_shapes=[pltpu.VMEM((16, 1024, 128), BF), pltpu.SemaphoreType.DMA],
         ),
-        out_shape=[HBM((2048, rows), BF), HBM((1024, rows), BF), HBM((8, rows, 256), F32)],
-        compiler_params=pltpu.CompilerParams(vmem_limit_bytes=30 * 2**20),
+        out_shape=[VMEM((2048, rows), BF), VMEM((1024, rows), BF), HBM((8, rows, 256), F32)],
+        compiler_params=pltpu.CompilerParams(vmem_limit_bytes=24 * 2**20),
         cost_estimate=pl.CostEstimate(flops=5 * rows * 1024 * 2048, bytes_accessed=26_000_000, transcendentals=rows * 2048),
         name="pre_act",
     )(owners, in_hbm(x_own), *[in_hbm(u) for u in units], *x_other)
@@ -182,23 +189,23 @@
 def run_hid_first(owners, halves, dy_own, dy_other, slope, units):
     total = slope.shape[1]
     rows = total // 2
-    part = lambda size: pl.BlockSpec((1, rows, 256), lambda i, *_: (jnp.minimum(i, size - 1), 0, 0))
+    part = lambda size: pl.BlockSpec((size, rows, 256), lambda i, *_: (i, 0, 0))
     return pl.pallas_call(
         functools.partial(hid_first_kernel, halves),
         grid_spec=pltpu.PrefetchScalarGridSpec(
             num_scalar_prefetch=1,
-            grid=(8,),
+            grid=(4,),
             in_specs=[
                 pl.BlockSpec((rows, 512), lambda i, *_: (0, 0)),
                 pl.BlockSpec(dy_other.shape, lambda i, *_: (0, 0)),
-                part(8),
+                part(2),
                 *[ANY] * len(units),
             ],
-            out_specs=[part(8), part(4), pl.BlockSpec((1, 1024, 256), lambda i, *_: (i, 0, 0))],
+            out_specs=[part(2), part(1), pl.BlockSpec((2, 1024, 256), lambda i, *_: (i, 0, 0))],
             scratch_shapes=[pltpu.VMEM((8, 2048, 128), BF), pltpu.SemaphoreType.DMA],
         ),
-        out_shape=[HBM((8, total, 256), BF), HBM((4, total, 256), BF), HBM((8, 1024, 256), BF)],
-        compiler_params=pltpu.CompilerParams(vmem_limit_bytes=24 * 2**20),
+        out_shape=[VMEM((8, total, 256), BF), VMEM((4, total, 256), BF), VMEM((8, 1024, 256), BF)],
+        compiler_params=pltpu.CompilerParams(vmem_limit_bytes=22 * 2**20),
         cost_estimate=pl.CostEstimate(flops=4 * rows * 1024 * 2048, bytes_accessed=18_000_000, transcendentals=0),
         name="hid_first",
     )(owners, in_hbm(dy_own), dy_other, in_hbm(slope), *[in_hbm(u) for u in units])
@@ -206,44 +213,44 @@
 
 def run_hid_second(dy_own, dy_other, slope, w2_t, hid, dy):
     rows = dy_other.shape[0]
-    part = lambda size: pl.BlockSpec((1, rows, 256), lambda i: (jnp.minimum(i, size - 1), 1, 0))
+    part = lambda size: pl.BlockSpec((size, rows, 256), lambda i: (i, 1, 0))
     return pl.pallas_call(
         hid_second_kernel,
-        grid=(8,),
+        grid=(4,),
         in_specs=[
             pl.BlockSpec((rows, 512), lambda i: (1, 0)),
             pl.BlockSpec((rows, 512), lambda i: (0, 0)),
-            part(8),
-            pl.BlockSpec((1, 1024, 256), lambda i: (i, 0, 0)),
+            part(2),
+            pl.BlockSpec((2, 1024, 256), lambda i: (i, 0, 0)),
             ANY,
             ANY,
         ],
-        out_specs=[part(8), part(4)],
-        out_shape=[HBM(hid.shape, BF), HBM(dy.shape, BF)],
+        out_specs=[part(2), part(1)],
+        out_shape=[VMEM(hid.shape, BF), VMEM(dy.shape, BF)],
         input_output_aliases={4: 0, 5: 1},
-        compiler_params=pltpu.CompilerParams(vmem_limit_bytes=20 * 2**20),
+        compiler_params=pltpu.CompilerParams(vmem_limit_bytes=18 * 2**20),
         cost_estimate=pl.CostEstimate(flops=3 * rows * 1024 * 2048, bytes_accessed=15_000_000, transcendentals=0),
         name="hid_second",
-    )(in_hbm(dy_own), dy_other, in_hbm(slope), in_hbm(w2_t), in_hbm(hid), in_hbm(dy))
-
-
-def run_grads(info, flags, x_t, act_t, hid, dy, residual, new_res, count):
+    )(in_hbm(dy_own), dy_other, in_hbm(slope), in_vmem(w2_t), in_vmem(hid), in_vmem(dy))
+
+
+def run_grads(info, flags, x_t, act_t, hid, dy, residual, new_res, count, pin):
     rows = hid.shape[1]
-    block = pl.BlockSpec((1, 32, 128, 128), lambda i, h, n, info, *_: (info[2 * i], 0, 0, 0))
-    local_block = pl.BlockSpec((1, 16, 128, 128), lambda i, h, n, *_: (i, 0, 0, 0))
+    block = pl.BlockSpec((1, 32, 128, 128), lambda i, h, info, *_: (info[2 * i], 0, 0, 0))
+    local_block = pl.BlockSpec((1, 16, 128, 128), lambda i, h, *_: (i, 0, 0, 0))
 
     def spec(shape, first, index):
-        def at(i, h, n, info, *_):
-            return tuple(jnp.where((info[2 * i] < 4) == first, t, 0) for t in index(info[2 * i + 1], h, n))
+        def at(i, h, info, *_):
+            return tuple(jnp.where((info[2 * i] < 4) == first, t, 0) for t in index(info[2 * i + 1], h))
 
         return pl.BlockSpec(shape, at)
 
-    operands = [info, flags, *[in_hbm(t) for t in (x_t, act_t, hid, dy, residual)]]
+    operands = [info, flags, *[pin(t) for t in (x_t, act_t, hid, dy)], in_hbm(residual)]
     specs = [
-        spec((256, rows), True, lambda a, h, n: (a, 0)),
-        spec((256, rows), False, lambda a, h, n: (a + h, 0)),
-        spec((2, rows, 256), True, lambda a, h, n: (2 * h + n, 0, 0)),
-        spec((2, rows, 256), False, lambda a, h, n: (n, 0, 0)),
+        spec((256, rows), True, lambda a, h: (a, 0)),
+        spec((256, rows), False, lambda a, h: (a + h, 0)),
+        spec((4, rows, 256), True, lambda a, h: (h, 0, 0)),
+        spec((4, rows, 256), False, lambda a, h: (0, 0, 0)),
         block,
     ]
     alias = {}
@@ -256,13 +263,13 @@
         grad_kernel,
         grid_spec=pltpu.PrefetchScalarGridSpec(
             num_scalar_prefetch=2,
-            grid=(count, 2, 2),
+            grid=(count, 2),
             in_specs=specs,
             out_specs=[block, local_block, local_block],
         ),
         out_shape=[HBM(residual.shape, BF), sent, sent],
         input_output_aliases=alias,
-        compiler_params=pltpu.CompilerParams(vmem_limit_bytes=24 * 2**20),
+        compiler_params=pltpu.CompilerParams(vmem_limit_bytes=28 * 2**20),
         cost_estimate=pl.CostEstimate(flops=3 * rows * 1024 * 512 * count, bytes_accessed=10_000_000 * count, transcendentals=0),
         name="grad_blocks",
     )(*operands)
@@ -338,10 +345,10 @@
 
     new_res, sums, up, down = None, {}, {}, {}
 
-    def add_up(distances):
+    def add_up(distances, pin):
         nonlocal new_res
         new_res, own_sum, other_sum = run_grads(
-            info_of(distances), flags, x_t, act_t, hid, dy, stored, new_res, len(distances)
+            info_of(distances), flags, x_t, act_t, hid, dy, stored, new_res, len(distances), pin
         )
         other_sum = hop(other_sum, CORES)
         for i, k in enumerate(distances):
@@ -358,12 +365,12 @@
         up.update({key: hop(t, UP) for key, t in ups.items()})
         down.update({key: hop(t, DOWN) for key, t in downs.items()})
 
-    add_up([4])
-    add_up([3, 5])
+    add_up([4], in_vmem)
+    add_up([3, 5], in_vmem)
     send(4)
-    add_up([2, 6])
+    add_up([2, 6], in_hbm)
     send(3)
-    add_up([1, 7, 0])
+    add_up([1, 7, 0], in_hbm)
     send(2)
     send(1)
     owned = jnp.concatenate([sums[0, h] + up[1, h].astype(F32) + down[1, h].astype(F32) for h in range(2)], axis=0)

time: 214 us -> 196 us (0.916)
  Pallas kernels: 98.8 us -> 77.5 us
  local copies, waits for them, and re-layouts: 2.66 us -> 7.61 us
    pallas_call x4, Pallas kernels: 55.7 us -> 42.5 us  [run_grads(): pl.pallas_call(grad_kernel, grid_spec=pltpu.PrefetchScalarGridSpec(num_sc...]
    pallas_call x1, Pallas kernels: 10.3 us -> 6.37 us  [run_hid_second(): pl.pallas_call(hid_second_kernel, grid=(4,), in_specs=[pl.BlockSpec((rows...]
    pallas_call x1, Pallas kernels: 13.6 us -> 9.85 us  [run_hid_first(): pl.pallas_call(functools.partial(hid_first_kernel, halves), grid_spec=plt...]
    unnamed x40 -> x50, local copies, waits for them, and re-layouts: 0.08 us -> 3.14 us
  transfers between devices with their start and end apart: 38 -> 38, of which waited for: 19 -> 19; matrix products, arithmetic and copies ran while one was open for 2% -> 4% of each run, Pallas kernels for 38% -> 33%
where the time goes in v5:
time: 196 us
  Pallas kernels  77.5 us (40%)
  waiting for transfers between devices  73.2 us (37%)
  starting transfers between devices  29 us (15%)
  local copies, waits for them, and re-layouts  7.61 us (4%)
  other arithmetic  7.38 us (4%)
    ppermute x35, waiting for transfers between devices, hop(): return lax.ppermute(array, 'dp', pairs)  58.7 us
    pallas_call x4, Pallas kernels, run_grads(): pl.pallas_call(grad_kernel, grid_spec=pltpu.PrefetchScalarGridSpec(num_sc...  42.5 us
    ppermute x35, starting transfers between devices, hop(): return lax.ppermute(array, 'dp', pairs)  24.9 us
    pallas_call x1, Pallas kernels, run_pre(): pl.pallas_call(functools.partial(pre_kernel, halves), grid_spec=pltpu.Pre...  18.8 us
    ppermute x3, waiting for transfers between devices, local_ring(): swap = lambda t: lax.ppermute(t, 'mp', PAIR)  14.4 us
    pallas_call x1, Pallas kernels, run_hid_first(): pl.pallas_call(functools.partial(hid_first_kernel, halves), grid_spec=plt...  9.85 us
    pallas_call x1, Pallas kernels, run_hid_second(): pl.pallas_call(hid_second_kernel, grid=(4,), in_specs=[pl.BlockSpec((rows...  6.37 us
    ppermute x3, starting transfers between devices, local_ring(): swap = lambda t: lax.ppermute(t, 'mp', PAIR)  4.1 us
  transfers between devices with their start and end apart: 38, of which 19 were waited for; matrix products, arithmetic and copies ran while one was open for 4% of the time, Pallas kernels for 33%

profile of v5, /device:TPU:0, one launch (start us, length us, event | category | flops | bytes accessed | tf_op | source)
XLA Modules:
  0.0 195.7 jit_solution(14325973317467879747)
XLA Ops:
  1.9 3.0 %collective-permute-start.2 = (bf16[512,512]{1,0:T(8,128)(2,1)S(1)}, bf16[512,512]{1,0:T(8,128)(2,1)S(1)}, u32[]{:S(2)}, u32[]{:S(2)}) collective-permute-start(bf16[512,512]{1,0:T(8,128)(2,1)S(1)} %slice.114), channel_id=1, source_target_pairs={{0,1},{1,0},{2,3},{3,2},{4,5},{5,4},{6,7},{7,6},{8,9},{9,8},{10,11... | collective-permute-start | bytes 1572872 | tf_op jit(solution)/shard_map/ppermute | solution.py:307
  9.3 7.5 %collective-permute-done.2.refs_18_ = bf16[512,512]{1,0:T(8,128)(2,1)S(1)} collective-permute-done((bf16[512,512]{1,0:T(8,128)(2,1)S(1)}, bf16[512,512]{1,0:T(8,128)(2,1)S(1)}, u32[]{:S(2)}, u32[]{:S(2)}) %collective-permute-start.2) | collective-permute-done | bytes 524320 | tf_op jit(solution)/shard_map/ppermute | solution.py:307
  16.8 2.8 %collective-permute-done.1.refs_2_ = bf16[16,128,128]{2,1,0:T(8,128)(2,1)S(1)} collective-permute-done((bf16[16,128,128]{2,1,0:T(8,128)(2,1)S(1)}, bf16[16,128,128]{2,1,0:T(8,128)(2,1)S(1)}, u32[]{:S(2)}, u32[]{:S(2)}) %collective-permute-start.1) | collective-permute-done | bytes 524320 | tf_op jit(solution)/shard_map/ppermute | solution.py:295
  24.8 8.3 %collective-permute-done.3.refs_3_ = bf16[16,128,128]{2,1,0:T(8,128)(2,1)S(1)} collective-permute-done((bf16[16,128,128]{2,1,0:T(8,128)(2,1)S(1)}, bf16[16,128,128]{2,1,0:T(8,128)(2,1)S(1)}, u32[]{:S(2)}, u32[]{:S(2)}) %collective-permute-start.3) | collective-permute-done | bytes 524320 | tf_op jit(solution)/shard_map/ppermute | solution.py:295
  35.7 8.7 %collective-permute-done.5.refs_5_ = bf16[16,128,128]{2,1,0:T(8,128)(2,1)} collective-permute-done((bf16[16,128,128]{2,1,0:T(8,128)(2,1)S(1)}, bf16[16,128,128]{2,1,0:T(8,128)(2,1)}, u32[]{:S(2)}, u32[]{:S(2)}) %collective-permute-start.5) | collective-permute-done | bytes 524320 | tf_op jit(solution)/shard_map/ppermute | solution.py:295
  49.9 5.8 %collective-permute-done.7.refs_7_ = bf16[8,128,128]{2,1,0:T(8,128)(2,1)S(1)} collective-permute-done((bf16[8,128,128]{2,1,0:T(8,128)(2,1)S(1)}, bf16[8,128,128]{2,1,0:T(8,128)(2,1)S(1)}, u32[]{:S(2)}, u32[]{:S(2)}) %collective-permute-start.7) | collective-permute-done | bytes 262176 | tf_op jit(solution)/shard_map/ppermute | solution.py:295
  57.5 6.9 %collective-permute-done.18.refs_19_.dy_other = bf16[1792,512]{1,0:T(8,128)(2,1)S(1)} collective-permute-done((bf16[1792,512]{1,0:T(8,128)(2,1)}, bf16[1792,512]{1,0:T(8,128)(2,1)S(1)}, u32[]{:S(2)}, u32[]{:S(2)}) %collective-permute-start.18) | collective-permute-done | bytes 1835040 | tf_op jit(solution)/shard_map/ppermute | solution.py:307
  65.0 18.8 %pre_act.1 = (bf16[2048,1536]{1,0:T(8,128)(2,1)S(1)}, bf16[1024,1536]{1,0:T(8,128)(2,1)S(1)}, f32[8,1536,256]{2,1,0:T(8,128)}) custom-call(s32[19]{0:T(128)S(1)} %stack.160.owners, bf16[1536,512]{1,0:T(8,128)(2,1)} %x_own.1, bf16[16,128,128]{2,1,0:T(8,128)(2,1)} %copy-done.8, bf16[16,128,128]{2,1,0:T(8,128)(2,1)} %copy-done.14, ...), custom_call_target="tpu_custom_call" | custom-call | flops 16106127360 | bytes 26000000 | tf_op jit(solution)/shard_map/pre_act/pallas_call | solution.py:169
  83.9 2.9 %copy-done.5 = bf16[1792,512]{1,0:T(8,128)(2,1)S(1)} copy-done((bf16[1792,512]{1,0:T(8,128)(2,1)S(1)}, bf16[1792,512]{1,0:T(8,128)(2,1)}, u32[]{:S(2)}) %copy-start.5) | copy-done | bytes 1835032
  86.8 9.8 %hid_first.1 = (bf16[8,1536,256]{2,1,0:T(8,128)(2,1)S(1)}, bf16[4,1536,256]{2,1,0:T(8,128)(2,1)S(1)}, bf16[8,1024,256]{2,1,0:T(8,128)(2,1)S(1)}) custom-call(s32[19]{0:T(128)S(1)} %stack.160.owners, bf16[1536,512]{1,0:T(8,128)(2,1)} %dy_own.3, bf16[1792,512]{1,0:T(8,128)(2,1)S(1)} %copy-done.5, f32[8,1536,256]{2,1,0:T(8,128)} %get-tuple-element.47.slope_ref, ...), custom_call_target="tpu_custom_call" | custom-call | flops 6442450944 | bytes 18000000 | tf_op jit(solution)/shard_map/hid_first/pallas_call | solution.py:193
  96.6 6.4 %hid_second.1 = (bf16[8,1536,256]{2,1,0:T(8,128)(2,1)S(1)}, bf16[4,1536,256]{2,1,0:T(8,128)(2,1)S(1)}) custom-call(bf16[1536,512]{1,0:T(8,128)(2,1)} %dy_own.3, bf16[768,512]{1,0:T(8,128)(2,1)S(1)} %collective-permute-done.19.dy_other, f32[8,1536,256]{2,1,0:T(8,128)} %get-tuple-element.47.slope_ref, ...), custom_call_target="tpu_custom_call", output_to_operand_aliasing={{0}: (4, {}), {1}: (5, {})} | custom-call | flops 4831838208 | bytes 15000000 | tf_op jit(solution)/shard_map/hid_second/pallas_call | solution.py:217
  103.0 6.0 %grad_blocks.4 = (bf16[8,32,128,128]{3,2,1,0:T(8,128)(2,1)}, bf16[1,16,128,128]{3,2,1,0:T(8,128)(2,1)}, bf16[1,16,128,128]{3,2,1,0:T(8,128)(2,1)}) custom-call(s32[4]{0:T(128)S(1)} %pad_add_fusion.info, s32[256]{0:T(256)S(1)} %convert_element_type.232.flags, bf16[1024,1536]{1,0:T(8,128)(2,1)S(1)} %get-tuple-element.45.x_t, ...), custom_call_target="tpu_custom_call" | custom-call | flops 2415919104 | bytes 10000000 | tf_op jit(solution)/shard_map/grad_blocks/pallas_call | solution.py:262
  109.1 7.8 %grad_blocks.5 = (bf16[8,32,128,128]{3,2,1,0:T(8,128)(2,1)}, bf16[2,16,128,128]{3,2,1,0:T(8,128)(2,1)}, bf16[2,16,128,128]{3,2,1,0:T(8,128)(2,1)}) custom-call(s32[6]{0:T(128)S(1)} %stack.165.info, s32[256]{0:T(256)S(1)} %convert_element_type.232.flags, bf16[1024,1536]{1,0:T(8,128)(2,1)S(1)} %get-tuple-element.45.x_t, ...), custom_call_target="tpu_custom_call", output_to_operand_aliasing={{0}: (7, {})} | custom-call | flops 4831838208 | bytes 20000000 | tf_op jit(solution)/shard_map/grad_blocks/pallas_call | solution.py:262
  120.9 12.0 %grad_blocks.6 = (bf16[8,32,128,128]{3,2,1,0:T(8,128)(2,1)}, bf16[2,16,128,128]{3,2,1,0:T(8,128)(2,1)}, bf16[2,16,128,128]{3,2,1,0:T(8,128)(2,1)}) custom-call(s32[6]{0:T(128)S(1)} %stack.170.info, s32[256]{0:T(256)S(1)} %convert_element_type.232.flags, bf16[1024,1536]{1,0:T(8,128)(2,1)} %copy-done.3, ...), custom_call_target="tpu_custom_call", output_to_operand_aliasing={{0}: (7, {})} | custom-call | flops 4831838208 | bytes 20000000 | tf_op jit(solution)/shard_map/grad_blocks/pallas_call | solution.py:262
  133.3 16.7 %grad_blocks.7 = (bf16[8,32,128,128]{3,2,1,0:T(8,128)(2,1)}, bf16[3,16,128,128]{3,2,1,0:T(8,128)(2,1)}, bf16[3,16,128,128]{3,2,1,0:T(8,128)(2,1)}) custom-call(s32[8]{0:T(128)S(1)} %stack.138.info, s32[256]{0:T(256)S(1)} %convert_element_type.232.flags, bf16[1024,1536]{1,0:T(8,128)(2,1)} %copy-done.3, ...), custom_call_target="tpu_custom_call", output_to_operand_aliasing={{0}: (7, {})} | custom-call | flops 7247757312 | bytes 30000000 | tf_op jit(solution)/shard_map/grad_blocks/pallas_call | solution.py:262
  152.6 7.1 %collective-permute-done.26 = bf16[8,128,128]{2,1,0:T(8,128)(2,1)S(1)} collective-permute-done((bf16[8,128,128]{2,1,0:T(8,128)(2,1)S(1)}, bf16[8,128,128]{2,1,0:T(8,128)(2,1)S(1)}, u32[]{:S(2)}, u32[]{:S(2)}) %collective-permute-start.26) | collective-permute-done | bytes 262176 | tf_op jit(solution)/shard_map/ppermute | solution.py:295
  159.7 2.1 %collective-permute-start.29 = (bf16[8,128,128]{2,1,0:T(8,128)(2,1)S(1)}, bf16[8,128,128]{2,1,0:T(8,128)(2,1)S(1)}, u32[]{:S(2)}, u32[]{:S(2)}) collective-permute-start(bf16[8,128,128]{2,1,0:T(8,128)(2,1)S(1)} %get-tuple-element.71), channel_id=1, source_target_pairs={{0,4},{2,6},{8,0},{10,2},{16,8},{18,10},{24,16},{26,18},{28,24},{3... | collective-permute-start | bytes 786440 | tf_op jit(solution)/shard_map/ppermute | solution.py:295
  161.8 3.0 %collective-permute-done.27 = bf16[8,128,128]{2,1,0:T(8,128)(2,1)S(1)} collective-permute-done((bf16[8,128,128]{2,1,0:T(8,128)(2,1)S(1)}, bf16[8,128,128]{2,1,0:T(8,128)(2,1)S(1)}, u32[]{:S(2)}, u32[]{:S(2)}) %collective-permute-start.27) | collective-permute-done | bytes 262176 | tf_op jit(solution)/shard_map/ppermute | solution.py:295
  164.8 2.1 %collective-permute-done.29 = bf16[8,128,128]{2,1,0:T(8,128)(2,1)S(1)} collective-permute-done((bf16[8,128,128]{2,1,0:T(8,128)(2,1)S(1)}, bf16[8,128,128]{2,1,0:T(8,128)(2,1)S(1)}, u32[]{:S(2)}, u32[]{:S(2)}) %collective-permute-start.29) | collective-permute-done | bytes 262176 | tf_op jit(solution)/shard_map/ppermute | solution.py:295
  169.6 2.0 %collective-permute-start.33 = (bf16[8,128,128]{2,1,0:T(8,128)(2,1)S(1)}, bf16[8,128,128]{2,1,0:T(8,128)(2,1)S(1)}, u32[]{:S(2)}, u32[]{:S(2)}) collective-permute-start(bf16[8,128,128]{2,1,0:T(8,128)(2,1)S(1)} %get-tuple-element.75), channel_id=1, source_target_pairs={{0,4},{2,6},{8,0},{10,2},{16,8},{18,10},{24,16},{26,18},{28,24},{3... | collective-permute-start | bytes 786440 | tf_op jit(solution)/shard_map/ppermute | solution.py:295
  171.5 5.0 %collective-permute-done.30 = bf16[8,128,128]{2,1,0:T(8,128)(2,1)S(1)} collective-permute-done((bf16[8,128,128]{2,1,0:T(8,128)(2,1)S(1)}, bf16[8,128,128]{2,1,0:T(8,128)(2,1)S(1)}, u32[]{:S(2)}, u32[]{:S(2)}) %collective-permute-start.30) | collective-permute-done | bytes 262176 | tf_op jit(solution)/shard_map/ppermute | solution.py:295
  176.6 2.8 %collective-permute-done.31 = bf16[8,128,128]{2,1,0:T(8,128)(2,1)S(1)} collective-permute-done((bf16[8,128,128]{2,1,0:T(8,128)(2,1)S(1)}, bf16[8,128,128]{2,1,0:T(8,128)(2,1)S(1)}, u32[]{:S(2)}, u32[]{:S(2)}) %collective-permute-start.31) | collective-permute-done | bytes 262176 | tf_op jit(solution)/shard_map/ppermute | solution.py:295
  185.8 4.4 %collective-permute-done.34 = bf16[8,128,128]{2,1,0:T(8,128)(2,1)S(1)} collective-permute-done((bf16[8,128,128]{2,1,0:T(8,128)(2,1)S(1)}, bf16[8,128,128]{2,1,0:T(8,128)(2,1)S(1)}, u32[]{:S(2)}, u32[]{:S(2)}) %collective-permute-start.34) | collective-permute-done | bytes 262176 | tf_op jit(solution)/shard_map/ppermute | solution.py:295
  191.0 2.0 %collective-permute-done.36 = bf16[8,128,128]{2,1,0:T(8,128)(2,1)S(1)} collective-permute-done((bf16[8,128,128]{2,1,0:T(8,128)(2,1)S(1)}, bf16[8,128,128]{2,1,0:T(8,128)(2,1)S(1)}, u32[]{:S(2)}, u32[]{:S(2)}) %collective-permute-start.36) | collective-permute-done | bytes 262176 | tf_op jit(solution)/shard_map/ppermute | solution.py:295
  (131 shorter events, 40.7 us)
Async XLA Ops:
  1.9 15.0 %collective-permute-start.2 = (bf16[512,512]{1,0:T(8,128)(2,1)S(1)}, bf16[512,512]{1,0:T(8,128)(2,1)S(1)}, u32[]{:S(2)}, u32[]{:S(2)}) collective-permute-start(bf16[512,512]{1,0:T(8,128)(2,1)S(1)} %slice.114), channel_id=1, source_target_pairs={{0,1},{1,0},{2,3},{3,2},{4,5},{5,4},{6,7},{7,6},{8,9},{9,8},{10,11... | collective-permute-start | bytes 1572872 | tf_op jit(solution)/shard_map/ppermute | solution.py:307
  6.2 13.4 %collective-permute-start.1 = (bf16[16,128,128]{2,1,0:T(8,128)(2,1)S(1)}, bf16[16,128,128]{2,1,0:T(8,128)(2,1)S(1)}, u32[]{:S(2)}, u32[]{:S(2)}) collective-permute-start(bf16[16,128,128]{2,1,0:T(8,128)(2,1)S(1)} %convert_bitcast_fusion.refs_0_), channel_id=1, source_target_pairs={{0,4},{2,6},{8,0},{10,2},{16,8},{18,10},{24,16},{26,18},{28,24},{3... | collective-permute-start | bytes 1572872 | tf_op jit(solution)/shard_map/ppermute | solution.py:295
  7.8 13.1 %collective-permute-start = (bf16[16,128,128]{2,1,0:T(8,128)(2,1)S(1)}, bf16[16,128,128]{2,1,0:T(8,128)(2,1)S(1)}, u32[]{:S(2)}, u32[]{:S(2)}) collective-permute-start(bf16[16,128,128]{2,1,0:T(8,128)(2,1)S(1)} %convert_bitcast_fusion.refs_0_), channel_id=1, source_target_pairs={{0,8},{2,10},{8,16},{10,18},{16,24},{18,26},{24,28},{26,30},{28,20... | collective-permute-start | bytes 1572872 | tf_op jit(solution)/shard_map/ppermute | solution.py:295
  20.9 12.2 %collective-permute-start.3 = (bf16[16,128,128]{2,1,0:T(8,128)(2,1)S(1)}, bf16[16,128,128]{2,1,0:T(8,128)(2,1)S(1)}, u32[]{:S(2)}, u32[]{:S(2)}) collective-permute-start(bf16[16,128,128]{2,1,0:T(8,128)(2,1)S(1)} %collective-permute-done.refs_1_), channel_id=1, source_target_pairs={{0,8},{2,10},{8,16},{10,18},{16,24},{18,26},{24,28},{26,30},{28,20... | collective-permute-start | bytes 1572872 | tf_op jit(solution)/shard_map/ppermute | solution.py:295
  21.4 12.4 %collective-permute-start.4 = (bf16[16,128,128]{2,1,0:T(8,128)(2,1)S(1)}, bf16[16,128,128]{2,1,0:T(8,128)(2,1)S(1)}, u32[]{:S(2)}, u32[]{:S(2)}) collective-permute-start(bf16[16,128,128]{2,1,0:T(8,128)(2,1)S(1)} %collective-permute-done.1.refs_2_), channel_id=1, source_target_pairs={{0,4},{2,6},{8,0},{10,2},{16,8},{18,10},{24,16},{26,18},{28,24},{3... | collective-permute-start | bytes 1572872 | tf_op jit(solution)/shard_map/ppermute | solution.py:295
  24.2 40.2 %collective-permute-start.18 = (bf16[1792,512]{1,0:T(8,128)(2,1)}, bf16[1792,512]{1,0:T(8,128)(2,1)S(1)}, u32[]{:S(2)}, u32[]{:S(2)}) collective-permute-start(bf16[1792,512]{1,0:T(8,128)(2,1)} %pad_maximum_fusion), channel_id=1, source_target_pairs={{0,1},{1,0},{2,3},{3,2},{4,5},{5,4},{6,7},{7,6},{8,9},{9,8},{10,11... | collective-permute-start | bytes 5505032 | tf_op jit(solution)/shard_map/ppermute | solution.py:307
  24.8 10.3 %collective-permute-start.9 = (bf16[16,128,128]{2,1,0:T(8,128)(2,1)S(1)}, bf16[16,128,128]{2,1,0:T(8,128)(2,1)S(1)}, u32[]{:S(2)}, u32[]{:S(2)}) collective-permute-start(bf16[16,128,128]{2,1,0:T(8,128)(2,1)S(1)} %convert_bitcast_fusion.refs_0_), channel_id=1, source_target_pairs={{0,2},{2,0},{4,6},{6,4},{8,10},{10,8},{12,14},{14,12},{16,18},{18,... | collective-permute-start | bytes 1572872 | tf_op jit(solution)/shard_map/ppermute | solution.py:295
  33.0 11.4 %collective-permute-start.5 = (bf16[16,128,128]{2,1,0:T(8,128)(2,1)S(1)}, bf16[16,128,128]{2,1,0:T(8,128)(2,1)}, u32[]{:S(2)}, u32[]{:S(2)}) collective-permute-start(bf16[16,128,128]{2,1,0:T(8,128)(2,1)S(1)} %collective-permute-done.3.refs_3_), channel_id=1, source_target_pairs={{0,8},{2,10},{8,16},{10,18},{16,24},{18,26},{24,28},{26,30},{28,20... | collective-permute-start | bytes 1572872 | tf_op jit(solution)/shard_map/ppermute | solution.py:295
  33.8 11.3 %collective-permute-start.6 = (bf16[16,128,128]{2,1,0:T(8,128)(2,1)S(1)}, bf16[16,128,128]{2,1,0:T(8,128)(2,1)}, u32[]{:S(2)}, u32[]{:S(2)}) collective-permute-start(bf16[16,128,128]{2,1,0:T(8,128)(2,1)S(1)} %collective-permute-done.4.refs_4_), channel_id=1, source_target_pairs={{0,4},{2,6},{8,0},{10,2},{16,8},{18,10},{24,16},{26,18},{28,24},{3... | collective-permute-start | bytes 1572872 | tf_op jit(solution)/shard_map/ppermute | solution.py:295
  35.1 11.9 %collective-permute-start.11 = (bf16[16,128,128]{2,1,0:T(8,128)(2,1)S(1)}, bf16[16,128,128]{2,1,0:T(8,128)(2,1)S(1)}, u32[]{:S(2)}, u32[]{:S(2)}) collective-permute-start(bf16[16,128,128]{2,1,0:T(8,128)(2,1)S(1)} %collective-permute-done.1.refs_2_), channel_id=1, source_target_pairs={{0,2},{2,0},{4,6},{6,4},{8,10},{10,8},{12,14},{14,12},{16,18},{18,... | collective-permute-start | bytes 1572872 | tf_op jit(solution)/shard_map/ppermute | solution.py:295
  35.1 13.5 %collective-permute-start.10 = (bf16[16,128,128]{2,1,0:T(8,128)(2,1)S(1)}, bf16[16,128,128]{2,1,0:T(8,128)(2,1)S(1)}, u32[]{:S(2)}, u32[]{:S(2)}) collective-permute-start(bf16[16,128,128]{2,1,0:T(8,128)(2,1)S(1)} %collective-permute-done.refs_1_), channel_id=1, source_target_pairs={{0,2},{2,0},{4,6},{6,4},{8,10},{10,8},{12,14},{14,12},{16,18},{18,... | collective-permute-start | bytes 1572872 | tf_op jit(solution)/shard_map/ppermute | solution.py:295
  49.1 15.8 %collective-permute-start.14 = (bf16[16,128,128]{2,1,0:T(8,128)(2,1)}, bf16[16,128,128]{2,1,0:T(8,128)(2,1)}, u32[]{:S(2)}, u32[]{:S(2)}) collective-permute-start(bf16[16,128,128]{2,1,0:T(8,128)(2,1)} %collective-permute-done.5.refs_5_), channel_id=1, source_target_pairs={{0,2},{2,0},{4,6},{6,4},{8,10},{10,8},{12,14},{14,12},{16,18},{18,... | collective-permute-start | bytes 1572872 | tf_op jit(solution)/shard_map/ppermute | solution.py:295
  49.3 15.7 %collective-permute-start.15 = (bf16[16,128,128]{2,1,0:T(8,128)(2,1)}, bf16[16,128,128]{2,1,0:T(8,128)(2,1)}, u32[]{:S(2)}, u32[]{:S(2)}) collective-permute-start(bf16[16,128,128]{2,1,0:T(8,128)(2,1)} %collective-permute-done.6.refs_6_), channel_id=1, source_target_pairs={{0,2},{2,0},{4,6},{6,4},{8,10},{10,8},{12,14},{14,12},{16,18},{18,... | collective-permute-start | bytes 1572872 | tf_op jit(solution)/shard_map/ppermute | solution.py:295
  64.4 32.2 %collective-permute-start.19 = (bf16[768,512]{1,0:T(8,128)(2,1)}, bf16[768,512]{1,0:T(8,128)(2,1)S(1)}, u32[]{:S(2)}, u32[]{:S(2)}) collective-permute-start(bf16[768,512]{1,0:T(8,128)(2,1)} %get-tuple-element.97), channel_id=1, source_target_pairs={{0,1},{1,0},{2,3},{3,2},{4,5},{5,4},{6,7},{7,6},{8,9},{9,8},{10,11... | collective-permute-start | bytes 2359304 | tf_op jit(solution)/shard_map/ppermute | solution.py:307
  116.8 16.1 %collective-permute-start.21 = (bf16[2,16,128,128]{3,2,1,0:T(8,128)(2,1)}, bf16[2,16,128,128]{3,2,1,0:T(8,128)(2,1)S(1)}, u32[]{:S(2)}, u32[]{:S(2)}) collective-permute-start(bf16[2,16,128,128]{3,2,1,0:T(8,128)(2,1)} %get-tuple-element.58), channel_id=1, source_target_pairs={{0,2},{2,0},{4,6},{6,4},{8,10},{10,8},{12,14},{14,12},{16,18},{18,... | collective-permute-start | bytes 3145736 | tf_op jit(solution)/shard_map/ppermute | solution.py:295
  118.8 14.2 %collective-permute-start.22 = (bf16[8,128,128]{2,1,0:T(8,128)(2,1)S(1)}, bf16[8,128,128]{2,1,0:T(8,128)(2,1)S(1)}, u32[]{:S(2)}, u32[]{:S(2)}) collective-permute-start(bf16[8,128,128]{2,1,0:T(8,128)(2,1)S(1)} %get-tuple-element.59), channel_id=1, source_target_pairs={{0,8},{2,10},{8,16},{10,18},{16,24},{18,26},{24,28},{26,30},{28,20... | collective-permute-start | bytes 786440 | tf_op jit(solution)/shard_map/ppermute | solution.py:295
  119.4 13.7 %collective-permute-start.23 = (bf16[8,128,128]{2,1,0:T(8,128)(2,1)S(1)}, bf16[8,128,128]{2,1,0:T(8,128)(2,1)S(1)}, u32[]{:S(2)}, u32[]{:S(2)}) collective-permute-start(bf16[8,128,128]{2,1,0:T(8,128)(2,1)S(1)} %get-tuple-element.60), channel_id=1, source_target_pairs={{0,4},{2,6},{8,0},{10,2},{16,8},{18,10},{24,16},{26,18},{28,24},{3... | collective-permute-start | bytes 786440 | tf_op jit(solution)/shard_map/ppermute | solution.py:295
  132.9 34.0 %collective-permute-start.25 = (bf16[2,16,128,128]{3,2,1,0:T(8,128)(2,1)}, bf16[2,16,128,128]{3,2,1,0:T(8,128)(2,1)S(1)}, u32[]{:S(2)}, u32[]{:S(2)}) collective-permute-start(bf16[2,16,128,128]{3,2,1,0:T(8,128)(2,1)} %get-tuple-element.67), channel_id=1, source_target_pairs={{0,2},{2,0},{4,6},{6,4},{8,10},{10,8},{12,14},{14,12},{16,18},{18,... | collective-permute-start | bytes 3145736 | tf_op jit(solution)/shard_map/ppermute | solution.py:295
  150.0 31.1 %collective-permute-start.24 = (bf16[3,16,128,128]{3,2,1,0:T(8,128)(2,1)}, bf16[3,16,128,128]{3,2,1,0:T(8,128)(2,1)S(1)}, u32[]{:S(2)}, u32[]{:S(2)}) collective-permute-start(bf16[3,16,128,128]{3,2,1,0:T(8,128)(2,1)} %get-tuple-element.65), channel_id=1, source_target_pairs={{0,2},{2,0},{4,6},{6,4},{8,10},{10,8},{12,14},{14,12},{16,18},{18,... | collective-permute-start | bytes 4718600 | tf_op jit(solution)/shard_map/ppermute | solution.py:295
  150.6 14.2 %collective-permute-start.27 = (bf16[8,128,128]{2,1,0:T(8,128)(2,1)S(1)}, bf16[8,128,128]{2,1,0:T(8,128)(2,1)S(1)}, u32[]{:S(2)}, u32[]{:S(2)}) collective-permute-start(bf16[8,128,128]{2,1,0:T(8,128)(2,1)S(1)} %get-tuple-element.69), channel_id=1, source_target_pairs={{0,8},{2,10},{8,16},{10,18},{16,24},{18,26},{24,28},{26,30},{28,20... | collective-permute-start | bytes 786440 | tf_op jit(solution)/shard_map/ppermute | solution.py:295
  151.2 13.6 %collective-permute-start.28 = (bf16[8,128,128]{2,1,0:T(8,128)(2,1)S(1)}, bf16[8,128,128]{2,1,0:T(8,128)(2,1)S(1)}, u32[]{:S(2)}, u32[]{:S(2)}) collective-permute-start(bf16[8,128,128]{2,1,0:T(8,128)(2,1)S(1)} %get-tuple-element.70), channel_id=1, source_target_pairs={{0,4},{2,6},{8,0},{10,2},{16,8},{18,10},{24,16},{26,18},{28,24},{3... | collective-permute-start | bytes 786440 | tf_op jit(solution)/shard_map/ppermute | solution.py:295
  167.5 11.9 %collective-permute-start.31 = (bf16[8,128,128]{2,1,0:T(8,128)(2,1)S(1)}, bf16[8,128,128]{2,1,0:T(8,128)(2,1)S(1)}, u32[]{:S(2)}, u32[]{:S(2)}) collective-permute-start(bf16[8,128,128]{2,1,0:T(8,128)(2,1)S(1)} %get-tuple-element.73), channel_id=1, source_target_pairs={{0,8},{2,10},{8,16},{10,18},{16,24},{18,26},{24,28},{26,30},{28,20... | collective-permute-start | bytes 786440 | tf_op jit(solution)/shard_map/ppermute | solution.py:295
  169.0 10.4 %collective-permute-start.32 = (bf16[8,128,128]{2,1,0:T(8,128)(2,1)S(1)}, bf16[8,128,128]{2,1,0:T(8,128)(2,1)S(1)}, u32[]{:S(2)}, u32[]{:S(2)}) collective-permute-start(bf16[8,128,128]{2,1,0:T(8,128)(2,1)S(1)} %get-tuple-element.74), channel_id=1, source_target_pairs={{0,4},{2,6},{8,0},{10,2},{16,8},{18,10},{24,16},{26,18},{28,24},{3... | collective-permute-start | bytes 786440 | tf_op jit(solution)/shard_map/ppermute | solution.py:295
  169.6 11.6 %collective-permute-start.33 = (bf16[8,128,128]{2,1,0:T(8,128)(2,1)S(1)}, bf16[8,128,128]{2,1,0:T(8,128)(2,1)S(1)}, u32[]{:S(2)}, u32[]{:S(2)}) collective-permute-start(bf16[8,128,128]{2,1,0:T(8,128)(2,1)S(1)} %get-tuple-element.75), channel_id=1, source_target_pairs={{0,4},{2,6},{8,0},{10,2},{16,8},{18,10},{24,16},{26,18},{28,24},{3... | collective-permute-start | bytes 786440 | tf_op jit(solution)/shard_map/ppermute | solution.py:295
  (40 other events, 519.5 us)

commit v6 on v5

--- a/solution.py
+++ b/solution.py
@@ -58,9 +58,9 @@
 
 
 def pre_kernel(halves, owners, x_own, *refs):
-    units, (*x_other, act_t, x_t, slope_ref, w1, sem) = refs[: len(halves)], refs[len(halves) :]
+    units, (x_first, x_second, left_t, slope_ref, w1, sem) = refs[: len(halves)], refs[len(halves) :]
     step = pl.program_id(0)
-    size = x_other[0].shape[0]
+    rows, size = x_own.shape[0], x_first.shape[0]
 
     @pl.when(step == 0)
     def _():
@@ -72,63 +72,83 @@
         def _(s=s):
             lanes = slice(256 * (s % 2), 256 * (s % 2) + 256)
             if s < 2:
-                x_t[...] = x_own[:, lanes].T
+                left_t[...] = x_own[:, lanes].T
             else:
-                x_t[:, :size] = x_other[0][:, lanes].T
-                x_t[:, size:] = x_other[1][: x_own.shape[0] - size, lanes].T
-
-    @pl.when(step == 0)
+                left_t[:, :size] = x_first[:, lanes].T
+                left_t[:, size:] = x_second[: rows - size, lanes].T
+
+    @pl.when(step == 4)
     def _():
         pltpu.make_async_copy(w1, w1, sem).wait()
 
-    w = jnp.concatenate([w1[2 * step], w1[2 * step + 1]], axis=1)
-    half = w.shape[0] // 2
-    for r in range(0, x_own.shape[0], 256):
-        i, o = (0, r) if r < size else (1, r - size)
-        pre = jnp.dot(x_own[r : r + 256, :], w[:half], preferred_element_type=F32)
-        pre += jnp.dot(x_other[i][o : o + 256, :], w[half:], preferred_element_type=F32)
-        act, slope = gelu_and_slope(pre)
-        act_t[:, r : r + 256] = act.astype(BF).T
-        slope_ref[0, r : r + 256, :] = slope
+    @pl.when(step >= 4)
+    def _():
+        c = 2 * (step - 4)
+        w = jnp.concatenate([w1[c], w1[c + 1]], axis=1)
+        block = size // 2
+
+        def product(r):
+            part, o = (x_first, r) if r < size else (x_second, r - size)
+            x = jnp.concatenate([x_own[r : r + block, :], part[o : o + block, :]], axis=1)
+            return jnp.dot(x, w, preferred_element_type=F32)
+
+        starts = list(range(0, rows, block))
+        ahead = product(starts[0])
+        for i, r in enumerate(starts):
+            pre = ahead
+            if i + 1 < len(starts):
+                ahead = product(starts[i + 1])
+            act, slope = gelu_and_slope(pre)
+            left_t[:, r : r + block] = act.astype(BF).T
+            slope_ref[0, r : r + block, :] = slope
 
 
 def hid_first_kernel(halves, owners, dy_own, dy_other, slope_ref, *refs):
-    units, (hid, dy, w2_t, w2, sem) = refs[: len(halves)], refs[len(halves) :]
+    units, (right, w2_t, w2, sem) = refs[: len(halves)], refs[len(halves) :]
     step = pl.program_id(0)
     shift = owners[len(halves)]
 
     @pl.when(step == 0)
     def _():
         load_weight(halves, False, owners, units, w2, sem)
+
+    @pl.when(step == 2)
+    def _():
         pltpu.make_async_copy(w2, w2, sem).wait()
 
-    for j in range(2):
-        row = pl.multiple_of(512 * step + 256 * j, 256)
-        for c in range(8):
-            w2_t[j, 128 * c : 128 * c + 128, :] = w2[(c + shift) & 7, pl.ds(row, 256), :].T
-    hid_block(dy_own, dy_other, w2_t, slope_ref, hid, dy)
-
-
-def hid_block(dy_own, dy_other, w2_t, slope_ref, hid, dy):
-    half = w2_t.shape[1] // 2
+    @pl.when(step >= 2)
+    def _():
+        for j in range(2):
+            row = pl.multiple_of(512 * (step - 2) + 256 * j, 256)
+            for c in range(8):
+                w2_t[j, 128 * c : 128 * c + 128, :] = w2[(c + shift) & 7, pl.ds(row, 256), :].T
+
+    hid_block(dy_own, dy_other, w2_t, slope_ref, right)
+
+
+def hid_block(dy_own, dy_other, w2_t, slope_ref, right):
+    step = pl.program_id(0)
     skip = dy_other.shape[0] - dy_own.shape[0]
-    for j in range(2):
-        g = jnp.dot(dy_own[...], w2_t[j, :half, :], preferred_element_type=F32)
-        g += jnp.dot(dy_other[skip:, :], w2_t[j, half:, :], preferred_element_type=F32)
-        hid[j] = (g * slope_ref[j]).astype(BF)
-    for s in range(4):
-
-        @pl.when(pl.program_id(0) == s)
-        def _(s=s):
-            lanes = slice(256 * (s % 2), 256 * (s % 2) + 256)
-            dy[0] = dy_own[:, lanes] if s < 2 else dy_other[skip:, lanes]
-
-
-def hid_second_kernel(dy_own, dy_other, slope_ref, w2_t, _, __, hid, dy):
-    hid_block(dy_own, dy_other, w2_t, slope_ref, hid, dy)
-
-
-def grad_kernel(info, flags, x_t, act_t, hid_ref, dy_ref, res_ref, *refs):
+
+    @pl.when(step < 2)
+    def _():
+        for j in range(2):
+            lanes = slice(256 * j, 256 * j + 256)
+            right[j] = jnp.where(step == 0, dy_own[:, lanes], dy_other[skip:, lanes])
+
+    @pl.when(step >= 2)
+    def _():
+        dy = jnp.concatenate([dy_own[...], dy_other[skip:, :]], axis=1)
+        for j in range(2):
+            g = jnp.dot(dy, w2_t[j], preferred_element_type=F32)
+            right[j] = (g * slope_ref[j]).astype(BF)
+
+
+def hid_second_kernel(dy_own, dy_other, slope_ref, w2_t, _, right):
+    hid_block(dy_own, dy_other, w2_t, slope_ref, right)
+
+
+def grad_kernel(info, flags, left_ref, right_ref, res_ref, *refs):
     new_res, mine, other = refs[-3:]
     group, h = pl.program_id(0), pl.program_id(1)
     g = info[2 * group]
@@ -144,7 +164,7 @@
     @pl.when(g < 4)
     def _():
         for c in range(4):
-            grad = dot(x_t[...], hid_ref[c])
+            grad = dot(left_ref[...], right_ref[c])
             for out, row in ((mine, core), (other, 1 - core)):
                 for j in range(2):
                     lanes = slice(128 * j, 128 * j + 128)
@@ -156,7 +176,7 @@
         @pl.when((g >= 4) & here)
         def _(out=out):
             for c in range(4):
-                grad = dot(act_t[...], dy_ref[c])
+                grad = dot(left_ref[...], right_ref[c])
                 for i in range(2):
                     for j in range(2):
                         slot = 8 * i + ((2 * c + j + shift) & 7)
@@ -170,16 +190,15 @@
         functools.partial(pre_kernel, halves),
         grid_spec=pltpu.PrefetchScalarGridSpec(
             num_scalar_prefetch=1,
-            grid=(8,),
+            grid=(12,),
             in_specs=[whole(x_own)] + [ANY] * len(units) + [whole(t) for t in x_other],
             out_specs=[
                 pl.BlockSpec((256, rows), lambda i, *_: (i, 0)),
-                pl.BlockSpec((256, rows), lambda i, *_: (jnp.minimum(i, 3), 0)),
-                pl.BlockSpec((1, rows, 256), lambda i, *_: (i, 0, 0)),
+                pl.BlockSpec((1, rows, 256), lambda i, *_: (jnp.maximum(i - 4, 0), 0, 0)),
             ],
             scratch_shapes=[pltpu.VMEM((16, 1024, 128), BF), pltpu.SemaphoreType.DMA],
         ),
-        out_shape=[VMEM((2048, rows), BF), VMEM((1024, rows), BF), HBM((8, rows, 256), F32)],
+        out_shape=[VMEM((3072, rows), BF), HBM((8, rows, 256), F32)],
         compiler_params=pltpu.CompilerParams(vmem_limit_bytes=24 * 2**20),
         cost_estimate=pl.CostEstimate(flops=5 * rows * 1024 * 2048, bytes_accessed=26_000_000, transcendentals=rows * 2048),
         name="pre_act",
@@ -189,68 +208,62 @@
 def run_hid_first(owners, halves, dy_own, dy_other, slope, units):
     total = slope.shape[1]
     rows = total // 2
-    part = lambda size: pl.BlockSpec((size, rows, 256), lambda i, *_: (i, 0, 0))
+    later = lambda i: jnp.maximum(i - 2, 0)
     return pl.pallas_call(
         functools.partial(hid_first_kernel, halves),
         grid_spec=pltpu.PrefetchScalarGridSpec(
             num_scalar_prefetch=1,
-            grid=(4,),
+            grid=(6,),
             in_specs=[
                 pl.BlockSpec((rows, 512), lambda i, *_: (0, 0)),
                 pl.BlockSpec(dy_other.shape, lambda i, *_: (0, 0)),
-                part(2),
+                pl.BlockSpec((2, rows, 256), lambda i, *_: (later(i), 0, 0)),
                 *[ANY] * len(units),
             ],
-            out_specs=[part(2), part(1), pl.BlockSpec((2, 1024, 256), lambda i, *_: (i, 0, 0))],
+            out_specs=[
+                pl.BlockSpec((2, rows, 256), lambda i, *_: (jnp.where(i < 2, i + 4, i - 2), 0, 0)),
+                pl.BlockSpec((2, 1024, 256), lambda i, *_: (later(i), 0, 0)),
+            ],
             scratch_shapes=[pltpu.VMEM((8, 2048, 128), BF), pltpu.SemaphoreType.DMA],
         ),
-        out_shape=[VMEM((8, total, 256), BF), VMEM((4, total, 256), BF), VMEM((8, 1024, 256), BF)],
+        out_shape=[VMEM((12, total, 256), BF), VMEM((8, 1024, 256), BF)],
         compiler_params=pltpu.CompilerParams(vmem_limit_bytes=22 * 2**20),
         cost_estimate=pl.CostEstimate(flops=4 * rows * 1024 * 2048, bytes_accessed=18_000_000, transcendentals=0),
         name="hid_first",
-    )(owners, in_hbm(dy_own), dy_other, in_hbm(slope), *[in_hbm(u) for u in units])
-
-
-def run_hid_second(dy_own, dy_other, slope, w2_t, hid, dy):
+    )(owners, in_hbm(dy_own), in_hbm(dy_other), in_hbm(slope), *[in_hbm(u) for u in units])
+
+
+def run_hid_second(dy_own, dy_other, slope, w2_t, right):
     rows = dy_other.shape[0]
-    part = lambda size: pl.BlockSpec((size, rows, 256), lambda i: (i, 1, 0))
+    later = lambda i: jnp.maximum(i - 2, 0)
     return pl.pallas_call(
         hid_second_kernel,
-        grid=(4,),
+        grid=(6,),
         in_specs=[
             pl.BlockSpec((rows, 512), lambda i: (1, 0)),
             pl.BlockSpec((rows, 512), lambda i: (0, 0)),
-            part(2),
-            pl.BlockSpec((2, 1024, 256), lambda i: (i, 0, 0)),
-            ANY,
+            pl.BlockSpec((2, rows, 256), lambda i: (later(i), 1, 0)),
+            pl.BlockSpec((2, 1024, 256), lambda i: (later(i), 0, 0)),
             ANY,
         ],
-        out_specs=[part(2), part(1)],
-        out_shape=[VMEM(hid.shape, BF), VMEM(dy.shape, BF)],
-        input_output_aliases={4: 0, 5: 1},
+        out_specs=pl.BlockSpec((2, rows, 256), lambda i: (jnp.where(i < 2, i + 4, i - 2), 1, 0)),
+        out_shape=VMEM(right.shape, BF),
+        input_output_aliases={4: 0},
         compiler_params=pltpu.CompilerParams(vmem_limit_bytes=18 * 2**20),
         cost_estimate=pl.CostEstimate(flops=3 * rows * 1024 * 2048, bytes_accessed=15_000_000, transcendentals=0),
         name="hid_second",
-    )(in_hbm(dy_own), dy_other, in_hbm(slope), in_vmem(w2_t), in_vmem(hid), in_vmem(dy))
-
-
-def run_grads(info, flags, x_t, act_t, hid, dy, residual, new_res, count, pin):
-    rows = hid.shape[1]
+    )(in_hbm(dy_own), dy_other, in_hbm(slope), in_vmem(w2_t), in_vmem(right))
+
+
+def run_grads(info, flags, left_t, right, residual, new_res, count, pin):
+    rows = right.shape[1]
     block = pl.BlockSpec((1, 32, 128, 128), lambda i, h, info, *_: (info[2 * i], 0, 0, 0))
     local_block = pl.BlockSpec((1, 16, 128, 128), lambda i, h, *_: (i, 0, 0, 0))
-
-    def spec(shape, first, index):
-        def at(i, h, info, *_):
-            return tuple(jnp.where((info[2 * i] < 4) == first, t, 0) for t in index(info[2 * i + 1], h))
-
-        return pl.BlockSpec(shape, at)
-
-    operands = [info, flags, *[pin(t) for t in (x_t, act_t, hid, dy)], in_hbm(residual)]
+    pick = lambda i, info, first, second: jnp.where(info[2 * i] < 4, first, second)
+    operands = [info, flags, pin(left_t), pin(right), in_hbm(residual)]
     specs = [
-        spec((256, rows), True, lambda a, h: (a, 0)),
-        spec((256, rows), False, lambda a, h: (a + h, 0)),
-        spec((4, rows, 256), True, lambda a, h: (h, 0, 0)),
-        spec((4, rows, 256), False, lambda a, h: (0, 0, 0)),
+        pl.BlockSpec((256, rows), lambda i, h, info, *_: (pick(i, info, info[2 * i + 1], info[2 * i + 1] + h + 4), 0)),
+        pl.BlockSpec((4, rows, 256), lambda i, h, info, *_: (pick(i, info, h, 2), 0, 0)),
         block,
     ]
     alias = {}
@@ -269,8 +282,8 @@
         ),
         out_shape=[HBM(residual.shape, BF), sent, sent],
         input_output_aliases=alias,
-        compiler_params=pltpu.CompilerParams(vmem_limit_bytes=28 * 2**20),
-        cost_estimate=pl.CostEstimate(flops=3 * rows * 1024 * 512 * count, bytes_accessed=10_000_000 * count, transcendentals=0),
+        compiler_params=pltpu.CompilerParams(vmem_limit_bytes=20 * 2**20),
+        cost_estimate=pl.CostEstimate(flops=4 * rows * 1024 * 512 * count, bytes_accessed=10_000_000 * count, transcendentals=0),
         name="grad_blocks",
     )(*operands)
 
@@ -303,9 +316,9 @@
     place = jnp.where((chip & 1) == 0, chip >> 1, 7 - (chip >> 1))
     rows = tokens.shape[0]
 
-    third, half = rows // 3, rows // 2
+    half = rows // 2
     swap = lambda t: lax.ppermute(t, "mp", PAIR)
-    x_other = [swap(tokens[:third]), swap(jnp.concatenate([tokens[third:], out_grad[:half]], axis=0))]
+    x_other = [swap(tokens[:half]), swap(jnp.concatenate([tokens[half:], out_grad[:half]], axis=0))]
     dy_late = swap(out_grad[half:])
 
     shift = 4 * shard
@@ -329,9 +342,9 @@
     flags = jnp.any(jnp.arange(block_count, dtype=jnp.int32)[None, :] == kept_blocks[0, 0][:, None], axis=0)
     flags = flags.astype(jnp.int32)
 
-    act_t, x_t, slope = run_pre(owners, halves, tokens, x_other, units)
-    hid, dy, w2_t = run_hid_first(owners, halves, out_grad, x_other[1], slope, units)
-    hid, dy = run_hid_second(out_grad, dy_late, slope, w2_t, hid, dy)
+    left_t, slope = run_pre(owners, halves, tokens, x_other, units)
+    right, w2_t = run_hid_first(owners, halves, out_grad, x_other[1], slope, units)
+    right = run_hid_second(out_grad, dy_late, slope, w2_t, right)
 
     stored = residual.reshape(8, 32, 128, 128)
 
@@ -348,7 +361,7 @@
     def add_up(distances, pin):
         nonlocal new_res
         new_res, own_sum, other_sum = run_grads(
-            info_of(distances), flags, x_t, act_t, hid, dy, stored, new_res, len(distances), pin
+            info_of(distances), flags, left_t, right, stored, new_res, len(distances), pin
         )
         other_sum = hop(other_sum, CORES)
         for i, k in enumerate(distances):
@@ -368,10 +381,13 @@
     add_up([4], in_vmem)
     add_up([3, 5], in_vmem)
     send(4)
-    add_up([2, 6], in_hbm)
+    add_up([2], in_hbm)
+    add_up([6], in_hbm)
     send(3)
-    add_up([1, 7, 0], in_hbm)
+    add_up([1], in_hbm)
+    add_up([7], in_hbm)
     send(2)
+    add_up([0], in_hbm)
     send(1)
     owned = jnp.concatenate([sums[0, h] + up[1, h].astype(F32) + down[1, h].astype(F32) for h in range(2)], axis=0)
     new_momentum = momentum_decay * momentum + owned[None]

time: 196 us -> 200 us (1.020)
  Pallas kernels: 77.5 us -> 85.4 us
  other arithmetic: 7.38 us -> 3.93 us
  starting transfers between devices: 29 us -> 31.9 us
  local copies, waits for them, and re-layouts: 7.61 us -> 5.22 us
    ppermute x3, waiting for transfers between devices: 14.4 us -> 8.71 us  [local_ring(): swap = lambda t: lax.ppermute(t, 'mp', PAIR)]
    pallas_call x4 -> x7, Pallas kernels: 42.5 us -> 46.6 us  [run_grads(): pl.pallas_call(grad_kernel, grid_spec=pltpu.PrefetchScalarGridSpec(num_sc...]
    ppermute x35 -> x38, waiting for transfers between devices: 58.7 us -> 62.7 us  [hop(): return lax.ppermute(array, 'dp', pairs)]
    pallas_call x1, Pallas kernels: 9.85 us -> 13.3 us  [run_hid_first(): pl.pallas_call(functools.partial(hid_first_kernel, halves), grid_spec=plt...]
    unnamed x50 -> x46, local copies, waits for them, and re-layouts: 3.14 us -> 0.09 us
    ppermute x3, starting transfers between devices: 4.1 us -> 6.24 us  [local_ring(): swap = lambda t: lax.ppermute(t, 'mp', PAIR)]
    slice x1, local copies, waits for them, and re-layouts: 0.98 us -> 3.02 us  [local_ring(): dy_late = swap(out_grad[half:])]
    ppermute x35 -> x38, starting transfers between devices: 24.9 us -> 25.6 us  [hop(): return lax.ppermute(array, 'dp', pairs)]
  transfers between devices with their start and end apart: 38 -> 41, of which waited for: 19 -> 16; matrix products, arithmetic and copies ran while one was open for 4% -> 2% of each run, Pallas kernels for 33% -> 36%
where the time goes in v6:
time: 200 us; the launch traced here: 199 us
  Pallas kernels  85.4 us (43%)
  waiting for transfers between devices  71.4 us (36%)
  starting transfers between devices  31.9 us (16%)
  local copies, waits for them, and re-layouts  5.22 us (3%)
  other arithmetic  3.93 us (2%)
    ppermute x38, waiting for transfers between devices, hop(): return lax.ppermute(array, 'dp', pairs)  62.7 us
    pallas_call x7, Pallas kernels, run_grads(): pl.pallas_call(grad_kernel, grid_spec=pltpu.PrefetchScalarGridSpec(num_sc...  46.6 us
    ppermute x38, starting transfers between devices, hop(): return lax.ppermute(array, 'dp', pairs)  25.6 us
    pallas_call x1, Pallas kernels, run_pre(): pl.pallas_call(functools.partial(pre_kernel, halves), grid_spec=pltpu.Pre...  18.6 us
    pallas_call x1, Pallas kernels, run_hid_first(): pl.pallas_call(functools.partial(hid_first_kernel, halves), grid_spec=plt...  13.3 us
    ppermute x3, waiting for transfers between devices, local_ring(): swap = lambda t: lax.ppermute(t, 'mp', PAIR)  8.71 us
    pallas_call x1, Pallas kernels, run_hid_second(): pl.pallas_call(hid_second_kernel, grid=(6,), in_specs=[pl.BlockSpec((rows...  6.97 us
    ppermute x3, starting transfers between devices, local_ring(): swap = lambda t: lax.ppermute(t, 'mp', PAIR)  6.24 us
  transfers between devices with their start and end apart: 41, of which 16 were waited for; matrix products, arithmetic and copies ran while one was open for 2% of the time, Pallas kernels for 36%

profile of v6, /device:TPU:0, one launch (start us, length us, event | category | flops | bytes accessed | tf_op | source)
XLA Modules:
  0.0 199.2 jit_solution(5527549466701741626)
XLA Ops:
  0.6 3.0 %fusion.19 = (bf16[768,512]{1,0:T(8,128)(2,1)}, bf16[768,512]{1,0:T(8,128)(2,1)S(1)}, bf16[768,512]{1,0:T(8,128)(2,1)S(1)}, bf16[768,512]{1,0:T(8,128)(2,1)S(1)}) fusion(bf16[1536,512]{1,0:T(8,128)(2,1)} %dy_own.3, bf16[1536,512]{1,0:T(8,128)(2,1)} %x_own.1), kind=kLoop, calls=%fused_computation.45 | loop fusion | bytes 6291456 | tf_op jit(solution)/shard_map/slice | solution.py:322
  3.7 3.0 %collective-permute-start.2 = (bf16[768,512]{1,0:T(8,128)(2,1)S(1)}, bf16[768,512]{1,0:T(8,128)(2,1)S(1)}, u32[]{:S(2)}, u32[]{:S(2)}) collective-permute-start(bf16[768,512]{1,0:T(8,128)(2,1)S(1)} %get-tuple-element.121), channel_id=1, source_target_pairs={{0,1},{1,0},{2,3},{3,2},{4,5},{5,4},{6,7},{7,6},{8,9},{9,8},{10,11... | collective-permute-start | bytes 2359304 | tf_op jit(solution)/shard_map/ppermute | solution.py:320
  8.8 11.4 %collective-permute-done.refs_1_ = bf16[16,128,128]{2,1,0:T(8,128)(2,1)S(1)} collective-permute-done((bf16[16,128,128]{2,1,0:T(8,128)(2,1)S(1)}, bf16[16,128,128]{2,1,0:T(8,128)(2,1)S(1)}, u32[]{:S(2)}, u32[]{:S(2)}) %collective-permute-start) | collective-permute-done | bytes 524320 | tf_op jit(solution)/shard_map/ppermute | solution.py:308
  21.5 2.7 %collective-permute-done.2.refs_18_ = bf16[768,512]{1,0:T(8,128)(2,1)S(1)} collective-permute-done((bf16[768,512]{1,0:T(8,128)(2,1)S(1)}, bf16[768,512]{1,0:T(8,128)(2,1)S(1)}, u32[]{:S(2)}, u32[]{:S(2)}) %collective-permute-start.2) | collective-permute-done | bytes 786464 | tf_op jit(solution)/shard_map/ppermute | solution.py:320
  24.2 1.8 collective-permute-start.3
  28.1 9.2 %collective-permute-done.3.refs_3_ = bf16[16,128,128]{2,1,0:T(8,128)(2,1)S(1)} collective-permute-done((bf16[16,128,128]{2,1,0:T(8,128)(2,1)S(1)}, bf16[16,128,128]{2,1,0:T(8,128)(2,1)S(1)}, u32[]{:S(2)}, u32[]{:S(2)}) %collective-permute-start.3) | collective-permute-done | bytes 524320 | tf_op jit(solution)/shard_map/ppermute | solution.py:308
  39.8 9.9 %collective-permute-done.5.refs_5_ = bf16[16,128,128]{2,1,0:T(8,128)(2,1)} collective-permute-done((bf16[16,128,128]{2,1,0:T(8,128)(2,1)S(1)}, bf16[16,128,128]{2,1,0:T(8,128)(2,1)}, u32[]{:S(2)}, u32[]{:S(2)}) %collective-permute-start.5) | collective-permute-done | bytes 524320 | tf_op jit(solution)/shard_map/ppermute | solution.py:308
  55.4 6.0 %collective-permute-done.18.refs_19_.dy_other = bf16[1536,512]{1,0:T(8,128)(2,1)S(1)} collective-permute-done((bf16[1536,512]{1,0:T(8,128)(2,1)S(1)}, bf16[1536,512]{1,0:T(8,128)(2,1)S(1)}, u32[]{:S(2)}, u32[]{:S(2)}) %collective-permute-start.18) | collective-permute-done | bytes 1572896 | tf_op jit(solution)/shard_map/ppermute | solution.py:320
  65.3 18.6 %pre_act.1 = (bf16[3072,1536]{1,0:T(8,128)(2,1)S(1)}, f32[8,1536,256]{2,1,0:T(8,128)}) custom-call(s32[19]{0:T(128)S(1)} %stack.171.owners, bf16[1536,512]{1,0:T(8,128)(2,1)} %x_own.1, bf16[16,128,128]{2,1,0:T(8,128)(2,1)} %copy-done.4, bf16[16,128,128]{2,1,0:T(8,128)(2,1)} %copy-done.13, bf16[16,128,128]{2,1,0:T(8,128)(2,1)} %copy-done.14, ...), custom_call_target="tpu_custom_call" | custom-call | flops 16106127360 | bytes 26000000 | tf_op jit(solution)/shard_map/pre_act/pallas_call | solution.py:189
  83.9 13.3 %hid_first.1 = (bf16[12,1536,256]{2,1,0:T(8,128)(2,1)S(1)}, bf16[8,1024,256]{2,1,0:T(8,128)(2,1)S(1)}) custom-call(s32[19]{0:T(128)S(1)} %stack.171.owners, bf16[1536,512]{1,0:T(8,128)(2,1)} %dy_own.3, bf16[1536,512]{1,0:T(8,128)(2,1)} %copy-done.2, f32[8,1536,256]{2,1,0:T(8,128)} %get-tuple-element.52.slope_ref, bf16[16,128,128]{2,1,0:T(8,128)(2,1)} %copy-done.4, ...), custom_call_target="tpu_custom_call" | custom-call | flops 6442450944 | bytes 18000000 | tf_op jit(solution)/shard_map/hid_first/pallas_call | solution.py:212
  97.2 7.0 %hid_second.1.right_ref = bf16[12,1536,256]{2,1,0:T(8,128)(2,1)S(1)} custom-call(bf16[1536,512]{1,0:T(8,128)(2,1)} %dy_own.3, bf16[768,512]{1,0:T(8,128)(2,1)S(1)} %collective-permute-done.19.dy_other, f32[8,1536,256]{2,1,0:T(8,128)} %get-tuple-element.52.slope_ref, ...), custom_call_target="tpu_custom_call", output_to_operand_aliasing={{}: (4, {})} | custom-call | flops 4831838208 | bytes 15000000 | tf_op jit(solution)/shard_map/hid_second/pallas_call | solution.py:239
  104.2 6.0 %grad_blocks.7 = (bf16[8,32,128,128]{3,2,1,0:T(8,128)(2,1)}, bf16[1,16,128,128]{3,2,1,0:T(8,128)(2,1)}, bf16[1,16,128,128]{3,2,1,0:T(8,128)(2,1)}) custom-call(s32[4]{0:T(128)S(1)} %get-tuple-element.116.info, s32[256]{0:T(256)S(1)} %convert_element_type.232.flags, bf16[3072,1536]{1,0:T(8,128)(2,1)S(1)} %get-tuple-element.51.left_ref, ...), custom_call_target="tpu_custom_call" | custom-call | flops 3221225472 | bytes 10000000 | tf_op jit(solution)/shard_map/grad_blocks/pallas_call | solution.py:275
  110.2 7.8 %grad_blocks.8 = (bf16[8,32,128,128]{3,2,1,0:T(8,128)(2,1)}, bf16[2,16,128,128]{3,2,1,0:T(8,128)(2,1)}, bf16[2,16,128,128]{3,2,1,0:T(8,128)(2,1)}) custom-call(s32[6]{0:T(128)S(1)} %stack.176.info, s32[256]{0:T(256)S(1)} %convert_element_type.232.flags, bf16[3072,1536]{1,0:T(8,128)(2,1)S(1)} %get-tuple-element.51.left_ref, ...), custom_call_target="tpu_custom_call", output_to_operand_aliasing={{0}: (5, {})} | custom-call | flops 6442450944 | bytes 20000000 | tf_op jit(solution)/shard_map/grad_blocks/pallas_call | solution.py:275
  120.8 6.4 %grad_blocks.9 = (bf16[8,32,128,128]{3,2,1,0:T(8,128)(2,1)}, bf16[1,16,128,128]{3,2,1,0:T(8,128)(2,1)}, bf16[1,16,128,128]{3,2,1,0:T(8,128)(2,1)}) custom-call(s32[4]{0:T(128)S(1)} %get-tuple-element.117.info, s32[256]{0:T(256)S(1)} %convert_element_type.232.flags, bf16[3072,1536]{1,0:T(8,128)(2,1)} %copy-done.1, ...), custom_call_target="tpu_custom_call", output_to_operand_aliasing={{0}: (5, {})} | custom-call | flops 3221225472 | bytes 10000000 | tf_op jit(solution)/shard_map/grad_blocks/pallas_call | solution.py:275
  127.3 6.6 %grad_blocks.10 = (bf16[8,32,128,128]{3,2,1,0:T(8,128)(2,1)}, bf16[1,16,128,128]{3,2,1,0:T(8,128)(2,1)}, bf16[1,16,128,128]{3,2,1,0:T(8,128)(2,1)}) custom-call(s32[4]{0:T(128)S(1)} %get-tuple-element.118.info, s32[256]{0:T(256)S(1)} %convert_element_type.232.flags, bf16[3072,1536]{1,0:T(8,128)(2,1)} %copy-done.1, ...), custom_call_target="tpu_custom_call", output_to_operand_aliasing={{0}: (5, {})} | custom-call | flops 3221225472 | bytes 10000000 | tf_op jit(solution)/shard_map/grad_blocks/pallas_call | solution.py:275
  138.1 6.6 %grad_blocks.11 = (bf16[8,32,128,128]{3,2,1,0:T(8,128)(2,1)}, bf16[1,16,128,128]{3,2,1,0:T(8,128)(2,1)}, bf16[1,16,128,128]{3,2,1,0:T(8,128)(2,1)}) custom-call(s32[4]{0:T(128)S(1)} %get-tuple-element.120.info, s32[256]{0:T(256)S(1)} %convert_element_type.232.flags, bf16[3072,1536]{1,0:T(8,128)(2,1)} %copy-done.1, ...), custom_call_target="tpu_custom_call", output_to_operand_aliasing={{0}: (5, {})} | custom-call | flops 3221225472 | bytes 10000000 | tf_op jit(solution)/shard_map/grad_blocks/pallas_call | solution.py:275
  144.7 6.6 %grad_blocks.12 = (bf16[8,32,128,128]{3,2,1,0:T(8,128)(2,1)}, bf16[1,16,128,128]{3,2,1,0:T(8,128)(2,1)}, bf16[1,16,128,128]{3,2,1,0:T(8,128)(2,1)}) custom-call(s32[4]{0:T(128)S(1)} %get-tuple-element.119.info, s32[256]{0:T(256)S(1)} %convert_element_type.232.flags, bf16[3072,1536]{1,0:T(8,128)(2,1)} %copy-done.1, ...), custom_call_target="tpu_custom_call", output_to_operand_aliasing={{0}: (5, {})} | custom-call | flops 3221225472 | bytes 10000000 | tf_op jit(solution)/shard_map/grad_blocks/pallas_call | solution.py:275
  152.8 6.0 %collective-permute-done.26 = bf16[8,128,128]{2,1,0:T(8,128)(2,1)S(1)} collective-permute-done((bf16[8,128,128]{2,1,0:T(8,128)(2,1)S(1)}, bf16[8,128,128]{2,1,0:T(8,128)(2,1)S(1)}, u32[]{:S(2)}, u32[]{:S(2)}) %collective-permute-start.26) | collective-permute-done | bytes 262176 | tf_op jit(solution)/shard_map/ppermute | solution.py:308
  159.0 1.8 collective-permute-start.35
  162.3 6.6 %grad_blocks.13 = (bf16[8,32,128,128]{3,2,1,0:T(8,128)(2,1)}, bf16[1,16,128,128]{3,2,1,0:T(8,128)(2,1)}, bf16[1,16,128,128]{3,2,1,0:T(8,128)(2,1)}) custom-call(s32[4]{0:T(128)S(1)} %get-tuple-element.115.info, s32[256]{0:T(256)S(1)} %convert_element_type.232.flags, bf16[3072,1536]{1,0:T(8,128)(2,1)} %copy-done.1, ...), custom_call_target="tpu_custom_call", output_to_operand_aliasing={{0}: (5, {})} | custom-call | flops 3221225472 | bytes 10000000 | tf_op jit(solution)/shard_map/grad_blocks/pallas_call | solution.py:275
  171.4 6.7 %collective-permute-done.32 = bf16[8,128,128]{2,1,0:T(8,128)(2,1)S(1)} collective-permute-done((bf16[8,128,128]{2,1,0:T(8,128)(2,1)S(1)}, bf16[8,128,128]{2,1,0:T(8,128)(2,1)S(1)}, u32[]{:S(2)}, u32[]{:S(2)}) %collective-permute-start.32) | collective-permute-done | bytes 262176 | tf_op jit(solution)/shard_map/ppermute | solution.py:308
  178.1 5.2 %collective-permute-done.33 = bf16[8,128,128]{2,1,0:T(8,128)(2,1)S(1)} collective-permute-done((bf16[8,128,128]{2,1,0:T(8,128)(2,1)S(1)}, bf16[8,128,128]{2,1,0:T(8,128)(2,1)S(1)}, u32[]{:S(2)}, u32[]{:S(2)}) %collective-permute-start.33) | collective-permute-done | bytes 262176 | tf_op jit(solution)/shard_map/ppermute | solution.py:308
  187.6 5.2 %collective-permute-done.37 = bf16[8,128,128]{2,1,0:T(8,128)(2,1)S(1)} collective-permute-done((bf16[8,128,128]{2,1,0:T(8,128)(2,1)S(1)}, bf16[8,128,128]{2,1,0:T(8,128)(2,1)S(1)}, u32[]{:S(2)}, u32[]{:S(2)}) %collective-permute-start.37) | collective-permute-done | bytes 262176 | tf_op jit(solution)/shard_map/ppermute | solution.py:308
  193.2 3.8 %collective-permute-done.39 = bf16[8,128,128]{2,1,0:T(8,128)(2,1)S(1)} collective-permute-done((bf16[8,128,128]{2,1,0:T(8,128)(2,1)S(1)}, bf16[8,128,128]{2,1,0:T(8,128)(2,1)S(1)}, u32[]{:S(2)}, u32[]{:S(2)}) %collective-permute-start.39) | collective-permute-done | bytes 262176 | tf_op jit(solution)/shard_map/ppermute | solution.py:308
  (135 shorter events, 37.0 us)
Async XLA Ops:
  3.7 20.5 %collective-permute-start.2 = (bf16[768,512]{1,0:T(8,128)(2,1)S(1)}, bf16[768,512]{1,0:T(8,128)(2,1)S(1)}, u32[]{:S(2)}, u32[]{:S(2)}) collective-permute-start(bf16[768,512]{1,0:T(8,128)(2,1)S(1)} %get-tuple-element.121), channel_id=1, source_target_pairs={{0,1},{1,0},{2,3},{3,2},{4,5},{5,4},{6,7},{7,6},{8,9},{9,8},{10,11... | collective-permute-start | bytes 2359304 | tf_op jit(solution)/shard_map/ppermute | solution.py:320
  6.7 13.4 %collective-permute-start = (bf16[16,128,128]{2,1,0:T(8,128)(2,1)S(1)}, bf16[16,128,128]{2,1,0:T(8,128)(2,1)S(1)}, u32[]{:S(2)}, u32[]{:S(2)}) collective-permute-start(bf16[16,128,128]{2,1,0:T(8,128)(2,1)S(1)} %convert_bitcast_fusion.refs_0_), channel_id=1, source_target_pairs={{0,8},{2,10},{8,16},{10,18},{16,24},{18,26},{24,28},{26,30},{28,20... | collective-permute-start | bytes 1572872 | tf_op jit(solution)/shard_map/ppermute | solution.py:308
  8.4 13.1 %collective-permute-start.1 = (bf16[16,128,128]{2,1,0:T(8,128)(2,1)S(1)}, bf16[16,128,128]{2,1,0:T(8,128)(2,1)S(1)}, u32[]{:S(2)}, u32[]{:S(2)}) collective-permute-start(bf16[16,128,128]{2,1,0:T(8,128)(2,1)S(1)} %convert_bitcast_fusion.refs_0_), channel_id=1, source_target_pairs={{0,4},{2,6},{8,0},{10,2},{16,8},{18,10},{24,16},{26,18},{28,24},{3... | collective-permute-start | bytes 1572872 | tf_op jit(solution)/shard_map/ppermute | solution.py:308
  24.2 13.1 %collective-permute-start.3 = (bf16[16,128,128]{2,1,0:T(8,128)(2,1)S(1)}, bf16[16,128,128]{2,1,0:T(8,128)(2,1)S(1)}, u32[]{:S(2)}, u32[]{:S(2)}) collective-permute-start(bf16[16,128,128]{2,1,0:T(8,128)(2,1)S(1)} %collective-permute-done.refs_1_), channel_id=1, source_target_pairs={{0,8},{2,10},{8,16},{10,18},{16,24},{18,26},{24,28},{26,30},{28,20... | collective-permute-start | bytes 1572872 | tf_op jit(solution)/shard_map/ppermute | solution.py:308
  26.1 12.7 %collective-permute-start.4 = (bf16[16,128,128]{2,1,0:T(8,128)(2,1)S(1)}, bf16[16,128,128]{2,1,0:T(8,128)(2,1)}, u32[]{:S(2)}, u32[]{:S(2)}) collective-permute-start(bf16[16,128,128]{2,1,0:T(8,128)(2,1)S(1)} %collective-permute-done.1.refs_2_), channel_id=1, source_target_pairs={{0,4},{2,6},{8,0},{10,2},{16,8},{18,10},{24,16},{26,18},{28,24},{3... | collective-permute-start | bytes 1572872 | tf_op jit(solution)/shard_map/ppermute | solution.py:308
  26.3 35.0 %collective-permute-start.18 = (bf16[1536,512]{1,0:T(8,128)(2,1)S(1)}, bf16[1536,512]{1,0:T(8,128)(2,1)S(1)}, u32[]{:S(2)}, u32[]{:S(2)}) collective-permute-start(bf16[1536,512]{1,0:T(8,128)(2,1)S(1)} %pad_maximum_fusion), channel_id=1, source_target_pairs={{0,1},{1,0},{2,3},{3,2},{4,5},{5,4},{6,7},{7,6},{8,9},{9,8},{10,11... | collective-permute-start | bytes 4718600 | tf_op jit(solution)/shard_map/ppermute | solution.py:320
  37.3 12.4 %collective-permute-start.5 = (bf16[16,128,128]{2,1,0:T(8,128)(2,1)S(1)}, bf16[16,128,128]{2,1,0:T(8,128)(2,1)}, u32[]{:S(2)}, u32[]{:S(2)}) collective-permute-start(bf16[16,128,128]{2,1,0:T(8,128)(2,1)S(1)} %collective-permute-done.3.refs_3_), channel_id=1, source_target_pairs={{0,8},{2,10},{8,16},{10,18},{16,24},{18,26},{24,28},{26,30},{28,20... | collective-permute-start | bytes 1572872 | tf_op jit(solution)/shard_map/ppermute | solution.py:308
  38.8 12.0 %collective-permute-start.6 = (bf16[16,128,128]{2,1,0:T(8,128)(2,1)}, bf16[16,128,128]{2,1,0:T(8,128)(2,1)}, u32[]{:S(2)}, u32[]{:S(2)}) collective-permute-start(bf16[16,128,128]{2,1,0:T(8,128)(2,1)} %collective-permute-done.4.refs_4_), channel_id=1, source_target_pairs={{0,4},{2,6},{8,0},{10,2},{16,8},{18,10},{24,16},{26,18},{28,24},{3... | collective-permute-start | bytes 1572872 | tf_op jit(solution)/shard_map/ppermute | solution.py:308
  39.3 13.4 %collective-permute-start.9 = (bf16[16,128,128]{2,1,0:T(8,128)(2,1)S(1)}, bf16[16,128,128]{2,1,0:T(8,128)(2,1)S(1)}, u32[]{:S(2)}, u32[]{:S(2)}) collective-permute-start(bf16[16,128,128]{2,1,0:T(8,128)(2,1)S(1)} %convert_bitcast_fusion.refs_0_), channel_id=1, source_target_pairs={{0,2},{2,0},{4,6},{6,4},{8,10},{10,8},{12,14},{14,12},{16,18},{18,... | collective-permute-start | bytes 1572872 | tf_op jit(solution)/shard_map/ppermute | solution.py:308
  39.3 14.0 %collective-permute-start.10 = (bf16[16,128,128]{2,1,0:T(8,128)(2,1)S(1)}, bf16[16,128,128]{2,1,0:T(8,128)(2,1)S(1)}, u32[]{:S(2)}, u32[]{:S(2)}) collective-permute-start(bf16[16,128,128]{2,1,0:T(8,128)(2,1)S(1)} %collective-permute-done.refs_1_), channel_id=1, source_target_pairs={{0,2},{2,0},{4,6},{6,4},{8,10},{10,8},{12,14},{14,12},{16,18},{18,... | collective-permute-start | bytes 1572872 | tf_op jit(solution)/shard_map/ppermute | solution.py:308
  63.8 33.4 %collective-permute-start.19 = (bf16[768,512]{1,0:T(8,128)(2,1)}, bf16[768,512]{1,0:T(8,128)(2,1)S(1)}, u32[]{:S(2)}, u32[]{:S(2)}) collective-permute-start(bf16[768,512]{1,0:T(8,128)(2,1)} %get-tuple-element.99), channel_id=1, source_target_pairs={{0,1},{1,0},{2,3},{3,2},{4,5},{5,4},{6,7},{7,6},{8,9},{9,8},{10,11... | collective-permute-start | bytes 2359304 | tf_op jit(solution)/shard_map/ppermute | solution.py:320
  118.0 16.5 %collective-permute-start.21 = (bf16[2,16,128,128]{3,2,1,0:T(8,128)(2,1)}, bf16[2,16,128,128]{3,2,1,0:T(8,128)(2,1)S(1)}, u32[]{:S(2)}, u32[]{:S(2)}) collective-permute-start(bf16[2,16,128,128]{3,2,1,0:T(8,128)(2,1)} %get-tuple-element.60), channel_id=1, source_target_pairs={{0,2},{2,0},{4,6},{6,4},{8,10},{10,8},{12,14},{14,12},{16,18},{18,... | collective-permute-start | bytes 3145736 | tf_op jit(solution)/shard_map/ppermute | solution.py:308
  118.8 15.8 %collective-permute-start.22 = (bf16[8,128,128]{2,1,0:T(8,128)(2,1)S(1)}, bf16[8,128,128]{2,1,0:T(8,128)(2,1)S(1)}, u32[]{:S(2)}, u32[]{:S(2)}) collective-permute-start(bf16[8,128,128]{2,1,0:T(8,128)(2,1)S(1)} %get-tuple-element.61), channel_id=1, source_target_pairs={{0,8},{2,10},{8,16},{10,18},{16,24},{18,26},{24,28},{26,30},{28,20... | collective-permute-start | bytes 786440 | tf_op jit(solution)/shard_map/ppermute | solution.py:308
  120.4 14.2 %collective-permute-start.23 = (bf16[8,128,128]{2,1,0:T(8,128)(2,1)S(1)}, bf16[8,128,128]{2,1,0:T(8,128)(2,1)S(1)}, u32[]{:S(2)}, u32[]{:S(2)}) collective-permute-start(bf16[8,128,128]{2,1,0:T(8,128)(2,1)S(1)} %get-tuple-element.62), channel_id=1, source_target_pairs={{0,4},{2,6},{8,0},{10,2},{16,8},{18,10},{24,16},{26,18},{28,24},{3... | collective-permute-start | bytes 786440 | tf_op jit(solution)/shard_map/ppermute | solution.py:308
  133.9 17.4 %collective-permute-start.27 = (bf16[1,16,128,128]{3,2,1,0:T(8,128)(2,1)}, bf16[1,16,128,128]{3,2,1,0:T(8,128)(2,1)S(1)}, u32[]{:S(2)}, u32[]{:S(2)}) collective-permute-start(bf16[1,16,128,128]{3,2,1,0:T(8,128)(2,1)} %get-tuple-element.71), channel_id=1, source_target_pairs={{0,2},{2,0},{4,6},{6,4},{8,10},{10,8},{12,14},{14,12},{16,18},{18,... | collective-permute-start | bytes 1572872 | tf_op jit(solution)/shard_map/ppermute | solution.py:308
  133.9 18.8 %collective-permute-start.24 = (bf16[1,16,128,128]{3,2,1,0:T(8,128)(2,1)S(1)}, bf16[1,16,128,128]{3,2,1,0:T(8,128)(2,1)S(1)}, u32[]{:S(2)}, u32[]{:S(2)}) collective-permute-start(bf16[1,16,128,128]{3,2,1,0:T(8,128)(2,1)S(1)} %copy-done.21), channel_id=1, source_target_pairs={{0,2},{2,0},{4,6},{6,4},{8,10},{10,8},{12,14},{14,12},{16,18},{18,... | collective-permute-start | bytes 1572872 | tf_op jit(solution)/shard_map/ppermute | solution.py:308
  134.8 17.1 %collective-permute-start.28 = (bf16[8,128,128]{2,1,0:T(8,128)(2,1)S(1)}, bf16[8,128,128]{2,1,0:T(8,128)(2,1)S(1)}, u32[]{:S(2)}, u32[]{:S(2)}) collective-permute-start(bf16[8,128,128]{2,1,0:T(8,128)(2,1)S(1)} %get-tuple-element.72), channel_id=1, source_target_pairs={{0,4},{2,6},{8,0},{10,2},{16,8},{18,10},{24,16},{26,18},{28,24},{3... | collective-permute-start | bytes 786440 | tf_op jit(solution)/shard_map/ppermute | solution.py:308
  136.1 15.9 %collective-permute-start.29 = (bf16[8,128,128]{2,1,0:T(8,128)(2,1)S(1)}, bf16[8,128,128]{2,1,0:T(8,128)(2,1)S(1)}, u32[]{:S(2)}, u32[]{:S(2)}) collective-permute-start(bf16[8,128,128]{2,1,0:T(8,128)(2,1)S(1)} %get-tuple-element.73), channel_id=1, source_target_pairs={{0,4},{2,6},{8,0},{10,2},{16,8},{18,10},{24,16},{26,18},{28,24},{3... | collective-permute-start | bytes 786440 | tf_op jit(solution)/shard_map/ppermute | solution.py:308
  137.8 15.0 %collective-permute-start.25 = (bf16[8,128,128]{2,1,0:T(8,128)(2,1)S(1)}, bf16[8,128,128]{2,1,0:T(8,128)(2,1)S(1)}, u32[]{:S(2)}, u32[]{:S(2)}) collective-permute-start(bf16[8,128,128]{2,1,0:T(8,128)(2,1)S(1)} %get-tuple-element.67), channel_id=1, source_target_pairs={{0,8},{2,10},{8,16},{10,18},{16,24},{18,26},{24,28},{26,30},{28,20... | collective-permute-start | bytes 786440 | tf_op jit(solution)/shard_map/ppermute | solution.py:308
  152.0 16.9 %collective-permute-start.34 = (bf16[1,16,128,128]{3,2,1,0:T(8,128)(2,1)}, bf16[1,16,128,128]{3,2,1,0:T(8,128)(2,1)S(1)}, u32[]{:S(2)}, u32[]{:S(2)}) collective-permute-start(bf16[1,16,128,128]{3,2,1,0:T(8,128)(2,1)} %get-tuple-element.85), channel_id=1, source_target_pairs={{0,2},{2,0},{4,6},{6,4},{8,10},{10,8},{12,14},{14,12},{16,18},{18,... | collective-permute-start | bytes 1572872 | tf_op jit(solution)/shard_map/ppermute | solution.py:308
  152.0 19.4 %collective-permute-start.31 = (bf16[1,16,128,128]{3,2,1,0:T(8,128)(2,1)S(1)}, bf16[1,16,128,128]{3,2,1,0:T(8,128)(2,1)S(1)}, u32[]{:S(2)}, u32[]{:S(2)}) collective-permute-start(bf16[1,16,128,128]{3,2,1,0:T(8,128)(2,1)S(1)} %copy-done.20), channel_id=1, source_target_pairs={{0,2},{2,0},{4,6},{6,4},{8,10},{10,8},{12,14},{14,12},{16,18},{18,... | collective-permute-start | bytes 1572872 | tf_op jit(solution)/shard_map/ppermute | solution.py:308
  168.9 18.7 %collective-permute-start.30 = (bf16[1,16,128,128]{3,2,1,0:T(8,128)(2,1)}, bf16[1,16,128,128]{3,2,1,0:T(8,128)(2,1)S(1)}, u32[]{:S(2)}, u32[]{:S(2)}) collective-permute-start(bf16[1,16,128,128]{3,2,1,0:T(8,128)(2,1)} %get-tuple-element.79), channel_id=1, source_target_pairs={{0,2},{2,0},{4,6},{6,4},{8,10},{10,8},{12,14},{14,12},{16,18},{18,... | collective-permute-start | bytes 1572872 | tf_op jit(solution)/shard_map/ppermute | solution.py:308
  169.4 13.8 %collective-permute-start.33 = (bf16[8,128,128]{2,1,0:T(8,128)(2,1)S(1)}, bf16[8,128,128]{2,1,0:T(8,128)(2,1)S(1)}, u32[]{:S(2)}, u32[]{:S(2)}) collective-permute-start(bf16[8,128,128]{2,1,0:T(8,128)(2,1)S(1)} %get-tuple-element.83), channel_id=1, source_target_pairs={{0,8},{2,10},{8,16},{10,18},{16,24},{18,26},{24,28},{26,30},{28,20... | collective-permute-start | bytes 786440 | tf_op jit(solution)/shard_map/ppermute | solution.py:308
  185.6 11.5 %collective-permute-start.39 = (bf16[8,128,128]{2,1,0:T(8,128)(2,1)S(1)}, bf16[8,128,128]{2,1,0:T(8,128)(2,1)S(1)}, u32[]{:S(2)}, u32[]{:S(2)}) collective-permute-start(bf16[8,128,128]{2,1,0:T(8,128)(2,1)S(1)} %get-tuple-element.90), channel_id=1, source_target_pairs={{0,8},{2,10},{8,16},{10,18},{16,24},{18,26},{24,28},{26,30},{28,20... | collective-permute-start | bytes 786440 | tf_op jit(solution)/shard_map/ppermute | solution.py:308
  (40 other events, 579.6 us)

commit v7 on v6

--- a/solution.py
+++ b/solution.py
@@ -89,8 +89,8 @@
 
         def product(r):
             part, o = (x_first, r) if r < size else (x_second, r - size)
-            x = jnp.concatenate([x_own[r : r + block, :], part[o : o + block, :]], axis=1)
-            return jnp.dot(x, w, preferred_element_type=F32)
+            pre = jnp.dot(x_own[r : r + block, :], w[: w.shape[0] // 2], preferred_element_type=F32)
+            return pre + jnp.dot(part[o : o + block, :], w[w.shape[0] // 2 :], preferred_element_type=F32)
 
         starts = list(range(0, rows, block))
         ahead = product(starts[0])
@@ -138,9 +138,10 @@
 
     @pl.when(step >= 2)
     def _():
-        dy = jnp.concatenate([dy_own[...], dy_other[skip:, :]], axis=1)
+        half = w2_t.shape[1] // 2
         for j in range(2):
-            g = jnp.dot(dy, w2_t[j], preferred_element_type=F32)
+            g = jnp.dot(dy_own[...], w2_t[j, :half, :], preferred_element_type=F32)
+            g += jnp.dot(dy_other[skip:, :], w2_t[j, half:, :], preferred_element_type=F32)
             right[j] = (g * slope_ref[j]).astype(BF)
 
 
@@ -152,6 +153,8 @@
     new_res, mine, other = refs[-3:]
     group, h = pl.program_id(0), pl.program_id(1)
     g = info[2 * group]
+    row = pl.multiple_of(256 * (info[2 * group + 1] + jnp.where(g < 4, 0, h + 4)), 256)
+    left = left_ref.at[pl.ds(row, 256)]
     shift, core = info[info.shape[0] - 2], info[info.shape[0] - 1]
     dot = functools.partial(jnp.dot, preferred_element_type=F32)
 
@@ -164,7 +167,7 @@
     @pl.when(g < 4)
     def _():
         for c in range(4):
-            grad = dot(left_ref[...], right_ref[c])
+            grad = dot(left[...], right_ref[4 * h + c])
             for out, row in ((mine, core), (other, 1 - core)):
                 for j in range(2):
                     lanes = slice(128 * j, 128 * j + 128)
@@ -176,7 +179,7 @@
         @pl.when((g >= 4) & here)
         def _(out=out):
             for c in range(4):
-                grad = dot(left_ref[...], right_ref[c])
+                grad = dot(left[...], right_ref[8 + c])
                 for i in range(2):
                     for j in range(2):
                         slot = 8 * i + ((2 * c + j + shift) & 7)
@@ -255,15 +258,14 @@
     )(in_hbm(dy_own), dy_other, in_hbm(slope), in_vmem(w2_t), in_vmem(right))
 
 
-def run_grads(info, flags, left_t, right, residual, new_res, count, pin):
+def run_grads(info, flags, left_t, right, residual, new_res, count):
     rows = right.shape[1]
     block = pl.BlockSpec((1, 32, 128, 128), lambda i, h, info, *_: (info[2 * i], 0, 0, 0))
     local_block = pl.BlockSpec((1, 16, 128, 128), lambda i, h, *_: (i, 0, 0, 0))
-    pick = lambda i, info, first, second: jnp.where(info[2 * i] < 4, first, second)
-    operands = [info, flags, pin(left_t), pin(right), in_hbm(residual)]
+    operands = [info, flags, in_vmem(left_t), in_vmem(right), in_hbm(residual)]
     specs = [
-        pl.BlockSpec((256, rows), lambda i, h, info, *_: (pick(i, info, info[2 * i + 1], info[2 * i + 1] + h + 4), 0)),
-        pl.BlockSpec((4, rows, 256), lambda i, h, info, *_: (pick(i, info, h, 2), 0, 0)),
+        pl.BlockSpec(left_t.shape, lambda i, h, *_: (0, 0)),
+        pl.BlockSpec(right.shape, lambda i, h, *_: (0, 0, 0)),
         block,
     ]
     alias = {}
@@ -358,10 +360,10 @@
 
     new_res, sums, up, down = None, {}, {}, {}
 
-    def add_up(distances, pin):
+    def add_up(distances):
         nonlocal new_res
         new_res, own_sum, other_sum = run_grads(
-            info_of(distances), flags, left_t, right, stored, new_res, len(distances), pin
+            info_of(distances), flags, left_t, right, stored, new_res, len(distances)
         )
         other_sum = hop(other_sum, CORES)
         for i, k in enumerate(distances):
@@ -378,16 +380,12 @@
         up.update({key: hop(t, UP) for key, t in ups.items()})
         down.update({key: hop(t, DOWN) for key, t in downs.items()})
 
-    add_up([4], in_vmem)
-    add_up([3, 5], in_vmem)
+    add_up([4])
+    add_up([3, 5])
     send(4)
-    add_up([2], in_hbm)
-    add_up([6], in_hbm)
+    add_up([2, 6, 1, 7, 0])
     send(3)
-    add_up([1], in_hbm)
-    add_up([7], in_hbm)
     send(2)
-    add_up([0], in_hbm)
     send(1)
     owned = jnp.concatenate([sums[0, h] + up[1, h].astype(F32) + down[1, h].astype(F32) for h in range(2)], axis=0)
     new_momentum = momentum_decay * momentum + owned[None]

time: 200 us -> 184 us (0.920)
  Pallas kernels: 85.4 us -> 64.2 us
  waiting for transfers between devices: 71.4 us -> 77.4 us
    pallas_call x7 -> x3, Pallas kernels: 46.6 us -> 28.1 us  [run_grads(): pl.pallas_call(grad_kernel, grid_spec=pltpu.PrefetchScalarGridSpec(num_sc...]
    ppermute x38 -> x34, waiting for transfers between devices: 62.7 us -> 68.6 us  [hop(): return lax.ppermute(array, 'dp', pairs)]
    pallas_call x1, Pallas kernels: 13.3 us -> 10.5 us  [run_hid_first(): pl.pallas_call(functools.partial(hid_first_kernel, halves), grid_spec=plt...]
    ppermute x38 -> x34, starting transfers between devices: 25.6 us -> 24.9 us  [hop(): return lax.ppermute(array, 'dp', pairs)]
  transfers between devices with their start and end apart: 41 -> 37, of which waited for: 16 -> 21; matrix products, arithmetic and copies ran while one was open for 2% -> 2% of each run, Pallas kernels for 36% -> 20%
where the time goes in v7:
time: 184 us; the launch traced here: 183 us
  waiting for transfers between devices  77.4 us (42%)
  Pallas kernels  64.2 us (35%)
  starting transfers between devices  31.1 us (17%)
  local copies, waits for them, and re-layouts  5.3 us (3%)
  other arithmetic  3.87 us (2%)
    ppermute x34, waiting for transfers between devices, hop(): return lax.ppermute(array, 'dp', pairs)  68.6 us
    pallas_call x3, Pallas kernels, run_grads(): pl.pallas_call(grad_kernel, grid_spec=pltpu.PrefetchScalarGridSpec(num_sc...  28.1 us
    ppermute x34, starting transfers between devices, hop(): return lax.ppermute(array, 'dp', pairs)  24.9 us
    pallas_call x1, Pallas kernels, run_pre(): pl.pallas_call(functools.partial(pre_kernel, halves), grid_spec=pltpu.Pre...  18.7 us
    pallas_call x1, Pallas kernels, run_hid_first(): pl.pallas_call(functools.partial(hid_first_kernel, halves), grid_spec=plt...  10.5 us
    ppermute x3, waiting for transfers between devices, local_ring(): swap = lambda t: lax.ppermute(t, 'mp', PAIR)  8.78 us
    pallas_call x1, Pallas kernels, run_hid_second(): pl.pallas_call(hid_second_kernel, grid=(6,), in_specs=[pl.BlockSpec((rows...  6.97 us
    ppermute x3, starting transfers between devices, local_ring(): swap = lambda t: lax.ppermute(t, 'mp', PAIR)  6.24 us
  transfers between devices with their start and end apart: 37, of which 21 were waited for; matrix products, arithmetic and copies ran while one was open for 2% of the time, Pallas kernels for 20%

profile of v7, /device:TPU:0, one launch (start us, length us, event | category | flops | bytes accessed | tf_op | source)
XLA Modules:
  0.0 183.2 jit_solution(3598480663210264506)
XLA Ops:
  0.6 3.0 %fusion.19 = (bf16[768,512]{1,0:T(8,128)(2,1)}, bf16[768,512]{1,0:T(8,128)(2,1)S(1)}, bf16[768,512]{1,0:T(8,128)(2,1)S(1)}, bf16[768,512]{1,0:T(8,128)(2,1)S(1)}) fusion(bf16[1536,512]{1,0:T(8,128)(2,1)} %dy_own.3, bf16[1536,512]{1,0:T(8,128)(2,1)} %x_own.1), kind=kLoop, calls=%fused_computation.40 | loop fusion | bytes 6291456 | tf_op jit(solution)/shard_map/slice | solution.py:324
  3.7 3.0 %collective-permute-start.2 = (bf16[768,512]{1,0:T(8,128)(2,1)S(1)}, bf16[768,512]{1,0:T(8,128)(2,1)S(1)}, u32[]{:S(2)}, u32[]{:S(2)}) collective-permute-start(bf16[768,512]{1,0:T(8,128)(2,1)S(1)} %get-tuple-element.87), channel_id=1, source_target_pairs={{0,1},{1,0},{2,3},{3,2},{4,5},{5,4},{6,7},{7,6},{8,9},{9,8},{10,11... | collective-permute-start | bytes 2359304 | tf_op jit(solution)/shard_map/ppermute | solution.py:322
  8.8 11.4 %collective-permute-done.1.refs_2_ = bf16[16,128,128]{2,1,0:T(8,128)(2,1)S(1)} collective-permute-done((bf16[16,128,128]{2,1,0:T(8,128)(2,1)S(1)}, bf16[16,128,128]{2,1,0:T(8,128)(2,1)S(1)}, u32[]{:S(2)}, u32[]{:S(2)}) %collective-permute-start.1) | collective-permute-done | bytes 524320 | tf_op jit(solution)/shard_map/ppermute | solution.py:310
  21.4 2.8 %collective-permute-done.2.refs_18_ = bf16[768,512]{1,0:T(8,128)(2,1)S(1)} collective-permute-done((bf16[768,512]{1,0:T(8,128)(2,1)S(1)}, bf16[768,512]{1,0:T(8,128)(2,1)S(1)}, u32[]{:S(2)}, u32[]{:S(2)}) %collective-permute-start.2) | collective-permute-done | bytes 786464 | tf_op jit(solution)/shard_map/ppermute | solution.py:322
  24.2 1.8 collective-permute-start.3
  26.3 1.7 collective-permute-start.18
  28.1 9.2 %collective-permute-done.3.refs_3_ = bf16[16,128,128]{2,1,0:T(8,128)(2,1)S(1)} collective-permute-done((bf16[16,128,128]{2,1,0:T(8,128)(2,1)S(1)}, bf16[16,128,128]{2,1,0:T(8,128)(2,1)S(1)}, u32[]{:S(2)}, u32[]{:S(2)}) %collective-permute-start.3) | collective-permute-done | bytes 524320 | tf_op jit(solution)/shard_map/ppermute | solution.py:310
  39.8 9.9 %collective-permute-done.5.refs_5_ = bf16[16,128,128]{2,1,0:T(8,128)(2,1)} collective-permute-done((bf16[16,128,128]{2,1,0:T(8,128)(2,1)S(1)}, bf16[16,128,128]{2,1,0:T(8,128)(2,1)}, u32[]{:S(2)}, u32[]{:S(2)}) %collective-permute-start.5) | collective-permute-done | bytes 524320 | tf_op jit(solution)/shard_map/ppermute | solution.py:310
  55.4 6.0 %collective-permute-done.18.refs_19_.dy_other = bf16[1536,512]{1,0:T(8,128)(2,1)S(1)} collective-permute-done((bf16[1536,512]{1,0:T(8,128)(2,1)S(1)}, bf16[1536,512]{1,0:T(8,128)(2,1)S(1)}, u32[]{:S(2)}, u32[]{:S(2)}) %collective-permute-start.18) | collective-permute-done | bytes 1572896 | tf_op jit(solution)/shard_map/ppermute | solution.py:322
  65.4 18.7 %pre_act.1 = (bf16[3072,1536]{1,0:T(8,128)(2,1)S(1)}, f32[8,1536,256]{2,1,0:T(8,128)}) custom-call(s32[19]{0:T(128)S(1)} %stack.159.owners, bf16[1536,512]{1,0:T(8,128)(2,1)} %x_own.1, bf16[16,128,128]{2,1,0:T(8,128)(2,1)} %copy-done.3, bf16[16,128,128]{2,1,0:T(8,128)(2,1)} %copy-done.8, bf16[16,128,128]{2,1,0:T(8,128)(2,1)} %copy-done.7, ...), custom_call_target="tpu_custom_call" | custom-call | flops 16106127360 | bytes 26000000 | tf_op jit(solution)/shard_map/pre_act/pallas_call | solution.py:192
  84.1 10.5 %hid_first.1 = (bf16[12,1536,256]{2,1,0:T(8,128)(2,1)S(1)}, bf16[8,1024,256]{2,1,0:T(8,128)(2,1)S(1)}) custom-call(s32[19]{0:T(128)S(1)} %stack.159.owners, bf16[1536,512]{1,0:T(8,128)(2,1)} %dy_own.3, bf16[1536,512]{1,0:T(8,128)(2,1)} %copy-done, f32[8,1536,256]{2,1,0:T(8,128)} %get-tuple-element.38.slope_ref, bf16[16,128,128]{2,1,0:T(8,128)(2,1)} %copy-done.3, ...), custom_call_target="tpu_custom_call" | custom-call | flops 6442450944 | bytes 18000000 | tf_op jit(solution)/shard_map/hid_first/pallas_call | solution.py:215
  94.6 7.0 %hid_second.1.right_ref = bf16[12,1536,256]{2,1,0:T(8,128)(2,1)S(1)} custom-call(bf16[1536,512]{1,0:T(8,128)(2,1)} %dy_own.3, bf16[768,512]{1,0:T(8,128)(2,1)S(1)} %collective-permute-done.19.dy_other, f32[8,1536,256]{2,1,0:T(8,128)} %get-tuple-element.38.slope_ref, ...), custom_call_target="tpu_custom_call", output_to_operand_aliasing={{}: (4, {})} | custom-call | flops 4831838208 | bytes 15000000 | tf_op jit(solution)/shard_map/hid_second/pallas_call | solution.py:242
  101.6 5.2 %grad_blocks.3 = (bf16[8,32,128,128]{3,2,1,0:T(8,128)(2,1)}, bf16[1,16,128,128]{3,2,1,0:T(8,128)(2,1)}, bf16[1,16,128,128]{3,2,1,0:T(8,128)(2,1)}) custom-call(s32[4]{0:T(128)S(1)} %pad_add_fusion.info, s32[256]{0:T(256)S(1)} %convert_element_type.232.flags, bf16[3072,1536]{1,0:T(8,128)(2,1)S(1)} %get-tuple-element.37.left_ref, ...), custom_call_target="tpu_custom_call" | custom-call | flops 3221225472 | bytes 10000000 | tf_op jit(solution)/shard_map/grad_blocks/pallas_call | solution.py:277
  106.9 7.7 %grad_blocks.4 = (bf16[8,32,128,128]{3,2,1,0:T(8,128)(2,1)}, bf16[2,16,128,128]{3,2,1,0:T(8,128)(2,1)}, bf16[2,16,128,128]{3,2,1,0:T(8,128)(2,1)}) custom-call(s32[6]{0:T(128)S(1)} %stack.164.info, s32[256]{0:T(256)S(1)} %convert_element_type.232.flags, bf16[3072,1536]{1,0:T(8,128)(2,1)S(1)} %get-tuple-element.37.left_ref, ...), custom_call_target="tpu_custom_call", output_to_operand_aliasing={{0}: (5, {})} | custom-call | flops 6442450944 | bytes 20000000 | tf_op jit(solution)/shard_map/grad_blocks/pallas_call | solution.py:277
  114.8 15.1 %grad_blocks.5 = (bf16[8,32,128,128]{3,2,1,0:T(8,128)(2,1)}, bf16[5,16,128,128]{3,2,1,0:T(8,128)(2,1)}, bf16[5,16,128,128]{3,2,1,0:T(8,128)(2,1)}) custom-call(s32[12]{0:T(128)S(1)} %stack.137.info, s32[256]{0:T(256)S(1)} %convert_element_type.232.flags, bf16[3072,1536]{1,0:T(8,128)(2,1)S(1)} %get-tuple-element.37.left_ref, ...), custom_call_target="tpu_custom_call", output_to_operand_aliasing={{0}: (5, {})} | custom-call | flops 16106127360 | bytes 50000000 | tf_op jit(solution)/shard_map/grad_blocks/pallas_call | solution.py:277
  132.5 3.8 %collective-permute-done.22 = bf16[2,16,128,128]{3,2,1,0:T(8,128)(2,1)S(1)} collective-permute-done((bf16[2,16,128,128]{3,2,1,0:T(8,128)(2,1)S(1)}, bf16[2,16,128,128]{3,2,1,0:T(8,128)(2,1)S(1)}, u32[]{:S(2)}, u32[]{:S(2)}) %collective-permute-start.22) | collective-permute-done | bytes 1048608 | tf_op jit(solution)/shard_map/ppermute | solution.py:310
  136.4 2.7 %collective-permute-done.23 = bf16[8,128,128]{2,1,0:T(8,128)(2,1)S(1)} collective-permute-done((bf16[8,128,128]{2,1,0:T(8,128)(2,1)S(1)}, bf16[8,128,128]{2,1,0:T(8,128)(2,1)S(1)}, u32[]{:S(2)}, u32[]{:S(2)}) %collective-permute-start.23) | collective-permute-done | bytes 262176 | tf_op jit(solution)/shard_map/ppermute | solution.py:310
  144.8 5.2 %collective-permute-done.25 = bf16[8,128,128]{2,1,0:T(8,128)(2,1)S(1)} collective-permute-done((bf16[8,128,128]{2,1,0:T(8,128)(2,1)S(1)}, bf16[8,128,128]{2,1,0:T(8,128)(2,1)S(1)}, u32[]{:S(2)}, u32[]{:S(2)}) %collective-permute-start.25) | collective-permute-done | bytes 262176 | tf_op jit(solution)/shard_map/ppermute | solution.py:310
  150.0 3.9 %collective-permute-done.26 = bf16[8,128,128]{2,1,0:T(8,128)(2,1)S(1)} collective-permute-done((bf16[8,128,128]{2,1,0:T(8,128)(2,1)S(1)}, bf16[8,128,128]{2,1,0:T(8,128)(2,1)S(1)}, u32[]{:S(2)}, u32[]{:S(2)}) %collective-permute-start.26) | collective-permute-done | bytes 262176 | tf_op jit(solution)/shard_map/ppermute | solution.py:310
  153.9 2.2 %collective-permute-done.28 = bf16[8,128,128]{2,1,0:T(8,128)(2,1)S(1)} collective-permute-done((bf16[8,128,128]{2,1,0:T(8,128)(2,1)S(1)}, bf16[8,128,128]{2,1,0:T(8,128)(2,1)S(1)}, u32[]{:S(2)}, u32[]{:S(2)}) %collective-permute-start.28) | collective-permute-done | bytes 262176 | tf_op jit(solution)/shard_map/ppermute | solution.py:310
  160.7 4.7 %collective-permute-done.29 = bf16[8,128,128]{2,1,0:T(8,128)(2,1)S(1)} collective-permute-done((bf16[8,128,128]{2,1,0:T(8,128)(2,1)S(1)}, bf16[8,128,128]{2,1,0:T(8,128)(2,1)S(1)}, u32[]{:S(2)}, u32[]{:S(2)}) %collective-permute-start.29) | collective-permute-done | bytes 262176 | tf_op jit(solution)/shard_map/ppermute | solution.py:310
  165.5 2.8 %collective-permute-done.30 = bf16[8,128,128]{2,1,0:T(8,128)(2,1)S(1)} collective-permute-done((bf16[8,128,128]{2,1,0:T(8,128)(2,1)S(1)}, bf16[8,128,128]{2,1,0:T(8,128)(2,1)S(1)}, u32[]{:S(2)}, u32[]{:S(2)}) %collective-permute-start.30) | collective-permute-done | bytes 262176 | tf_op jit(solution)/shard_map/ppermute | solution.py:310
  174.6 3.4 %collective-permute-done.33 = bf16[8,128,128]{2,1,0:T(8,128)(2,1)S(1)} collective-permute-done((bf16[8,128,128]{2,1,0:T(8,128)(2,1)S(1)}, bf16[8,128,128]{2,1,0:T(8,128)(2,1)S(1)}, u32[]{:S(2)}, u32[]{:S(2)}) %collective-permute-start.33) | collective-permute-done | bytes 262176 | tf_op jit(solution)/shard_map/ppermute | solution.py:310
  178.4 2.4 %collective-permute-done.35 = bf16[8,128,128]{2,1,0:T(8,128)(2,1)S(1)} collective-permute-done((bf16[8,128,128]{2,1,0:T(8,128)(2,1)S(1)}, bf16[8,128,128]{2,1,0:T(8,128)(2,1)S(1)}, u32[]{:S(2)}, u32[]{:S(2)}) %collective-permute-start.35) | collective-permute-done | bytes 262176 | tf_op jit(solution)/shard_map/ppermute | solution.py:310
  (106 shorter events, 37.9 us)
Async XLA Ops:
  3.7 20.5 %collective-permute-start.2 = (bf16[768,512]{1,0:T(8,128)(2,1)S(1)}, bf16[768,512]{1,0:T(8,128)(2,1)S(1)}, u32[]{:S(2)}, u32[]{:S(2)}) collective-permute-start(bf16[768,512]{1,0:T(8,128)(2,1)S(1)} %get-tuple-element.87), channel_id=1, source_target_pairs={{0,1},{1,0},{2,3},{3,2},{4,5},{5,4},{6,7},{7,6},{8,9},{9,8},{10,11... | collective-permute-start | bytes 2359304 | tf_op jit(solution)/shard_map/ppermute | solution.py:322
  6.7 13.4 %collective-permute-start.1 = (bf16[16,128,128]{2,1,0:T(8,128)(2,1)S(1)}, bf16[16,128,128]{2,1,0:T(8,128)(2,1)S(1)}, u32[]{:S(2)}, u32[]{:S(2)}) collective-permute-start(bf16[16,128,128]{2,1,0:T(8,128)(2,1)S(1)} %convert_bitcast_fusion.refs_0_), channel_id=1, source_target_pairs={{0,4},{2,6},{8,0},{10,2},{16,8},{18,10},{24,16},{26,18},{28,24},{3... | collective-permute-start | bytes 1572872 | tf_op jit(solution)/shard_map/ppermute | solution.py:310
  8.3 13.1 %collective-permute-start = (bf16[16,128,128]{2,1,0:T(8,128)(2,1)S(1)}, bf16[16,128,128]{2,1,0:T(8,128)(2,1)S(1)}, u32[]{:S(2)}, u32[]{:S(2)}) collective-permute-start(bf16[16,128,128]{2,1,0:T(8,128)(2,1)S(1)} %convert_bitcast_fusion.refs_0_), channel_id=1, source_target_pairs={{0,8},{2,10},{8,16},{10,18},{16,24},{18,26},{24,28},{26,30},{28,20... | collective-permute-start | bytes 1572872 | tf_op jit(solution)/shard_map/ppermute | solution.py:310
  24.2 13.1 %collective-permute-start.3 = (bf16[16,128,128]{2,1,0:T(8,128)(2,1)S(1)}, bf16[16,128,128]{2,1,0:T(8,128)(2,1)S(1)}, u32[]{:S(2)}, u32[]{:S(2)}) collective-permute-start(bf16[16,128,128]{2,1,0:T(8,128)(2,1)S(1)} %collective-permute-done.refs_1_), channel_id=1, source_target_pairs={{0,8},{2,10},{8,16},{10,18},{16,24},{18,26},{24,28},{26,30},{28,20... | collective-permute-start | bytes 1572872 | tf_op jit(solution)/shard_map/ppermute | solution.py:310
  26.1 12.7 %collective-permute-start.4 = (bf16[16,128,128]{2,1,0:T(8,128)(2,1)S(1)}, bf16[16,128,128]{2,1,0:T(8,128)(2,1)}, u32[]{:S(2)}, u32[]{:S(2)}) collective-permute-start(bf16[16,128,128]{2,1,0:T(8,128)(2,1)S(1)} %collective-permute-done.1.refs_2_), channel_id=1, source_target_pairs={{0,4},{2,6},{8,0},{10,2},{16,8},{18,10},{24,16},{26,18},{28,24},{3... | collective-permute-start | bytes 1572872 | tf_op jit(solution)/shard_map/ppermute | solution.py:310
  26.3 35.0 %collective-permute-start.18 = (bf16[1536,512]{1,0:T(8,128)(2,1)S(1)}, bf16[1536,512]{1,0:T(8,128)(2,1)S(1)}, u32[]{:S(2)}, u32[]{:S(2)}) collective-permute-start(bf16[1536,512]{1,0:T(8,128)(2,1)S(1)} %pad_maximum_fusion), channel_id=1, source_target_pairs={{0,1},{1,0},{2,3},{3,2},{4,5},{5,4},{6,7},{7,6},{8,9},{9,8},{10,11... | collective-permute-start | bytes 4718600 | tf_op jit(solution)/shard_map/ppermute | solution.py:322
  37.3 12.4 %collective-permute-start.5 = (bf16[16,128,128]{2,1,0:T(8,128)(2,1)S(1)}, bf16[16,128,128]{2,1,0:T(8,128)(2,1)}, u32[]{:S(2)}, u32[]{:S(2)}) collective-permute-start(bf16[16,128,128]{2,1,0:T(8,128)(2,1)S(1)} %collective-permute-done.3.refs_3_), channel_id=1, source_target_pairs={{0,8},{2,10},{8,16},{10,18},{16,24},{18,26},{24,28},{26,30},{28,20... | collective-permute-start | bytes 1572872 | tf_op jit(solution)/shard_map/ppermute | solution.py:310
  38.8 12.0 %collective-permute-start.6 = (bf16[16,128,128]{2,1,0:T(8,128)(2,1)}, bf16[16,128,128]{2,1,0:T(8,128)(2,1)}, u32[]{:S(2)}, u32[]{:S(2)}) collective-permute-start(bf16[16,128,128]{2,1,0:T(8,128)(2,1)} %collective-permute-done.4.refs_4_), channel_id=1, source_target_pairs={{0,4},{2,6},{8,0},{10,2},{16,8},{18,10},{24,16},{26,18},{28,24},{3... | collective-permute-start | bytes 1572872 | tf_op jit(solution)/shard_map/ppermute | solution.py:310
  39.3 13.4 %collective-permute-start.9 = (bf16[16,128,128]{2,1,0:T(8,128)(2,1)S(1)}, bf16[16,128,128]{2,1,0:T(8,128)(2,1)S(1)}, u32[]{:S(2)}, u32[]{:S(2)}) collective-permute-start(bf16[16,128,128]{2,1,0:T(8,128)(2,1)S(1)} %convert_bitcast_fusion.refs_0_), channel_id=1, source_target_pairs={{0,2},{2,0},{4,6},{6,4},{8,10},{10,8},{12,14},{14,12},{16,18},{18,... | collective-permute-start | bytes 1572872 | tf_op jit(solution)/shard_map/ppermute | solution.py:310
  39.3 14.0 %collective-permute-start.11 = (bf16[16,128,128]{2,1,0:T(8,128)(2,1)S(1)}, bf16[16,128,128]{2,1,0:T(8,128)(2,1)S(1)}, u32[]{:S(2)}, u32[]{:S(2)}) collective-permute-start(bf16[16,128,128]{2,1,0:T(8,128)(2,1)S(1)} %collective-permute-done.1.refs_2_), channel_id=1, source_target_pairs={{0,2},{2,0},{4,6},{6,4},{8,10},{10,8},{12,14},{14,12},{16,18},{18,... | collective-permute-start | bytes 1572872 | tf_op jit(solution)/shard_map/ppermute | solution.py:310
  50.8 10.6 %collective-permute-start.12 = (bf16[16,128,128]{2,1,0:T(8,128)(2,1)S(1)}, bf16[16,128,128]{2,1,0:T(8,128)(2,1)S(1)}, u32[]{:S(2)}, u32[]{:S(2)}) collective-permute-start(bf16[16,128,128]{2,1,0:T(8,128)(2,1)S(1)} %collective-permute-done.3.refs_3_), channel_id=1, source_target_pairs={{0,2},{2,0},{4,6},{6,4},{8,10},{10,8},{12,14},{14,12},{16,18},{18,... | collective-permute-start | bytes 1572872 | tf_op jit(solution)/shard_map/ppermute | solution.py:310
  52.7 11.1 %collective-permute-start.13 = (bf16[16,128,128]{2,1,0:T(8,128)(2,1)}, bf16[16,128,128]{2,1,0:T(8,128)(2,1)}, u32[]{:S(2)}, u32[]{:S(2)}) collective-permute-start(bf16[16,128,128]{2,1,0:T(8,128)(2,1)} %collective-permute-done.4.refs_4_), channel_id=1, source_target_pairs={{0,2},{2,0},{4,6},{6,4},{8,10},{10,8},{12,14},{14,12},{16,18},{18,... | collective-permute-start | bytes 1572872 | tf_op jit(solution)/shard_map/ppermute | solution.py:310
  53.3 8.7 %collective-permute-start.7 = (bf16[8,128,128]{2,1,0:T(8,128)(2,1)S(1)}, bf16[8,128,128]{2,1,0:T(8,128)(2,1)}, u32[]{:S(2)}, u32[]{:S(2)}) collective-permute-start(bf16[8,128,128]{2,1,0:T(8,128)(2,1)S(1)} %slice.152), channel_id=1, source_target_pairs={{0,8},{2,10},{8,16},{10,18},{16,24},{18,26},{24,28},{26,30},{28,20... | collective-permute-start | bytes 786440 | tf_op jit(solution)/shard_map/ppermute | solution.py:310
  63.9 30.8 %collective-permute-start.19 = (bf16[768,512]{1,0:T(8,128)(2,1)}, bf16[768,512]{1,0:T(8,128)(2,1)S(1)}, u32[]{:S(2)}, u32[]{:S(2)}) collective-permute-start(bf16[768,512]{1,0:T(8,128)(2,1)} %get-tuple-element.81), channel_id=1, source_target_pairs={{0,1},{1,0},{2,3},{3,2},{4,5},{5,4},{6,7},{7,6},{8,9},{9,8},{10,11... | collective-permute-start | bytes 2359304 | tf_op jit(solution)/shard_map/ppermute | solution.py:322
  129.9 26.2 %collective-permute-start.21 = (bf16[5,16,128,128]{3,2,1,0:T(8,128)(2,1)}, bf16[5,16,128,128]{3,2,1,0:T(8,128)(2,1)S(1)}, u32[]{:S(2)}, u32[]{:S(2)}) collective-permute-start(bf16[5,16,128,128]{3,2,1,0:T(8,128)(2,1)} %get-tuple-element.47), channel_id=1, source_target_pairs={{0,2},{2,0},{4,6},{6,4},{8,10},{10,8},{12,14},{14,12},{16,18},{18,... | collective-permute-start | bytes 7864328 | tf_op jit(solution)/shard_map/ppermute | solution.py:310
  130.5 8.7 %collective-permute-start.23 = (bf16[8,128,128]{2,1,0:T(8,128)(2,1)S(1)}, bf16[8,128,128]{2,1,0:T(8,128)(2,1)S(1)}, u32[]{:S(2)}, u32[]{:S(2)}) collective-permute-start(bf16[8,128,128]{2,1,0:T(8,128)(2,1)S(1)} %get-tuple-element.50), channel_id=1, source_target_pairs={{0,8},{2,10},{8,16},{10,18},{16,24},{18,26},{24,28},{26,30},{28,20... | collective-permute-start | bytes 786440 | tf_op jit(solution)/shard_map/ppermute | solution.py:310
  140.7 9.3 %collective-permute-start.25 = (bf16[8,128,128]{2,1,0:T(8,128)(2,1)S(1)}, bf16[8,128,128]{2,1,0:T(8,128)(2,1)S(1)}, u32[]{:S(2)}, u32[]{:S(2)}) collective-permute-start(bf16[8,128,128]{2,1,0:T(8,128)(2,1)S(1)} %get-tuple-element.52), channel_id=1, source_target_pairs={{0,8},{2,10},{8,16},{10,18},{16,24},{18,26},{24,28},{26,30},{28,20... | collective-permute-start | bytes 786440 | tf_op jit(solution)/shard_map/ppermute | solution.py:310
  142.3 11.6 %collective-permute-start.26 = (bf16[8,128,128]{2,1,0:T(8,128)(2,1)S(1)}, bf16[8,128,128]{2,1,0:T(8,128)(2,1)S(1)}, u32[]{:S(2)}, u32[]{:S(2)}) collective-permute-start(bf16[8,128,128]{2,1,0:T(8,128)(2,1)S(1)} %get-tuple-element.53), channel_id=1, source_target_pairs={{0,8},{2,10},{8,16},{10,18},{16,24},{18,26},{24,28},{26,30},{28,20... | collective-permute-start | bytes 786440 | tf_op jit(solution)/shard_map/ppermute | solution.py:310
  143.6 10.3 %collective-permute-start.27 = (bf16[8,128,128]{2,1,0:T(8,128)(2,1)S(1)}, bf16[8,128,128]{2,1,0:T(8,128)(2,1)S(1)}, u32[]{:S(2)}, u32[]{:S(2)}) collective-permute-start(bf16[8,128,128]{2,1,0:T(8,128)(2,1)S(1)} %get-tuple-element.54), channel_id=1, source_target_pairs={{0,4},{2,6},{8,0},{10,2},{16,8},{18,10},{24,16},{26,18},{28,24},{3... | collective-permute-start | bytes 786440 | tf_op jit(solution)/shard_map/ppermute | solution.py:310
  144.3 11.8 %collective-permute-start.28 = (bf16[8,128,128]{2,1,0:T(8,128)(2,1)S(1)}, bf16[8,128,128]{2,1,0:T(8,128)(2,1)S(1)}, u32[]{:S(2)}, u32[]{:S(2)}) collective-permute-start(bf16[8,128,128]{2,1,0:T(8,128)(2,1)S(1)} %get-tuple-element.55), channel_id=1, source_target_pairs={{0,4},{2,6},{8,0},{10,2},{16,8},{18,10},{24,16},{26,18},{28,24},{3... | collective-permute-start | bytes 786440 | tf_op jit(solution)/shard_map/ppermute | solution.py:310
  156.6 8.8 %collective-permute-start.29 = (bf16[8,128,128]{2,1,0:T(8,128)(2,1)S(1)}, bf16[8,128,128]{2,1,0:T(8,128)(2,1)S(1)}, u32[]{:S(2)}, u32[]{:S(2)}) collective-permute-start(bf16[8,128,128]{2,1,0:T(8,128)(2,1)S(1)} %get-tuple-element.56), channel_id=1, source_target_pairs={{0,8},{2,10},{8,16},{10,18},{16,24},{18,26},{24,28},{26,30},{28,20... | collective-permute-start | bytes 786440 | tf_op jit(solution)/shard_map/ppermute | solution.py:310
  158.2 10.1 %collective-permute-start.30 = (bf16[8,128,128]{2,1,0:T(8,128)(2,1)S(1)}, bf16[8,128,128]{2,1,0:T(8,128)(2,1)S(1)}, u32[]{:S(2)}, u32[]{:S(2)}) collective-permute-start(bf16[8,128,128]{2,1,0:T(8,128)(2,1)S(1)} %get-tuple-element.57), channel_id=1, source_target_pairs={{0,8},{2,10},{8,16},{10,18},{16,24},{18,26},{24,28},{26,30},{28,20... | collective-permute-start | bytes 786440 | tf_op jit(solution)/shard_map/ppermute | solution.py:310
  158.8 9.5 %collective-permute-start.31 = (bf16[8,128,128]{2,1,0:T(8,128)(2,1)S(1)}, bf16[8,128,128]{2,1,0:T(8,128)(2,1)S(1)}, u32[]{:S(2)}, u32[]{:S(2)}) collective-permute-start(bf16[8,128,128]{2,1,0:T(8,128)(2,1)S(1)} %get-tuple-element.58), channel_id=1, source_target_pairs={{0,4},{2,6},{8,0},{10,2},{16,8},{18,10},{24,16},{26,18},{28,24},{3... | collective-permute-start | bytes 786440 | tf_op jit(solution)/shard_map/ppermute | solution.py:310
  160.2 9.8 %collective-permute-start.32 = (bf16[8,128,128]{2,1,0:T(8,128)(2,1)S(1)}, bf16[8,128,128]{2,1,0:T(8,128)(2,1)S(1)}, u32[]{:S(2)}, u32[]{:S(2)}) collective-permute-start(bf16[8,128,128]{2,1,0:T(8,128)(2,1)S(1)} %get-tuple-element.59), channel_id=1, source_target_pairs={{0,4},{2,6},{8,0},{10,2},{16,8},{18,10},{24,16},{26,18},{28,24},{3... | collective-permute-start | bytes 786440 | tf_op jit(solution)/shard_map/ppermute | solution.py:310
  (29 other events, 436.2 us)

commit v8 on v7

--- a/solution.py
+++ b/solution.py
@@ -58,9 +58,9 @@
 
 
 def pre_kernel(halves, owners, x_own, *refs):
-    units, (x_first, x_second, left_t, slope_ref, w1, sem) = refs[: len(halves)], refs[len(halves) :]
+    units, (x_other, left_t, slope_ref, w1, sem) = refs[: len(halves)], refs[len(halves) :]
     step = pl.program_id(0)
-    rows, size = x_own.shape[0], x_first.shape[0]
+    rows = x_own.shape[0]
 
     @pl.when(step == 0)
     def _():
@@ -71,11 +71,7 @@
         @pl.when(step == s)
         def _(s=s):
             lanes = slice(256 * (s % 2), 256 * (s % 2) + 256)
-            if s < 2:
-                left_t[...] = x_own[:, lanes].T
-            else:
-                left_t[:, :size] = x_first[:, lanes].T
-                left_t[:, size:] = x_second[: rows - size, lanes].T
+            left_t[...] = (x_own if s < 2 else x_other)[:, lanes].T
 
     @pl.when(step == 4)
     def _():
@@ -85,12 +81,11 @@
     def _():
         c = 2 * (step - 4)
         w = jnp.concatenate([w1[c], w1[c + 1]], axis=1)
-        block = size // 2
+        block = rows // 4
 
         def product(r):
-            part, o = (x_first, r) if r < size else (x_second, r - size)
             pre = jnp.dot(x_own[r : r + block, :], w[: w.shape[0] // 2], preferred_element_type=F32)
-            return pre + jnp.dot(part[o : o + block, :], w[w.shape[0] // 2 :], preferred_element_type=F32)
+            return pre + jnp.dot(x_other[r : r + block, :], w[w.shape[0] // 2 :], preferred_element_type=F32)
 
         starts = list(range(0, rows, block))
         ahead = product(starts[0])
@@ -149,9 +144,23 @@
     hid_block(dy_own, dy_other, w2_t, slope_ref, right)
 
 
-def grad_kernel(info, flags, left_ref, right_ref, res_ref, *refs):
-    new_res, mine, other = refs[-3:]
+def grad_kernel(layout, info, flags, left_ref, right_ref, res_ref, *refs):
+    new_res, *sent, held, sems = refs[len(refs) - 2 * len(layout) - 3 :]
+    places = [(array, i) for array, size in enumerate(layout) for i in range(size)]
+    count = len(places)
     group, h = pl.program_id(0), pl.program_id(1)
+    slot_now = group & 1
+    mine, other = held.at[slot_now, 0], held.at[slot_now, 1]
+
+    def copy_out(slot, which, k):
+        array, i = places[k]
+        return pltpu.make_async_copy(held.at[slot, which], sent[2 * array + which].at[i], sems.at[slot, which])
+
+    @pl.when((h == 0) & (group >= 2))
+    def _():
+        for which in range(2):
+            copy_out(slot_now, which, 0).wait()
+
     g = info[2 * group]
     row = pl.multiple_of(256 * (info[2 * group + 1] + jnp.where(g < 4, 0, h + 4)), 256)
     left = left_ref.at[pl.ds(row, 256)]
@@ -172,7 +181,7 @@
                 for j in range(2):
                     lanes = slice(128 * j, 128 * j + 128)
                     slot = 8 * h + 2 * c + j
-                    out[0, slot] = finish(jnp.where(row == 0, grad[:128, lanes], grad[128:, lanes]), 16 * row + slot)
+                    out[slot] = finish(jnp.where(row == 0, grad[:128, lanes], grad[128:, lanes]), 16 * row + slot)
 
     for out, here in ((mine, h == core), (other, h != core)):
 
@@ -183,7 +192,20 @@
                 for i in range(2):
                     for j in range(2):
                         slot = 8 * i + ((2 * c + j + shift) & 7)
-                        out[0, slot] = finish(grad[128 * i : 128 * i + 128, 128 * j : 128 * j + 128], 16 * h + slot)
+                        out[slot] = finish(grad[128 * i : 128 * i + 128, 128 * j : 128 * j + 128], 16 * h + slot)
+
+    for k in range(count):
+
+        @pl.when((h == 1) & (group == k))
+        def _(k=k):
+            for which in range(2):
+                copy_out(k & 1, which, k).start()
+
+    @pl.when((h == 1) & (group == count - 1))
+    def _():
+        for k in range(max(count - 2, 0), count):
+            for which in range(2):
+                copy_out(k & 1, which, k).wait()
 
 
 def run_pre(owners, halves, x_own, x_other, units):
@@ -194,7 +216,7 @@
         grid_spec=pltpu.PrefetchScalarGridSpec(
             num_scalar_prefetch=1,
             grid=(12,),
-            in_specs=[whole(x_own)] + [ANY] * len(units) + [whole(t) for t in x_other],
+            in_specs=[whole(x_own)] + [ANY] * len(units) + [whole(x_other)],
             out_specs=[
                 pl.BlockSpec((256, rows), lambda i, *_: (i, 0)),
                 pl.BlockSpec((1, rows, 256), lambda i, *_: (jnp.maximum(i - 4, 0), 0, 0)),
@@ -203,9 +225,9 @@
         ),
         out_shape=[VMEM((3072, rows), BF), HBM((8, rows, 256), F32)],
         compiler_params=pltpu.CompilerParams(vmem_limit_bytes=24 * 2**20),
-        cost_estimate=pl.CostEstimate(flops=5 * rows * 1024 * 2048, bytes_accessed=26_000_000, transcendentals=rows * 2048),
+        cost_estimate=pl.CostEstimate(flops=rows * 512 * 1024, bytes_accessed=2_000_000, transcendentals=0),
         name="pre_act",
-    )(owners, in_hbm(x_own), *[in_hbm(u) for u in units], *x_other)
+    )(owners, in_hbm(x_own), *[in_hbm(u) for u in units], x_other)
 
 
 def run_hid_first(owners, halves, dy_own, dy_other, slope, units):
@@ -231,9 +253,9 @@
         ),
         out_shape=[VMEM((12, total, 256), BF), VMEM((8, 1024, 256), BF)],
         compiler_params=pltpu.CompilerParams(vmem_limit_bytes=22 * 2**20),
-        cost_estimate=pl.CostEstimate(flops=4 * rows * 1024 * 2048, bytes_accessed=18_000_000, transcendentals=0),
+        cost_estimate=pl.CostEstimate(flops=rows * 512 * 1024, bytes_accessed=2_000_000, transcendentals=0),
         name="hid_first",
-    )(owners, in_hbm(dy_own), in_hbm(dy_other), in_hbm(slope), *[in_hbm(u) for u in units])
+    )(owners, in_hbm(dy_own), dy_other, in_hbm(slope), *[in_hbm(u) for u in units])
 
 
 def run_hid_second(dy_own, dy_other, slope, w2_t, right):
@@ -258,10 +280,9 @@
     )(in_hbm(dy_own), dy_other, in_hbm(slope), in_vmem(w2_t), in_vmem(right))
 
 
-def run_grads(info, flags, left_t, right, residual, new_res, count):
+def run_grads(info, flags, left_t, right, residual, new_res, layout):
     rows = right.shape[1]
     block = pl.BlockSpec((1, 32, 128, 128), lambda i, h, info, *_: (info[2 * i], 0, 0, 0))
-    local_block = pl.BlockSpec((1, 16, 128, 128), lambda i, h, *_: (i, 0, 0, 0))
     operands = [info, flags, in_vmem(left_t), in_vmem(right), in_hbm(residual)]
     specs = [
         pl.BlockSpec(left_t.shape, lambda i, h, *_: (0, 0)),
@@ -273,16 +294,18 @@
         alias = {len(operands): 0}
         operands.append(in_hbm(new_res))
         specs.append(ANY)
-    sent = HBM((count, 16, 128, 128), BF)
+    count = sum(layout)
+    sent = [HBM((size, 16, 128, 128), BF) for size in layout for _ in range(2)]
     return pl.pallas_call(
-        grad_kernel,
+        functools.partial(grad_kernel, layout),
         grid_spec=pltpu.PrefetchScalarGridSpec(
             num_scalar_prefetch=2,
             grid=(count, 2),
             in_specs=specs,
-            out_specs=[block, local_block, local_block],
+            out_specs=[block] + [ANY] * len(sent),
+            scratch_shapes=[pltpu.VMEM((2, 2, 16, 128, 128), BF), pltpu.SemaphoreType.DMA((2, 2))],
         ),
-        out_shape=[HBM(residual.shape, BF), sent, sent],
+        out_shape=[HBM(residual.shape, BF), *sent],
         input_output_aliases=alias,
         compiler_params=pltpu.CompilerParams(vmem_limit_bytes=20 * 2**20),
         cost_estimate=pl.CostEstimate(flops=4 * rows * 1024 * 512 * count, bytes_accessed=10_000_000 * count, transcendentals=0),
@@ -320,7 +343,8 @@
 
     half = rows // 2
     swap = lambda t: lax.ppermute(t, "mp", PAIR)
-    x_other = [swap(tokens[:half]), swap(jnp.concatenate([tokens[half:], out_grad[:half]], axis=0))]
+    x_other = swap(tokens)
+    dy_early = swap(out_grad[:half])
     dy_late = swap(out_grad[half:])
 
     shift = 4 * shard
@@ -328,8 +352,8 @@
     up = down = own
     units, halves, owners = [own], [None], [mine]
     for k in range(1, 5):
-        if k == 2:
-            x_other[0], up, down = lax.optimization_barrier((x_other[0], up, down))
+        if k == 4:
+            x_other, up, down = lax.optimization_barrier((x_other, up, down))
         if k == 4:
             up, down = up[:8], down[8:]
         up, down = hop(up, UP), hop(down, DOWN)
@@ -345,7 +369,7 @@
     flags = flags.astype(jnp.int32)
 
     left_t, slope = run_pre(owners, halves, tokens, x_other, units)
-    right, w2_t = run_hid_first(owners, halves, out_grad, x_other[1], slope, units)
+    right, w2_t = run_hid_first(owners, halves, out_grad, dy_early, slope, units)
     right = run_hid_second(out_grad, dy_late, slope, w2_t, right)
 
     stored = residual.reshape(8, 32, 128, 128)
@@ -360,16 +384,17 @@
 
     new_res, sums, up, down = None, {}, {}, {}
 
-    def add_up(distances):
+    def add_up(*arrays):
         nonlocal new_res
-        new_res, own_sum, other_sum = run_grads(
-            info_of(distances), flags, left_t, right, stored, new_res, len(distances)
+        new_res, *sent = run_grads(
+            info_of(sum(arrays, [])), flags, left_t, right, stored, new_res, tuple(len(t) for t in arrays)
         )
-        other_sum = hop(other_sum, CORES)
-        for i, k in enumerate(distances):
-            for h in range(2):
-                part = slice(8 * h, 8 * h + 8)
-                sums[k, h] = own_sum[i, part].astype(F32) + other_sum[i, part].astype(F32)
+        for a, distances in enumerate(arrays):
+            own_sum, other_sum = sent[2 * a], hop(sent[2 * a + 1], CORES)
+            for i, k in enumerate(distances):
+                for h in range(2):
+                    part = slice(8 * h, 8 * h + 8)
+                    sums[k, h] = own_sum[i, part].astype(F32) + other_sum[i, part].astype(F32)
 
     def send(k):
         nonlocal flags
@@ -383,7 +408,7 @@
     add_up([4])
     add_up([3, 5])
     send(4)
-    add_up([2, 6, 1, 7, 0])
+    add_up([2, 6], [1, 7, 0])
     send(3)
     send(2)
     send(1)

time: 184 us -> 176 us (0.957)
  waiting for transfers between devices: 77.4 us -> 68.4 us
    ppermute x3, waiting for transfers between devices: 8.78 us -> 0.01 us  [local_ring(): swap = lambda t: lax.ppermute(t, 'mp', PAIR)]
    ppermute x3, starting transfers between devices: 6.24 us -> 4 us  [local_ring(): swap = lambda t: lax.ppermute(t, 'mp', PAIR)]
    pallas_call x3, Pallas kernels: 28.1 us -> 30.2 us  [run_grads(): pl.pallas_call(functools.partial(grad_kernel, layout), grid_spec=pltpu.Pr...]
    ppermute x34 -> x35, starting transfers between devices: 24.9 us -> 26.7 us  [hop(): return lax.ppermute(array, 'dp', pairs)]
    ppermute x34 -> x35, waiting for transfers between devices: 68.6 us -> 68.4 us  [hop(): return lax.ppermute(array, 'dp', pairs)]
  transfers between devices with their start and end apart: 37 -> 38, of which waited for: 21 -> 18; matrix products, arithmetic and copies ran while one was open for 2% -> 2% of each run, Pallas kernels for 20% -> 30%
where the time goes in v8:
time: 176 us; the launch traced here: 175 us
  waiting for transfers between devices  68.4 us (39%)
  Pallas kernels  65.6 us (37%)
  starting transfers between devices  30.7 us (17%)
  other arithmetic  5.16 us (3%)
  local copies, waits for them, and re-layouts  4.26 us (2%)
    ppermute x35, waiting for transfers between devices, hop(): return lax.ppermute(array, 'dp', pairs)  68.4 us
    pallas_call x3, Pallas kernels, run_grads(): pl.pallas_call(functools.partial(grad_kernel, layout), grid_spec=pltpu.Pr...  30.2 us
    ppermute x35, starting transfers between devices, hop(): return lax.ppermute(array, 'dp', pairs)  26.7 us
    pallas_call x1, Pallas kernels, run_pre(): pl.pallas_call(functools.partial(pre_kernel, halves), grid_spec=pltpu.Pre...  18.5 us
    pallas_call x1, Pallas kernels, run_hid_first(): pl.pallas_call(functools.partial(hid_first_kernel, halves), grid_spec=plt...  9.96 us
    pallas_call x1, Pallas kernels, run_hid_second(): pl.pallas_call(hid_second_kernel, grid=(6,), in_specs=[pl.BlockSpec((rows...  6.96 us
    ppermute x3, starting transfers between devices, local_ring(): swap = lambda t: lax.ppermute(t, 'mp', PAIR)  4 us
  transfers between devices with their start and end apart: 38, of which 18 were waited for; matrix products, arithmetic and copies ran while one was open for 2% of the time, Pallas kernels for 30%

profile of v8, /device:TPU:0, one launch (start us, length us, event | category | flops | bytes accessed | tf_op | source)
XLA Modules:
  0.0 175.2 jit_solution(1636392912751514387)
XLA Ops:
  2.1 3.0 %collective-permute-start.1 = (bf16[16,128,128]{2,1,0:T(8,128)(2,1)S(1)}, bf16[16,128,128]{2,1,0:T(8,128)(2,1)S(1)}, u32[]{:S(2)}, u32[]{:S(2)}) collective-permute-start(bf16[16,128,128]{2,1,0:T(8,128)(2,1)S(1)} %convert_bitcast_fusion.refs_0_), channel_id=1, source_target_pairs={{0,4},{2,6},{8,0},{10,2},{16,8},{18,10},{24,16},{26,18},{28,24},{3... | collective-permute-start | bytes 1572872 | tf_op jit(solution)/shard_map/ppermute | solution.py:333
  5.2 1.9 %collective-permute-start.6 = (bf16[1536,512]{1,0:T(8,128)(2,1)}, bf16[1536,512]{1,0:T(8,128)(2,1)S(1)}, u32[]{:S(2)}, u32[]{:S(2)}) collective-permute-start(bf16[1536,512]{1,0:T(8,128)(2,1)} %x_own.1), channel_id=1, source_target_pairs={{0,1},{1,0},{2,3},{3,2},{4,5},{5,4},{6,7},{7,6},{8,9},{9,8},{10,11... | collective-permute-start | bytes 4718600 | tf_op jit(solution)/shard_map/ppermute | solution.py:345
  7.1 10.0 %collective-permute-done.1.refs_2_ = bf16[16,128,128]{2,1,0:T(8,128)(2,1)S(1)} collective-permute-done((bf16[16,128,128]{2,1,0:T(8,128)(2,1)S(1)}, bf16[16,128,128]{2,1,0:T(8,128)(2,1)S(1)}, u32[]{:S(2)}, u32[]{:S(2)}) %collective-permute-start.1) | collective-permute-done | bytes 524320 | tf_op jit(solution)/shard_map/ppermute | solution.py:333
  19.1 11.1 %collective-permute-done.3.refs_4_ = bf16[16,128,128]{2,1,0:T(8,128)(2,1)S(1)} collective-permute-done((bf16[16,128,128]{2,1,0:T(8,128)(2,1)S(1)}, bf16[16,128,128]{2,1,0:T(8,128)(2,1)S(1)}, u32[]{:S(2)}, u32[]{:S(2)}) %collective-permute-start.3) | collective-permute-done | bytes 524320 | tf_op jit(solution)/shard_map/ppermute | solution.py:333
  32.7 9.6 %collective-permute-done.5.refs_6_ = bf16[16,128,128]{2,1,0:T(8,128)(2,1)S(1)} collective-permute-done((bf16[16,128,128]{2,1,0:T(8,128)(2,1)S(1)}, bf16[16,128,128]{2,1,0:T(8,128)(2,1)S(1)}, u32[]{:S(2)}, u32[]{:S(2)}) %collective-permute-start.5) | collective-permute-done | bytes 524320 | tf_op jit(solution)/shard_map/ppermute | solution.py:333
  51.9 1.8 %collective-permute-done.8.refs_8_ = bf16[8,128,128]{2,1,0:T(8,128)(2,1)S(1)} collective-permute-done((bf16[8,128,128]{2,1,0:T(8,128)(2,1)S(1)}, bf16[8,128,128]{2,1,0:T(8,128)(2,1)S(1)}, u32[]{:S(2)}, u32[]{:S(2)}) %collective-permute-start.8) | collective-permute-done | bytes 262176 | tf_op jit(solution)/shard_map/ppermute | solution.py:333
  53.7 5.3 %collective-permute-done.7.refs_7_ = bf16[8,128,128]{2,1,0:T(8,128)(2,1)} collective-permute-done((bf16[8,128,128]{2,1,0:T(8,128)(2,1)S(1)}, bf16[8,128,128]{2,1,0:T(8,128)(2,1)}, u32[]{:S(2)}, u32[]{:S(2)}) %collective-permute-start.7) | collective-permute-done | bytes 262176 | tf_op jit(solution)/shard_map/ppermute | solution.py:333
  61.2 18.5 %pre_act.1 = (bf16[3072,1536]{1,0:T(8,128)(2,1)S(1)}, f32[8,1536,256]{2,1,0:T(8,128)}) custom-call(s32[19]{0:T(128)S(1)} %stack.159.owners, bf16[1536,512]{1,0:T(8,128)(2,1)} %x_own.1, bf16[16,128,128]{2,1,0:T(8,128)(2,1)} %copy-done.1, bf16[16,128,128]{2,1,0:T(8,128)(2,1)} %copy-done.5, bf16[16,128,128]{2,1,0:T(8,128)(2,1)} %copy-done.4, ...), custom_call_target="tpu_custom_call" | custom-call | flops 805306368 | bytes 2000000 | tf_op jit(solution)/shard_map/pre_act/pallas_call | solution.py:214
  79.7 10.0 %hid_first.1 = (bf16[12,1536,256]{2,1,0:T(8,128)(2,1)S(1)}, bf16[8,1024,256]{2,1,0:T(8,128)(2,1)S(1)}) custom-call(s32[19]{0:T(128)S(1)} %stack.159.owners, bf16[1536,512]{1,0:T(8,128)(2,1)} %dy_own.3, bf16[768,512]{1,0:T(8,128)(2,1)S(1)} %collective-permute-done.19.dy_other, f32[8,1536,256]{2,1,0:T(8,128)} %get-tuple-element.40.slope_ref, ...), custom_call_target="tpu_custom_call" | custom-call | flops 402653184 | bytes 2000000 | tf_op jit(solution)/shard_map/hid_first/pallas_call | solution.py:237
  89.7 7.0 %hid_second.1.right_ref = bf16[12,1536,256]{2,1,0:T(8,128)(2,1)S(1)} custom-call(bf16[1536,512]{1,0:T(8,128)(2,1)} %dy_own.3, bf16[768,512]{1,0:T(8,128)(2,1)S(1)} %collective-permute-done.18.dy_other, f32[8,1536,256]{2,1,0:T(8,128)} %get-tuple-element.40.slope_ref, ...), custom_call_target="tpu_custom_call", output_to_operand_aliasing={{}: (4, {})} | custom-call | flops 4831838208 | bytes 15000000 | tf_op jit(solution)/shard_map/hid_second/pallas_call | solution.py:264
  96.7 5.9 %grad_blocks.3 = (bf16[8,32,128,128]{3,2,1,0:T(8,128)(2,1)}, bf16[1,16,128,128]{3,2,1,0:T(8,128)(2,1)}, bf16[1,16,128,128]{3,2,1,0:T(8,128)(2,1)}) custom-call(s32[4]{0:T(128)S(1)} %pad_add_fusion.info, s32[256]{0:T(256)S(1)} %convert_element_type.232.flags, bf16[3072,1536]{1,0:T(8,128)(2,1)S(1)} %get-tuple-element.39.left_ref, ...), custom_call_target="tpu_custom_call" | custom-call | flops 3221225472 | bytes 10000000 | tf_op jit(solution)/shard_map/grad_blocks/pallas_call | solution.py:299
  102.9 8.4 %grad_blocks.4 = (bf16[8,32,128,128]{3,2,1,0:T(8,128)(2,1)}, bf16[2,16,128,128]{3,2,1,0:T(8,128)(2,1)}, bf16[2,16,128,128]{3,2,1,0:T(8,128)(2,1)}) custom-call(s32[6]{0:T(128)S(1)} %stack.164.info, s32[256]{0:T(256)S(1)} %convert_element_type.232.flags, bf16[3072,1536]{1,0:T(8,128)(2,1)S(1)} %get-tuple-element.39.left_ref, ...), custom_call_target="tpu_custom_call", output_to_operand_aliasing={{0}: (5, {})} | custom-call | flops 6442450944 | bytes 20000000 | tf_op jit(solution)/shard_map/grad_blocks/pallas_call | solution.py:299
  113.9 15.9 %grad_blocks.5 = (bf16[8,32,128,128]{3,2,1,0:T(8,128)(2,1)}, bf16[2,16,128,128]{3,2,1,0:T(8,128)(2,1)}, bf16[2,16,128,128]{3,2,1,0:T(8,128)(2,1)}, bf16[3,16,128...) custom-call(s32[12]{0:T(128)S(1)} %stack.137.info, ...), custom_call_target="tpu_custom_call", output_to_operand_aliasing={{0}: (5, {})} | custom-call | flops 16106127360 | bytes 50000000 | tf_op jit(solution)/shard_map/grad_blocks/pallas_call | solution.py:299
  133.4 6.6 %collective-permute-done.26 = bf16[8,128,128]{2,1,0:T(8,128)(2,1)S(1)} collective-permute-done((bf16[8,128,128]{2,1,0:T(8,128)(2,1)S(1)}, bf16[8,128,128]{2,1,0:T(8,128)(2,1)S(1)}, u32[]{:S(2)}, u32[]{:S(2)}) %collective-permute-start.26) | collective-permute-done | bytes 262176 | tf_op jit(solution)/shard_map/ppermute | solution.py:333
  141.7 3.1 %collective-permute-done.27 = bf16[8,128,128]{2,1,0:T(8,128)(2,1)S(1)} collective-permute-done((bf16[8,128,128]{2,1,0:T(8,128)(2,1)S(1)}, bf16[8,128,128]{2,1,0:T(8,128)(2,1)S(1)}, u32[]{:S(2)}, u32[]{:S(2)}) %collective-permute-start.27) | collective-permute-done | bytes 262176 | tf_op jit(solution)/shard_map/ppermute | solution.py:333
  144.8 1.8 %collective-permute-done.29 = bf16[8,128,128]{2,1,0:T(8,128)(2,1)S(1)} collective-permute-done((bf16[8,128,128]{2,1,0:T(8,128)(2,1)S(1)}, bf16[8,128,128]{2,1,0:T(8,128)(2,1)S(1)}, u32[]{:S(2)}, u32[]{:S(2)}) %collective-permute-start.29) | collective-permute-done | bytes 262176 | tf_op jit(solution)/shard_map/ppermute | solution.py:333
  151.4 4.4 %collective-permute-done.30 = bf16[8,128,128]{2,1,0:T(8,128)(2,1)S(1)} collective-permute-done((bf16[8,128,128]{2,1,0:T(8,128)(2,1)S(1)}, bf16[8,128,128]{2,1,0:T(8,128)(2,1)S(1)}, u32[]{:S(2)}, u32[]{:S(2)}) %collective-permute-start.30) | collective-permute-done | bytes 262176 | tf_op jit(solution)/shard_map/ppermute | solution.py:333
  155.8 2.8 %collective-permute-done.31 = bf16[8,128,128]{2,1,0:T(8,128)(2,1)S(1)} collective-permute-done((bf16[8,128,128]{2,1,0:T(8,128)(2,1)S(1)}, bf16[8,128,128]{2,1,0:T(8,128)(2,1)S(1)}, u32[]{:S(2)}, u32[]{:S(2)}) %collective-permute-start.31) | collective-permute-done | bytes 262176 | tf_op jit(solution)/shard_map/ppermute | solution.py:333
  158.6 2.1 %collective-permute-done.33 = bf16[8,128,128]{2,1,0:T(8,128)(2,1)S(1)} collective-permute-done((bf16[8,128,128]{2,1,0:T(8,128)(2,1)S(1)}, bf16[8,128,128]{2,1,0:T(8,128)(2,1)S(1)}, u32[]{:S(2)}, u32[]{:S(2)}) %collective-permute-start.33) | collective-permute-done | bytes 262176 | tf_op jit(solution)/shard_map/ppermute | solution.py:333
  161.3 1.8 %collective-permute-start.34 = (bf16[8,128,128]{2,1,0:T(8,128)(2,1)S(1)}, bf16[8,128,128]{2,1,0:T(8,128)(2,1)S(1)}, u32[]{:S(2)}, u32[]{:S(2)}) collective-permute-start(bf16[8,128,128]{2,1,0:T(8,128)(2,1)S(1)} %get-tuple-element.64), channel_id=1, source_target_pairs={{0,8},{2,10},{8,16},{10,18},{16,24},{18,26},{24,28},{26,30},{28,20... | collective-permute-start | bytes 786440 | tf_op jit(solution)/shard_map/ppermute | solution.py:333
  163.3 1.7 collective-permute-start.36
  165.4 3.5 %collective-permute-done.34 = bf16[8,128,128]{2,1,0:T(8,128)(2,1)S(1)} collective-permute-done((bf16[8,128,128]{2,1,0:T(8,128)(2,1)S(1)}, bf16[8,128,128]{2,1,0:T(8,128)(2,1)S(1)}, u32[]{:S(2)}, u32[]{:S(2)}) %collective-permute-start.34) | collective-permute-done | bytes 262176 | tf_op jit(solution)/shard_map/ppermute | solution.py:333
  168.8 1.7 collective-permute-done.35
  171.7 1.7 collective-permute-done.37
  (117 shorter events, 34.7 us)
Async XLA Ops:
  2.1 15.0 %collective-permute-start.1 = (bf16[16,128,128]{2,1,0:T(8,128)(2,1)S(1)}, bf16[16,128,128]{2,1,0:T(8,128)(2,1)S(1)}, u32[]{:S(2)}, u32[]{:S(2)}) collective-permute-start(bf16[16,128,128]{2,1,0:T(8,128)(2,1)S(1)} %convert_bitcast_fusion.refs_0_), channel_id=1, source_target_pairs={{0,4},{2,6},{8,0},{10,2},{16,8},{18,10},{24,16},{26,18},{28,24},{3... | collective-permute-start | bytes 1572872 | tf_op jit(solution)/shard_map/ppermute | solution.py:333
  5.1 13.7 %collective-permute-start = (bf16[16,128,128]{2,1,0:T(8,128)(2,1)S(1)}, bf16[16,128,128]{2,1,0:T(8,128)(2,1)S(1)}, u32[]{:S(2)}, u32[]{:S(2)}) collective-permute-start(bf16[16,128,128]{2,1,0:T(8,128)(2,1)S(1)} %convert_bitcast_fusion.refs_0_), channel_id=1, source_target_pairs={{0,8},{2,10},{8,16},{10,18},{16,24},{18,26},{24,28},{26,30},{28,20... | collective-permute-start | bytes 1572872 | tf_op jit(solution)/shard_map/ppermute | solution.py:333
  5.2 38.0 %collective-permute-start.6 = (bf16[1536,512]{1,0:T(8,128)(2,1)}, bf16[1536,512]{1,0:T(8,128)(2,1)S(1)}, u32[]{:S(2)}, u32[]{:S(2)}) collective-permute-start(bf16[1536,512]{1,0:T(8,128)(2,1)} %x_own.1), channel_id=1, source_target_pairs={{0,1},{1,0},{2,3},{3,2},{4,5},{5,4},{6,7},{7,6},{8,9},{9,8},{10,11... | collective-permute-start | bytes 4718600 | tf_op jit(solution)/shard_map/ppermute | solution.py:345
  17.1 13.1 %collective-permute-start.3 = (bf16[16,128,128]{2,1,0:T(8,128)(2,1)S(1)}, bf16[16,128,128]{2,1,0:T(8,128)(2,1)S(1)}, u32[]{:S(2)}, u32[]{:S(2)}) collective-permute-start(bf16[16,128,128]{2,1,0:T(8,128)(2,1)S(1)} %collective-permute-done.1.refs_2_), channel_id=1, source_target_pairs={{0,4},{2,6},{8,0},{10,2},{16,8},{18,10},{24,16},{26,18},{28,24},{3... | collective-permute-start | bytes 1572872 | tf_op jit(solution)/shard_map/ppermute | solution.py:333
  18.8 12.8 %collective-permute-start.2 = (bf16[16,128,128]{2,1,0:T(8,128)(2,1)S(1)}, bf16[16,128,128]{2,1,0:T(8,128)(2,1)S(1)}, u32[]{:S(2)}, u32[]{:S(2)}) collective-permute-start(bf16[16,128,128]{2,1,0:T(8,128)(2,1)S(1)} %collective-permute-done.refs_1_), channel_id=1, source_target_pairs={{0,8},{2,10},{8,16},{10,18},{16,24},{18,26},{24,28},{26,30},{28,20... | collective-permute-start | bytes 1572872 | tf_op jit(solution)/shard_map/ppermute | solution.py:333
  30.2 12.2 %collective-permute-start.5 = (bf16[16,128,128]{2,1,0:T(8,128)(2,1)S(1)}, bf16[16,128,128]{2,1,0:T(8,128)(2,1)S(1)}, u32[]{:S(2)}, u32[]{:S(2)}) collective-permute-start(bf16[16,128,128]{2,1,0:T(8,128)(2,1)S(1)} %collective-permute-done.3.refs_4_), channel_id=1, source_target_pairs={{0,4},{2,6},{8,0},{10,2},{16,8},{18,10},{24,16},{26,18},{28,24},{3... | collective-permute-start | bytes 1572872 | tf_op jit(solution)/shard_map/ppermute | solution.py:333
  31.5 11.7 %collective-permute-start.4 = (bf16[16,128,128]{2,1,0:T(8,128)(2,1)S(1)}, bf16[16,128,128]{2,1,0:T(8,128)(2,1)}, u32[]{:S(2)}, u32[]{:S(2)}) collective-permute-start(bf16[16,128,128]{2,1,0:T(8,128)(2,1)S(1)} %collective-permute-done.2.refs_3_), channel_id=1, source_target_pairs={{0,8},{2,10},{8,16},{10,18},{16,24},{18,26},{24,28},{26,30},{28,20... | collective-permute-start | bytes 1572872 | tf_op jit(solution)/shard_map/ppermute | solution.py:333
  32.2 11.6 %collective-permute-start.9 = (bf16[16,128,128]{2,1,0:T(8,128)(2,1)S(1)}, bf16[16,128,128]{2,1,0:T(8,128)(2,1)S(1)}, u32[]{:S(2)}, u32[]{:S(2)}) collective-permute-start(bf16[16,128,128]{2,1,0:T(8,128)(2,1)S(1)} %convert_bitcast_fusion.refs_0_), channel_id=1, source_target_pairs={{0,2},{2,0},{4,6},{6,4},{8,10},{10,8},{12,14},{14,12},{16,18},{18,... | collective-permute-start | bytes 1572872 | tf_op jit(solution)/shard_map/ppermute | solution.py:333
  32.2 11.7 %collective-permute-start.11 = (bf16[16,128,128]{2,1,0:T(8,128)(2,1)S(1)}, bf16[16,128,128]{2,1,0:T(8,128)(2,1)S(1)}, u32[]{:S(2)}, u32[]{:S(2)}) collective-permute-start(bf16[16,128,128]{2,1,0:T(8,128)(2,1)S(1)} %collective-permute-done.1.refs_2_), channel_id=1, source_target_pairs={{0,2},{2,0},{4,6},{6,4},{8,10},{10,8},{12,14},{14,12},{16,18},{18,... | collective-permute-start | bytes 1572872 | tf_op jit(solution)/shard_map/ppermute | solution.py:333
  43.8 15.1 %collective-permute-start.15 = (bf16[16,128,128]{2,1,0:T(8,128)(2,1)S(1)}, bf16[16,128,128]{2,1,0:T(8,128)(2,1)S(1)}, u32[]{:S(2)}, u32[]{:S(2)}) collective-permute-start(bf16[16,128,128]{2,1,0:T(8,128)(2,1)S(1)} %collective-permute-done.5.refs_6_), channel_id=1, source_target_pairs={{0,2},{2,0},{4,6},{6,4},{8,10},{10,8},{12,14},{14,12},{16,18},{18,... | collective-permute-start | bytes 1572872 | tf_op jit(solution)/shard_map/ppermute | solution.py:333
  48.3 31.4 %collective-permute-start.19 = (bf16[768,512]{1,0:T(8,128)(2,1)}, bf16[768,512]{1,0:T(8,128)(2,1)S(1)}, u32[]{:S(2)}, u32[]{:S(2)}) collective-permute-start(bf16[768,512]{1,0:T(8,128)(2,1)} %get-tuple-element.85), channel_id=1, source_target_pairs={{0,1},{1,0},{2,3},{3,2},{4,5},{5,4},{6,7},{7,6},{8,9},{9,8},{10,11... | collective-permute-start | bytes 2359304 | tf_op jit(solution)/shard_map/ppermute | solution.py:345
  49.9 39.8 %collective-permute-start.18 = (bf16[768,512]{1,0:T(8,128)(2,1)}, bf16[768,512]{1,0:T(8,128)(2,1)S(1)}, u32[]{:S(2)}, u32[]{:S(2)}) collective-permute-start(bf16[768,512]{1,0:T(8,128)(2,1)} %get-tuple-element.86), channel_id=1, source_target_pairs={{0,1},{1,0},{2,3},{3,2},{4,5},{5,4},{6,7},{7,6},{8,9},{9,8},{10,11... | collective-permute-start | bytes 2359304 | tf_op jit(solution)/shard_map/ppermute | solution.py:345
  102.6 9.0 %collective-permute-start.20 = (bf16[1,16,128,128]{3,2,1,0:T(8,128)(2,1)}, bf16[1,16,128,128]{3,2,1,0:T(8,128)(2,1)S(1)}, u32[]{:S(2)}, u32[]{:S(2)}) collective-permute-start(bf16[1,16,128,128]{3,2,1,0:T(8,128)(2,1)} %get-tuple-element.44), channel_id=1, source_target_pairs={{0,2},{2,0},{4,6},{6,4},{8,10},{10,8},{12,14},{14,12},{16,18},{18,... | collective-permute-start | bytes 1572872 | tf_op jit(solution)/shard_map/ppermute | solution.py:333
  111.3 19.1 %collective-permute-start.23 = (bf16[2,16,128,128]{3,2,1,0:T(8,128)(2,1)}, bf16[2,16,128,128]{3,2,1,0:T(8,128)(2,1)S(1)}, u32[]{:S(2)}, u32[]{:S(2)}) collective-permute-start(bf16[2,16,128,128]{3,2,1,0:T(8,128)(2,1)} %get-tuple-element.53), channel_id=1, source_target_pairs={{0,2},{2,0},{4,6},{6,4},{8,10},{10,8},{12,14},{14,12},{16,18},{18,... | collective-permute-start | bytes 3145736 | tf_op jit(solution)/shard_map/ppermute | solution.py:333
  111.8 18.8 %collective-permute-start.24 = (bf16[8,128,128]{2,1,0:T(8,128)(2,1)S(1)}, bf16[8,128,128]{2,1,0:T(8,128)(2,1)S(1)}, u32[]{:S(2)}, u32[]{:S(2)}) collective-permute-start(bf16[8,128,128]{2,1,0:T(8,128)(2,1)S(1)} %get-tuple-element.54), channel_id=1, source_target_pairs={{0,8},{2,10},{8,16},{10,18},{16,24},{18,26},{24,28},{26,30},{28,20... | collective-permute-start | bytes 786440 | tf_op jit(solution)/shard_map/ppermute | solution.py:333
  112.4 18.2 %collective-permute-start.25 = (bf16[8,128,128]{2,1,0:T(8,128)(2,1)S(1)}, bf16[8,128,128]{2,1,0:T(8,128)(2,1)S(1)}, u32[]{:S(2)}, u32[]{:S(2)}) collective-permute-start(bf16[8,128,128]{2,1,0:T(8,128)(2,1)S(1)} %get-tuple-element.55), channel_id=1, source_target_pairs={{0,4},{2,6},{8,0},{10,2},{16,8},{18,10},{24,16},{26,18},{28,24},{3... | collective-permute-start | bytes 786440 | tf_op jit(solution)/shard_map/ppermute | solution.py:333
  129.8 16.8 %collective-permute-start.22 = (bf16[2,16,128,128]{3,2,1,0:T(8,128)(2,1)}, bf16[2,16,128,128]{3,2,1,0:T(8,128)(2,1)S(1)}, u32[]{:S(2)}, u32[]{:S(2)}) collective-permute-start(bf16[2,16,128,128]{3,2,1,0:T(8,128)(2,1)} %get-tuple-element.51), channel_id=1, source_target_pairs={{0,2},{2,0},{4,6},{6,4},{8,10},{10,8},{12,14},{14,12},{16,18},{18,... | collective-permute-start | bytes 3145736 | tf_op jit(solution)/shard_map/ppermute | solution.py:333
  129.9 30.9 %collective-permute-start.21 = (bf16[3,16,128,128]{3,2,1,0:T(8,128)(2,1)}, bf16[3,16,128,128]{3,2,1,0:T(8,128)(2,1)S(1)}, u32[]{:S(2)}, u32[]{:S(2)}) collective-permute-start(bf16[3,16,128,128]{3,2,1,0:T(8,128)(2,1)} %get-tuple-element.49), channel_id=1, source_target_pairs={{0,2},{2,0},{4,6},{6,4},{8,10},{10,8},{12,14},{14,12},{16,18},{18,... | collective-permute-start | bytes 4718600 | tf_op jit(solution)/shard_map/ppermute | solution.py:333
  130.8 9.2 %collective-permute-start.26 = (bf16[8,128,128]{2,1,0:T(8,128)(2,1)S(1)}, bf16[8,128,128]{2,1,0:T(8,128)(2,1)S(1)}, u32[]{:S(2)}, u32[]{:S(2)}) collective-permute-start(bf16[8,128,128]{2,1,0:T(8,128)(2,1)S(1)} %get-tuple-element.56), channel_id=1, source_target_pairs={{0,8},{2,10},{8,16},{10,18},{16,24},{18,26},{24,28},{26,30},{28,20... | collective-permute-start | bytes 786440 | tf_op jit(solution)/shard_map/ppermute | solution.py:333
  131.4 13.4 %collective-permute-start.27 = (bf16[8,128,128]{2,1,0:T(8,128)(2,1)S(1)}, bf16[8,128,128]{2,1,0:T(8,128)(2,1)S(1)}, u32[]{:S(2)}, u32[]{:S(2)}) collective-permute-start(bf16[8,128,128]{2,1,0:T(8,128)(2,1)S(1)} %get-tuple-element.57), channel_id=1, source_target_pairs={{0,8},{2,10},{8,16},{10,18},{16,24},{18,26},{24,28},{26,30},{28,20... | collective-permute-start | bytes 786440 | tf_op jit(solution)/shard_map/ppermute | solution.py:333
  132.5 12.3 %collective-permute-start.28 = (bf16[8,128,128]{2,1,0:T(8,128)(2,1)S(1)}, bf16[8,128,128]{2,1,0:T(8,128)(2,1)S(1)}, u32[]{:S(2)}, u32[]{:S(2)}) collective-permute-start(bf16[8,128,128]{2,1,0:T(8,128)(2,1)S(1)} %get-tuple-element.58), channel_id=1, source_target_pairs={{0,4},{2,6},{8,0},{10,2},{16,8},{18,10},{24,16},{26,18},{28,24},{3... | collective-permute-start | bytes 786440 | tf_op jit(solution)/shard_map/ppermute | solution.py:333
  147.8 10.8 %collective-permute-start.31 = (bf16[8,128,128]{2,1,0:T(8,128)(2,1)S(1)}, bf16[8,128,128]{2,1,0:T(8,128)(2,1)S(1)}, u32[]{:S(2)}, u32[]{:S(2)}) collective-permute-start(bf16[8,128,128]{2,1,0:T(8,128)(2,1)S(1)} %get-tuple-element.61), channel_id=1, source_target_pairs={{0,8},{2,10},{8,16},{10,18},{16,24},{18,26},{24,28},{26,30},{28,20... | collective-permute-start | bytes 786440 | tf_op jit(solution)/shard_map/ppermute | solution.py:333
  149.5 9.1 %collective-permute-start.32 = (bf16[8,128,128]{2,1,0:T(8,128)(2,1)S(1)}, bf16[8,128,128]{2,1,0:T(8,128)(2,1)S(1)}, u32[]{:S(2)}, u32[]{:S(2)}) collective-permute-start(bf16[8,128,128]{2,1,0:T(8,128)(2,1)S(1)} %get-tuple-element.62), channel_id=1, source_target_pairs={{0,4},{2,6},{8,0},{10,2},{16,8},{18,10},{24,16},{26,18},{28,24},{3... | collective-permute-start | bytes 786440 | tf_op jit(solution)/shard_map/ppermute | solution.py:333
  149.9 10.9 %collective-permute-start.33 = (bf16[8,128,128]{2,1,0:T(8,128)(2,1)S(1)}, bf16[8,128,128]{2,1,0:T(8,128)(2,1)S(1)}, u32[]{:S(2)}, u32[]{:S(2)}) collective-permute-start(bf16[8,128,128]{2,1,0:T(8,128)(2,1)S(1)} %get-tuple-element.63), channel_id=1, source_target_pairs={{0,4},{2,6},{8,0},{10,2},{16,8},{18,10},{24,16},{26,18},{28,24},{3... | collective-permute-start | bytes 786440 | tf_op jit(solution)/shard_map/ppermute | solution.py:333
  (35 other events, 412.9 us)

commit v9 on v8

--- a/solution.py
+++ b/solution.py
@@ -81,7 +81,7 @@
     def _():
         c = 2 * (step - 4)
         w = jnp.concatenate([w1[c], w1[c + 1]], axis=1)
-        block = rows // 4
+        block = rows // 3
 
         def product(r):
             pre = jnp.dot(x_own[r : r + block, :], w[: w.shape[0] // 2], preferred_element_type=F32)

time: 176 us -> 175 us (level)
  no operation moved by 1% of the time
where the time goes in v9:
time: 175 us
  waiting for transfers between devices  68.4 us (39%)
  Pallas kernels  65.2 us (37%)
  starting transfers between devices  30.7 us (18%)
  other arithmetic  5.16 us (3%)
  local copies, waits for them, and re-layouts  4.26 us (2%)
    ppermute x35, waiting for transfers between devices, hop(): return lax.ppermute(array, 'dp', pairs)  68.4 us
    pallas_call x3, Pallas kernels, run_grads(): pl.pallas_call(functools.partial(grad_kernel, layout), grid_spec=pltpu.Pr...  30.2 us
    ppermute x35, starting transfers between devices, hop(): return lax.ppermute(array, 'dp', pairs)  26.8 us
    pallas_call x1, Pallas kernels, run_pre(): pl.pallas_call(functools.partial(pre_kernel, halves), grid_spec=pltpu.Pre...  18 us
    pallas_call x1, Pallas kernels, run_hid_first(): pl.pallas_call(functools.partial(hid_first_kernel, halves), grid_spec=plt...  9.96 us
    pallas_call x1, Pallas kernels, run_hid_second(): pl.pallas_call(hid_second_kernel, grid=(6,), in_specs=[pl.BlockSpec((rows...  6.96 us
    ppermute x3, starting transfers between devices, local_ring(): swap = lambda t: lax.ppermute(t, 'mp', PAIR)  4 us
  transfers between devices with their start and end apart: 38, of which 18 were waited for; matrix products, arithmetic and copies ran while one was open for 2% of the time, Pallas kernels for 30%

profile of v9, /device:TPU:0, one launch (start us, length us, event | category | flops | bytes accessed | tf_op | source)
XLA Modules:
  0.0 174.7 jit_solution(2474332909369859490)
XLA Ops:
  2.1 3.0 %collective-permute-start.1 = (bf16[16,128,128]{2,1,0:T(8,128)(2,1)S(1)}, bf16[16,128,128]{2,1,0:T(8,128)(2,1)S(1)}, u32[]{:S(2)}, u32[]{:S(2)}) collective-permute-start(bf16[16,128,128]{2,1,0:T(8,128)(2,1)S(1)} %convert_bitcast_fusion.refs_0_), channel_id=1, source_target_pairs={{0,4},{2,6},{8,0},{10,2},{16,8},{18,10},{24,16},{26,18},{28,24},{3... | collective-permute-start | bytes 1572872 | tf_op jit(solution)/shard_map/ppermute | solution.py:333
  5.2 1.9 %collective-permute-start.6 = (bf16[1536,512]{1,0:T(8,128)(2,1)}, bf16[1536,512]{1,0:T(8,128)(2,1)S(1)}, u32[]{:S(2)}, u32[]{:S(2)}) collective-permute-start(bf16[1536,512]{1,0:T(8,128)(2,1)} %x_own.1), channel_id=1, source_target_pairs={{0,1},{1,0},{2,3},{3,2},{4,5},{5,4},{6,7},{7,6},{8,9},{9,8},{10,11... | collective-permute-start | bytes 4718600 | tf_op jit(solution)/shard_map/ppermute | solution.py:345
  7.1 10.0 %collective-permute-done.1.refs_2_ = bf16[16,128,128]{2,1,0:T(8,128)(2,1)S(1)} collective-permute-done((bf16[16,128,128]{2,1,0:T(8,128)(2,1)S(1)}, bf16[16,128,128]{2,1,0:T(8,128)(2,1)S(1)}, u32[]{:S(2)}, u32[]{:S(2)}) %collective-permute-start.1) | collective-permute-done | bytes 524320 | tf_op jit(solution)/shard_map/ppermute | solution.py:333
  19.1 11.1 %collective-permute-done.3.refs_4_ = bf16[16,128,128]{2,1,0:T(8,128)(2,1)S(1)} collective-permute-done((bf16[16,128,128]{2,1,0:T(8,128)(2,1)S(1)}, bf16[16,128,128]{2,1,0:T(8,128)(2,1)S(1)}, u32[]{:S(2)}, u32[]{:S(2)}) %collective-permute-start.3) | collective-permute-done | bytes 524320 | tf_op jit(solution)/shard_map/ppermute | solution.py:333
  32.7 9.6 %collective-permute-done.5.refs_6_ = bf16[16,128,128]{2,1,0:T(8,128)(2,1)S(1)} collective-permute-done((bf16[16,128,128]{2,1,0:T(8,128)(2,1)S(1)}, bf16[16,128,128]{2,1,0:T(8,128)(2,1)S(1)}, u32[]{:S(2)}, u32[]{:S(2)}) %collective-permute-start.5) | collective-permute-done | bytes 524320 | tf_op jit(solution)/shard_map/ppermute | solution.py:333
  51.9 1.8 %collective-permute-done.8.refs_8_ = bf16[8,128,128]{2,1,0:T(8,128)(2,1)S(1)} collective-permute-done((bf16[8,128,128]{2,1,0:T(8,128)(2,1)S(1)}, bf16[8,128,128]{2,1,0:T(8,128)(2,1)S(1)}, u32[]{:S(2)}, u32[]{:S(2)}) %collective-permute-start.8) | collective-permute-done | bytes 262176 | tf_op jit(solution)/shard_map/ppermute | solution.py:333
  53.7 5.3 %collective-permute-done.7.refs_7_ = bf16[8,128,128]{2,1,0:T(8,128)(2,1)} collective-permute-done((bf16[8,128,128]{2,1,0:T(8,128)(2,1)S(1)}, bf16[8,128,128]{2,1,0:T(8,128)(2,1)}, u32[]{:S(2)}, u32[]{:S(2)}) %collective-permute-start.7) | collective-permute-done | bytes 262176 | tf_op jit(solution)/shard_map/ppermute | solution.py:333
  61.2 18.0 %pre_act.1 = (bf16[3072,1536]{1,0:T(8,128)(2,1)S(1)}, f32[8,1536,256]{2,1,0:T(8,128)}) custom-call(s32[19]{0:T(128)S(1)} %stack.159.owners, bf16[1536,512]{1,0:T(8,128)(2,1)} %x_own.1, bf16[16,128,128]{2,1,0:T(8,128)(2,1)} %copy-done.1, bf16[16,128,128]{2,1,0:T(8,128)(2,1)} %copy-done.5, bf16[16,128,128]{2,1,0:T(8,128)(2,1)} %copy-done.4, ...), custom_call_target="tpu_custom_call" | custom-call | flops 805306368 | bytes 2000000 | tf_op jit(solution)/shard_map/pre_act/pallas_call | solution.py:214
  79.3 10.0 %hid_first.1 = (bf16[12,1536,256]{2,1,0:T(8,128)(2,1)S(1)}, bf16[8,1024,256]{2,1,0:T(8,128)(2,1)S(1)}) custom-call(s32[19]{0:T(128)S(1)} %stack.159.owners, bf16[1536,512]{1,0:T(8,128)(2,1)} %dy_own.3, bf16[768,512]{1,0:T(8,128)(2,1)S(1)} %collective-permute-done.19.dy_other, f32[8,1536,256]{2,1,0:T(8,128)} %get-tuple-element.40.slope_ref, ...), custom_call_target="tpu_custom_call" | custom-call | flops 402653184 | bytes 2000000 | tf_op jit(solution)/shard_map/hid_first/pallas_call | solution.py:237
  89.3 7.0 %hid_second.1.right_ref = bf16[12,1536,256]{2,1,0:T(8,128)(2,1)S(1)} custom-call(bf16[1536,512]{1,0:T(8,128)(2,1)} %dy_own.3, bf16[768,512]{1,0:T(8,128)(2,1)S(1)} %collective-permute-done.18.dy_other, f32[8,1536,256]{2,1,0:T(8,128)} %get-tuple-element.40.slope_ref, ...), custom_call_target="tpu_custom_call", output_to_operand_aliasing={{}: (4, {})} | custom-call | flops 4831838208 | bytes 15000000 | tf_op jit(solution)/shard_map/hid_second/pallas_call | solution.py:264
  96.2 5.9 %grad_blocks.3 = (bf16[8,32,128,128]{3,2,1,0:T(8,128)(2,1)}, bf16[1,16,128,128]{3,2,1,0:T(8,128)(2,1)}, bf16[1,16,128,128]{3,2,1,0:T(8,128)(2,1)}) custom-call(s32[4]{0:T(128)S(1)} %pad_add_fusion.info, s32[256]{0:T(256)S(1)} %convert_element_type.232.flags, bf16[3072,1536]{1,0:T(8,128)(2,1)S(1)} %get-tuple-element.39.left_ref, ...), custom_call_target="tpu_custom_call" | custom-call | flops 3221225472 | bytes 10000000 | tf_op jit(solution)/shard_map/grad_blocks/pallas_call | solution.py:299
  102.5 8.4 %grad_blocks.4 = (bf16[8,32,128,128]{3,2,1,0:T(8,128)(2,1)}, bf16[2,16,128,128]{3,2,1,0:T(8,128)(2,1)}, bf16[2,16,128,128]{3,2,1,0:T(8,128)(2,1)}) custom-call(s32[6]{0:T(128)S(1)} %stack.164.info, s32[256]{0:T(256)S(1)} %convert_element_type.232.flags, bf16[3072,1536]{1,0:T(8,128)(2,1)S(1)} %get-tuple-element.39.left_ref, ...), custom_call_target="tpu_custom_call", output_to_operand_aliasing={{0}: (5, {})} | custom-call | flops 6442450944 | bytes 20000000 | tf_op jit(solution)/shard_map/grad_blocks/pallas_call | solution.py:299
  113.5 15.9 %grad_blocks.5 = (bf16[8,32,128,128]{3,2,1,0:T(8,128)(2,1)}, bf16[2,16,128,128]{3,2,1,0:T(8,128)(2,1)}, bf16[2,16,128,128]{3,2,1,0:T(8,128)(2,1)}, bf16[3,16,128...) custom-call(s32[12]{0:T(128)S(1)} %stack.137.info, ...), custom_call_target="tpu_custom_call", output_to_operand_aliasing={{0}: (5, {})} | custom-call | flops 16106127360 | bytes 50000000 | tf_op jit(solution)/shard_map/grad_blocks/pallas_call | solution.py:299
  133.0 6.6 %collective-permute-done.26 = bf16[8,128,128]{2,1,0:T(8,128)(2,1)S(1)} collective-permute-done((bf16[8,128,128]{2,1,0:T(8,128)(2,1)S(1)}, bf16[8,128,128]{2,1,0:T(8,128)(2,1)S(1)}, u32[]{:S(2)}, u32[]{:S(2)}) %collective-permute-start.26) | collective-permute-done | bytes 262176 | tf_op jit(solution)/shard_map/ppermute | solution.py:333
  141.3 3.1 %collective-permute-done.27 = bf16[8,128,128]{2,1,0:T(8,128)(2,1)S(1)} collective-permute-done((bf16[8,128,128]{2,1,0:T(8,128)(2,1)S(1)}, bf16[8,128,128]{2,1,0:T(8,128)(2,1)S(1)}, u32[]{:S(2)}, u32[]{:S(2)}) %collective-permute-start.27) | collective-permute-done | bytes 262176 | tf_op jit(solution)/shard_map/ppermute | solution.py:333
  144.3 1.8 %collective-permute-done.29 = bf16[8,128,128]{2,1,0:T(8,128)(2,1)S(1)} collective-permute-done((bf16[8,128,128]{2,1,0:T(8,128)(2,1)S(1)}, bf16[8,128,128]{2,1,0:T(8,128)(2,1)S(1)}, u32[]{:S(2)}, u32[]{:S(2)}) %collective-permute-start.29) | collective-permute-done | bytes 262176 | tf_op jit(solution)/shard_map/ppermute | solution.py:333
  150.9 4.4 %collective-permute-done.30 = bf16[8,128,128]{2,1,0:T(8,128)(2,1)S(1)} collective-permute-done((bf16[8,128,128]{2,1,0:T(8,128)(2,1)S(1)}, bf16[8,128,128]{2,1,0:T(8,128)(2,1)S(1)}, u32[]{:S(2)}, u32[]{:S(2)}) %collective-permute-start.30) | collective-permute-done | bytes 262176 | tf_op jit(solution)/shard_map/ppermute | solution.py:333
  155.3 2.8 %collective-permute-done.31 = bf16[8,128,128]{2,1,0:T(8,128)(2,1)S(1)} collective-permute-done((bf16[8,128,128]{2,1,0:T(8,128)(2,1)S(1)}, bf16[8,128,128]{2,1,0:T(8,128)(2,1)S(1)}, u32[]{:S(2)}, u32[]{:S(2)}) %collective-permute-start.31) | collective-permute-done | bytes 262176 | tf_op jit(solution)/shard_map/ppermute | solution.py:333
  158.2 2.1 %collective-permute-done.33 = bf16[8,128,128]{2,1,0:T(8,128)(2,1)S(1)} collective-permute-done((bf16[8,128,128]{2,1,0:T(8,128)(2,1)S(1)}, bf16[8,128,128]{2,1,0:T(8,128)(2,1)S(1)}, u32[]{:S(2)}, u32[]{:S(2)}) %collective-permute-start.33) | collective-permute-done | bytes 262176 | tf_op jit(solution)/shard_map/ppermute | solution.py:333
  160.8 1.8 %collective-permute-start.34 = (bf16[8,128,128]{2,1,0:T(8,128)(2,1)S(1)}, bf16[8,128,128]{2,1,0:T(8,128)(2,1)S(1)}, u32[]{:S(2)}, u32[]{:S(2)}) collective-permute-start(bf16[8,128,128]{2,1,0:T(8,128)(2,1)S(1)} %get-tuple-element.64), channel_id=1, source_target_pairs={{0,8},{2,10},{8,16},{10,18},{16,24},{18,26},{24,28},{26,30},{28,20... | collective-permute-start | bytes 786440 | tf_op jit(solution)/shard_map/ppermute | solution.py:333
  162.9 1.7 collective-permute-start.36
  164.9 3.5 %collective-permute-done.34 = bf16[8,128,128]{2,1,0:T(8,128)(2,1)S(1)} collective-permute-done((bf16[8,128,128]{2,1,0:T(8,128)(2,1)S(1)}, bf16[8,128,128]{2,1,0:T(8,128)(2,1)S(1)}, u32[]{:S(2)}, u32[]{:S(2)}) %collective-permute-start.34) | collective-permute-done | bytes 262176 | tf_op jit(solution)/shard_map/ppermute | solution.py:333
  168.4 1.7 collective-permute-done.35
  171.2 1.7 collective-permute-done.37
  (117 shorter events, 34.7 us)
Async XLA Ops:
  2.1 15.0 %collective-permute-start.1 = (bf16[16,128,128]{2,1,0:T(8,128)(2,1)S(1)}, bf16[16,128,128]{2,1,0:T(8,128)(2,1)S(1)}, u32[]{:S(2)}, u32[]{:S(2)}) collective-permute-start(bf16[16,128,128]{2,1,0:T(8,128)(2,1)S(1)} %convert_bitcast_fusion.refs_0_), channel_id=1, source_target_pairs={{0,4},{2,6},{8,0},{10,2},{16,8},{18,10},{24,16},{26,18},{28,24},{3... | collective-permute-start | bytes 1572872 | tf_op jit(solution)/shard_map/ppermute | solution.py:333
  5.1 13.7 %collective-permute-start = (bf16[16,128,128]{2,1,0:T(8,128)(2,1)S(1)}, bf16[16,128,128]{2,1,0:T(8,128)(2,1)S(1)}, u32[]{:S(2)}, u32[]{:S(2)}) collective-permute-start(bf16[16,128,128]{2,1,0:T(8,128)(2,1)S(1)} %convert_bitcast_fusion.refs_0_), channel_id=1, source_target_pairs={{0,8},{2,10},{8,16},{10,18},{16,24},{18,26},{24,28},{26,30},{28,20... | collective-permute-start | bytes 1572872 | tf_op jit(solution)/shard_map/ppermute | solution.py:333
  5.2 38.0 %collective-permute-start.6 = (bf16[1536,512]{1,0:T(8,128)(2,1)}, bf16[1536,512]{1,0:T(8,128)(2,1)S(1)}, u32[]{:S(2)}, u32[]{:S(2)}) collective-permute-start(bf16[1536,512]{1,0:T(8,128)(2,1)} %x_own.1), channel_id=1, source_target_pairs={{0,1},{1,0},{2,3},{3,2},{4,5},{5,4},{6,7},{7,6},{8,9},{9,8},{10,11... | collective-permute-start | bytes 4718600 | tf_op jit(solution)/shard_map/ppermute | solution.py:345
  17.1 13.1 %collective-permute-start.3 = (bf16[16,128,128]{2,1,0:T(8,128)(2,1)S(1)}, bf16[16,128,128]{2,1,0:T(8,128)(2,1)S(1)}, u32[]{:S(2)}, u32[]{:S(2)}) collective-permute-start(bf16[16,128,128]{2,1,0:T(8,128)(2,1)S(1)} %collective-permute-done.1.refs_2_), channel_id=1, source_target_pairs={{0,4},{2,6},{8,0},{10,2},{16,8},{18,10},{24,16},{26,18},{28,24},{3... | collective-permute-start | bytes 1572872 | tf_op jit(solution)/shard_map/ppermute | solution.py:333
  18.8 12.8 %collective-permute-start.2 = (bf16[16,128,128]{2,1,0:T(8,128)(2,1)S(1)}, bf16[16,128,128]{2,1,0:T(8,128)(2,1)S(1)}, u32[]{:S(2)}, u32[]{:S(2)}) collective-permute-start(bf16[16,128,128]{2,1,0:T(8,128)(2,1)S(1)} %collective-permute-done.refs_1_), channel_id=1, source_target_pairs={{0,8},{2,10},{8,16},{10,18},{16,24},{18,26},{24,28},{26,30},{28,20... | collective-permute-start | bytes 1572872 | tf_op jit(solution)/shard_map/ppermute | solution.py:333
  30.2 12.2 %collective-permute-start.5 = (bf16[16,128,128]{2,1,0:T(8,128)(2,1)S(1)}, bf16[16,128,128]{2,1,0:T(8,128)(2,1)S(1)}, u32[]{:S(2)}, u32[]{:S(2)}) collective-permute-start(bf16[16,128,128]{2,1,0:T(8,128)(2,1)S(1)} %collective-permute-done.3.refs_4_), channel_id=1, source_target_pairs={{0,4},{2,6},{8,0},{10,2},{16,8},{18,10},{24,16},{26,18},{28,24},{3... | collective-permute-start | bytes 1572872 | tf_op jit(solution)/shard_map/ppermute | solution.py:333
  31.5 11.7 %collective-permute-start.4 = (bf16[16,128,128]{2,1,0:T(8,128)(2,1)S(1)}, bf16[16,128,128]{2,1,0:T(8,128)(2,1)}, u32[]{:S(2)}, u32[]{:S(2)}) collective-permute-start(bf16[16,128,128]{2,1,0:T(8,128)(2,1)S(1)} %collective-permute-done.2.refs_3_), channel_id=1, source_target_pairs={{0,8},{2,10},{8,16},{10,18},{16,24},{18,26},{24,28},{26,30},{28,20... | collective-permute-start | bytes 1572872 | tf_op jit(solution)/shard_map/ppermute | solution.py:333
  32.2 11.6 %collective-permute-start.9 = (bf16[16,128,128]{2,1,0:T(8,128)(2,1)S(1)}, bf16[16,128,128]{2,1,0:T(8,128)(2,1)S(1)}, u32[]{:S(2)}, u32[]{:S(2)}) collective-permute-start(bf16[16,128,128]{2,1,0:T(8,128)(2,1)S(1)} %convert_bitcast_fusion.refs_0_), channel_id=1, source_target_pairs={{0,2},{2,0},{4,6},{6,4},{8,10},{10,8},{12,14},{14,12},{16,18},{18,... | collective-permute-start | bytes 1572872 | tf_op jit(solution)/shard_map/ppermute | solution.py:333
  32.2 11.7 %collective-permute-start.11 = (bf16[16,128,128]{2,1,0:T(8,128)(2,1)S(1)}, bf16[16,128,128]{2,1,0:T(8,128)(2,1)S(1)}, u32[]{:S(2)}, u32[]{:S(2)}) collective-permute-start(bf16[16,128,128]{2,1,0:T(8,128)(2,1)S(1)} %collective-permute-done.1.refs_2_), channel_id=1, source_target_pairs={{0,2},{2,0},{4,6},{6,4},{8,10},{10,8},{12,14},{14,12},{16,18},{18,... | collective-permute-start | bytes 1572872 | tf_op jit(solution)/shard_map/ppermute | solution.py:333
  43.8 15.1 %collective-permute-start.15 = (bf16[16,128,128]{2,1,0:T(8,128)(2,1)S(1)}, bf16[16,128,128]{2,1,0:T(8,128)(2,1)S(1)}, u32[]{:S(2)}, u32[]{:S(2)}) collective-permute-start(bf16[16,128,128]{2,1,0:T(8,128)(2,1)S(1)} %collective-permute-done.5.refs_6_), channel_id=1, source_target_pairs={{0,2},{2,0},{4,6},{6,4},{8,10},{10,8},{12,14},{14,12},{16,18},{18,... | collective-permute-start | bytes 1572872 | tf_op jit(solution)/shard_map/ppermute | solution.py:333
  48.3 31.0 %collective-permute-start.19 = (bf16[768,512]{1,0:T(8,128)(2,1)}, bf16[768,512]{1,0:T(8,128)(2,1)S(1)}, u32[]{:S(2)}, u32[]{:S(2)}) collective-permute-start(bf16[768,512]{1,0:T(8,128)(2,1)} %get-tuple-element.85), channel_id=1, source_target_pairs={{0,1},{1,0},{2,3},{3,2},{4,5},{5,4},{6,7},{7,6},{8,9},{9,8},{10,11... | collective-permute-start | bytes 2359304 | tf_op jit(solution)/shard_map/ppermute | solution.py:345
  49.9 39.4 %collective-permute-start.18 = (bf16[768,512]{1,0:T(8,128)(2,1)}, bf16[768,512]{1,0:T(8,128)(2,1)S(1)}, u32[]{:S(2)}, u32[]{:S(2)}) collective-permute-start(bf16[768,512]{1,0:T(8,128)(2,1)} %get-tuple-element.86), channel_id=1, source_target_pairs={{0,1},{1,0},{2,3},{3,2},{4,5},{5,4},{6,7},{7,6},{8,9},{9,8},{10,11... | collective-permute-start | bytes 2359304 | tf_op jit(solution)/shard_map/ppermute | solution.py:345
  102.2 9.0 %collective-permute-start.20 = (bf16[1,16,128,128]{3,2,1,0:T(8,128)(2,1)}, bf16[1,16,128,128]{3,2,1,0:T(8,128)(2,1)S(1)}, u32[]{:S(2)}, u32[]{:S(2)}) collective-permute-start(bf16[1,16,128,128]{3,2,1,0:T(8,128)(2,1)} %get-tuple-element.44), channel_id=1, source_target_pairs={{0,2},{2,0},{4,6},{6,4},{8,10},{10,8},{12,14},{14,12},{16,18},{18,... | collective-permute-start | bytes 1572872 | tf_op jit(solution)/shard_map/ppermute | solution.py:333
  110.9 19.1 %collective-permute-start.23 = (bf16[2,16,128,128]{3,2,1,0:T(8,128)(2,1)}, bf16[2,16,128,128]{3,2,1,0:T(8,128)(2,1)S(1)}, u32[]{:S(2)}, u32[]{:S(2)}) collective-permute-start(bf16[2,16,128,128]{3,2,1,0:T(8,128)(2,1)} %get-tuple-element.53), channel_id=1, source_target_pairs={{0,2},{2,0},{4,6},{6,4},{8,10},{10,8},{12,14},{14,12},{16,18},{18,... | collective-permute-start | bytes 3145736 | tf_op jit(solution)/shard_map/ppermute | solution.py:333
  111.4 18.8 %collective-permute-start.24 = (bf16[8,128,128]{2,1,0:T(8,128)(2,1)S(1)}, bf16[8,128,128]{2,1,0:T(8,128)(2,1)S(1)}, u32[]{:S(2)}, u32[]{:S(2)}) collective-permute-start(bf16[8,128,128]{2,1,0:T(8,128)(2,1)S(1)} %get-tuple-element.54), channel_id=1, source_target_pairs={{0,8},{2,10},{8,16},{10,18},{16,24},{18,26},{24,28},{26,30},{28,20... | collective-permute-start | bytes 786440 | tf_op jit(solution)/shard_map/ppermute | solution.py:333
  112.0 18.2 %collective-permute-start.25 = (bf16[8,128,128]{2,1,0:T(8,128)(2,1)S(1)}, bf16[8,128,128]{2,1,0:T(8,128)(2,1)S(1)}, u32[]{:S(2)}, u32[]{:S(2)}) collective-permute-start(bf16[8,128,128]{2,1,0:T(8,128)(2,1)S(1)} %get-tuple-element.55), channel_id=1, source_target_pairs={{0,4},{2,6},{8,0},{10,2},{16,8},{18,10},{24,16},{26,18},{28,24},{3... | collective-permute-start | bytes 786440 | tf_op jit(solution)/shard_map/ppermute | solution.py:333
  129.4 16.8 %collective-permute-start.22 = (bf16[2,16,128,128]{3,2,1,0:T(8,128)(2,1)}, bf16[2,16,128,128]{3,2,1,0:T(8,128)(2,1)S(1)}, u32[]{:S(2)}, u32[]{:S(2)}) collective-permute-start(bf16[2,16,128,128]{3,2,1,0:T(8,128)(2,1)} %get-tuple-element.51), channel_id=1, source_target_pairs={{0,2},{2,0},{4,6},{6,4},{8,10},{10,8},{12,14},{14,12},{16,18},{18,... | collective-permute-start | bytes 3145736 | tf_op jit(solution)/shard_map/ppermute | solution.py:333
  129.4 30.8 %collective-permute-start.21 = (bf16[3,16,128,128]{3,2,1,0:T(8,128)(2,1)}, bf16[3,16,128,128]{3,2,1,0:T(8,128)(2,1)S(1)}, u32[]{:S(2)}, u32[]{:S(2)}) collective-permute-start(bf16[3,16,128,128]{3,2,1,0:T(8,128)(2,1)} %get-tuple-element.49), channel_id=1, source_target_pairs={{0,2},{2,0},{4,6},{6,4},{8,10},{10,8},{12,14},{14,12},{16,18},{18,... | collective-permute-start | bytes 4718600 | tf_op jit(solution)/shard_map/ppermute | solution.py:333
  130.4 9.2 %collective-permute-start.26 = (bf16[8,128,128]{2,1,0:T(8,128)(2,1)S(1)}, bf16[8,128,128]{2,1,0:T(8,128)(2,1)S(1)}, u32[]{:S(2)}, u32[]{:S(2)}) collective-permute-start(bf16[8,128,128]{2,1,0:T(8,128)(2,1)S(1)} %get-tuple-element.56), channel_id=1, source_target_pairs={{0,8},{2,10},{8,16},{10,18},{16,24},{18,26},{24,28},{26,30},{28,20... | collective-permute-start | bytes 786440 | tf_op jit(solution)/shard_map/ppermute | solution.py:333
  130.9 13.4 %collective-permute-start.27 = (bf16[8,128,128]{2,1,0:T(8,128)(2,1)S(1)}, bf16[8,128,128]{2,1,0:T(8,128)(2,1)S(1)}, u32[]{:S(2)}, u32[]{:S(2)}) collective-permute-start(bf16[8,128,128]{2,1,0:T(8,128)(2,1)S(1)} %get-tuple-element.57), channel_id=1, source_target_pairs={{0,8},{2,10},{8,16},{10,18},{16,24},{18,26},{24,28},{26,30},{28,20... | collective-permute-start | bytes 786440 | tf_op jit(solution)/shard_map/ppermute | solution.py:333
  132.1 12.3 %collective-permute-start.28 = (bf16[8,128,128]{2,1,0:T(8,128)(2,1)S(1)}, bf16[8,128,128]{2,1,0:T(8,128)(2,1)S(1)}, u32[]{:S(2)}, u32[]{:S(2)}) collective-permute-start(bf16[8,128,128]{2,1,0:T(8,128)(2,1)S(1)} %get-tuple-element.58), channel_id=1, source_target_pairs={{0,4},{2,6},{8,0},{10,2},{16,8},{18,10},{24,16},{26,18},{28,24},{3... | collective-permute-start | bytes 786440 | tf_op jit(solution)/shard_map/ppermute | solution.py:333
  147.4 10.7 %collective-permute-start.31 = (bf16[8,128,128]{2,1,0:T(8,128)(2,1)S(1)}, bf16[8,128,128]{2,1,0:T(8,128)(2,1)S(1)}, u32[]{:S(2)}, u32[]{:S(2)}) collective-permute-start(bf16[8,128,128]{2,1,0:T(8,128)(2,1)S(1)} %get-tuple-element.61), channel_id=1, source_target_pairs={{0,8},{2,10},{8,16},{10,18},{16,24},{18,26},{24,28},{26,30},{28,20... | collective-permute-start | bytes 786440 | tf_op jit(solution)/shard_map/ppermute | solution.py:333
  149.0 9.1 %collective-permute-start.32 = (bf16[8,128,128]{2,1,0:T(8,128)(2,1)S(1)}, bf16[8,128,128]{2,1,0:T(8,128)(2,1)S(1)}, u32[]{:S(2)}, u32[]{:S(2)}) collective-permute-start(bf16[8,128,128]{2,1,0:T(8,128)(2,1)S(1)} %get-tuple-element.62), channel_id=1, source_target_pairs={{0,4},{2,6},{8,0},{10,2},{16,8},{18,10},{24,16},{26,18},{28,24},{3... | collective-permute-start | bytes 786440 | tf_op jit(solution)/shard_map/ppermute | solution.py:333
  149.4 10.8 %collective-permute-start.33 = (bf16[8,128,128]{2,1,0:T(8,128)(2,1)S(1)}, bf16[8,128,128]{2,1,0:T(8,128)(2,1)S(1)}, u32[]{:S(2)}, u32[]{:S(2)}) collective-permute-start(bf16[8,128,128]{2,1,0:T(8,128)(2,1)S(1)} %get-tuple-element.63), channel_id=1, source_target_pairs={{0,4},{2,6},{8,0},{10,2},{16,8},{18,10},{24,16},{26,18},{28,24},{3... | collective-permute-start | bytes 786440 | tf_op jit(solution)/shard_map/ppermute | solution.py:333
  (35 other events, 412.8 us)
